TPU v7x, 32 devices: a whole 2x2x4 slice. The times are simulated.
32 devices in a mesh: dp: 8 (over z, y), tensor: 4 (over x, core).
Axes of the slice: x: 2, y: 2, z: 4, core: 2. Of those that a mesh axis runs over, the one named last changes fastest.
Arguments:
- prefill_rows: bfloat16 [4096, 2048], P(('dp', 'tensor')), may hold values from -6 to 6
- decode_rows: bfloat16 [64, 2048], P(('dp', 'tensor')), may hold values from -6 to 6
- deal_order: int32 [64], replicated, may hold values from 0 to 63, each once
- prefill_offset: int32 [8], P('dp'), may hold values from 0 to 1024, as said below
- cache_length: int32 [64], P('dp'), may hold values from 1 to 1024, as said below
- prefill_cache: bfloat16 [2, 8, 1024, 1024], P(None, 'dp', None, 'tensor'), may hold values from -480 to 480, as said below
- decode_cache: bfloat16 [2, 64, 1024, 1024], P(None, 'dp', None, 'tensor'), may hold values from -480 to 480, as said below
- qkv_weight: bfloat16 [2048, 8, 512], P(None, 'tensor'), may hold values from -0.125 to 0.125
- out_weight: bfloat16 [2048, 2048], P('tensor'), may hold values from -0.125 to 0.125
- attention_gain: float32 [2048], replicated, may hold values from 0.1 to 1.9
- forward_gain: float32 [2048], replicated, may hold values from 0.1 to 1.9
- gate_weight: bfloat16 [2048, 8192], P(None, 'tensor'), may hold values from -0.125 to 0.125
- up_weight: bfloat16 [2048, 8192], P(None, 'tensor'), may hold values from -0.125 to 0.125
- down_weight: bfloat16 [8192, 2048], P('tensor'), may hold values from -0.0625 to 0.0625
Outputs:
- prefill_out: bfloat16 [4096, 2048], P(('dp', 'tensor'))
- decode_out: bfloat16 [64, 2048], P(('dp', 'tensor'))
- prefill_entries: bfloat16 [2, 4096, 1024], P(None, 'dp', 'tensor')
- decode_entries: bfloat16 [2, 64, 1024], P(None, 'dp', 'tensor')
Inputs may be any that keep to these rules, and one draw needn't show every extreme that they name: A permutation: request r is held in slot deal_order[r]; slot s belongs to request group s // 8. `prefill_offset`: stored positions of each prefill request; some request has exactly 1024. `cache_length`: stored positions of the decode request in each slot; some slot has exactly 1024. `prefill_cache`: stored rotated keys and values; positions at or past a request's stored count hold unrelated numbers. `decode_cache`: stored rotated keys and values; positions at or past a slot's stored count hold unrelated numbers.
All inputs are finite; a program needn't handle non-finite values.
Results may differ from a plain program's by a relative error of at most 0.015.
The roundings to bfloat16 on the way count: a program that leaves them out, or rounds other values in their place, can miss the bound.
Values may be sent and summed in bfloat16 or wider, within the bound.
No kernel may reach another device: no remote copies, remote signals or barrier semaphores. Data moves between devices by JAX's collectives and lax.ppermute only.
A program may use at most 128 MiB of HBM per device.

v0:
```python
import math

import jax
import jax.numpy as jnp
from jax import lax
from jax.sharding import PartitionSpec as P

HD = 128


EPSILON = 1e-06
THETA = 1000000.0
NEGATIVE = -1e30


def root_norm(rows, gain):
    values = rows.astype(jnp.float32)
    spread = jnp.mean(values * values, axis=-1, keepdims=True)
    return (values * lax.rsqrt(spread + EPSILON) * gain).astype(jnp.bfloat16)


def rotate(vectors, places):
    halfway = vectors.shape[-1] // 2
    powers = jnp.arange(halfway, dtype=jnp.float32) * (2.0 / vectors.shape[-1])
    inverse = THETA ** (-powers)
    angles = places.astype(jnp.float32)[:, None] * inverse[None, :]
    cosine = jnp.cos(angles)[:, None, :]
    sine_part = jnp.sin(angles)[:, None, :]
    leading = vectors[..., :halfway]
    trailing = vectors[..., halfway:]
    return jnp.concatenate(
        [leading * cosine - trailing * sine_part, trailing * cosine + leading * sine_part], axis=-1
    )


def project(normed, places, qkv_weight):
    heads = qkv_weight.shape[1]
    width = qkv_weight.shape[2]
    groups = width // HD - 2
    count = normed.shape[0]
    mixed = jnp.dot(
        normed,
        qkv_weight.reshape(qkv_weight.shape[0], heads * width),
        preferred_element_type=jnp.float32,
    )
    mixed = mixed.reshape(count, heads, groups + 2, HD)
    queries = rotate(mixed[:, :, :groups].reshape(count, heads * groups, HD), places)
    queries = queries.reshape(count, heads, groups, HD).astype(jnp.bfloat16)
    new_keys = rotate(mixed[:, :, groups], places).astype(jnp.bfloat16)
    new_values = mixed[:, :, groups + 1].astype(jnp.bfloat16)
    return (queries, new_keys, new_values)


def fill_attend(queries, new_keys, new_values, cache_keys, cache_values, offset):
    scaling = 1.0 / math.sqrt(HD)
    count = queries.shape[0]
    prior_count = cache_keys.shape[0]
    cached_scores = (
        jnp.einsum("qkgd,skd->kgqs", queries, cache_keys, preferred_element_type=jnp.float32)
        * scaling
    )
    fresh_scores = (
        jnp.einsum("qkgd,skd->kgqs", queries, new_keys, preferred_element_type=jnp.float32)
        * scaling
    )
    cached_allowed = jnp.arange(prior_count, dtype=jnp.int32)[None, :] < offset
    fresh_allowed = (
        jnp.arange(count, dtype=jnp.int32)[None, :] <= jnp.arange(count, dtype=jnp.int32)[:, None]
    )
    scores = jnp.concatenate(
        [
            jnp.where(cached_allowed, cached_scores, NEGATIVE),
            jnp.where(fresh_allowed, fresh_scores, NEGATIVE),
        ],
        axis=-1,
    )
    row_top = jnp.max(scores, axis=-1, keepdims=True)
    weights = jnp.exp(scores - row_top)
    weights = (weights / jnp.sum(weights, axis=-1, keepdims=True)).astype(jnp.bfloat16)
    attended = jnp.einsum(
        "kgqs,skd->qkgd",
        weights[..., :prior_count],
        cache_values,
        preferred_element_type=jnp.float32,
    )
    attended = attended + jnp.einsum(
        "kgqs,skd->qkgd", weights[..., prior_count:], new_values, preferred_element_type=jnp.float32
    )
    return attended.astype(jnp.bfloat16)


def step_attend(queries, new_keys, new_values, cache_keys, cache_values, lengths):
    scaling = 1.0 / math.sqrt(HD)
    stored = cache_keys.shape[1]
    cached_scores = (
        jnp.einsum("nkgd,nskd->nkgs", queries, cache_keys, preferred_element_type=jnp.float32)
        * scaling
    )
    own_scores = (
        jnp.einsum("nkgd,nkd->nkg", queries, new_keys, preferred_element_type=jnp.float32)[
            ..., None
        ]
        * scaling
    )
    allowed = (jnp.arange(stored, dtype=jnp.int32)[None, :] < lengths[:, None])[:, None, None, :]
    scores = jnp.concatenate([jnp.where(allowed, cached_scores, NEGATIVE), own_scores], axis=-1)
    row_top = jnp.max(scores, axis=-1, keepdims=True)
    weights = jnp.exp(scores - row_top)
    weights = (weights / jnp.sum(weights, axis=-1, keepdims=True)).astype(jnp.bfloat16)
    attended = jnp.einsum(
        "nkgs,nskd->nkgd", weights[..., :stored], cache_values, preferred_element_type=jnp.float32
    )
    attended = (
        attended
        + weights[..., stored:].astype(jnp.float32) * new_values.astype(jnp.float32)[:, :, None, :]
    )
    return attended.astype(jnp.bfloat16)


def feed_forward(inner, gate_weight, up_weight, down_weight):
    gate_part = jnp.dot(inner, gate_weight, preferred_element_type=jnp.float32)
    up_part = jnp.dot(inner, up_weight, preferred_element_type=jnp.float32)
    hidden = (jax.nn.silu(gate_part) * up_part).astype(jnp.bfloat16)
    return jnp.dot(hidden, down_weight, preferred_element_type=jnp.float32)


def on_device(
    prefill_rows,
    decode_rows,
    deal_order,
    prefill_offset,
    cache_length,
    prefill_cache,
    decode_cache,
    qkv_weight,
    out_weight,
    attention_gain,
    forward_gain,
    gate_weight,
    up_weight,
    down_weight,
):
    tensor_count = lax.axis_size("tensor")
    tensor_place = lax.axis_index("tensor")
    group_place = lax.axis_index("dp")
    per_device = decode_rows.shape[0]
    share_rows = prefill_rows.shape[0]
    everyone = lax.all_gather(decode_rows, ("dp", "tensor"), axis=0, tiled=True)
    first_slot = (group_place * tensor_count + tensor_place) * per_device
    my_slots = first_slot + jnp.arange(per_device, dtype=jnp.int32)
    chooser = (deal_order[None, :] == my_slots[:, None]).astype(jnp.bfloat16)
    dealt = jnp.dot(chooser, everyone, preferred_element_type=jnp.float32).astype(jnp.bfloat16)
    fill_raw, step_raw = (
        lax.all_gather(prefill_rows, "tensor", axis=0, tiled=True),
        lax.all_gather(dealt, "tensor", axis=0, tiled=True),
    )
    fill_normed = root_norm(fill_raw, attention_gain)
    step_normed = root_norm(step_raw, attention_gain)
    total_tokens = fill_normed.shape[0]
    slot_group = step_normed.shape[0]
    local_heads = qkv_weight.shape[1]
    fill_places = prefill_offset[0] + jnp.arange(total_tokens, dtype=jnp.int32)
    fill_query, fill_keys, fill_values = project(fill_normed, fill_places, qkv_weight)
    step_query, step_keys, step_values = project(step_normed, cache_length, qkv_weight)
    prior_count = prefill_cache.shape[2]
    fill_att = fill_attend(
        fill_query,
        fill_keys,
        fill_values,
        prefill_cache[0, 0].reshape(prior_count, local_heads, HD),
        prefill_cache[1, 0].reshape(prior_count, local_heads, HD),
        prefill_offset[0],
    )
    stored = decode_cache.shape[2]
    step_att = step_attend(
        step_query,
        step_keys,
        step_values,
        decode_cache[0].reshape(slot_group, stored, local_heads, HD),
        decode_cache[1].reshape(slot_group, stored, local_heads, HD),
        cache_length,
    )
    fill_part = jnp.dot(
        fill_att.reshape(total_tokens, -1), out_weight, preferred_element_type=jnp.float32
    )
    step_part = jnp.dot(
        step_att.reshape(slot_group, -1), out_weight, preferred_element_type=jnp.float32
    )
    fill_sum, step_sum = lax.psum((fill_part, step_part), "tensor")
    fill_resid = (fill_raw.astype(jnp.float32) + fill_sum).astype(jnp.bfloat16)
    step_resid = (step_raw.astype(jnp.float32) + step_sum).astype(jnp.bfloat16)
    fill_inner = root_norm(fill_resid, forward_gain)
    step_inner = root_norm(step_resid, forward_gain)
    fill_keep = lax.dynamic_slice_in_dim(fill_resid, tensor_place * share_rows, share_rows, 0)
    step_keep = lax.dynamic_slice_in_dim(step_resid, tensor_place * per_device, per_device, 0)
    fill_more = feed_forward(fill_inner, gate_weight, up_weight, down_weight)
    step_more = feed_forward(step_inner, gate_weight, up_weight, down_weight)
    fill_add, step_add = (
        lax.psum_scatter(
            fill_more.astype(jnp.bfloat16), "tensor", scatter_dimension=0, tiled=True
        ).astype(jnp.float32),
        lax.psum_scatter(
            step_more.astype(jnp.bfloat16), "tensor", scatter_dimension=0, tiled=True
        ).astype(jnp.float32),
    )
    prefill_out = (fill_keep.astype(jnp.float32) + fill_add).astype(jnp.bfloat16)
    step_final = (step_keep.astype(jnp.float32) + step_add).astype(jnp.bfloat16)
    every_slot = lax.all_gather(step_final, ("dp", "tensor"), axis=0, tiled=True)
    wanted = lax.dynamic_slice_in_dim(deal_order, first_slot, per_device, 0)
    picker = (wanted[:, None] == jnp.arange(every_slot.shape[0], dtype=jnp.int32)[None, :]).astype(
        jnp.bfloat16
    )
    decode_out = jnp.dot(picker, every_slot, preferred_element_type=jnp.float32).astype(
        jnp.bfloat16
    )
    prefill_entries = jnp.stack(
        [
            fill_keys.reshape(total_tokens, local_heads * HD),
            fill_values.reshape(total_tokens, local_heads * HD),
        ]
    )
    decode_entries = jnp.stack(
        [
            step_keys.reshape(slot_group, local_heads * HD),
            step_values.reshape(slot_group, local_heads * HD),
        ]
    )
    return (prefill_out, decode_out, prefill_entries, decode_entries)


def solution(mesh):
    placed = (
        P(("dp", "tensor"), None),
        P(("dp", "tensor"), None),
        P(),
        P("dp"),
        P("dp"),
        P(None, "dp", None, "tensor"),
        P(None, "dp", None, "tensor"),
        P(None, "tensor", None),
        P("tensor", None),
        P(),
        P(),
        P(None, "tensor"),
        P(None, "tensor"),
        P("tensor", None),
    )
    return jax.shard_map(
        on_device,
        mesh=mesh,
        in_specs=placed,
        out_specs=(
            P(("dp", "tensor"), None),
            P(("dp", "tensor"), None),
            P(None, "dp", "tensor"),
            P(None, "dp", "tensor"),
        ),
        check_vma=False,
    )
```

profile of v0, /device:TPU:0, one launch (start us, length us, event | category | flops | bytes accessed | tf_op | source)
XLA Modules:
  0.0 324.7 jit_solution(14492199741888575668)
XLA Ops:
  8.0 44.5 %all-gather = bf16[32,2,2048]{2,1,0:T(2,128)(2,1)S(1)} all-gather(bf16[1,2,2048]{2,1,0:T(2,128)(2,1)} %bitcast.135), channel_id=1, replica_groups=mesh['dp'=8,'tensor'=4] {'dp','tensor'}, dimensions={0}, use_global_device_ids=true | all-gather | bytes 270336 | tf_op jit(solution)/shard_map/all_gather | solution.py:148
  53.5 5.2 %all-gather.1 = bf16[4,2,2048]{2,1,0:T(2,128)(2,1)S(1)} all-gather(bf16[1,2,2048]{2,1,0:T(2,128)(2,1)S(1)} %fusion.12), channel_id=1, replica_groups=mesh['dp'=8,'tensor'=4] {'tensor'}, dimensions={0}, use_global_device_ids=true | all-gather | bytes 40960 | tf_op jit(solution)/shard_map/all_gather | solution.py:155
  58.8 5.4 %copy.138 = bf16[256,8,2,512]{3,1,2,0:T(8,128)(2,1)} copy(bf16[256,8,2,512]{3,2,1,0:T(2,128)(2,1)} %bitcast.123) | data formatting | bytes 8388608
  64.2 6.5 %copy.90 = bf16[1024,2048]{1,0:T(8,128)(2,1)} copy(bf16[1024,2048]{0,1:T(8,128)(2,1)} %bitcast.121) | data formatting | bytes 8388608 | tf_op jit(solution)/shard_map/dot_general | solution.py:41
  70.6 3.4 %fusion.51 = f32[8,2,4,128]{3,0,2,1:T(8,128)S(1)} fusion(bf16[2,4,128,2048]{3,2,1,0:T(8,128)(2,1)} %bitcast.118, f32[8,2048]{1,0:T(8,128)S(1)} %reshape.268, f32[2048]{0:T(1024)S(1)} %copy-done.9, f32[8]{0:T(128)S(1)} %add_rsqrt_fusion.3), kind=kOutput, calls=%fused_computation.77 | convolution fusion | flops 33603584 | bytes 4300832 | tf_op jit(solution)/shard_map/dot_general | solution.py:41
  74.4 5.8 %fusion.72 = (bf16[1,8,1024,256]{3,2,1,0:T(8,128)(2,1)}, bf16[1,8,1024,256]{3,2,1,0:T(8,128)(2,1)}) fusion(bf16[2,8,1024,256]{3,2,1,0:T(8,128)(2,1)} %param.20), kind=kLoop, calls=%fused_computation.118 | loop fusion | bytes 16777216 | tf_op jit(solution)/shard_map/slice | solution.py:179
  80.2 6.5 %copy.132 = bf16[1,8,1024,256]{2,3,1,0:T(8,128)(2,1)} copy(bf16[1,8,1024,256]{3,2,1,0:T(8,128)(2,1)} %get-tuple-element.10) | data formatting | bytes 8388608
  87.0 3.0 fusion.76
  90.8 6.5 %copy.133 = bf16[1,8,1024,256]{2,3,1,0:T(8,128)(2,1)} copy(bf16[1,8,1024,256]{3,2,1,0:T(8,128)(2,1)} %get-tuple-element.11) | data formatting | bytes 8388608
  97.4 3.4 %fusion.33 = bf16[8,2,2,128]{3,2,1,0:T(2,128)(2,1)S(1)} fusion(bf16[8,1024,2,128]{1,3,2,0:T(8,128)(2,1)} %bitcast.124, bf16[8,2,2,1024]{3,0,2,1:T(8,128)(2,1)S(1)} %slice.103, f32[8,2,128]{2,1,0:T(2,128)S(1)} %copy.111, f32[8,2,2]{2,1,0:T(2,128)S(1)} %bitcast.136), kind=kOutput, calls=%fused_computation.41 | convolution fusion | flops 8400896 | bytes 4276352 | tf_op jit(solution)/shard_map/nkgs,nskd->nkgd/dot_general | solution.py:110
  101.4 2.1 fusion.73
  103.5 1.2 copy.131
  107.1 1.0 fusion.81
  108.1 2.1 fusion.5
  110.2 5.3 %fusion.14 = f32[512,2,4,128]{0,3,2,1:T(8,128)S(1)} fusion(bf16[2,4,128,2048]{3,2,1,0:T(8,128)(2,1)} %bitcast.119, bf16[512,2048]{1,0:T(8,128)(2,1)} %all-gather.5.cloned.1.call-done, f32[2048]{0:T(1024)S(1)} %copy-done.9, f32[512]{0:T(512)S(1)} %add_rsqrt_fusion.1), kind=kOutput, calls=%fused_computation.29 | convolution fusion | flops 2151677952 | bytes 8398848 | tf_op jit(solution)/shard_map/dot_general | solution.py:41
  115.9 1.6 fusion.74
  117.5 1.0 fusion.75
  118.5 2.3 fusion.1
  120.8 2.6 divide_convert_fusion
  123.4 1.5 fusion.23
  125.7 3.2 fusion.80
  129.0 83.0 %all-reduce.4.cloned.1.call-done = (f32[512,2048]{1,0:T(8,128)}, f32[8,2048]{1,0:T(8,128)}) async-done(((f32[512,2048]{1,0:T(8,128)}, f32[8,2048]{1,0:T(8,128)}), (f32[512,2048]{1,0:T(8,128)}, f32[8,2048]{1,0:T(8,128)})) %all-reduce.4.cloned.1.call-update) | async-done | bytes 4259856 | tf_op jit(solution)/shard_map/psum | solution.py:189
  212.0 2.9 fusion.2
  214.9 1.3 copy-done.3
  216.2 9.6 %fusion.35 = f32[512,2048]{1,0:T(8,128)} fusion(bf16[2048,2048]{1,0:T(8,128)(2,1)} %param.25, bf16[512,2048]{1,0:T(8,128)(2,1)S(1)} %get-tuple-element.9, f32[2048]{0:T(1024)S(1)} %copy-done.7, f32[512]{0:T(512)S(1)} %add_rsqrt_fusion), kind=kOutput, calls=%fused_computation.44 | convolution fusion | flops 4299161600 | bytes 14690304 | tf_op jit(solution)/shard_map/dot_general | solution.py:121
  225.8 18.1 %convolution_convert_fusion = bf16[512,2048]{1,0:T(8,128)(2,1)} fusion(bf16[2048,2048]{1,0:T(8,128)(2,1)} %param.27, f32[512,2048]{1,0:T(8,128)} %fusion.35, bf16[2048,2048]{1,0:T(8,128)(2,1)} %param.26, bf16[512,2048]{1,0:T(8,128)(2,1)} %copy-done.3, f32[2048]{0:T(1024)S(1)} %copy-done.7, f32[512]{0:T(512)S(1)} %add_rsqrt_fusion), kind=kOutput, calls=%fused_computation.21 | convolution fusion | flops 8601468928 | bytes 25176064 | tf_op jit(solution)/shard_map/dot_general | solution.py:124
  245.9 1.1 slice.143
  248.3 5.2 %fusion.61 = f32[8,2048]{1,0:T(8,128)S(1)} fusion(bf16[2048,2048]{1,0:T(8,128)(2,1)} %param.25, bf16[8,2048]{1,0:T(8,128)(2,1)S(1)} %get-tuple-element.7, f32[2048]{0:T(1024)S(1)} %copy-done.7, f32[8]{0:T(128)S(1)} %add_rsqrt_fusion.2), kind=kOutput, calls=%fused_computation.100 | convolution fusion | flops 67174400 | bytes 8495136 | tf_op jit(solution)/shard_map/dot_general | solution.py:121
  253.4 8.2 %convolution_convert_fusion.1 = bf16[8,2048]{1,0:T(8,128)(2,1)S(1)} fusion(bf16[2048,2048]{1,0:T(8,128)(2,1)} %param.27, bf16[2048,2048]{1,0:T(8,128)(2,1)} %param.26, f32[8,2048]{1,0:T(8,128)S(1)} %fusion.61, bf16[8,2048]{1,0:T(8,128)(2,1)S(1)} %get-tuple-element.7, f32[2048]{0:T(1024)S(1)} %copy-done.7, f32[8]{0:T(128)S(1)} %add_rsqrt_fusion.2), kind=kOutput, calls=%fused_computation.24 | convolution fusion | flops 134397952 | bytes 16916512 | tf_op jit(solution)/shard_map/dot_general | solution.py:124
  261.7 11.6 %all-reduce = bf16[8,2048]{1,0:T(8,128)(2,1)S(1)} all-reduce(bf16[8,2048]{1,0:T(8,128)(2,1)S(1)} %convolution_convert_fusion.1), channel_id=3, replica_groups=mesh['dp'=8,'tensor'=4] {'tensor'}, use_global_device_ids=true, to_apply=%region_12.13.clone | all-reduce | flops 16384 | bytes 65536
  273.3 41.8 %all-gather.2 = bf16[32,2,2048]{2,1,0:T(2,128)(2,1)S(1)} all-gather(bf16[1,2,2048]{2,1,0:T(2,128)(2,1)S(1)} %fusion.56), channel_id=1, replica_groups=mesh['dp'=8,'tensor'=4] {'dp','tensor'}, dimensions={0}, use_global_device_ids=true | all-gather | bytes 270336 | tf_op jit(solution)/shard_map/all_gather | solution.py:208
  316.0 2.1 add_convert_fusion
  (90 shorter events, 10.7 us)
Async XLA Ops:
  7.2 99.9 %copy-start = (bf16[512,2048]{1,0:T(8,128)(2,1)S(1)}, bf16[512,2048]{1,0:T(8,128)(2,1)}, u32[]{:S(2)}) copy-start(bf16[512,2048]{1,0:T(8,128)(2,1)} %param.22) | copy-start | bytes 6291460
  7.2 100.9 %all-gather.5.cloned.1.call-start = ((), (), s32[]{:S(2)}) async-start(), calls=%async_computation.1 | async-start | bytes 2621440 | tf_op jit(solution)/shard_map/all_gather | solution.py:154
  7.9 204.1 %all-reduce.4.cloned.1.call-start = ((), (), s32[]{:S(2)}) async-start(), calls=%async_computation.3 | async-start | bytes 8519680 | tf_op jit(solution)/shard_map/psum | solution.py:189
  64.2 6.5 %copy-start.9 = (f32[2048]{0:T(1024)S(1)}, f32[2048]{0:T(1024)}, u32[]{:S(2)}) copy-start(f32[2048]{0:T(1024)} %param.23) | copy-start | bytes 24580
  70.6 3.4 %copy-start.10 = (s32[8]{0:T(128)S(1)}, s32[8]{0:T(128)}, u32[]{:S(2)}) copy-start(s32[8]{0:T(128)} %param.18) | copy-start | bytes 100
  115.4 9.4 %copy-start.4 = (f32[512,2,4,128]{0,3,2,1:T(8,128)}, f32[512,2,4,128]{0,3,2,1:T(8,128)S(1)}, u32[]{:S(2)}) copy-start(f32[512,2,4,128]{0,3,2,1:T(8,128)S(1)} %fusion.14) | copy-start | bytes 6291460
  115.9 1.6 copy-start.6
  120.8 2.6 copy-start.5
  128.9 83.0 %copy-start.2 = (bf16[512,2048]{1,0:T(8,128)(2,1)S(1)}, bf16[512,2048]{1,0:T(8,128)(2,1)}, u32[]{:S(2)}) copy-start(bf16[512,2048]{1,0:T(8,128)(2,1)} %all-gather.5.cloned.1.call-done) | copy-start | bytes 6291460
  129.0 187.0 %reduce-scatter.2.cloned.1.call-start = ((), (), s32[]{:S(2)}) async-start(), calls=%async_computation.2 | async-start | bytes 2621440 | tf_op jit(solution)/shard_map/reduce_scatter | solution.py:199
  212.0 4.2 %copy-start.7 = (f32[2048]{0:T(1024)S(1)}, f32[2048]{0:T(1024)}, u32[]{:S(2)}) copy-start(f32[2048]{0:T(1024)} %param.24) | copy-start | bytes 24580
  214.9 1.3 copy-start.3
  225.8 18.1 %copy-start.11 = (s32[64]{0:T(128)S(1)}, s32[64]{0:T(128)}, u32[]{:S(2)}) copy-start(s32[64]{0:T(128)} %param.16) | copy-start | bytes 772
  225.8 18.2 %copy-start.12 = (u32[32]{0:T(128)S(1)}, u32[32]{0:T(128)}, u32[]{:S(2)}) copy-start(u32[32]{0:T(128)} %constant.59) | copy-start | bytes 388
  243.8 4.3 %copy-start.8 = (f32[8,2048]{1,0:T(8,128)S(1)}, f32[8,2048]{1,0:T(8,128)}, u32[]{:S(2)}) copy-start(f32[8,2048]{1,0:T(8,128)} %get-tuple-element.5) | copy-start | bytes 196612
  253.4 64.7 %copy-start.1 = (bf16[512,2048]{1,0:T(8,128)(2,1)S(1)}, bf16[512,2048]{1,0:T(8,128)(2,1)}, u32[]{:S(2)}) copy-start(bf16[512,2048]{1,0:T(8,128)(2,1)} %param.22) | copy-start | bytes 6291460
Sparse Core Ops, SparseCore 0:
  9.6 26.3 all-gather.4
  129.1 82.8 all-reduce.3
  244.0 32.2 reduce-scatter.1
where the time goes:
time: 326 us; the launch traced here: 325 us
  blocking collectives  103 us (32%)
  waiting for transfers between devices  83.7 us (26%)
  matrix products  67 us (21%)
  local copies, waits for them, and re-layouts  39.2 us (12%)
  other arithmetic  16.2 us (5%)
  between operations  15.4 us (5%)
    psum x1, waiting for transfers between devices, on_device(): fill_sum, step_sum = lax.psum((fill_part, step_part), 'tensor')  83 us
    all_gather x1, blocking collectives, on_device(): everyone = lax.all_gather(decode_rows, ('dp', 'tensor'), axis=0, tiled=True)  44.5 us
    all_gather x1, blocking collectives, on_device(): lax.all_gather(step_final, ('dp', 'tensor'), axis=0, tiled=True)  41.8 us
    dot_general x2, matrix products, feed_forward(): return jnp.dot(hidden, down_weight, preferred_element_type=jnp.float32)  26.3 us
    unnamed x35, local copies, waits for them, and re-layouts  22 us
    dot_general x2, matrix products, feed_forward(): gate_part = jnp.dot(inner, gate_weight, preferred_element_type=jnp.float32)  14.8 us
    unnamed x1, blocking collectives  11.6 us
    dot_general x2, matrix products, project(): jnp.dot(normed, qkv_weight.reshape(qkv_weight.shape[0], heads * width), p...  8.64 us
  transfers between devices with their start and end apart: 3, of which 1 were waited for; matrix products, arithmetic and copies ran while one was open for 21% of the time, Pallas kernels for 0%

commit v1 on v0

v1 whole, which is shorter than its diff:
```python
import functools
import math

import jax
import jax.numpy as jnp
from jax import lax
from jax.experimental import pallas as pl
from jax.experimental.pallas import tpu as pltpu
from jax.sharding import PartitionSpec as P

HD = 128
EPSILON = 1e-06
THETA = 1000000.0
NEGATIVE = -1e30
MIB = 1 << 20


def swap_cores(value):
    count = lax.axis_size("tensor")
    return lax.ppermute(value, "tensor", [(i, i ^ 1) for i in range(count)])


def from_chip(value, step):
    count = lax.axis_size("tensor")
    chips = count // 2
    return lax.ppermute(
        value, "tensor", [(i, (i // 2 - step) % chips * 2 + i % 2) for i in range(count)]
    )


def swap_groups(value, mask):
    count = lax.axis_size("dp")
    return lax.ppermute(value, "dp", [(i, i ^ mask) for i in range(count)])


def whole(shape):
    return pl.BlockSpec(shape, lambda *_: (0,) * len(shape))


def params(mib):
    return pltpu.CompilerParams(vmem_limit_bytes=mib * MIB)


def cost(flops, moved, exps=0):
    return pl.CostEstimate(flops=int(flops), bytes_accessed=int(moved), transcendentals=int(exps))


def normed(values, gain):
    spread = jnp.mean(values * values, axis=-1, keepdims=True)
    return (values * lax.rsqrt(spread + EPSILON) * gain).astype(jnp.bfloat16)


def turn(vectors, cosine, sine):
    return vectors * cosine + pltpu.roll(vectors, HD // 2, 1) * sine


def project_kernel(n_dec, groups, place, *refs):
    refs = list(refs)
    mine, sib, gain, weight, cosine, sine = refs[:6]
    refs = refs[6:]
    if n_dec:
        dec, dec_cos, dec_sin = refs[:3]
        refs = refs[4:]
        query, entries, dec_query, dec_entries, inner = refs
    else:
        query, entries, inner = refs
    piece = mine.shape[0]
    core = place[0]

    @pl.when(pl.program_id(0) == 0)
    def _():
        scale = gain[...]
        for ref, at in ((mine, core), (sib, 1 - core)):
            start = pl.multiple_of(at * piece, piece)
            inner[pl.ds(start, piece), :] = normed(ref[...].astype(jnp.float32), scale)
        if n_dec:
            inner[2 * piece :, :] = normed(dec[...].astype(jnp.float32), scale)

    mixed = jnp.dot(inner[...], weight[...], preferred_element_type=jnp.float32)

    def put(rows, cos, sin, query_out, entry_out):
        for g in range(groups):
            part = rows[:, g * HD : (g + 1) * HD]
            query_out[:, g * HD : (g + 1) * HD] = turn(part, cos, sin).astype(jnp.bfloat16)
        key = rows[:, groups * HD : (groups + 1) * HD]
        entry_out[0] = turn(key, cos, sin).astype(jnp.bfloat16)
        entry_out[1] = rows[:, (groups + 1) * HD :].astype(jnp.bfloat16)

    put(mixed[: 2 * piece], cosine[...], sine[...], query, entries)
    if n_dec:
        put(mixed[2 * piece :], dec_cos[...], dec_sin[...], dec_query, dec_entries)


def project(place, mine, sib, gain, weight, tables, total, dec=None, dec_tables=None, entries=None):
    piece, width = mine.shape
    cosine, sine = tables
    depth = weight.shape[1] // total["heads"]
    heads = total["heads"]
    groups = depth // HD - 2
    block = 2 * piece
    n_dec = 0 if dec is None else dec.shape[0]
    at_block = pl.BlockSpec((block, HD), lambda j, s: (s[1], 0))
    in_specs = [
        whole((piece, width)),
        whole((piece, width)),
        whole((1, width)),
        pl.BlockSpec((width, depth), lambda j, s: (0, j)),
        at_block,
        at_block,
    ]
    args = [mine, sib, gain, weight, cosine, sine]
    out_shape = [
        jax.ShapeDtypeStruct((block, heads * groups * HD), jnp.bfloat16),
        jax.ShapeDtypeStruct((2, total["tokens"], heads * HD), jnp.bfloat16),
    ]
    out_specs = [
        pl.BlockSpec((block, groups * HD), lambda j, s: (0, j)),
        pl.BlockSpec((2, block, HD), lambda j, s: (0, s[1], j)),
    ]
    aliases = {}
    if n_dec:
        in_specs += [whole((n_dec, width)), whole((n_dec, HD)), whole((n_dec, HD))]
        args += [dec, *dec_tables]
        out_shape += [
            jax.ShapeDtypeStruct((n_dec, heads * groups * HD), jnp.bfloat16),
            jax.ShapeDtypeStruct((2, n_dec, heads * HD), jnp.bfloat16),
        ]
        out_specs += [
            pl.BlockSpec((n_dec, groups * HD), lambda j, s: (0, j)),
            pl.BlockSpec((2, n_dec, HD), lambda j, s: (0, 0, j)),
        ]
    if entries is not None:
        in_specs.append(pl.BlockSpec(memory_space=pl.ANY))
        args.append(entries)
        aliases = {len(args): 1}
    if n_dec and entries is None or entries is not None and not n_dec:
        kernel = functools.partial(project_kernel_plain, entries is not None, n_dec, groups)
    else:
        kernel = functools.partial(project_kernel, n_dec, groups)
    rows = block + n_dec
    return pl.pallas_call(
        kernel,
        out_shape=out_shape,
        grid_spec=pltpu.PrefetchScalarGridSpec(
            num_scalar_prefetch=1,
            grid=(heads,),
            in_specs=in_specs,
            out_specs=out_specs,
            scratch_shapes=[pltpu.VMEM((rows, width), jnp.bfloat16)],
        ),
        input_output_aliases=aliases,
        compiler_params=params(32),
        cost_estimate=cost(2 * rows * weight.size, 2 * (weight.size + 2 * rows * width)),
        name="project",
    )(place, *args)


def project_kernel_plain(has_entries, n_dec, groups, place, *refs):
    refs = list(refs)
    if has_entries:
        del refs[6]
        project_kernel(0, groups, place, *refs)
    else:
        refs.insert(9, None)
        project_kernel(n_dec, groups, place, *refs)


def fill_kernel(groups, place, query, cache_key, cache_value, new_key, new_value, out):
    scaling = 1.0 / math.sqrt(HD)
    count = query.shape[0]
    stored = cache_key.shape[2]
    fresh = new_key.shape[1]
    offset = place[2]
    start = place[1] * count
    old_seen = lax.broadcasted_iota(jnp.int32, (1, stored), 1) < offset
    new_seen = lax.broadcasted_iota(jnp.int32, (count, fresh), 1) <= (
        lax.broadcasted_iota(jnp.int32, (count, fresh), 0) + start
    )
    across = (((1,), (1,)), ((), ()))
    old_key, old_value = cache_key[0, 0], cache_value[0, 0]
    for g in range(groups):
        rows = query[:, g * HD : (g + 1) * HD]
        old = lax.dot_general(rows, old_key, across, preferred_element_type=jnp.float32)
        new = lax.dot_general(rows, new_key[0], across, preferred_element_type=jnp.float32)
        old = jnp.where(old_seen, old * scaling, NEGATIVE)
        new = jnp.where(new_seen, new * scaling, NEGATIVE)
        top = jnp.maximum(
            jnp.max(old, axis=-1, keepdims=True), jnp.max(new, axis=-1, keepdims=True)
        )
        old = jnp.exp(old - top)
        new = jnp.exp(new - top)
        total = jnp.sum(old, axis=-1, keepdims=True) + jnp.sum(new, axis=-1, keepdims=True)
        mix = jnp.dot(old.astype(jnp.bfloat16), old_value, preferred_element_type=jnp.float32)
        mix += jnp.dot(new.astype(jnp.bfloat16), new_value[0], preferred_element_type=jnp.float32)
        out[:, g * HD : (g + 1) * HD] = (mix / total).astype(jnp.bfloat16)


def fill_attend(place, query, cache, entries, heads):
    count = query.shape[0]
    groups = query.shape[1] // heads // HD
    stored = cache.shape[2]
    fresh = entries.shape[1]
    pairs = count * groups * heads * (stored + fresh)
    return pl.pallas_call(
        functools.partial(fill_kernel, groups),
        out_shape=jax.ShapeDtypeStruct(query.shape, jnp.bfloat16),
        grid_spec=pltpu.PrefetchScalarGridSpec(
            num_scalar_prefetch=1,
            grid=(heads,),
            in_specs=[
                pl.BlockSpec((count, groups * HD), lambda j, s: (0, j)),
                pl.BlockSpec((1, 1, stored, HD), lambda j, s: (0, 0, 0, j)),
                pl.BlockSpec((1, 1, stored, HD), lambda j, s: (1, 0, 0, j)),
                pl.BlockSpec((1, fresh, HD), lambda j, s: (0, 0, j)),
                pl.BlockSpec((1, fresh, HD), lambda j, s: (1, 0, j)),
            ],
            out_specs=pl.BlockSpec((count, groups * HD), lambda j, s: (0, j)),
        ),
        compiler_params=params(32),
        cost_estimate=cost(8 * pairs * HD, 2 * (cache.size + entries.size), pairs),
        name="fill_attend",
    )(place, query, cache, cache, entries, entries)


def step_kernel(heads, groups, lengths, query, cache_key, cache_value, new_key, new_value, out):
    scaling = 1.0 / math.sqrt(HD)
    stored = cache_key.shape[2]
    length = lengths[pl.program_id(0)]
    rows = query[0]
    old_key, old_value = cache_key[0, 0], cache_value[0, 0]
    across = (((1,), (1,)), ((), ()))
    old = lax.dot_general(rows, old_key, across, preferred_element_type=jnp.float32)
    seen = lax.broadcasted_iota(jnp.int32, (1, stored), 1) < length
    old = jnp.where(seen, old * scaling, NEGATIVE)
    own = jnp.sum(
        rows.astype(jnp.float32) * new_key[0].astype(jnp.float32), axis=-1, keepdims=True
    )
    own = own * scaling
    top = jnp.maximum(jnp.max(old, axis=-1, keepdims=True), own)
    old = jnp.exp(old - top)
    own = jnp.exp(own - top)
    total = jnp.sum(old, axis=-1, keepdims=True) + own
    mix = jnp.dot(
        (old / total).astype(jnp.bfloat16), old_value, preferred_element_type=jnp.float32
    )
    mix += (own / total).astype(jnp.bfloat16).astype(jnp.float32) * new_value[0].astype(jnp.float32)
    at = lax.broadcasted_iota(jnp.int32, (rows.shape[0], HD), 0) // groups
    picked = mix[:, :HD]
    for j in range(1, heads):
        picked = jnp.where(at == j, mix[:, j * HD : (j + 1) * HD], picked)
    out[0] = picked.astype(jnp.bfloat16)


def step_attend(lengths, query, cache, entries, slots, heads):
    groups = query.shape[1] // heads // HD
    stored = cache.shape[2]
    width = heads * HD
    pad = 16
    parts = query[:slots].reshape(slots, heads * groups, 1, HD)
    own = (
        jnp.arange(heads * groups, dtype=jnp.int32)[:, None] // groups
        == jnp.arange(heads, dtype=jnp.int32)[None, :]
    )
    spread = jnp.where(own[None, :, :, None], parts, jnp.bfloat16(0.0))
    spread = spread.reshape(slots, heads * groups, width)
    spread = jnp.pad(spread, ((0, 0), (0, pad - heads * groups), (0, 0)))
    new_key = entries[0, :slots].reshape(slots, 1, width)
    new_value = entries[1, :slots].reshape(slots, 1, width)
    out = pl.pallas_call(
        functools.partial(step_kernel, heads, groups),
        out_shape=jax.ShapeDtypeStruct((slots, pad, HD), jnp.bfloat16),
        grid_spec=pltpu.PrefetchScalarGridSpec(
            num_scalar_prefetch=1,
            grid=(slots,),
            in_specs=[
                pl.BlockSpec((1, pad, width), lambda s, n: (s, 0, 0)),
                pl.BlockSpec((1, 1, stored, width), lambda s, n: (0, s, 0, 0)),
                pl.BlockSpec((1, 1, stored, width), lambda s, n: (1, s, 0, 0)),
                pl.BlockSpec((1, 1, width), lambda s, n: (s, 0, 0)),
                pl.BlockSpec((1, 1, width), lambda s, n: (s, 0, 0)),
            ],
            out_specs=pl.BlockSpec((1, pad, HD), lambda s, n: (s, 0, 0)),
        ),
        compiler_params=params(32),
        cost_estimate=cost(64 * cache.size, 2 * cache.size, slots * stored * pad),
        name="step_attend",
    )(lengths, spread, cache, cache, new_key, new_value)
    return out[:, : heads * groups].reshape(slots, heads * groups * HD)


def out_kernel(place, mine, sib, weight, sib_weight, out):
    part = jnp.dot(mine[...], weight[...], preferred_element_type=jnp.float32)
    part += jnp.dot(sib[...], sib_weight[...], preferred_element_type=jnp.float32)
    out[...] = part.astype(jnp.bfloat16)


def out_project(place, mine, sib, weight, sib_weight):
    rows, depth = mine.shape
    half = weight.shape[1] // 2
    return pl.pallas_call(
        out_kernel,
        out_shape=jax.ShapeDtypeStruct((rows, half), jnp.bfloat16),
        grid_spec=pltpu.PrefetchScalarGridSpec(
            num_scalar_prefetch=1,
            grid=(1,),
            in_specs=[
                whole((rows, depth)),
                whole((rows, depth)),
                pl.BlockSpec((depth, half), lambda i, s: (0, s[0])),
                whole((depth, half)),
            ],
            out_specs=whole((rows, half)),
        ),
        compiler_params=params(32),
        cost_estimate=cost(4 * rows * depth * half, 4 * depth * half + 6 * rows * half),
        name="out_project",
    )(place, mine, sib, weight, sib_weight)


def forward_kernel(chips, n_dec, place, *refs):
    refs = list(refs)
    mine, sib = refs[:2]
    shares = refs[2 : 2 + 2 * chips]
    refs = refs[2 + 2 * chips :]
    if n_dec:
        dec, dec_shares = refs[0], refs[1 : 1 + 2 * chips]
        refs = refs[1 + 2 * chips :]
    gain, gate, up, down, keep, give, resid = refs[:7]
    refs = refs[7:]
    if n_dec:
        dec_out, dec_resid = refs[:2]
        refs = refs[2:]
    held, inner, total = refs
    piece = mine.shape[0]
    half = shares[0].shape[1]
    core = place[0]
    step = pl.program_id(0)

    @pl.when(step == 0)
    def _():
        jobs = [(mine, shares, core * piece, 0), (sib, shares, (1 - core) * piece, piece)]
        if n_dec:
            jobs.append((dec, dec_shares, 0, 2 * piece))
        for rows, parts, start, put in jobs:
            size = rows.shape[0]
            if not isinstance(start, int):
                start = pl.multiple_of(start, piece)
            for side in range(2):
                at = core if side == 0 else 1 - core
                cols = pl.ds(pl.multiple_of(at * half, half), half)
                added = parts[side][pl.ds(start, size), :].astype(jnp.float32)
                for k in range(1, chips):
                    added += parts[2 * k + side][pl.ds(start, size), :].astype(jnp.float32)
                value = rows[:, cols].astype(jnp.float32) + added
                held[put : put + size, cols] = value.astype(jnp.bfloat16)
            inner[put : put + size, :] = normed(
                held[put : put + size, :].astype(jnp.float32), gain[...]
            )
        resid[...] = held[:piece, :]
        if n_dec:
            dec_resid[...] = held[2 * piece :, :]

    rows = inner[...]
    gated = jnp.dot(rows, gate[...], preferred_element_type=jnp.float32)
    raised = jnp.dot(rows, up[...], preferred_element_type=jnp.float32)
    hidden = (gated / (1.0 + jnp.exp(-gated)) * raised).astype(jnp.bfloat16)
    part = jnp.dot(hidden, down[...], preferred_element_type=jnp.float32)

    @pl.when(step == 0)
    def _():
        total[...] = part

    @pl.when(step > 0)
    def _():
        total[...] += part

    @pl.when(step == pl.num_programs(0) - 1)
    def _():
        keep[...] = total[:piece, :].astype(jnp.bfloat16)
        give[...] = total[piece : 2 * piece, :].astype(jnp.bfloat16)
        if n_dec:
            dec_out[...] = total[2 * piece :, :].astype(jnp.bfloat16)


def feed_forward(place, mine, sib, shares, gain, gate, up, down, dec=None, dec_shares=None):
    piece, width = mine.shape
    chips = len(shares) // 2
    units = gate.shape[1]
    chunk = min(256, units)
    n_dec = 0 if dec is None else dec.shape[0]
    rows = 2 * piece + n_dec
    in_specs = [whole(mine.shape), whole(sib.shape)] + [whole(s.shape) for s in shares]
    args = [mine, sib, *shares]
    if n_dec:
        in_specs += [whole(dec.shape)] + [whole(s.shape) for s in dec_shares]
        args += [dec, *dec_shares]
    in_specs += [
        whole((1, width)),
        pl.BlockSpec((width, chunk), lambda i, s: (0, i)),
        pl.BlockSpec((width, chunk), lambda i, s: (0, i)),
        pl.BlockSpec((chunk, width), lambda i, s: (i, 0)),
    ]
    args += [gain, gate, up, down]
    sizes = [piece] * 3 + [n_dec] * 2 * bool(n_dec)
    return pl.pallas_call(
        functools.partial(forward_kernel, chips, n_dec),
        out_shape=[jax.ShapeDtypeStruct((n, width), jnp.bfloat16) for n in sizes],
        grid_spec=pltpu.PrefetchScalarGridSpec(
            num_scalar_prefetch=1,
            grid=(units // chunk,),
            in_specs=in_specs,
            out_specs=[whole((n, width)) for n in sizes],
            scratch_shapes=[
                pltpu.VMEM((rows, width), jnp.bfloat16),
                pltpu.VMEM((rows, width), jnp.bfloat16),
                pltpu.VMEM((rows, width), jnp.float32),
            ],
        ),
        compiler_params=params(48),
        cost_estimate=cost(6 * rows * width * units, 6 * width * units, rows * units),
        name="feed_forward",
    )(place, *args)


def angle_tables(places):
    halfway = HD // 2
    powers = jnp.arange(halfway, dtype=jnp.float32) * (2.0 / HD)
    inverse = THETA ** (-powers)
    angles = places.astype(jnp.float32)[:, None] * inverse[None, :]
    cosine, sine = jnp.cos(angles), jnp.sin(angles)
    return jnp.concatenate([cosine, cosine], axis=-1), jnp.concatenate([-sine, sine], axis=-1)


def add(*values):
    total = values[0].astype(jnp.float32)
    for value in values[1:]:
        total = total + value.astype(jnp.float32)
    return total.astype(jnp.bfloat16)


def on_device(
    prefill_rows,
    decode_rows,
    deal_order,
    prefill_offset,
    cache_length,
    prefill_cache,
    decode_cache,
    qkv_weight,
    out_weight,
    attention_gain,
    forward_gain,
    gate_weight,
    up_weight,
    down_weight,
):
    tensor_count = lax.axis_size("tensor")
    dp_count = lax.axis_size("dp")
    chips = tensor_count // 2
    tensor_place = lax.axis_index("tensor")
    group_place = lax.axis_index("dp")
    chip, core = tensor_place // 2, tensor_place % 2
    piece, width = prefill_rows.shape
    per_device = decode_rows.shape[0]
    requests = deal_order.shape[0]
    slots = cache_length.shape[0]
    padded = -(-slots // 16) * 16
    heads = qkv_weight.shape[1]
    tokens = piece * tensor_count
    half = width // 2

    def place_of(k):
        return jnp.stack([core, (chip + k) % chips, prefill_offset[0]]).astype(jnp.int32)

    places = [place_of(k) for k in range(chips)]

    mines = [prefill_rows] + [from_chip(prefill_rows, k) for k in range(1, chips)]
    sibs = [swap_cores(rows) for rows in mines]

    pool = decode_rows
    mask = 1
    while mask < dp_count:
        pool = jnp.concatenate([pool, swap_groups(pool, mask)], axis=0)
        mask *= 2
    index = jnp.arange(dp_count * per_device, dtype=jnp.int32)
    origin = jnp.bitwise_xor(group_place, index // per_device)
    request = (origin * tensor_count + tensor_place) * per_device + index % per_device
    slot_of = jnp.sum(
        jnp.where(
            request[:, None] == jnp.arange(requests, dtype=jnp.int32)[None, :],
            deal_order[None, :],
            0,
        ),
        axis=1,
    )
    in_group = slot_of - group_place * slots
    chooser = (jnp.arange(padded, dtype=jnp.int32)[:, None] == in_group[None, :]) & (
        in_group[None, :] < slots
    )
    dealt = jnp.dot(
        chooser.astype(jnp.bfloat16), pool, preferred_element_type=jnp.float32
    ).astype(jnp.bfloat16)
    dealt = add(dealt, swap_cores(dealt))
    dealt = add(dealt, *[from_chip(dealt, k) for k in range(1, chips)])

    weight = qkv_weight.reshape(width, -1)
    gain = attention_gain.reshape(1, width)
    tables = angle_tables(prefill_offset[0] + jnp.arange(tokens, dtype=jnp.int32))
    dec_tables = angle_tables(jnp.pad(cache_length, (0, padded - slots)))
    total = {"heads": heads, "tokens": tokens}
    queries = [None] * chips
    entries = None
    for k in range(chips):
        last = k == chips - 1
        got = project(
            places[k],
            mines[k],
            sibs[k],
            gain,
            weight,
            tables,
            total,
            dealt if last else None,
            dec_tables if last else None,
            entries,
        )
        queries[k], entries = got[:2]
        if last:
            dec_query, dec_entries = got[2:]

    col = pl.multiple_of((1 - core) * half, half)
    sib_weight = swap_cores(lax.dynamic_slice_in_dim(out_weight, col, half, 1))

    def finish(attended, place):
        return out_project(place, attended, swap_cores(attended), out_weight, sib_weight)

    parts = []
    for k in range(chips):
        attended = fill_attend(places[k], queries[k], prefill_cache, entries, heads)
        parts.append(finish(attended, places[k]))
    dec_att = step_attend(cache_length, dec_query, decode_cache, dec_entries, slots, heads)
    dec_att = jnp.pad(dec_att, ((0, padded - slots), (0, 0)))
    dec_part = finish(dec_att, places[0])

    def shares_of(own, others):
        pairs = []
        for value in [own, *others]:
            pairs += [value, swap_cores(value)]
        return pairs

    shares = []
    for b in range(chips):
        others = [from_chip(parts[(b - j) % chips], j) for j in range(1, chips)]
        shares.append(shares_of(parts[b], others))
    dec_shares = shares_of(dec_part, [from_chip(dec_part, j) for j in range(1, chips)])

    gain = forward_gain.reshape(1, width)
    arrived = []
    for n, b in enumerate([*range(1, chips), 0]):
        got = feed_forward(
            places[b],
            mines[b],
            sibs[b],
            shares[b],
            gain,
            gate_weight,
            up_weight,
            down_weight,
            dealt if n == 0 else None,
            dec_shares if n == 0 else None,
        )
        keep, give, resid = got[:3]
        if n == 0:
            dec_sum, dec_resid = got[3:]
        if b:
            arrived.append(from_chip(add(keep, swap_cores(give)), chips - b))
        else:
            prefill_out = add(resid, keep, swap_cores(give), *arrived)

    dec_sum = add(dec_sum, swap_cores(dec_sum))
    others = [from_chip(dec_sum, j) for j in range(1, chips)]
    final = add(dec_resid, dec_sum, *others)
    picker = in_group[:, None] == jnp.arange(padded, dtype=jnp.int32)[None, :]
    picker = picker & (in_group[:, None] < slots)
    routed = jnp.dot(
        picker.astype(jnp.bfloat16), final, preferred_element_type=jnp.float32
    ).astype(jnp.bfloat16)
    mask = dp_count // 2
    while mask:
        cut = mask * per_device
        routed = add(routed[:cut], swap_groups(routed[cut:], mask))
        mask //= 2
    return (prefill_out, routed, entries, dec_entries[:, :slots])


def solution(mesh):
    placed = (
        P(("dp", "tensor"), None),
        P(("dp", "tensor"), None),
        P(),
        P("dp"),
        P("dp"),
        P(None, "dp", None, "tensor"),
        P(None, "dp", None, "tensor"),
        P(None, "tensor", None),
        P("tensor", None),
        P(),
        P(),
        P(None, "tensor"),
        P(None, "tensor"),
        P("tensor", None),
    )
    return jax.shard_map(
        on_device,
        mesh=mesh,
        in_specs=placed,
        out_specs=(
            P(("dp", "tensor"), None),
            P(("dp", "tensor"), None),
            P(None, "dp", "tensor"),
            P(None, "dp", "tensor"),
        ),
        check_vma=False,
    )
```

time: 326 us -> 150 us (0.46)
  blocking collectives: 103 us -> 0 us
  matrix products: 67 us -> 0.37 us
  Pallas kernels: 0 us -> 63.1 us
  waiting for transfers between devices: 83.7 us -> 35.6 us
  starting transfers between devices: 0.12 us -> 17.3 us
  local copies, waits for them, and re-layouts: 39.2 us -> 23.5 us
  between operations: 15.4 us -> 1.71 us
  other arithmetic: 16.2 us -> 7.2 us
    all_gather x3 -> x0, blocking collectives: 91.5 us -> none  [the longest x1 44.5 us: on_device(): everyone = lax.all_gather(decode_rows, ('dp', 'tensor'), axis=0, tiled=True)]
    psum x1 -> x0, waiting for transfers between devices: 83 us -> none  [on_device(): fill_sum, step_sum = lax.psum((fill_part, step_part), 'tensor')]
    dot_general x17 -> x2, matrix products: 67 us -> 0.37 us  [the longest x1 0.2 us: on_device(): jnp.dot(picker.astype(jnp.bfloat16), final, preferred_element_type=jnp.fl...]
    pallas_call x0 -> x10, Pallas kernels: none -> 63.1 us  [the longest x2 35 us: feed_forward(): pl.pallas_call(functools.partial(forward_kernel, chips, n_dec), out_shape...]
    ppermute x0 -> x29, waiting for transfers between devices: none -> 35.6 us  [the longest x7 23.6 us: from_chip(): lax.ppermute(value, 'tensor', [(i, (i // 2 - step) % chips * 2 + i % 2) f...]
    ppermute x0 -> x29, starting transfers between devices: none -> 17.3 us  [the longest x6 8.43 us: swap_groups(): return lax.ppermute(value, 'dp', [(i, i ^ mask) for i in range(count)])]
    unnamed x1 -> x0, blocking collectives: 11.6 us -> none
    slice x7 -> x4, local copies, waits for them, and re-layouts: 10 us -> 0.63 us  [the longest x1 0.6 us: on_device(): return (prefill_out, routed, entries, dec_entries[:, :slots])]
  transfers between devices with their start and end apart: 3 -> 29, of which waited for: 1 -> 14; matrix products, arithmetic and copies ran while one was open for 21% -> 10% of each run, Pallas kernels for 0% -> 41%
where the time goes in v1:
time: 150 us; the launch traced here: 149 us
  Pallas kernels  63.1 us (42%)
  waiting for transfers between devices  35.6 us (24%)
  local copies, waits for them, and re-layouts  23.5 us (16%)
  starting transfers between devices  17.3 us (12%)
  other arithmetic  7.2 us (5%)
  between operations  1.71 us (1%)
    pallas_call x2, Pallas kernels, feed_forward(): pl.pallas_call(functools.partial(forward_kernel, chips, n_dec), out_shape...  35 us
    ppermute x7, waiting for transfers between devices, from_chip(): lax.ppermute(value, 'tensor', [(i, (i // 2 - step) % chips * 2 + i % 2) f...  23.6 us
    unnamed x43, local copies, waits for them, and re-layouts  20.4 us
    ppermute x6, starting transfers between devices, swap_groups(): return lax.ppermute(value, 'dp', [(i, i ^ mask) for i in range(count)])  8.43 us
    pallas_call x2, Pallas kernels, project(): pl.pallas_call(kernel, out_shape=out_shape, grid_spec=pltpu.PrefetchScala...  8.37 us
    pallas_call x2, Pallas kernels, fill_attend(): pl.pallas_call(functools.partial(fill_kernel, groups), out_shape=jax.Shap...  8.24 us
    ppermute x7, starting transfers between devices, from_chip(): lax.ppermute(value, 'tensor', [(i, (i // 2 - step) % chips * 2 + i % 2) f...  6.56 us
    pallas_call x1, Pallas kernels, step_attend(): pl.pallas_call(functools.partial(step_kernel, heads, groups), out_shape=j...  6.3 us
  transfers between devices with their start and end apart: 29, of which 14 were waited for; matrix products, arithmetic and copies ran while one was open for 10% of the time, Pallas kernels for 41%

profile of v1, /device:TPU:0, one launch (start us, length us, event | category | flops | bytes accessed | tf_op | source)
XLA Modules:
  0.0 148.7 jit_solution(9017641146945724001)
XLA Ops:
  1.2 2.6 %collective-permute-start.1 = (bf16[128,2048]{1,0:T(8,128)(2,1)}, bf16[128,2048]{1,0:T(8,128)(2,1)}, u32[]{:S(2)}, u32[]{:S(2)}) collective-permute-start(bf16[128,2048]{1,0:T(8,128)(2,1)} %refs_0_.3), channel_id=1, source_target_pairs={{0,2},{1,3},{2,0},{3,1},{4,6},{5,7},{6,4},{7,5},{8,10},{9,11},{10,... | collective-permute-start | bytes 1572872 | tf_op jit(solution)/shard_map/ppermute | solution.py:26
  3.7 1.5 %collective-permute-start.3 = (bf16[2,2048]{1,0:T(2,128)(2,1)}, bf16[2,2048]{1,0:T(2,128)(2,1)S(1)}, u32[]{:S(2)}, u32[]{:S(2)}) collective-permute-start(bf16[2,2048]{1,0:T(2,128)(2,1)} %param.15), channel_id=1, source_target_pairs={{0,4},{4,0},{8,12},{12,8},{16,20},{20,16},{24,28},{28,24},{1,5},{5... | collective-permute-start | bytes 24584 | tf_op jit(solution)/shard_map/ppermute | solution.py:33
  5.3 2.3 %constant_dynamic-slice_fusion = bf16[512,1024]{1,0:T(8,128)(2,1)} fusion(bf16[512,2048]{1,0:T(8,128)(2,1)} %weight.5, s32[]{:T(128)S(6)} %select_n.67), kind=kLoop, calls=%fused_computation.69 | loop fusion | bytes 2097156 | tf_op jit(solution)/shard_map/dynamic_slice | solution.py:532
  12.5 1.6 %collective-permute-start.4 = (bf16[4,2048]{1,0:T(4,128)(2,1)S(1)}, bf16[4,2048]{1,0:T(4,128)(2,1)S(1)}, u32[]{:S(2)}, u32[]{:S(2)}) collective-permute-start(bf16[4,2048]{1,0:T(4,128)(2,1)S(1)} %pad_maximum_fusion.3), channel_id=1, source_target_pairs={{0,8},{4,12},{8,0},{12,4},{16,24},{20,28},{24,16},{28,20},{1,9},{5... | collective-permute-start | bytes 49160 | tf_op jit(solution)/shard_map/ppermute | solution.py:33
  14.2 2.1 %collective-permute-done.4 = bf16[4,2048]{1,0:T(4,128)(2,1)S(1)} collective-permute-done((bf16[4,2048]{1,0:T(4,128)(2,1)S(1)}, bf16[4,2048]{1,0:T(4,128)(2,1)S(1)}, u32[]{:S(2)}, u32[]{:S(2)}) %collective-permute-start.4) | collective-permute-done | bytes 16416 | tf_op jit(solution)/shard_map/ppermute | solution.py:33
  17.1 2.7 %collective-permute-start.5 = (bf16[8,2048]{1,0:T(8,128)(2,1)S(1)}, bf16[8,2048]{1,0:T(8,128)(2,1)S(1)}, u32[]{:S(2)}, u32[]{:S(2)}) collective-permute-start(bf16[8,2048]{1,0:T(8,128)(2,1)S(1)} %pad_maximum_fusion.2), channel_id=1, source_target_pairs={{0,16},{4,20},{8,24},{12,28},{16,0},{20,4},{24,8},{28,12},{1,17},{... | collective-permute-start | bytes 98312 | tf_op jit(solution)/shard_map/ppermute | solution.py:33
  19.7 5.4 %copy.26 = bf16[256,8,2,512]{3,1,2,0:T(8,128)(2,1)} copy(bf16[256,8,2,512]{3,2,1,0:T(2,128)(2,1)} %bitcast.28) | data formatting | bytes 8388608
  25.4 1.2 collective-permute-done.6
  27.3 3.6 %collective-permute-done.7 = bf16[16,2048]{1,0:T(8,128)(2,1)S(1)} collective-permute-done((bf16[16,2048]{1,0:T(8,128)(2,1)S(1)}, bf16[16,2048]{1,0:T(8,128)(2,1)S(1)}, u32[]{:S(2)}, u32[]{:S(2)}) %collective-permute-start.7) | collective-permute-done | bytes 65568 | tf_op jit(solution)/shard_map/ppermute | solution.py:26
  31.8 2.2 %copy-done = bf16[256,8,2,512]{3,1,2,0:T(8,128)(2,1)S(1)} copy-done((bf16[256,8,2,512]{3,1,2,0:T(8,128)(2,1)S(1)}, bf16[256,8,2,512]{3,1,2,0:T(8,128)(2,1)}, u32[]{:S(2)}) %copy-start) | copy-done | bytes 4194328
  37.0 3.8 %project.2 = (bf16[256,512]{1,0:T(8,128)(2,1)S(1)}, bf16[2,512,256]{2,1,0:T(8,128)(2,1)}) custom-call(s32[3]{0:T(128)S(1)} %add_add_fusion.place, bf16[128,2048]{1,0:T(8,128)(2,1)S(1)} %copy-done.8, bf16[128,2048]{1,0:T(8,128)(2,1)S(1)} %copy-done.11, f32[1,2048]{1,0:T(1,128)S(1)} %bitcast.24, bf16[2048,1024]{1,0:T(8,128)(2,1)S(1)} %bitcast.22, ...), custom_call_target="tpu_custom_call" | custom-call | flops 1073741824 | bytes 6291456 | tf_op jit(solution)/shard_map/project/pallas_call | solution.py:141
  40.8 2.4 %copy-done.1 = bf16[256,8,2,512]{3,1,2,0:T(8,128)(2,1)S(1)} copy-done((bf16[256,8,2,512]{3,1,2,0:T(8,128)(2,1)S(1)}, bf16[256,8,2,512]{3,1,2,0:T(8,128)(2,1)}, u32[]{:S(2)}) %copy-start.1) | copy-done | bytes 4194328
  44.1 4.6 %project.3 = (bf16[256,512]{1,0:T(8,128)(2,1)S(1)}, bf16[2,512,256]{2,1,0:T(8,128)(2,1)}, bf16[16,512]{1,0:T(8,128)(2,1)S(1)}, bf16[2,16,256]{2,1,0:T(8,128)(2,1)S(1)}) custom-call(s32[3]{0:T(128)S(1)} %add_add_fusion.1.place, bf16[128,2048]{1,0:T(8,128)(2,1)} %collective-permute-done.1.refs_0_, ...), custom_call_target="tpu_custom_call", output_to_operand_aliasing={{1}: (10, {})} | custom-call | flops 1140850688 | bytes 6422528 | tf_op jit(solution)/shard_map/project/pallas_call | solution.py:141
  49.7 1.2 copy-done.18
  51.0 4.1 %fill_attend.2.mine = bf16[256,512]{1,0:T(8,128)(2,1)S(1)} custom-call(s32[3]{0:T(128)S(1)} %add_add_fusion.place, bf16[256,512]{1,0:T(8,128)(2,1)S(1)} %get-tuple-element.17.query, bf16[2,1,1024,256]{3,2,1,0:T(8,128)(2,1)S(1)} %copy-done.18, bf16[2,1,1024,256]{3,2,1,0:T(8,128)(2,1)S(1)} %copy-done.18, bf16[2,512,256]{2,1,0:T(8,128)(2,1)S(1)} %copy-done.13, ...), custom_call_target="tpu_custom_call" | custom-call | flops 1610612736 | bytes 1572864 | tf_op jit(solution)/shard_map/fill_attend/pallas_call | solution.py:204
  55.3 1.4 collective-permute-done.8.sib
  56.7 2.1 %out_project.3.refs_2_ = bf16[256,1024]{1,0:T(8,128)(2,1)} custom-call(s32[3]{0:T(128)S(1)} %add_add_fusion.place, bf16[256,512]{1,0:T(8,128)(2,1)S(1)} %fill_attend.2.mine, bf16[256,512]{1,0:T(8,128)(2,1)S(1)} %collective-permute-done.8.sib, bf16[512,2048]{1,0:T(8,128)(2,1)S(1)} %copy-done.3, bf16[512,1024]{1,0:T(8,128)(2,1)S(1)} %collective-permute-done.9.sib_weight), custom_call_target="tpu_custom_call" | custom-call | flops 536870912 | bytes 3670016 | tf_op jit(solution)/shard_map/out_project/pallas_call | solution.py:300
  59.3 4.1 %fill_attend.3.mine = bf16[256,512]{1,0:T(8,128)(2,1)S(1)} custom-call(s32[3]{0:T(128)S(1)} %add_add_fusion.1.place, bf16[256,512]{1,0:T(8,128)(2,1)S(1)} %get-tuple-element.20.query, bf16[2,1,1024,256]{3,2,1,0:T(8,128)(2,1)S(1)} %copy-done.18, bf16[2,1,1024,256]{3,2,1,0:T(8,128)(2,1)S(1)} %copy-done.18, bf16[2,512,256]{2,1,0:T(8,128)(2,1)S(1)} %copy-done.14, ...), custom_call_target="tpu_custom_call" | custom-call | flops 1610612736 | bytes 1572864 | tf_op jit(solution)/shard_map/fill_attend/pallas_call | solution.py:204
  63.6 1.5 %collective-permute-done.11.sib = bf16[256,512]{1,0:T(8,128)(2,1)} collective-permute-done((bf16[256,512]{1,0:T(8,128)(2,1)S(1)}, bf16[256,512]{1,0:T(8,128)(2,1)}, u32[]{:S(2)}, u32[]{:S(2)}) %collective-permute-start.11) | collective-permute-done | bytes 262176 | tf_op jit(solution)/shard_map/ppermute | solution.py:20
  65.2 2.2 %out_project.4.refs_2_ = bf16[256,1024]{1,0:T(8,128)(2,1)S(1)} custom-call(s32[3]{0:T(128)S(1)} %add_add_fusion.1.place, bf16[256,512]{1,0:T(8,128)(2,1)S(1)} %fill_attend.3.mine, bf16[256,512]{1,0:T(8,128)(2,1)} %collective-permute-done.11.sib, bf16[512,2048]{1,0:T(8,128)(2,1)S(1)} %copy-done.3, bf16[512,1024]{1,0:T(8,128)(2,1)S(1)} %collective-permute-done.9.sib_weight), custom_call_target="tpu_custom_call" | custom-call | flops 536870912 | bytes 3670016 | tf_op jit(solution)/shard_map/out_project/pallas_call | solution.py:300
  67.6 5.5 %collective-permute-done.16.refs_4_ = bf16[256,1024]{1,0:T(8,128)(2,1)} collective-permute-done((bf16[256,1024]{1,0:T(8,128)(2,1)}, bf16[256,1024]{1,0:T(8,128)(2,1)}, u32[]{:S(2)}, u32[]{:S(2)}) %collective-permute-start.16) | collective-permute-done | bytes 524320 | tf_op jit(solution)/shard_map/ppermute | solution.py:26
  73.1 3.4 %copy-done.2 = bf16[2,8,1024,256]{3,2,1,0:T(8,128)(2,1)S(1)} copy-done((bf16[2,8,1024,256]{3,2,1,0:T(8,128)(2,1)S(1)}, bf16[2,8,1024,256]{3,2,1,0:T(8,128)(2,1)}, u32[]{:S(2)}) %copy-start.2) | copy-done | bytes 8388632
  76.5 6.3 %step_attend.1 = bf16[8,16,128]{2,1,0:T(8,128)(2,1)S(1)} custom-call(s32[8]{0:T(128)S(1)} %copy-done.17, bf16[8,16,256]{2,1,0:T(8,128)(2,1)S(1)} %pad.13.query, bf16[2,8,1024,256]{3,2,1,0:T(8,128)(2,1)S(1)} %copy-done.2, bf16[2,8,1024,256]{3,2,1,0:T(8,128)(2,1)S(1)} %copy-done.2, bf16[8,1,256]{2,1,0:T(2,128)(2,1)S(1)} %copy.24.new_key, ...), custom_call_target="tpu_custom_call" | custom-call | flops 268435456 | bytes 8388608 | tf_op jit(solution)/shard_map/step_attend/pallas_call | solution.py:269
  85.8 3.3 %collective-permute-done.20.refs_9_ = bf16[16,1024]{1,0:T(8,128)(2,1)S(1)} collective-permute-done((bf16[16,1024]{1,0:T(8,128)(2,1)S(1)}, bf16[16,1024]{1,0:T(8,128)(2,1)S(1)}, u32[]{:S(2)}, u32[]{:S(2)}) %collective-permute-start.20) | collective-permute-done | bytes 32800 | tf_op jit(solution)/shard_map/ppermute | solution.py:26
  90.3 18.0 %feed_forward.3 = (bf16[128,2048]{1,0:T(8,128)(2,1)S(1)}, bf16[128,2048]{1,0:T(8,128)(2,1)S(1)}, bf16[128,2048]{1,0:T(8,128)(2,1)}, bf16[16,2048]{1,0:T(8,128)(2,1)S(1)}, bf16[16,2048]{1,0:T(8,128)(2,1)S(1)}) custom-call(s32[3]{0:T(128)S(1)} %add_add_fusion.1.place, bf16[128,2048]{1,0:T(8,128)(2,1)} %collective-permute-done.1.refs_0_, ...), custom_call_target="tpu_custom_call" | custom-call | flops 6845104128 | bytes 25165824 | tf_op jit(solution)/shard_map/feed_forward/pallas_call | solution.py:405
  110.5 3.4 %collective-permute-done.25 = bf16[16,2048]{1,0:T(8,128)(2,1)S(1)} collective-permute-done((bf16[16,2048]{1,0:T(8,128)(2,1)S(1)}, bf16[16,2048]{1,0:T(8,128)(2,1)S(1)}, u32[]{:S(2)}, u32[]{:S(2)}) %collective-permute-start.25) | collective-permute-done | bytes 65568 | tf_op jit(solution)/shard_map/ppermute | solution.py:26
  114.6 17.0 %feed_forward.2 = (bf16[128,2048]{1,0:T(8,128)(2,1)S(1)}, bf16[128,2048]{1,0:T(8,128)(2,1)S(1)}, bf16[128,2048]{1,0:T(8,128)(2,1)S(1)}) custom-call(s32[3]{0:T(128)S(1)} %add_add_fusion.place, bf16[128,2048]{1,0:T(8,128)(2,1)S(1)} %copy-done.9, bf16[128,2048]{1,0:T(8,128)(2,1)S(1)} %copy-done.12, bf16[256,1024]{1,0:T(8,128)(2,1)} %out_project.3.refs_2_, ...), custom_call_target="tpu_custom_call" | custom-call | flops 6442450944 | bytes 25165824 | tf_op jit(solution)/shard_map/feed_forward/pallas_call | solution.py:405
  131.7 1.6 %collective-permute-start.27 = (bf16[4,2048]{1,0:T(4,128)(2,1)S(1)}, bf16[4,2048]{1,0:T(4,128)(2,1)S(1)}, u32[]{:S(2)}, u32[]{:S(2)}) collective-permute-start(bf16[4,2048]{1,0:T(4,128)(2,1)S(1)} %slice.48), channel_id=1, source_target_pairs={{0,8},{4,12},{8,0},{12,4},{16,24},{20,28},{24,16},{28,20},{1,9},{5... | collective-permute-start | bytes 49160 | tf_op jit(solution)/shard_map/ppermute | solution.py:33
  134.4 1.1 collective-permute-done.27
  136.7 2.5 %collective-permute-done.28 = bf16[2,2048]{1,0:T(2,128)(2,1)S(1)} collective-permute-done((bf16[2,2048]{1,0:T(2,128)(2,1)S(1)}, bf16[2,2048]{1,0:T(2,128)(2,1)S(1)}, u32[]{:S(2)}, u32[]{:S(2)}) %collective-permute-start.28) | collective-permute-done | bytes 8224 | tf_op jit(solution)/shard_map/ppermute | solution.py:33
  139.9 7.7 %collective-permute-done.23 = bf16[128,2048]{1,0:T(8,128)(2,1)S(1)} collective-permute-done((bf16[128,2048]{1,0:T(8,128)(2,1)S(1)}, bf16[128,2048]{1,0:T(8,128)(2,1)S(1)}, u32[]{:S(2)}, u32[]{:S(2)}) %collective-permute-start.23) | collective-permute-done | bytes 524320 | tf_op jit(solution)/shard_map/ppermute | solution.py:26
  147.6 1.1 add_convert_fusion
  (121 shorter events, 23.4 us)
Async XLA Ops:
  0.6 24.4 %copy-start.19 = (bf16[2,2048]{1,0:T(2,128)(2,1)S(1)}, bf16[2,2048]{1,0:T(2,128)(2,1)}, u32[]{:S(2)}) copy-start(bf16[2,2048]{1,0:T(2,128)(2,1)} %param.15) | copy-start | bytes 24580
  0.6 31.1 %copy-start.15 = (f32[2048]{0:T(1024)S(1)}, f32[2048]{0:T(1024)}, u32[]{:S(2)}) copy-start(f32[2048]{0:T(1024)} %param.23) | copy-start | bytes 24580
  0.7 30.3 %collective-permute-start = (bf16[128,2048]{1,0:T(8,128)(2,1)}, bf16[128,2048]{1,0:T(8,128)(2,1)S(1)}, u32[]{:S(2)}, u32[]{:S(2)}) collective-permute-start(bf16[128,2048]{1,0:T(8,128)(2,1)} %refs_0_.3), channel_id=1, source_target_pairs={{0,1},{1,0},{2,3},{3,2},{4,5},{5,4},{6,7},{7,6},{8,9},{9,8},{10,11... | collective-permute-start | bytes 1572872 | tf_op jit(solution)/shard_map/ppermute | solution.py:20
  1.2 26.1 %collective-permute-start.1 = (bf16[128,2048]{1,0:T(8,128)(2,1)}, bf16[128,2048]{1,0:T(8,128)(2,1)}, u32[]{:S(2)}, u32[]{:S(2)}) collective-permute-start(bf16[128,2048]{1,0:T(8,128)(2,1)} %refs_0_.3), channel_id=1, source_target_pairs={{0,2},{1,3},{2,0},{3,1},{4,6},{5,7},{6,4},{7,5},{8,10},{9,11},{10,... | collective-permute-start | bytes 1572872 | tf_op jit(solution)/shard_map/ppermute | solution.py:26
  3.7 8.1 %collective-permute-start.3 = (bf16[2,2048]{1,0:T(2,128)(2,1)}, bf16[2,2048]{1,0:T(2,128)(2,1)S(1)}, u32[]{:S(2)}, u32[]{:S(2)}) collective-permute-start(bf16[2,2048]{1,0:T(2,128)(2,1)} %param.15), channel_id=1, source_target_pairs={{0,4},{4,0},{8,12},{12,8},{16,20},{20,16},{24,28},{28,24},{1,5},{5... | collective-permute-start | bytes 24584 | tf_op jit(solution)/shard_map/ppermute | solution.py:33
  7.5 47.7 %collective-permute-start.9 = (bf16[512,1024]{1,0:T(8,128)(2,1)}, bf16[512,1024]{1,0:T(8,128)(2,1)S(1)}, u32[]{:S(2)}, u32[]{:S(2)}) collective-permute-start(bf16[512,1024]{1,0:T(8,128)(2,1)} %constant_dynamic-slice_fusion), channel_id=1, source_target_pairs={{0,1},{1,0},{2,3},{3,2},{4,5},{5,4},{6,7},{7,6},{8,9},{9,8},{10,11... | collective-permute-start | bytes 3145736 | tf_op jit(solution)/shard_map/ppermute | solution.py:20
  12.5 3.8 %collective-permute-start.4 = (bf16[4,2048]{1,0:T(4,128)(2,1)S(1)}, bf16[4,2048]{1,0:T(4,128)(2,1)S(1)}, u32[]{:S(2)}, u32[]{:S(2)}) collective-permute-start(bf16[4,2048]{1,0:T(4,128)(2,1)S(1)} %pad_maximum_fusion.3), channel_id=1, source_target_pairs={{0,8},{4,12},{8,0},{12,4},{16,24},{20,28},{24,16},{28,20},{1,9},{5... | collective-permute-start | bytes 49160 | tf_op jit(solution)/shard_map/ppermute | solution.py:33
  17.1 8.0 %collective-permute-start.5 = (bf16[8,2048]{1,0:T(8,128)(2,1)S(1)}, bf16[8,2048]{1,0:T(8,128)(2,1)S(1)}, u32[]{:S(2)}, u32[]{:S(2)}) collective-permute-start(bf16[8,2048]{1,0:T(8,128)(2,1)S(1)} %pad_maximum_fusion.2), channel_id=1, source_target_pairs={{0,16},{4,20},{8,24},{12,28},{16,0},{20,4},{24,8},{28,12},{1,17},{... | collective-permute-start | bytes 98312 | tf_op jit(solution)/shard_map/ppermute | solution.py:33
  25.2 1.3 collective-permute-start.6
  26.6 4.3 %collective-permute-start.7 = (bf16[16,2048]{1,0:T(8,128)(2,1)S(1)}, bf16[16,2048]{1,0:T(8,128)(2,1)S(1)}, u32[]{:S(2)}, u32[]{:S(2)}) collective-permute-start(bf16[16,2048]{1,0:T(8,128)(2,1)S(1)} %add_convert_fusion.5), channel_id=1, source_target_pairs={{0,2},{1,3},{2,0},{3,1},{4,6},{5,7},{6,4},{7,5},{8,10},{9,11},{10,... | collective-permute-start | bytes 196616 | tf_op jit(solution)/shard_map/ppermute | solution.py:26
  27.3 13.5 %collective-permute-start.2 = (bf16[128,2048]{1,0:T(8,128)(2,1)}, bf16[128,2048]{1,0:T(8,128)(2,1)S(1)}, u32[]{:S(2)}, u32[]{:S(2)}) collective-permute-start(bf16[128,2048]{1,0:T(8,128)(2,1)} %collective-permute-done.1.refs_0_), channel_id=1, source_target_pairs={{0,1},{1,0},{2,3},{3,2},{4,5},{5,4},{6,7},{7,6},{8,9},{9,8},{10,11... | collective-permute-start | bytes 1572872 | tf_op jit(solution)/shard_map/ppermute | solution.py:20
  55.1 1.6 %collective-permute-start.8 = (bf16[256,512]{1,0:T(8,128)(2,1)S(1)}, bf16[256,512]{1,0:T(8,128)(2,1)S(1)}, u32[]{:S(2)}, u32[]{:S(2)}) collective-permute-start(bf16[256,512]{1,0:T(8,128)(2,1)S(1)} %fill_attend.2.mine), channel_id=1, source_target_pairs={{0,1},{1,0},{2,3},{3,2},{4,5},{5,4},{6,7},{7,6},{8,9},{9,8},{10,11... | collective-permute-start | bytes 786440 | tf_op jit(solution)/shard_map/ppermute | solution.py:20
  58.8 14.3 %collective-permute-start.16 = (bf16[256,1024]{1,0:T(8,128)(2,1)}, bf16[256,1024]{1,0:T(8,128)(2,1)}, u32[]{:S(2)}, u32[]{:S(2)}) collective-permute-start(bf16[256,1024]{1,0:T(8,128)(2,1)} %out_project.3.refs_2_), channel_id=1, source_target_pairs={{0,2},{1,3},{2,0},{3,1},{4,6},{5,7},{6,4},{7,5},{8,10},{9,11},{10,... | collective-permute-start | bytes 1572872 | tf_op jit(solution)/shard_map/ppermute | solution.py:26
  63.5 1.7 %collective-permute-start.11 = (bf16[256,512]{1,0:T(8,128)(2,1)S(1)}, bf16[256,512]{1,0:T(8,128)(2,1)}, u32[]{:S(2)}, u32[]{:S(2)}) collective-permute-start(bf16[256,512]{1,0:T(8,128)(2,1)S(1)} %fill_attend.3.mine), channel_id=1, source_target_pairs={{0,1},{1,0},{2,3},{3,2},{4,5},{5,4},{6,7},{7,6},{8,9},{9,8},{10,11... | collective-permute-start | bytes 786440 | tf_op jit(solution)/shard_map/ppermute | solution.py:20
  67.4 22.9 %collective-permute-start.15 = (bf16[256,1024]{1,0:T(8,128)(2,1)S(1)}, bf16[256,1024]{1,0:T(8,128)(2,1)S(1)}, u32[]{:S(2)}, u32[]{:S(2)}) collective-permute-start(bf16[256,1024]{1,0:T(8,128)(2,1)S(1)} %out_project.4.refs_2_), channel_id=1, source_target_pairs={{0,1},{1,0},{2,3},{3,2},{4,5},{5,4},{6,7},{7,6},{8,9},{9,8},{10,11... | collective-permute-start | bytes 1572872 | tf_op jit(solution)/shard_map/ppermute | solution.py:20
  73.1 17.3 %collective-permute-start.17 = (bf16[256,1024]{1,0:T(8,128)(2,1)}, bf16[256,1024]{1,0:T(8,128)(2,1)S(1)}, u32[]{:S(2)}, u32[]{:S(2)}) collective-permute-start(bf16[256,1024]{1,0:T(8,128)(2,1)} %collective-permute-done.16.refs_4_), channel_id=1, source_target_pairs={{0,1},{1,0},{2,3},{3,2},{4,5},{5,4},{6,7},{7,6},{8,9},{9,8},{10,11... | collective-permute-start | bytes 1572872 | tf_op jit(solution)/shard_map/ppermute | solution.py:20
  82.8 1.4 collective-permute-start.18
  85.2 3.9 %collective-permute-start.20 = (bf16[16,1024]{1,0:T(8,128)(2,1)S(1)}, bf16[16,1024]{1,0:T(8,128)(2,1)S(1)}, u32[]{:S(2)}, u32[]{:S(2)}) collective-permute-start(bf16[16,1024]{1,0:T(8,128)(2,1)S(1)} %out_project.5.refs_7_), channel_id=1, source_target_pairs={{0,2},{1,3},{2,0},{3,1},{4,6},{5,7},{6,4},{7,5},{8,10},{9,11},{10,... | collective-permute-start | bytes 98312 | tf_op jit(solution)/shard_map/ppermute | solution.py:26
  85.7 3.9 %collective-permute-start.19 = (bf16[16,1024]{1,0:T(8,128)(2,1)S(1)}, bf16[16,1024]{1,0:T(8,128)(2,1)S(1)}, u32[]{:S(2)}, u32[]{:S(2)}) collective-permute-start(bf16[16,1024]{1,0:T(8,128)(2,1)S(1)} %out_project.5.refs_7_), channel_id=1, source_target_pairs={{0,1},{1,0},{2,3},{3,2},{4,5},{5,4},{6,7},{7,6},{8,9},{9,8},{10,11... | collective-permute-start | bytes 98312 | tf_op jit(solution)/shard_map/ppermute | solution.py:20
  89.1 1.2 collective-permute-start.21
  89.1 19.8 %collective-permute-start.12 = (bf16[256,1024]{1,0:T(8,128)(2,1)S(1)}, bf16[256,1024]{1,0:T(8,128)(2,1)S(1)}, u32[]{:S(2)}, u32[]{:S(2)}) collective-permute-start(bf16[256,1024]{1,0:T(8,128)(2,1)S(1)} %out_project.4.refs_2_), channel_id=1, source_target_pairs={{0,2},{1,3},{2,0},{3,1},{4,6},{5,7},{6,4},{7,5},{8,10},{9,11},{10,... | collective-permute-start | bytes 1572872 | tf_op jit(solution)/shard_map/ppermute | solution.py:26
  90.3 24.3 %copy-start.9 = (bf16[128,2048]{1,0:T(8,128)(2,1)S(1)}, bf16[128,2048]{1,0:T(8,128)(2,1)}, u32[]{:S(2)}) copy-start(bf16[128,2048]{1,0:T(8,128)(2,1)} %refs_0_.3) | copy-start | bytes 1572868
  108.4 1.3 collective-permute-start.24
  108.5 6.1 %collective-permute-start.10 = (bf16[256,1024]{1,0:T(8,128)(2,1)}, bf16[256,1024]{1,0:T(8,128)(2,1)S(1)}, u32[]{:S(2)}, u32[]{:S(2)}) collective-permute-start(bf16[256,1024]{1,0:T(8,128)(2,1)} %out_project.3.refs_2_), channel_id=1, source_target_pairs={{0,1},{1,0},{2,3},{3,2},{4,5},{5,4},{6,7},{7,6},{8,9},{9,8},{10,11... | collective-permute-start | bytes 1572872 | tf_op jit(solution)/shard_map/ppermute | solution.py:20
  108.9 5.7 %collective-permute-start.13 = (bf16[256,1024]{1,0:T(8,128)(2,1)S(1)}, bf16[256,1024]{1,0:T(8,128)(2,1)S(1)}, u32[]{:S(2)}, u32[]{:S(2)}) collective-permute-start(bf16[256,1024]{1,0:T(8,128)(2,1)S(1)} %collective-permute-done.12.refs_4_), channel_id=1, source_target_pairs={{0,1},{1,0},{2,3},{3,2},{4,5},{5,4},{6,7},{7,6},{8,9},{9,8},{10,11... | collective-permute-start | bytes 1572872 | tf_op jit(solution)/shard_map/ppermute | solution.py:20
  109.6 4.3 %collective-permute-start.25 = (bf16[16,2048]{1,0:T(8,128)(2,1)S(1)}, bf16[16,2048]{1,0:T(8,128)(2,1)S(1)}, u32[]{:S(2)}, u32[]{:S(2)}) collective-permute-start(bf16[16,2048]{1,0:T(8,128)(2,1)S(1)} %add_convert_fusion.3), channel_id=1, source_target_pairs={{0,2},{1,3},{2,0},{3,1},{4,6},{5,7},{6,4},{7,5},{8,10},{9,11},{10,... | collective-permute-start | bytes 196616 | tf_op jit(solution)/shard_map/ppermute | solution.py:26
  110.5 22.8 %collective-permute-start.22 = (bf16[128,2048]{1,0:T(8,128)(2,1)S(1)}, bf16[128,2048]{1,0:T(8,128)(2,1)S(1)}, u32[]{:S(2)}, u32[]{:S(2)}) collective-permute-start(bf16[128,2048]{1,0:T(8,128)(2,1)S(1)} %get-tuple-element.27), channel_id=1, source_target_pairs={{0,1},{1,0},{2,3},{3,2},{4,5},{5,4},{6,7},{7,6},{8,9},{9,8},{10,11... | collective-permute-start | bytes 1572872 | tf_op jit(solution)/shard_map/ppermute | solution.py:20
  114.2 17.5 %collective-permute-start.26 = (bf16[8,2048]{1,0:T(8,128)(2,1)S(1)}, bf16[8,2048]{1,0:T(8,128)(2,1)S(1)}, u32[]{:S(2)}, u32[]{:S(2)}) collective-permute-start(bf16[8,2048]{1,0:T(8,128)(2,1)S(1)} %slice.46), channel_id=1, source_target_pairs={{0,16},{4,20},{8,24},{12,28},{16,0},{20,4},{24,8},{28,12},{1,17},{... | collective-permute-start | bytes 98312 | tf_op jit(solution)/shard_map/ppermute | solution.py:33
  131.6 8.3 %collective-permute-start.14 = (bf16[128,2048]{1,0:T(8,128)(2,1)S(1)}, bf16[128,2048]{1,0:T(8,128)(2,1)S(1)}, u32[]{:S(2)}, u32[]{:S(2)}) collective-permute-start(bf16[128,2048]{1,0:T(8,128)(2,1)S(1)} %get-tuple-element.23), channel_id=1, source_target_pairs={{0,1},{1,0},{2,3},{3,2},{4,5},{5,4},{6,7},{7,6},{8,9},{9,8},{10,11... | collective-permute-start | bytes 1572872 | tf_op jit(solution)/shard_map/ppermute | solution.py:20
  131.7 3.8 %collective-permute-start.27 = (bf16[4,2048]{1,0:T(4,128)(2,1)S(1)}, bf16[4,2048]{1,0:T(4,128)(2,1)S(1)}, u32[]{:S(2)}, u32[]{:S(2)}) collective-permute-start(bf16[4,2048]{1,0:T(4,128)(2,1)S(1)} %slice.48), channel_id=1, source_target_pairs={{0,8},{4,12},{8,0},{12,4},{16,24},{20,28},{24,16},{28,20},{1,9},{5... | collective-permute-start | bytes 49160 | tf_op jit(solution)/shard_map/ppermute | solution.py:33
  133.5 14.1 %collective-permute-start.23 = (bf16[128,2048]{1,0:T(8,128)(2,1)S(1)}, bf16[128,2048]{1,0:T(8,128)(2,1)S(1)}, u32[]{:S(2)}, u32[]{:S(2)}) collective-permute-start(bf16[128,2048]{1,0:T(8,128)(2,1)S(1)} %add_convert_fusion.1), channel_id=1, source_target_pairs={{0,2},{1,3},{2,0},{3,1},{4,6},{5,7},{6,4},{7,5},{8,10},{9,11},{10,... | collective-permute-start | bytes 1572872 | tf_op jit(solution)/shard_map/ppermute | solution.py:26
  135.6 3.7 %collective-permute-start.28 = (bf16[2,2048]{1,0:T(2,128)(2,1)S(1)}, bf16[2,2048]{1,0:T(2,128)(2,1)S(1)}, u32[]{:S(2)}, u32[]{:S(2)}) collective-permute-start(bf16[2,2048]{1,0:T(2,128)(2,1)S(1)} %slice.50), channel_id=1, source_target_pairs={{0,4},{4,0},{8,12},{12,8},{16,20},{20,16},{24,28},{28,24},{1,5},{5... | collective-permute-start | bytes 24584 | tf_op jit(solution)/shard_map/ppermute | solution.py:33
  (17 other events, 135.7 us)

commit v2 on v1

v2 whole, which is shorter than its diff:
```python
import functools
import math

import jax
import jax.numpy as jnp
from jax import lax
from jax.experimental import pallas as pl
from jax.experimental.pallas import tpu as pltpu
from jax.sharding import PartitionSpec as P

HD = 128
EPSILON = 1e-06
THETA = 1000000.0
NEGATIVE = -1e30
MIB = 1 << 20


def swap_cores(value):
    count = lax.axis_size("tensor")
    return lax.ppermute(value, "tensor", [(i, i ^ 1) for i in range(count)])


def from_chip(value, step):
    count = lax.axis_size("tensor")
    chips = count // 2
    return lax.ppermute(
        value, "tensor", [(i, (i // 2 - step) % chips * 2 + i % 2) for i in range(count)]
    )


def swap_groups(value, mask):
    count = lax.axis_size("dp")
    return lax.ppermute(value, "dp", [(i, i ^ mask) for i in range(count)])


def whole(shape):
    return pl.BlockSpec(shape, lambda *_: (0,) * len(shape))


def params(mib):
    return pltpu.CompilerParams(vmem_limit_bytes=mib * MIB)


def cost(flops, moved, exps=0):
    return pl.CostEstimate(flops=int(flops), bytes_accessed=int(moved), transcendentals=int(exps))


def normed(values, gain):
    spread = jnp.mean(values * values, axis=-1, keepdims=True)
    return (values * lax.rsqrt(spread + EPSILON) * gain).astype(jnp.bfloat16)


def turn(vectors, cosine, sine):
    return vectors * cosine + pltpu.roll(vectors, HD // 2, 1) * sine


def in_vmem(value):
    return pltpu.with_memory_space_constraint(value, pltpu.VMEM)


def in_hbm(value):
    return pltpu.with_memory_space_constraint(value, pltpu.HBM)


VMEM_WHOLE = pl.BlockSpec(memory_space=pltpu.VMEM)
SMEM_WHOLE = pl.BlockSpec(memory_space=pltpu.SMEM)
UNREAD = pl.BlockSpec(memory_space=pl.ANY)


def project_kernel(n_dec, n_after, groups, heads, place, *refs):
    refs = list(refs)
    mine, sib, gain, weight, cosine, sine = refs[:6]
    refs = refs[6:]
    if n_dec:
        dec, dec_cos, dec_sin = refs[:3]
        refs = refs[3:]
    refs = refs[n_after:]
    query, entries = refs[:2]
    if n_dec:
        dec_query, dec_entries = refs[2:4]
    inner = refs[-1]
    piece = mine.shape[0]
    core = place[0]
    scale = gain[...]
    for ref, at in ((mine, core), (sib, 1 - core)):
        start = pl.multiple_of(at * piece, piece)
        inner[pl.ds(start, piece), :] = normed(ref[...].astype(jnp.float32), scale)
    if n_dec:
        inner[2 * piece :, :] = normed(dec[...].astype(jnp.float32), scale)
    here = pl.ds(pl.multiple_of(place[1] * 2 * piece, 2 * piece), 2 * piece)
    depth = (groups + 2) * HD
    for j in range(heads):
        mixed = jnp.dot(
            inner[...],
            weight[:, j * depth : (j + 1) * depth],
            preferred_element_type=jnp.float32,
        )

        def put(rows, cos, sin, query_out, entry_out):
            for g in range(groups):
                part = rows[:, g * HD : (g + 1) * HD]
                at = (j * groups + g) * HD
                query_out[:, at : at + HD] = turn(part, cos, sin).astype(jnp.bfloat16)
            key = rows[:, groups * HD : (groups + 1) * HD]
            entry_out[0, :, j * HD : (j + 1) * HD] = turn(key, cos, sin).astype(jnp.bfloat16)
            entry_out[1, :, j * HD : (j + 1) * HD] = rows[:, (groups + 1) * HD :].astype(
                jnp.bfloat16
            )

        put(mixed[: 2 * piece], cosine[here, :], sine[here, :], query, entries)
        if n_dec:
            put(mixed[2 * piece :], dec_cos[...], dec_sin[...], dec_query, dec_entries)


def project(place, mine, sib, gain, weight, tables, heads, dec=None, dec_tables=None, after=()):
    piece, width = mine.shape
    depth = weight.shape[1] // heads
    groups = depth // HD - 2
    block = 2 * piece
    n_dec = 0 if dec is None else dec.shape[0]
    args = [mine, sib, gain, weight, *tables]
    if n_dec:
        args += [dec, *dec_tables]
    out_shape = []
    for n in [block] + [n_dec] * bool(n_dec):
        out_shape += [
            jax.ShapeDtypeStruct((n, heads * groups * HD), jnp.bfloat16),
            jax.ShapeDtypeStruct((2, n, heads * HD), jnp.bfloat16),
        ]
    rows = block + n_dec
    return pl.pallas_call(
        functools.partial(project_kernel, n_dec, len(after), groups, heads),
        out_shape=out_shape,
        in_specs=[SMEM_WHOLE] + [VMEM_WHOLE] * len(args) + [UNREAD] * len(after),
        out_specs=[VMEM_WHOLE] * len(out_shape),
        scratch_shapes=[pltpu.VMEM((rows, width), jnp.bfloat16)],
        compiler_params=params(8),
        cost_estimate=cost(2 * rows * weight.size, 2 * (weight.size + 2 * rows * width)),
        name="project",
    )(place, *args, *after)


def fill_kernel(groups, chips, place, query, cache_key, cache_value, *refs):
    new_keys, new_values, out = refs[:chips], refs[chips : 2 * chips], refs[2 * chips]
    scaling = 1.0 / math.sqrt(HD)
    count = query.shape[0]
    stored = cache_key.shape[2]
    old_seen = lax.broadcasted_iota(jnp.int32, (1, stored), 1) < place[2]
    ahead = lax.broadcasted_iota(jnp.int32, (count, count), 1) - lax.broadcasted_iota(
        jnp.int32, (count, count), 0
    )
    across = (((1,), (1,)), ((), ()))
    for g in range(groups):
        rows = query[:, g * HD : (g + 1) * HD]
        scores = lax.dot_general(
            rows, cache_key[0, 0], across, preferred_element_type=jnp.float32
        )
        scores = [jnp.where(old_seen, scores * scaling, NEGATIVE)]
        for k in range(chips):
            fresh = lax.dot_general(
                rows, new_keys[k][0], across, preferred_element_type=jnp.float32
            )
            gap = (place[1] - place[3 + k]) * count
            scores.append(jnp.where(ahead <= gap, fresh * scaling, NEGATIVE))
        top = jnp.max(scores[0], axis=-1, keepdims=True)
        for part in scores[1:]:
            top = jnp.maximum(top, jnp.max(part, axis=-1, keepdims=True))
        mix, total = 0.0, 0.0
        for part, values in zip(scores, [cache_value[0, 0], *[v[0] for v in new_values]]):
            weights = jnp.exp(part - top)
            total += jnp.sum(weights, axis=-1, keepdims=True)
            mix += jnp.dot(
                weights.astype(jnp.bfloat16), values, preferred_element_type=jnp.float32
            )
        out[:, g * HD : (g + 1) * HD] = (mix / total).astype(jnp.bfloat16)


def fill_attend(place, query, cache, entries, heads):
    count = query.shape[0]
    groups = query.shape[1] // heads // HD
    stored = cache.shape[2]
    chips = len(entries)
    pairs = count * groups * heads * (stored + chips * count)
    return pl.pallas_call(
        functools.partial(fill_kernel, groups, chips),
        out_shape=jax.ShapeDtypeStruct(query.shape, jnp.bfloat16),
        grid_spec=pltpu.PrefetchScalarGridSpec(
            num_scalar_prefetch=1,
            grid=(heads,),
            in_specs=[
                pl.BlockSpec((count, groups * HD), lambda j, s: (0, j)),
                pl.BlockSpec((1, 1, stored, HD), lambda j, s: (0, 0, 0, j)),
                pl.BlockSpec((1, 1, stored, HD), lambda j, s: (1, 0, 0, j)),
            ]
            + [pl.BlockSpec((1, count, HD), lambda j, s: (0, 0, j))] * chips
            + [pl.BlockSpec((1, count, HD), lambda j, s: (1, 0, j))] * chips,
            out_specs=pl.BlockSpec((count, groups * HD), lambda j, s: (0, j)),
        ),
        compiler_params=params(12),
        cost_estimate=cost(8 * pairs * HD, 2 * cache.size, pairs),
        name="fill_attend",
    )(place, query, cache, cache, *entries, *entries)


def step_kernel(heads, groups, lengths, query, cache_key, cache_value, new_key, new_value, out):
    scaling = 1.0 / math.sqrt(HD)
    stored = cache_key.shape[2]
    length = lengths[pl.program_id(0)]
    rows = query[0]
    old_key, old_value = cache_key[0, 0], cache_value[0, 0]
    across = (((1,), (1,)), ((), ()))
    old = lax.dot_general(rows, old_key, across, preferred_element_type=jnp.float32)
    seen = lax.broadcasted_iota(jnp.int32, (1, stored), 1) < length
    old = jnp.where(seen, old * scaling, NEGATIVE)
    own = jnp.sum(
        rows.astype(jnp.float32) * new_key[0].astype(jnp.float32), axis=-1, keepdims=True
    )
    own = own * scaling
    top = jnp.maximum(jnp.max(old, axis=-1, keepdims=True), own)
    old = jnp.exp(old - top)
    own = jnp.exp(own - top)
    total = jnp.sum(old, axis=-1, keepdims=True) + own
    mix = jnp.dot(
        (old / total).astype(jnp.bfloat16), old_value, preferred_element_type=jnp.float32
    )
    mix += (own / total).astype(jnp.bfloat16).astype(jnp.float32) * new_value[0].astype(jnp.float32)
    at = lax.broadcasted_iota(jnp.int32, (rows.shape[0], HD), 0) // groups
    picked = mix[:, :HD]
    for j in range(1, heads):
        picked = jnp.where(at == j, mix[:, j * HD : (j + 1) * HD], picked)
    out[0] = picked.astype(jnp.bfloat16)


def step_attend(lengths, query, cache, entries, slots, heads):
    groups = query.shape[1] // heads // HD
    stored = cache.shape[2]
    width = heads * HD
    pad = 16
    parts = query[:slots].reshape(slots, heads * groups, 1, HD)
    own = (
        jnp.arange(heads * groups, dtype=jnp.int32)[:, None] // groups
        == jnp.arange(heads, dtype=jnp.int32)[None, :]
    )
    spread = jnp.where(own[None, :, :, None], parts, jnp.bfloat16(0.0))
    spread = spread.reshape(slots, heads * groups, width)
    spread = jnp.pad(spread, ((0, 0), (0, pad - heads * groups), (0, 0)))
    new_key = entries[0, :slots].reshape(slots, 1, width)
    new_value = entries[1, :slots].reshape(slots, 1, width)
    out = pl.pallas_call(
        functools.partial(step_kernel, heads, groups),
        out_shape=jax.ShapeDtypeStruct((slots, pad, HD), jnp.bfloat16),
        grid_spec=pltpu.PrefetchScalarGridSpec(
            num_scalar_prefetch=1,
            grid=(slots,),
            in_specs=[
                pl.BlockSpec((1, pad, width), lambda s, n: (s, 0, 0)),
                pl.BlockSpec((1, 1, stored, width), lambda s, n: (0, s, 0, 0)),
                pl.BlockSpec((1, 1, stored, width), lambda s, n: (1, s, 0, 0)),
                pl.BlockSpec((1, 1, width), lambda s, n: (s, 0, 0)),
                pl.BlockSpec((1, 1, width), lambda s, n: (s, 0, 0)),
            ],
            out_specs=pl.BlockSpec((1, pad, HD), lambda s, n: (s, 0, 0)),
        ),
        compiler_params=params(8),
        cost_estimate=cost(64 * cache.size, 2 * cache.size, slots * stored * pad),
        name="step_attend",
    )(lengths, spread, cache, cache, new_key, new_value)
    return out[:, : heads * groups].reshape(slots, heads * groups * HD)


def out_kernel(place, mine, sib, weight, sib_weight, out):
    half = out.shape[1]
    cols = pl.ds(pl.multiple_of(place[0] * half, half), half)
    part = jnp.dot(mine[...], weight[:, cols], preferred_element_type=jnp.float32)
    part += jnp.dot(sib[...], sib_weight[...], preferred_element_type=jnp.float32)
    out[...] = part.astype(jnp.bfloat16)


def out_project(place, mine, sib, weight, sib_weight):
    rows, depth = mine.shape
    half = weight.shape[1] // 2
    return pl.pallas_call(
        out_kernel,
        out_shape=jax.ShapeDtypeStruct((rows, half), jnp.bfloat16),
        in_specs=[SMEM_WHOLE] + [VMEM_WHOLE] * 4,
        out_specs=VMEM_WHOLE,
        compiler_params=params(8),
        cost_estimate=cost(4 * rows * depth * half, 4 * depth * half + 6 * rows * half),
        name="out_project",
    )(place, mine, sib, weight, sib_weight)


def forward_kernel(chips, n_dec, n_after, chunk, place, *refs):
    refs = list(refs)
    mine, sib = refs[:2]
    shares = refs[2 : 2 + 2 * chips]
    refs = refs[2 + 2 * chips :]
    if n_dec:
        dec, dec_shares = refs[0], refs[1 : 1 + 2 * chips]
        refs = refs[1 + 2 * chips :]
    gain, gate, up, down = refs[:4]
    refs = refs[4 + n_after :]
    keep, give, resid = refs[:3]
    refs = refs[3:]
    if n_dec:
        dec_out, dec_resid = refs[:2]
        refs = refs[2:]
    held, inner, hidden = refs
    piece = mine.shape[0]
    half = shares[0].shape[1]
    core = place[0]
    jobs = [(mine, shares, core * piece, 0), (sib, shares, (1 - core) * piece, piece)]
    if n_dec:
        jobs.append((dec, dec_shares, 0, 2 * piece))
    for rows, parts, start, put in jobs:
        size = rows.shape[0]
        if not isinstance(start, int):
            start = pl.multiple_of(start, piece)
        for side in range(2):
            at = core if side == 0 else 1 - core
            cols = pl.ds(pl.multiple_of(at * half, half), half)
            added = parts[side][pl.ds(start, size), :].astype(jnp.float32)
            for k in range(1, chips):
                added += parts[2 * k + side][pl.ds(start, size), :].astype(jnp.float32)
            value = rows[:, cols].astype(jnp.float32) + added
            held[put : put + size, cols] = value.astype(jnp.bfloat16)
        inner[put : put + size, :] = normed(held[put : put + size, :].astype(jnp.float32), gain[...])
    resid[...] = held[:piece, :]
    if n_dec:
        dec_resid[...] = held[2 * piece :, :]

    @pl.loop(0, gate.shape[1] // chunk)
    def _(i):
        at = pl.ds(pl.multiple_of(i * chunk, chunk), chunk)
        gated = jnp.dot(inner[...], gate[:, at], preferred_element_type=jnp.float32)
        raised = jnp.dot(inner[...], up[:, at], preferred_element_type=jnp.float32)
        hidden[:, at] = (gated / (1.0 + jnp.exp(-gated)) * raised).astype(jnp.bfloat16)

    @pl.loop(0, down.shape[1] // chunk)
    def _(i):
        at = pl.ds(pl.multiple_of(i * chunk, chunk), chunk)
        part = jnp.dot(hidden[...], down[:, at], preferred_element_type=jnp.float32)
        part = part.astype(jnp.bfloat16)
        keep[:, at] = part[:piece]
        give[:, at] = part[piece : 2 * piece]
        if n_dec:
            dec_out[:, at] = part[2 * piece :]


def feed_forward(
    place, mine, sib, shares, gain, gate, up, down, dec=None, dec_shares=None, after=()
):
    piece, width = mine.shape
    chips = len(shares) // 2
    units = gate.shape[1]
    chunk = min(512, units)
    n_dec = 0 if dec is None else dec.shape[0]
    rows = 2 * piece + n_dec
    args = [mine, sib, *shares]
    if n_dec:
        args += [dec, *dec_shares]
    args += [gain, gate, up, down]
    sizes = [piece] * 3 + [n_dec] * 2 * bool(n_dec)
    return pl.pallas_call(
        functools.partial(forward_kernel, chips, n_dec, len(after), chunk),
        out_shape=[jax.ShapeDtypeStruct((n, width), jnp.bfloat16) for n in sizes],
        in_specs=[SMEM_WHOLE] + [VMEM_WHOLE] * len(args) + [UNREAD] * len(after),
        out_specs=[VMEM_WHOLE] * len(sizes),
        scratch_shapes=[
            pltpu.VMEM((rows, width), jnp.bfloat16),
            pltpu.VMEM((rows, width), jnp.bfloat16),
            pltpu.VMEM((rows, units), jnp.bfloat16),
        ],
        compiler_params=params(10),
        cost_estimate=cost(6 * rows * width * units, 6 * width * units, rows * units),
        name="feed_forward",
    )(place, *args, *after)


def angle_tables(places):
    halfway = HD // 2
    powers = jnp.arange(halfway, dtype=jnp.float32) * (2.0 / HD)
    inverse = THETA ** (-powers)
    angles = places.astype(jnp.float32)[:, None] * inverse[None, :]
    cosine, sine = jnp.cos(angles), jnp.sin(angles)
    return jnp.concatenate([cosine, cosine], axis=-1), jnp.concatenate([-sine, sine], axis=-1)


def add(*values):
    total = values[0].astype(jnp.float32)
    for value in values[1:]:
        total = total + value.astype(jnp.float32)
    return total.astype(jnp.bfloat16)


def on_device(
    prefill_rows,
    decode_rows,
    deal_order,
    prefill_offset,
    cache_length,
    prefill_cache,
    decode_cache,
    qkv_weight,
    out_weight,
    attention_gain,
    forward_gain,
    gate_weight,
    up_weight,
    down_weight,
):
    tensor_count = lax.axis_size("tensor")
    dp_count = lax.axis_size("dp")
    chips = tensor_count // 2
    tensor_place = lax.axis_index("tensor")
    group_place = lax.axis_index("dp")
    chip, core = tensor_place // 2, tensor_place % 2
    piece, width = prefill_rows.shape
    per_device = decode_rows.shape[0]
    requests = deal_order.shape[0]
    slots = cache_length.shape[0]
    padded = -(-slots // 16) * 16
    heads = qkv_weight.shape[1]
    tokens = piece * tensor_count
    half = width // 2

    def place_of(k):
        spots = [core, (chip + k) % chips, prefill_offset[0]]
        return jnp.stack(spots + [(chip + j) % chips for j in range(chips)]).astype(jnp.int32)

    places = [place_of(k) for k in range(chips)]
    weight = in_vmem(qkv_weight.reshape(width, -1))
    gate_weight, up_weight, down_weight = map(in_vmem, (gate_weight, up_weight, down_weight))
    prefill_cache, decode_cache = in_hbm(prefill_cache), in_hbm(decode_cache)

    mines = [prefill_rows] + [from_chip(prefill_rows, k) for k in range(1, chips)]
    sibs = [swap_cores(rows) for rows in mines]

    low = max(dp_count // 4, 1)
    pool = [decode_rows] + [swap_groups(decode_rows, i) for i in range(1, low)]
    pool = jnp.concatenate(pool, axis=0)
    pool = [pool] + [swap_groups(pool, i * low) for i in range(1, dp_count // low)]
    pool = jnp.concatenate(pool, axis=0)
    index = jnp.arange(dp_count * per_device, dtype=jnp.int32)
    origin = jnp.bitwise_xor(group_place, index // per_device)
    request = (origin * tensor_count + tensor_place) * per_device + index % per_device
    slot_of = jnp.sum(
        jnp.where(
            request[:, None] == jnp.arange(requests, dtype=jnp.int32)[None, :],
            deal_order[None, :],
            0,
        ),
        axis=1,
    )
    in_group = slot_of - group_place * slots
    chooser = (jnp.arange(padded, dtype=jnp.int32)[:, None] == in_group[None, :]) & (
        in_group[None, :] < slots
    )
    dealt = jnp.dot(
        chooser.astype(jnp.bfloat16), pool, preferred_element_type=jnp.float32
    ).astype(jnp.bfloat16)

    gain = attention_gain.reshape(1, width)
    tables = angle_tables(prefill_offset[0] + jnp.arange(tokens, dtype=jnp.int32))
    dec_tables = angle_tables(jnp.pad(cache_length, (0, padded - slots)))
    queries, entries = [None] * chips, [None] * chips
    for k in range(chips):
        last = k == chips - 1
        if last:
            dealt = add(dealt, swap_cores(dealt))
            dealt, queries[0] = lax.optimization_barrier((dealt, queries[0]))
            dealt = add(dealt, *[from_chip(dealt, j) for j in range(1, chips)])
        got = project(
            places[k],
            mines[k],
            sibs[k],
            gain,
            weight,
            tables,
            heads,
            dealt if last else None,
            dec_tables if last else None,
            [dealt] if k == 0 else [],
        )
        queries[k], entries[k] = got[:2]
        if last:
            dec_query, dec_entries = got[2:]

    col = pl.multiple_of((1 - core) * half, half)
    sib_weight = in_vmem(swap_cores(lax.dynamic_slice_in_dim(out_weight, col, half, 1)))
    out_weight = in_vmem(out_weight)

    def finish(attended, place):
        return out_project(place, attended, swap_cores(attended), out_weight, sib_weight)

    parts = []
    for k in range(chips):
        attended = fill_attend(places[k], queries[k], prefill_cache, entries, heads)
        parts.append(finish(attended, places[k]))
    dec_att = step_attend(cache_length, dec_query, decode_cache, dec_entries, slots, heads)
    dec_att = jnp.pad(dec_att, ((0, padded - slots), (0, 0)))
    dec_part = finish(dec_att, places[0])

    def shares_of(own, others):
        pairs = []
        for value in [own, *others]:
            pairs += [value, swap_cores(value)]
        return pairs

    dec_shares = shares_of(dec_part, [from_chip(dec_part, j) for j in range(1, chips)])
    gain = forward_gain.reshape(1, width)
    order = [*range(1, chips), 0]

    def fetch(b):
        return [from_chip(parts[(b - j) % chips], j) for j in range(1, chips)]

    theirs = fetch(order[0])
    arrived = []
    for n, b in enumerate(order):
        got = feed_forward(
            places[b],
            mines[b],
            sibs[b],
            shares_of(parts[b], theirs),
            gain,
            gate_weight,
            up_weight,
            down_weight,
            dealt if n == 0 else None,
            dec_shares if n == 0 else None,
            [routed] if n + 1 == chips else [],
        )
        keep, give, resid = got[:3]
        if n + 1 < chips:
            theirs = fetch(order[n + 1])
            arrived.append(from_chip(add(keep, swap_cores(give)), chips - b))
        if n == 0:
            dec_sum, dec_resid = got[3:]
            dec_sum = add(dec_sum, swap_cores(dec_sum))
            dec_sum, theirs = lax.optimization_barrier((dec_sum, theirs))
            final = add(dec_resid, dec_sum, *[from_chip(dec_sum, j) for j in range(1, chips)])
            picker = in_group[:, None] == jnp.arange(padded, dtype=jnp.int32)[None, :]
            picker = picker & (in_group[:, None] < slots)
            routed = jnp.dot(
                picker.astype(jnp.bfloat16), final, preferred_element_type=jnp.float32
            ).astype(jnp.bfloat16)
    give = jnp.concatenate([swap_cores(part) for part in jnp.split(give, 2, axis=1)], axis=1)
    prefill_out = add(resid, keep, give, *arrived)

    low = max(dp_count // 4, 1)
    pairs = routed.reshape(dp_count // low, low * per_device, width)
    rows = add(
        pairs[0], *[swap_groups(pairs[i], i * low) for i in range(1, dp_count // low)]
    )
    pairs = rows.reshape(low, per_device, width)
    routed = add(pairs[0], *[swap_groups(pairs[i], i) for i in range(1, low)])

    around = jnp.concatenate(entries + entries[:-1], axis=1)
    prefill_entries = lax.dynamic_slice_in_dim(
        around, (chips - chip) % chips * 2 * piece, tokens, 1
    )
    return (prefill_out, routed, prefill_entries, dec_entries[:, :slots])


def solution(mesh):
    placed = (
        P(("dp", "tensor"), None),
        P(("dp", "tensor"), None),
        P(),
        P("dp"),
        P("dp"),
        P(None, "dp", None, "tensor"),
        P(None, "dp", None, "tensor"),
        P(None, "tensor", None),
        P("tensor", None),
        P(),
        P(),
        P(None, "tensor"),
        P(None, "tensor"),
        P("tensor", None),
    )
    return jax.shard_map(
        on_device,
        mesh=mesh,
        in_specs=placed,
        out_specs=(
            P(("dp", "tensor"), None),
            P(("dp", "tensor"), None),
            P(None, "dp", "tensor"),
            P(None, "dp", "tensor"),
        ),
        check_vma=False,
    )
```

time: 150 us -> 141 us (0.940)
  Pallas kernels: 63.1 us -> 51.2 us
  waiting for transfers between devices: 35.6 us -> 26.5 us
  local copies, waits for them, and re-layouts: 23.5 us -> 31.5 us
  starting transfers between devices: 17.3 us -> 20.9 us
    pallas_call x6, Pallas kernels: 51.6 us -> 36.5 us  [the longest x2 21.4 us: feed_forward(): pl.pallas_call(functools.partial(forward_kernel, chips, n_dec, len(after)...]
    ppermute x7, waiting for transfers between devices: 23.6 us -> 15.8 us  [from_chip(): lax.ppermute(value, 'tensor', [(i, (i // 2 - step) % chips * 2 + i % 2) f...]
    unnamed x43 -> x59, local copies, waits for them, and re-layouts: 20.4 us -> 28.1 us
    pallas_call x1, Pallas kernels: 6.3 us -> 9.82 us  [step_attend(): pl.pallas_call(functools.partial(step_kernel, heads, groups), out_shape=j...]
    ppermute x6 -> x8, waiting for transfers between devices: 5.78 us -> 2.5 us  [swap_groups(): return lax.ppermute(value, 'dp', [(i, i ^ mask) for i in range(count)])]
    ppermute x6 -> x8, starting transfers between devices: 8.43 us -> 11 us  [swap_groups(): return lax.ppermute(value, 'dp', [(i, i ^ mask) for i in range(count)])]
    ppermute x16 -> x17, waiting for transfers between devices: 6.26 us -> 8.24 us  [swap_cores(): return lax.ppermute(value, 'tensor', [(i, i ^ 1) for i in range(count)])]
    ppermute x16 -> x17, starting transfers between devices: 2.32 us -> 3.32 us  [swap_cores(): return lax.ppermute(value, 'tensor', [(i, i ^ 1) for i in range(count)])]
  transfers between devices with their start and end apart: 29 -> 32, of which waited for: 14 -> 13; matrix products, arithmetic and copies ran while one was open for 10% -> 11% of each run, Pallas kernels for 41% -> 35%
where the time goes in v2:
time: 141 us; the launch traced here: 140 us
  Pallas kernels  51.2 us (36%)
  local copies, waits for them, and re-layouts  31.5 us (22%)
  waiting for transfers between devices  26.5 us (19%)
  starting transfers between devices  20.9 us (15%)
  other arithmetic  8.06 us (6%)
  between operations  1.83 us (1%)
    unnamed x59, local copies, waits for them, and re-layouts  28.1 us
    pallas_call x2, Pallas kernels, feed_forward(): pl.pallas_call(functools.partial(forward_kernel, chips, n_dec, len(after)...  21.4 us
    ppermute x7, waiting for transfers between devices, from_chip(): lax.ppermute(value, 'tensor', [(i, (i // 2 - step) % chips * 2 + i % 2) f...  15.8 us
    ppermute x8, starting transfers between devices, swap_groups(): return lax.ppermute(value, 'dp', [(i, i ^ mask) for i in range(count)])  11 us
    pallas_call x1, Pallas kernels, step_attend(): pl.pallas_call(functools.partial(step_kernel, heads, groups), out_shape=j...  9.82 us
    pallas_call x2, Pallas kernels, fill_attend(): pl.pallas_call(functools.partial(fill_kernel, groups, chips), out_shape=j...  9.46 us
    ppermute x17, waiting for transfers between devices, swap_cores(): return lax.ppermute(value, 'tensor', [(i, i ^ 1) for i in range(count)])  8.24 us
    ppermute x7, starting transfers between devices, from_chip(): lax.ppermute(value, 'tensor', [(i, (i // 2 - step) % chips * 2 + i % 2) f...  6.57 us
  transfers between devices with their start and end apart: 32, of which 13 were waited for; matrix products, arithmetic and copies ran while one was open for 11% of the time, Pallas kernels for 35%

profile of v2, /device:TPU:0, one launch (start us, length us, event | category | flops | bytes accessed | tf_op | source)
XLA Modules:
  0.0 140.3 jit_solution(1992296322698947861)
XLA Ops:
  1.2 2.6 %collective-permute-start.6 = (bf16[128,2048]{1,0:T(8,128)(2,1)}, bf16[128,2048]{1,0:T(8,128)(2,1)}, u32[]{:S(2)}, u32[]{:S(2)}) collective-permute-start(bf16[128,2048]{1,0:T(8,128)(2,1)} %refs_0_.3), channel_id=1, source_target_pairs={{0,2},{1,3},{2,0},{3,1},{4,6},{5,7},{6,4},{7,5},{8,10},{9,11},{10,... | collective-permute-start | bytes 1572872 | tf_op jit(solution)/shard_map/ppermute | solution.py:26
  3.7 1.5 %collective-permute-start.1 = (bf16[2,2048]{1,0:T(2,128)(2,1)}, bf16[2,2048]{1,0:T(2,128)(2,1)S(1)}, u32[]{:S(2)}, u32[]{:S(2)}) collective-permute-start(bf16[2,2048]{1,0:T(2,128)(2,1)} %param.15), channel_id=1, source_target_pairs={{0,4},{4,0},{8,12},{12,8},{16,20},{20,16},{24,28},{28,24},{1,5},{5... | collective-permute-start | bytes 24584 | tf_op jit(solution)/shard_map/ppermute | solution.py:33
  8.6 2.3 %constant_dynamic-slice_fusion = bf16[512,1024]{1,0:T(8,128)(2,1)} fusion(bf16[512,2048]{1,0:T(8,128)(2,1)} %weight.5, s32[]{:T(128)S(6)} %select_n.82), kind=kLoop, calls=%fused_computation.54 | loop fusion | bytes 2097156 | tf_op jit(solution)/shard_map/dynamic_slice | solution.py:490
  12.5 1.6 %collective-permute-start.2 = (bf16[4,2048]{1,0:T(4,128)(2,1)S(1)}, bf16[4,2048]{1,0:T(4,128)(2,1)S(1)}, u32[]{:S(2)}, u32[]{:S(2)}) collective-permute-start(bf16[4,2048]{1,0:T(4,128)(2,1)S(1)} %pad_maximum_fusion.2), channel_id=1, source_target_pairs={{0,8},{4,12},{8,0},{12,4},{16,24},{20,28},{24,16},{28,20},{1,9},{5... | collective-permute-start | bytes 49160 | tf_op jit(solution)/shard_map/ppermute | solution.py:33
  14.1 2.6 %collective-permute-start.3 = (bf16[4,2048]{1,0:T(4,128)(2,1)S(1)}, bf16[4,2048]{1,0:T(4,128)(2,1)S(1)}, u32[]{:S(2)}, u32[]{:S(2)}) collective-permute-start(bf16[4,2048]{1,0:T(4,128)(2,1)S(1)} %pad_maximum_fusion.2), channel_id=1, source_target_pairs={{0,16},{4,20},{8,24},{12,28},{16,0},{20,4},{24,8},{28,12},{1,17},{... | collective-permute-start | bytes 49160 | tf_op jit(solution)/shard_map/ppermute | solution.py:33
  17.2 5.4 %copy.25 = bf16[256,8,2,512]{3,1,2,0:T(8,128)(2,1)} copy(bf16[256,8,2,512]{3,2,1,0:T(2,128)(2,1)} %bitcast.33) | data formatting | bytes 8388608
  23.4 1.9 %collective-permute-done.5 = bf16[16,2048]{1,0:T(8,128)(2,1)S(1)} collective-permute-done((bf16[16,2048]{1,0:T(8,128)(2,1)S(1)}, bf16[16,2048]{1,0:T(8,128)(2,1)S(1)}, u32[]{:S(2)}, u32[]{:S(2)}) %collective-permute-start.5) | collective-permute-done | bytes 65568 | tf_op jit(solution)/shard_map/ppermute | solution.py:20
  26.2 2.2 %copy-done = bf16[256,8,2,512]{3,1,2,0:T(8,128)(2,1)S(1)} copy-done((bf16[256,8,2,512]{3,1,2,0:T(8,128)(2,1)S(1)}, bf16[256,8,2,512]{3,1,2,0:T(8,128)(2,1)}, u32[]{:S(2)}) %copy-start) | copy-done | bytes 4194328
  31.4 2.4 %project.2 = (bf16[256,512]{1,0:T(8,128)(2,1)S(1)}, bf16[2,256,256]{2,1,0:T(8,128)(2,1)S(1)}) custom-call(s32[5]{0:T(128)S(1)} %stack.23.place, bf16[128,2048]{1,0:T(8,128)(2,1)S(1)} %copy-done.11, bf16[128,2048]{1,0:T(8,128)(2,1)S(1)} %copy-done.14, f32[1,2048]{1,0:T(1,128)S(1)} %bitcast.29, bf16[2048,1024]{1,0:T(8,128)(2,1)S(1)} %bitcast.23, ...), custom_call_target="tpu_custom_call" | custom-call | flops 1073741824 | bytes 6291456 | tf_op jit(solution)/shard_map/project/pallas_call | solution.py:131
  34.4 3.7 %collective-permute-done.8 = bf16[16,2048]{1,0:T(8,128)(2,1)S(1)} collective-permute-done((bf16[16,2048]{1,0:T(8,128)(2,1)S(1)}, bf16[16,2048]{1,0:T(8,128)(2,1)S(1)}, u32[]{:S(2)}, u32[]{:S(2)}) %collective-permute-start.8) | collective-permute-done | bytes 65568 | tf_op jit(solution)/shard_map/ppermute | solution.py:26
  38.2 2.2 %copy-done.1 = bf16[256,8,2,512]{3,1,2,0:T(8,128)(2,1)S(1)} copy-done((bf16[256,8,2,512]{3,1,2,0:T(8,128)(2,1)S(1)}, bf16[256,8,2,512]{3,1,2,0:T(8,128)(2,1)}, u32[]{:S(2)}) %copy-start.1) | copy-done | bytes 4194328
  41.3 3.3 %project.3 = (bf16[256,512]{1,0:T(8,128)(2,1)S(1)}, bf16[2,256,256]{2,1,0:T(8,128)(2,1)S(1)}, bf16[16,512]{1,0:T(8,128)(2,1)S(1)}, bf16[2,16,256]{2,1,0:T(8,128)(2,1)S(1)}) custom-call(s32[5]{0:T(128)S(1)} %stack.24.place, bf16[128,2048]{1,0:T(8,128)(2,1)} %collective-permute-done.6.refs_0_, bf16[128,2048]{1,0:T(8,128)(2,1)S(1)} %collective-permute-done.7.refs_1_, ...), custom_call_target="tpu_custom_call" | custom-call | flops 1140850688 | bytes 6422528 | tf_op jit(solution)/shard_map/project/pallas_call | solution.py:131
  44.6 4.8 %fill_attend.2.mine = bf16[256,512]{1,0:T(8,128)(2,1)S(1)} custom-call(s32[5]{0:T(128)S(1)} %stack.23.place, bf16[256,512]{1,0:T(8,128)(2,1)S(1)} %get-tuple-element.22.query, bf16[2,1,1024,256]{3,2,1,0:T(8,128)(2,1)} %cache_value.4, bf16[2,1,1024,256]{3,2,1,0:T(8,128)(2,1)} %cache_value.4, bf16[2,256,256]{2,1,0:T(8,128)(2,1)S(1)} %get-tuple-element.23.refs_0_.refs_2_, ...), custom_call_target="tpu_custom_call" | custom-call | flops 1610612736 | bytes 1048576 | tf_op jit(solution)/shard_map/fill_attend/pallas_call | solution.py:184
  49.6 1.4 %collective-permute-done.9.sib = bf16[256,512]{1,0:T(8,128)(2,1)S(1)} collective-permute-done((bf16[256,512]{1,0:T(8,128)(2,1)S(1)}, bf16[256,512]{1,0:T(8,128)(2,1)S(1)}, u32[]{:S(2)}, u32[]{:S(2)}) %collective-permute-start.9) | collective-permute-done | bytes 262176 | tf_op jit(solution)/shard_map/ppermute | solution.py:20
  51.1 2.1 %out_project.3.refs_2_ = bf16[256,1024]{1,0:T(8,128)(2,1)} custom-call(s32[5]{0:T(128)S(1)} %stack.23.place, bf16[256,512]{1,0:T(8,128)(2,1)S(1)} %fill_attend.2.mine, bf16[256,512]{1,0:T(8,128)(2,1)S(1)} %collective-permute-done.9.sib, bf16[512,2048]{1,0:T(8,128)(2,1)S(1)} %copy-done.6, bf16[512,1024]{1,0:T(8,128)(2,1)S(1)} %collective-permute-done.10.sib_weight), custom_call_target="tpu_custom_call" | custom-call | flops 536870912 | bytes 3670016 | tf_op jit(solution)/shard_map/out_project/pallas_call | solution.py:282
  53.7 4.6 %fill_attend.3.mine = bf16[256,512]{1,0:T(8,128)(2,1)S(1)} custom-call(s32[5]{0:T(128)S(1)} %stack.24.place, bf16[256,512]{1,0:T(8,128)(2,1)S(1)} %get-tuple-element.26.query, bf16[2,1,1024,256]{3,2,1,0:T(8,128)(2,1)} %cache_value.4, bf16[2,1,1024,256]{3,2,1,0:T(8,128)(2,1)} %cache_value.4, bf16[2,256,256]{2,1,0:T(8,128)(2,1)S(1)} %get-tuple-element.23.refs_0_.refs_2_, ...), custom_call_target="tpu_custom_call" | custom-call | flops 1610612736 | bytes 1048576 | tf_op jit(solution)/shard_map/fill_attend/pallas_call | solution.py:184
  58.5 1.5 %collective-permute-done.12.sib = bf16[256,512]{1,0:T(8,128)(2,1)} collective-permute-done((bf16[256,512]{1,0:T(8,128)(2,1)S(1)}, bf16[256,512]{1,0:T(8,128)(2,1)}, u32[]{:S(2)}, u32[]{:S(2)}) %collective-permute-start.12) | collective-permute-done | bytes 262176 | tf_op jit(solution)/shard_map/ppermute | solution.py:20
  60.1 1.8 %out_project.4.refs_2_ = bf16[256,1024]{1,0:T(8,128)(2,1)S(1)} custom-call(s32[5]{0:T(128)S(1)} %stack.24.place, bf16[256,512]{1,0:T(8,128)(2,1)S(1)} %fill_attend.3.mine, bf16[256,512]{1,0:T(8,128)(2,1)} %collective-permute-done.12.sib, bf16[512,2048]{1,0:T(8,128)(2,1)S(1)} %copy-done.6, bf16[512,1024]{1,0:T(8,128)(2,1)S(1)} %collective-permute-done.10.sib_weight), custom_call_target="tpu_custom_call" | custom-call | flops 536870912 | bytes 3670016 | tf_op jit(solution)/shard_map/out_project/pallas_call | solution.py:282
  62.1 5.3 %collective-permute-done.14.refs_4_ = bf16[256,1024]{1,0:T(8,128)(2,1)} collective-permute-done((bf16[256,1024]{1,0:T(8,128)(2,1)}, bf16[256,1024]{1,0:T(8,128)(2,1)}, u32[]{:S(2)}, u32[]{:S(2)}) %collective-permute-start.14) | collective-permute-done | bytes 524320 | tf_op jit(solution)/shard_map/ppermute | solution.py:26
  67.5 9.8 %step_attend.1 = bf16[8,16,128]{2,1,0:T(8,128)(2,1)S(1)} custom-call(s32[8]{0:T(128)S(1)} %copy-done.22, bf16[8,16,256]{2,1,0:T(8,128)(2,1)S(1)} %pad.13.query, bf16[2,8,1024,256]{3,2,1,0:T(8,128)(2,1)} %cache_value.5, bf16[2,8,1024,256]{3,2,1,0:T(8,128)(2,1)} %cache_value.5, bf16[8,1,256]{2,1,0:T(2,128)(2,1)S(1)} %copy.23.new_key, ...), custom_call_target="tpu_custom_call" | custom-call | flops 268435456 | bytes 8388608 | tf_op jit(solution)/shard_map/step_attend/pallas_call | solution.py:249
  80.3 3.3 %collective-permute-done.18.refs_9_ = bf16[16,1024]{1,0:T(8,128)(2,1)S(1)} collective-permute-done((bf16[16,1024]{1,0:T(8,128)(2,1)S(1)}, bf16[16,1024]{1,0:T(8,128)(2,1)S(1)}, u32[]{:S(2)}, u32[]{:S(2)}) %collective-permute-start.18) | collective-permute-done | bytes 32800 | tf_op jit(solution)/shard_map/ppermute | solution.py:26
  84.9 3.4 %copy-done.4 = bf16[2048,2048]{1,0:T(8,128)(2,1)S(1)} copy-done((bf16[2048,2048]{1,0:T(8,128)(2,1)S(1)}, bf16[2048,2048]{1,0:T(8,128)(2,1)}, u32[]{:S(2)}) %copy-start.4) | copy-done | bytes 8388632
  88.3 11.1 %feed_forward.2 = (bf16[128,2048]{1,0:T(8,128)(2,1)S(1)}, bf16[128,2048]{1,0:T(8,128)(2,1)S(1)}, bf16[128,2048]{1,0:T(8,128)(2,1)}, bf16[16,2048]{1,0:T(8,128)(2,1)S(1)}, bf16[16,2048]{1,0:T(8,128)(2,1)S(1)}) custom-call(s32[5]{0:T(128)S(1)} %stack.24.place, bf16[128,2048]{1,0:T(8,128)(2,1)} %collective-permute-done.6.refs_0_, ...), custom_call_target="tpu_custom_call" | custom-call | flops 6845104128 | bytes 25165824 | tf_op jit(solution)/shard_map/feed_forward/pallas_call | solution.py:364
  101.6 3.4 %collective-permute-done.23 = bf16[16,2048]{1,0:T(8,128)(2,1)S(1)} collective-permute-done((bf16[16,2048]{1,0:T(8,128)(2,1)S(1)}, bf16[16,2048]{1,0:T(8,128)(2,1)S(1)}, u32[]{:S(2)}, u32[]{:S(2)}) %collective-permute-start.23) | collective-permute-done | bytes 65568 | tf_op jit(solution)/shard_map/ppermute | solution.py:26
  106.0 3.5 %collective-permute-start.29 = (bf16[4,2048]{1,0:T(4,128)(2,1)S(1)}, bf16[4,2048]{1,0:T(4,128)(2,1)S(1)}, u32[]{:S(2)}, u32[]{:S(2)}) collective-permute-start(bf16[4,2048]{1,0:T(4,128)(2,1)S(1)} %get-tuple-element.44), channel_id=1, source_target_pairs={{0,16},{4,20},{8,24},{12,28},{16,0},{20,4},{24,8},{28,12},{1,17},{... | collective-permute-start | bytes 49160 | tf_op jit(solution)/shard_map/ppermute | solution.py:33
  109.8 1.7 %fusion.1 = bf16[2,512,256]{2,1,0:T(8,128)(2,1)} fusion(s32[]{:T(128)S(6)} %select_n.86, bf16[2,256,256]{2,1,0:T(8,128)(2,1)S(1)} %copy-done.17, bf16[2,256,256]{2,1,0:T(8,128)(2,1)S(1)} %copy-done.19), kind=kLoop, calls=%fused_computation.8 | loop fusion | flops 1572864 | bytes 1048580 | tf_op jit(solution)/shard_map/concatenate | solution.py:558
  112.6 2.5 %collective-permute-done.30 = bf16[4,2048]{1,0:T(4,128)(2,1)S(1)} collective-permute-done((bf16[4,2048]{1,0:T(4,128)(2,1)S(1)}, bf16[4,2048]{1,0:T(4,128)(2,1)S(1)}, u32[]{:S(2)}, u32[]{:S(2)}) %collective-permute-start.30) | collective-permute-done | bytes 16416 | tf_op jit(solution)/shard_map/ppermute | solution.py:33
  116.8 3.4 %copy-done.2 = bf16[2048,2048]{1,0:T(8,128)(2,1)S(1)} copy-done((bf16[2048,2048]{1,0:T(8,128)(2,1)S(1)}, bf16[2048,2048]{1,0:T(8,128)(2,1)}, u32[]{:S(2)}) %copy-start.2) | copy-done | bytes 8388632
  120.1 3.4 %copy-done.3 = bf16[2048,2048]{1,0:T(8,128)(2,1)S(1)} copy-done((bf16[2048,2048]{1,0:T(8,128)(2,1)S(1)}, bf16[2048,2048]{1,0:T(8,128)(2,1)}, u32[]{:S(2)}) %copy-start.3) | copy-done | bytes 8388632
  123.5 3.4 %copy-done.5 = bf16[2048,2048]{1,0:T(8,128)(2,1)S(1)} copy-done((bf16[2048,2048]{1,0:T(8,128)(2,1)S(1)}, bf16[2048,2048]{1,0:T(8,128)(2,1)}, u32[]{:S(2)}) %copy-start.5) | copy-done | bytes 8388632
  126.9 10.3 %feed_forward.3 = (bf16[128,2048]{1,0:T(8,128)(2,1)S(1)}, bf16[128,2048]{1,0:T(8,128)(2,1)S(1)}, bf16[128,2048]{1,0:T(8,128)(2,1)S(1)}) custom-call(s32[5]{0:T(128)S(1)} %stack.23.place, bf16[128,2048]{1,0:T(8,128)(2,1)S(1)} %copy-done.12, bf16[128,2048]{1,0:T(8,128)(2,1)S(1)} %copy-done.15, bf16[256,1024]{1,0:T(8,128)(2,1)} %out_project.3.refs_2_, ...), custom_call_target="tpu_custom_call" | custom-call | flops 6442450944 | bytes 25165824 | tf_op jit(solution)/shard_map/feed_forward/pallas_call | solution.py:364
  139.2 1.1 add_convert_fusion
  (145 shorter events, 25.0 us)
Async XLA Ops:
  0.7 24.7 %collective-permute-start = (bf16[128,2048]{1,0:T(8,128)(2,1)}, bf16[128,2048]{1,0:T(8,128)(2,1)S(1)}, u32[]{:S(2)}, u32[]{:S(2)}) collective-permute-start(bf16[128,2048]{1,0:T(8,128)(2,1)} %refs_0_.3), channel_id=1, source_target_pairs={{0,1},{1,0},{2,3},{3,2},{4,5},{5,4},{6,7},{7,6},{8,9},{9,8},{10,11... | collective-permute-start | bytes 1572872 | tf_op jit(solution)/shard_map/ppermute | solution.py:20
  1.2 33.3 %collective-permute-start.6 = (bf16[128,2048]{1,0:T(8,128)(2,1)}, bf16[128,2048]{1,0:T(8,128)(2,1)}, u32[]{:S(2)}, u32[]{:S(2)}) collective-permute-start(bf16[128,2048]{1,0:T(8,128)(2,1)} %refs_0_.3), channel_id=1, source_target_pairs={{0,2},{1,3},{2,0},{3,1},{4,6},{5,7},{6,4},{7,5},{8,10},{9,11},{10,... | collective-permute-start | bytes 1572872 | tf_op jit(solution)/shard_map/ppermute | solution.py:26
  3.7 8.0 %collective-permute-start.1 = (bf16[2,2048]{1,0:T(2,128)(2,1)}, bf16[2,2048]{1,0:T(2,128)(2,1)S(1)}, u32[]{:S(2)}, u32[]{:S(2)}) collective-permute-start(bf16[2,2048]{1,0:T(2,128)(2,1)} %param.15), channel_id=1, source_target_pairs={{0,4},{4,0},{8,12},{12,8},{16,20},{20,16},{24,28},{28,24},{1,5},{5... | collective-permute-start | bytes 24584 | tf_op jit(solution)/shard_map/ppermute | solution.py:33
  12.5 10.1 %collective-permute-start.2 = (bf16[4,2048]{1,0:T(4,128)(2,1)S(1)}, bf16[4,2048]{1,0:T(4,128)(2,1)S(1)}, u32[]{:S(2)}, u32[]{:S(2)}) collective-permute-start(bf16[4,2048]{1,0:T(4,128)(2,1)S(1)} %pad_maximum_fusion.2), channel_id=1, source_target_pairs={{0,8},{4,12},{8,0},{12,4},{16,24},{20,28},{24,16},{28,20},{1,9},{5... | collective-permute-start | bytes 49160 | tf_op jit(solution)/shard_map/ppermute | solution.py:33
  14.1 8.4 %collective-permute-start.3 = (bf16[4,2048]{1,0:T(4,128)(2,1)S(1)}, bf16[4,2048]{1,0:T(4,128)(2,1)S(1)}, u32[]{:S(2)}, u32[]{:S(2)}) collective-permute-start(bf16[4,2048]{1,0:T(4,128)(2,1)S(1)} %pad_maximum_fusion.2), channel_id=1, source_target_pairs={{0,16},{4,20},{8,24},{12,28},{16,0},{20,4},{24,8},{28,12},{1,17},{... | collective-permute-start | bytes 49160 | tf_op jit(solution)/shard_map/ppermute | solution.py:33
  16.7 5.8 %collective-permute-start.4 = (bf16[4,2048]{1,0:T(4,128)(2,1)S(1)}, bf16[4,2048]{1,0:T(4,128)(2,1)S(1)}, u32[]{:S(2)}, u32[]{:S(2)}) collective-permute-start(bf16[4,2048]{1,0:T(4,128)(2,1)S(1)} %pad_maximum_fusion.2), channel_id=1, source_target_pairs={{0,24},{4,28},{8,16},{12,20},{16,8},{20,12},{24,0},{28,4},{1,25},{... | collective-permute-start | bytes 49160 | tf_op jit(solution)/shard_map/ppermute | solution.py:33
  22.6 27.1 %collective-permute-start.10 = (bf16[512,1024]{1,0:T(8,128)(2,1)}, bf16[512,1024]{1,0:T(8,128)(2,1)S(1)}, u32[]{:S(2)}, u32[]{:S(2)}) collective-permute-start(bf16[512,1024]{1,0:T(8,128)(2,1)} %constant_dynamic-slice_fusion), channel_id=1, source_target_pairs={{0,1},{1,0},{2,3},{3,2},{4,5},{5,4},{6,7},{7,6},{8,9},{9,8},{10,11... | collective-permute-start | bytes 3145736 | tf_op jit(solution)/shard_map/ppermute | solution.py:20
  22.8 2.5 %collective-permute-start.5 = (bf16[16,2048]{1,0:T(8,128)(2,1)S(1)}, bf16[16,2048]{1,0:T(8,128)(2,1)S(1)}, u32[]{:S(2)}, u32[]{:S(2)}) collective-permute-start(bf16[16,2048]{1,0:T(8,128)(2,1)S(1)} %convolution_convert_fusion.1.refs_6_), channel_id=1, source_target_pairs={{0,1},{1,0},{2,3},{3,2},{4,5},{5,4},{6,7},{7,6},{8,9},{9,8},{10,11... | collective-permute-start | bytes 196616 | tf_op jit(solution)/shard_map/ppermute | solution.py:20
  33.8 4.3 %collective-permute-start.8 = (bf16[16,2048]{1,0:T(8,128)(2,1)S(1)}, bf16[16,2048]{1,0:T(8,128)(2,1)S(1)}, u32[]{:S(2)}, u32[]{:S(2)}) collective-permute-start(bf16[16,2048]{1,0:T(8,128)(2,1)S(1)} %add_convert_fusion.5), channel_id=1, source_target_pairs={{0,2},{1,3},{2,0},{3,1},{4,6},{5,7},{6,4},{7,5},{8,10},{9,11},{10,... | collective-permute-start | bytes 196616 | tf_op jit(solution)/shard_map/ppermute | solution.py:26
  34.4 3.8 %collective-permute-start.7 = (bf16[128,2048]{1,0:T(8,128)(2,1)}, bf16[128,2048]{1,0:T(8,128)(2,1)S(1)}, u32[]{:S(2)}, u32[]{:S(2)}) collective-permute-start(bf16[128,2048]{1,0:T(8,128)(2,1)} %collective-permute-done.6.refs_0_), channel_id=1, source_target_pairs={{0,1},{1,0},{2,3},{3,2},{4,5},{5,4},{6,7},{7,6},{8,9},{9,8},{10,11... | collective-permute-start | bytes 1572872 | tf_op jit(solution)/shard_map/ppermute | solution.py:20
  49.5 1.6 %collective-permute-start.9 = (bf16[256,512]{1,0:T(8,128)(2,1)S(1)}, bf16[256,512]{1,0:T(8,128)(2,1)S(1)}, u32[]{:S(2)}, u32[]{:S(2)}) collective-permute-start(bf16[256,512]{1,0:T(8,128)(2,1)S(1)} %fill_attend.2.mine), channel_id=1, source_target_pairs={{0,1},{1,0},{2,3},{3,2},{4,5},{5,4},{6,7},{7,6},{8,9},{9,8},{10,11... | collective-permute-start | bytes 786440 | tf_op jit(solution)/shard_map/ppermute | solution.py:20
  53.1 14.3 %collective-permute-start.14 = (bf16[256,1024]{1,0:T(8,128)(2,1)}, bf16[256,1024]{1,0:T(8,128)(2,1)}, u32[]{:S(2)}, u32[]{:S(2)}) collective-permute-start(bf16[256,1024]{1,0:T(8,128)(2,1)} %out_project.3.refs_2_), channel_id=1, source_target_pairs={{0,2},{1,3},{2,0},{3,1},{4,6},{5,7},{6,4},{7,5},{8,10},{9,11},{10,... | collective-permute-start | bytes 1572872 | tf_op jit(solution)/shard_map/ppermute | solution.py:26
  58.3 1.7 %collective-permute-start.12 = (bf16[256,512]{1,0:T(8,128)(2,1)S(1)}, bf16[256,512]{1,0:T(8,128)(2,1)}, u32[]{:S(2)}, u32[]{:S(2)}) collective-permute-start(bf16[256,512]{1,0:T(8,128)(2,1)S(1)} %fill_attend.3.mine), channel_id=1, source_target_pairs={{0,1},{1,0},{2,3},{3,2},{4,5},{5,4},{6,7},{7,6},{8,9},{9,8},{10,11... | collective-permute-start | bytes 786440 | tf_op jit(solution)/shard_map/ppermute | solution.py:20
  61.9 23.0 %collective-permute-start.13 = (bf16[256,1024]{1,0:T(8,128)(2,1)S(1)}, bf16[256,1024]{1,0:T(8,128)(2,1)S(1)}, u32[]{:S(2)}, u32[]{:S(2)}) collective-permute-start(bf16[256,1024]{1,0:T(8,128)(2,1)S(1)} %out_project.4.refs_2_), channel_id=1, source_target_pairs={{0,1},{1,0},{2,3},{3,2},{4,5},{5,4},{6,7},{7,6},{8,9},{9,8},{10,11... | collective-permute-start | bytes 1572872 | tf_op jit(solution)/shard_map/ppermute | solution.py:20
  67.4 17.4 %collective-permute-start.15 = (bf16[256,1024]{1,0:T(8,128)(2,1)}, bf16[256,1024]{1,0:T(8,128)(2,1)S(1)}, u32[]{:S(2)}, u32[]{:S(2)}) collective-permute-start(bf16[256,1024]{1,0:T(8,128)(2,1)} %collective-permute-done.14.refs_4_), channel_id=1, source_target_pairs={{0,1},{1,0},{2,3},{3,2},{4,5},{5,4},{6,7},{7,6},{8,9},{9,8},{10,11... | collective-permute-start | bytes 1572872 | tf_op jit(solution)/shard_map/ppermute | solution.py:20
  77.4 1.4 %collective-permute-start.16 = (bf16[16,512]{1,0:T(8,128)(2,1)S(1)}, bf16[16,512]{1,0:T(8,128)(2,1)S(1)}, u32[]{:S(2)}, u32[]{:S(2)}) collective-permute-start(bf16[16,512]{1,0:T(8,128)(2,1)S(1)} %pad.14.mine), channel_id=1, source_target_pairs={{0,1},{1,0},{2,3},{3,2},{4,5},{5,4},{6,7},{7,6},{8,9},{9,8},{10,11... | collective-permute-start | bytes 49160 | tf_op jit(solution)/shard_map/ppermute | solution.py:20
  79.7 3.9 %collective-permute-start.18 = (bf16[16,1024]{1,0:T(8,128)(2,1)S(1)}, bf16[16,1024]{1,0:T(8,128)(2,1)S(1)}, u32[]{:S(2)}, u32[]{:S(2)}) collective-permute-start(bf16[16,1024]{1,0:T(8,128)(2,1)S(1)} %out_project.5.refs_7_), channel_id=1, source_target_pairs={{0,2},{1,3},{2,0},{3,1},{4,6},{5,7},{6,4},{7,5},{8,10},{9,11},{10,... | collective-permute-start | bytes 98312 | tf_op jit(solution)/shard_map/ppermute | solution.py:26
  80.3 3.9 %collective-permute-start.17 = (bf16[16,1024]{1,0:T(8,128)(2,1)S(1)}, bf16[16,1024]{1,0:T(8,128)(2,1)S(1)}, u32[]{:S(2)}, u32[]{:S(2)}) collective-permute-start(bf16[16,1024]{1,0:T(8,128)(2,1)S(1)} %out_project.5.refs_7_), channel_id=1, source_target_pairs={{0,1},{1,0},{2,3},{3,2},{4,5},{5,4},{6,7},{7,6},{8,9},{9,8},{10,11... | collective-permute-start | bytes 98312 | tf_op jit(solution)/shard_map/ppermute | solution.py:20
  83.7 1.2 collective-permute-start.19
  83.7 17.1 %collective-permute-start.21 = (bf16[256,1024]{1,0:T(8,128)(2,1)S(1)}, bf16[256,1024]{1,0:T(8,128)(2,1)S(1)}, u32[]{:S(2)}, u32[]{:S(2)}) collective-permute-start(bf16[256,1024]{1,0:T(8,128)(2,1)S(1)} %out_project.4.refs_2_), channel_id=1, source_target_pairs={{0,2},{1,3},{2,0},{3,1},{4,6},{5,7},{6,4},{7,5},{8,10},{9,11},{10,... | collective-permute-start | bytes 1572872 | tf_op jit(solution)/shard_map/ppermute | solution.py:26
  99.4 1.3 collective-permute-start.20
  100.7 4.3 %collective-permute-start.23 = (bf16[16,2048]{1,0:T(8,128)(2,1)S(1)}, bf16[16,2048]{1,0:T(8,128)(2,1)S(1)}, u32[]{:S(2)}, u32[]{:S(2)}) collective-permute-start(bf16[16,2048]{1,0:T(8,128)(2,1)S(1)} %add_convert_fusion.3), channel_id=1, source_target_pairs={{0,2},{1,3},{2,0},{3,1},{4,6},{5,7},{6,4},{7,5},{8,10},{9,11},{10,... | collective-permute-start | bytes 196616 | tf_op jit(solution)/shard_map/ppermute | solution.py:26
  101.6 14.0 %collective-permute-start.26 = (bf16[128,2048]{1,0:T(8,128)(2,1)S(1)}, bf16[128,2048]{1,0:T(8,128)(2,1)S(1)}, u32[]{:S(2)}, u32[]{:S(2)}) collective-permute-start(bf16[128,2048]{1,0:T(8,128)(2,1)S(1)} %get-tuple-element.37), channel_id=1, source_target_pairs={{0,1},{1,0},{2,3},{3,2},{4,5},{5,4},{6,7},{7,6},{8,9},{9,8},{10,11... | collective-permute-start | bytes 1572872 | tf_op jit(solution)/shard_map/ppermute | solution.py:20
  105.3 6.8 %collective-permute-start.28 = (bf16[4,2048]{1,0:T(4,128)(2,1)S(1)}, bf16[4,2048]{1,0:T(4,128)(2,1)S(1)}, u32[]{:S(2)}, u32[]{:S(2)}) collective-permute-start(bf16[4,2048]{1,0:T(4,128)(2,1)S(1)} %get-tuple-element.42), channel_id=1, source_target_pairs={{0,8},{4,12},{8,0},{12,4},{16,24},{20,28},{24,16},{28,20},{1,9},{5... | collective-permute-start | bytes 49160 | tf_op jit(solution)/shard_map/ppermute | solution.py:33
  106.0 6.5 %collective-permute-start.29 = (bf16[4,2048]{1,0:T(4,128)(2,1)S(1)}, bf16[4,2048]{1,0:T(4,128)(2,1)S(1)}, u32[]{:S(2)}, u32[]{:S(2)}) collective-permute-start(bf16[4,2048]{1,0:T(4,128)(2,1)S(1)} %get-tuple-element.44), channel_id=1, source_target_pairs={{0,16},{4,20},{8,24},{12,28},{16,0},{20,4},{24,8},{28,12},{1,17},{... | collective-permute-start | bytes 49160 | tf_op jit(solution)/shard_map/ppermute | solution.py:33
  109.5 5.5 %collective-permute-start.30 = (bf16[4,2048]{1,0:T(4,128)(2,1)S(1)}, bf16[4,2048]{1,0:T(4,128)(2,1)S(1)}, u32[]{:S(2)}, u32[]{:S(2)}) collective-permute-start(bf16[4,2048]{1,0:T(4,128)(2,1)S(1)} %get-tuple-element.43), channel_id=1, source_target_pairs={{0,24},{4,28},{8,16},{12,20},{16,8},{20,12},{24,0},{28,4},{1,25},{... | collective-permute-start | bytes 49160 | tf_op jit(solution)/shard_map/ppermute | solution.py:33
  112.1 4.7 %collective-permute-start.11 = (bf16[256,1024]{1,0:T(8,128)(2,1)}, bf16[256,1024]{1,0:T(8,128)(2,1)S(1)}, u32[]{:S(2)}, u32[]{:S(2)}) collective-permute-start(bf16[256,1024]{1,0:T(8,128)(2,1)} %out_project.3.refs_2_), channel_id=1, source_target_pairs={{0,1},{1,0},{2,3},{3,2},{4,5},{5,4},{6,7},{7,6},{8,9},{9,8},{10,11... | collective-permute-start | bytes 1572872 | tf_op jit(solution)/shard_map/ppermute | solution.py:20
  112.1 4.7 %collective-permute-start.22 = (bf16[256,1024]{1,0:T(8,128)(2,1)S(1)}, bf16[256,1024]{1,0:T(8,128)(2,1)S(1)}, u32[]{:S(2)}, u32[]{:S(2)}) collective-permute-start(bf16[256,1024]{1,0:T(8,128)(2,1)S(1)} %collective-permute-done.21.refs_4_), channel_id=1, source_target_pairs={{0,1},{1,0},{2,3},{3,2},{4,5},{5,4},{6,7},{7,6},{8,9},{9,8},{10,11... | collective-permute-start | bytes 1572872 | tf_op jit(solution)/shard_map/ppermute | solution.py:20
  115.1 22.7 %collective-permute-start.31 = (bf16[2,2048]{1,0:T(2,128)(2,1)S(1)}, bf16[2,2048]{1,0:T(2,128)(2,1)S(1)}, u32[]{:S(2)}, u32[]{:S(2)}) collective-permute-start(bf16[2,2048]{1,0:T(2,128)(2,1)S(1)} %slice.56), channel_id=1, source_target_pairs={{0,4},{4,0},{8,12},{12,8},{16,20},{20,16},{24,28},{28,24},{1,5},{5... | collective-permute-start | bytes 24584 | tf_op jit(solution)/shard_map/ppermute | solution.py:33
  115.8 23.4 %collective-permute-start.27 = (bf16[128,2048]{1,0:T(8,128)(2,1)S(1)}, bf16[128,2048]{1,0:T(8,128)(2,1)S(1)}, u32[]{:S(2)}, u32[]{:S(2)}) collective-permute-start(bf16[128,2048]{1,0:T(8,128)(2,1)S(1)} %add_convert_fusion.1), channel_id=1, source_target_pairs={{0,2},{1,3},{2,0},{3,1},{4,6},{5,7},{6,4},{7,5},{8,10},{9,11},{10,... | collective-permute-start | bytes 1572872 | tf_op jit(solution)/shard_map/ppermute | solution.py:26
  137.2 1.6 %collective-permute-start.24 = (bf16[128,1024]{1,0:T(8,128)(2,1)S(1)}, bf16[128,1024]{1,0:T(8,128)(2,1)S(1)}, u32[]{:S(2)}, u32[]{:S(2)}) collective-permute-start(bf16[128,1024]{1,0:T(8,128)(2,1)S(1)} %get-tuple-element.40), channel_id=1, source_target_pairs={{0,1},{1,0},{2,3},{3,2},{4,5},{5,4},{6,7},{7,6},{8,9},{9,8},{10,11... | collective-permute-start | bytes 786440 | tf_op jit(solution)/shard_map/ppermute | solution.py:20
  137.3 1.9 %collective-permute-start.25 = (bf16[128,1024]{1,0:T(8,128)(2,1)S(1)}, bf16[128,1024]{1,0:T(8,128)(2,1)S(1)}, u32[]{:S(2)}, u32[]{:S(2)}) collective-permute-start(bf16[128,1024]{1,0:T(8,128)(2,1)S(1)} %get-tuple-element.41), channel_id=1, source_target_pairs={{0,1},{1,0},{2,3},{3,2},{4,5},{5,4},{6,7},{7,6},{8,9},{9,8},{10,11... | collective-permute-start | bytes 786440 | tf_op jit(solution)/shard_map/ppermute | solution.py:20
  (28 other events, 382.1 us)

commit v3 on v2

--- a/solution.py
+++ b/solution.py
@@ -28,6 +28,13 @@
     )
 
 
+def from_other(value, step):
+    count = lax.axis_size("tensor")
+    return lax.ppermute(
+        value, "tensor", [(i, (i // 2 - step) % (count // 2) * 2 + 1 - i % 2) for i in range(count)]
+    )
+
+
 def swap_groups(value, mask):
     count = lax.axis_size("dp")
     return lax.ppermute(value, "dp", [(i, i ^ mask) for i in range(count)])
@@ -64,7 +71,7 @@
 
 VMEM_WHOLE = pl.BlockSpec(memory_space=pltpu.VMEM)
 SMEM_WHOLE = pl.BlockSpec(memory_space=pltpu.SMEM)
-UNREAD = pl.BlockSpec(memory_space=pl.ANY)
+IN_PLACE = pl.BlockSpec(memory_space=pl.ANY)
 
 
 def project_kernel(n_dec, n_after, groups, heads, place, *refs):
@@ -131,7 +138,7 @@
     return pl.pallas_call(
         functools.partial(project_kernel, n_dec, len(after), groups, heads),
         out_shape=out_shape,
-        in_specs=[SMEM_WHOLE] + [VMEM_WHOLE] * len(args) + [UNREAD] * len(after),
+        in_specs=[SMEM_WHOLE] + [VMEM_WHOLE] * len(args) + [IN_PLACE] * len(after),
         out_specs=[VMEM_WHOLE] * len(out_shape),
         scratch_shapes=[pltpu.VMEM((rows, width), jnp.bfloat16)],
         compiler_params=params(8),
@@ -202,33 +209,42 @@
     )(place, query, cache, cache, *entries, *entries)
 
 
-def step_kernel(heads, groups, lengths, query, cache_key, cache_value, new_key, new_value, out):
+def step_kernel(heads, groups, lengths, query, cache, new_key, new_value, out, held, arrived):
     scaling = 1.0 / math.sqrt(HD)
-    stored = cache_key.shape[2]
-    length = lengths[pl.program_id(0)]
-    rows = query[0]
-    old_key, old_value = cache_key[0, 0], cache_value[0, 0]
+    slots, stored = cache.shape[1], cache.shape[2]
+    copies = [
+        [pltpu.make_async_copy(cache.at[w, s], held.at[w, s], arrived.at[w, s]) for w in range(2)]
+        for s in range(slots)
+    ]
+    for pair in copies:
+        for copy in pair:
+            copy.start()
     across = (((1,), (1,)), ((), ()))
-    old = lax.dot_general(rows, old_key, across, preferred_element_type=jnp.float32)
-    seen = lax.broadcasted_iota(jnp.int32, (1, stored), 1) < length
-    old = jnp.where(seen, old * scaling, NEGATIVE)
-    own = jnp.sum(
-        rows.astype(jnp.float32) * new_key[0].astype(jnp.float32), axis=-1, keepdims=True
-    )
-    own = own * scaling
-    top = jnp.maximum(jnp.max(old, axis=-1, keepdims=True), own)
-    old = jnp.exp(old - top)
-    own = jnp.exp(own - top)
-    total = jnp.sum(old, axis=-1, keepdims=True) + own
-    mix = jnp.dot(
-        (old / total).astype(jnp.bfloat16), old_value, preferred_element_type=jnp.float32
-    )
-    mix += (own / total).astype(jnp.bfloat16).astype(jnp.float32) * new_value[0].astype(jnp.float32)
-    at = lax.broadcasted_iota(jnp.int32, (rows.shape[0], HD), 0) // groups
-    picked = mix[:, :HD]
-    for j in range(1, heads):
-        picked = jnp.where(at == j, mix[:, j * HD : (j + 1) * HD], picked)
-    out[0] = picked.astype(jnp.bfloat16)
+    places = lax.broadcasted_iota(jnp.int32, (1, stored), 1)
+    for s in range(slots):
+        rows = query[s]
+        copies[s][0].wait()
+        old = lax.dot_general(rows, held[0, s], across, preferred_element_type=jnp.float32)
+        old = jnp.where(places < lengths[s], old * scaling, NEGATIVE)
+        own = jnp.sum(
+            rows.astype(jnp.float32) * new_key[s].astype(jnp.float32), axis=-1, keepdims=True
+        )
+        own = own * scaling
+        top = jnp.maximum(jnp.max(old, axis=-1, keepdims=True), own)
+        old = jnp.exp(old - top)
+        own = jnp.exp(own - top)
+        total = jnp.sum(old, axis=-1, keepdims=True) + own
+        copies[s][1].wait()
+        mix = jnp.dot(
+            (old / total).astype(jnp.bfloat16), held[1, s], preferred_element_type=jnp.float32
+        )
+        own = (own / total).astype(jnp.bfloat16).astype(jnp.float32)
+        mix += own * new_value[s].astype(jnp.float32)
+        at = lax.broadcasted_iota(jnp.int32, (rows.shape[0], HD), 0) // groups
+        picked = mix[:, :HD]
+        for j in range(1, heads):
+            picked = jnp.where(at == j, mix[:, j * HD : (j + 1) * HD], picked)
+        out[s] = picked.astype(jnp.bfloat16)
 
 
 def step_attend(lengths, query, cache, entries, slots, heads):
@@ -249,22 +265,16 @@
     out = pl.pallas_call(
         functools.partial(step_kernel, heads, groups),
         out_shape=jax.ShapeDtypeStruct((slots, pad, HD), jnp.bfloat16),
-        grid_spec=pltpu.PrefetchScalarGridSpec(
-            num_scalar_prefetch=1,
-            grid=(slots,),
-            in_specs=[
-                pl.BlockSpec((1, pad, width), lambda s, n: (s, 0, 0)),
-                pl.BlockSpec((1, 1, stored, width), lambda s, n: (0, s, 0, 0)),
-                pl.BlockSpec((1, 1, stored, width), lambda s, n: (1, s, 0, 0)),
-                pl.BlockSpec((1, 1, width), lambda s, n: (s, 0, 0)),
-                pl.BlockSpec((1, 1, width), lambda s, n: (s, 0, 0)),
-            ],
-            out_specs=pl.BlockSpec((1, pad, HD), lambda s, n: (s, 0, 0)),
-        ),
-        compiler_params=params(8),
+        in_specs=[SMEM_WHOLE, VMEM_WHOLE, IN_PLACE, VMEM_WHOLE, VMEM_WHOLE],
+        out_specs=VMEM_WHOLE,
+        scratch_shapes=[
+            pltpu.VMEM(cache.shape, jnp.bfloat16),
+            pltpu.SemaphoreType.DMA((2, slots)),
+        ],
+        compiler_params=params(16),
         cost_estimate=cost(64 * cache.size, 2 * cache.size, slots * stored * pad),
         name="step_attend",
-    )(lengths, spread, cache, cache, new_key, new_value)
+    )(lengths, spread, cache, new_key, new_value)
     return out[:, : heads * groups].reshape(slots, heads * groups * HD)
 
 
@@ -272,7 +282,7 @@
     half = out.shape[1]
     cols = pl.ds(pl.multiple_of(place[0] * half, half), half)
     part = jnp.dot(mine[...], weight[:, cols], preferred_element_type=jnp.float32)
-    part += jnp.dot(sib[...], sib_weight[...], preferred_element_type=jnp.float32)
+    part += jnp.dot(sib[...], sib_weight[:, cols], preferred_element_type=jnp.float32)
     out[...] = part.astype(jnp.bfloat16)
 
 
@@ -298,14 +308,29 @@
     if n_dec:
         dec, dec_shares = refs[0], refs[1 : 1 + 2 * chips]
         refs = refs[1 + 2 * chips :]
-    gain, gate, up, down = refs[:4]
+    gain, *weights = refs[:4]
     refs = refs[4 + n_after :]
     keep, give, resid = refs[:3]
     refs = refs[3:]
     if n_dec:
         dec_out, dec_resid = refs[:2]
         refs = refs[2:]
-    held, inner, hidden = refs
+    held, inner, hidden, gate, up, down, arrived = refs
+    chunks = gate.shape[0]
+    copies = [
+        [
+            pltpu.make_async_copy(
+                source.at[:, pl.ds(i * chunk, chunk)], target.at[i], arrived.at[w, i]
+            )
+            for i in range(chunks)
+        ]
+        for w, (source, target) in enumerate(zip(weights, (gate, up, down)))
+    ]
+    for i in range(chunks):
+        copies[0][i].start()
+        copies[1][i].start()
+    for i in range(chunks):
+        copies[2][i].start()
     piece = mine.shape[0]
     half = shares[0].shape[1]
     core = place[0]
@@ -329,17 +354,17 @@
     if n_dec:
         dec_resid[...] = held[2 * piece :, :]
 
-    @pl.loop(0, gate.shape[1] // chunk)
-    def _(i):
-        at = pl.ds(pl.multiple_of(i * chunk, chunk), chunk)
-        gated = jnp.dot(inner[...], gate[:, at], preferred_element_type=jnp.float32)
-        raised = jnp.dot(inner[...], up[:, at], preferred_element_type=jnp.float32)
+    for i in range(chunks):
+        at = slice(i * chunk, (i + 1) * chunk)
+        copies[0][i].wait()
+        gated = jnp.dot(inner[...], gate[i], preferred_element_type=jnp.float32)
+        copies[1][i].wait()
+        raised = jnp.dot(inner[...], up[i], preferred_element_type=jnp.float32)
         hidden[:, at] = (gated / (1.0 + jnp.exp(-gated)) * raised).astype(jnp.bfloat16)
-
-    @pl.loop(0, down.shape[1] // chunk)
-    def _(i):
-        at = pl.ds(pl.multiple_of(i * chunk, chunk), chunk)
-        part = jnp.dot(hidden[...], down[:, at], preferred_element_type=jnp.float32)
+    for i in range(chunks):
+        at = slice(i * chunk, (i + 1) * chunk)
+        copies[2][i].wait()
+        part = jnp.dot(hidden[...], down[i], preferred_element_type=jnp.float32)
         part = part.astype(jnp.bfloat16)
         keep[:, at] = part[:piece]
         give[:, at] = part[piece : 2 * piece]
@@ -353,25 +378,31 @@
     piece, width = mine.shape
     chips = len(shares) // 2
     units = gate.shape[1]
-    chunk = min(512, units)
+    chunks = 4
+    chunk = width // chunks
     n_dec = 0 if dec is None else dec.shape[0]
     rows = 2 * piece + n_dec
     args = [mine, sib, *shares]
     if n_dec:
         args += [dec, *dec_shares]
+    n_whole = len(args) + 1
     args += [gain, gate, up, down]
     sizes = [piece] * 3 + [n_dec] * 2 * bool(n_dec)
     return pl.pallas_call(
         functools.partial(forward_kernel, chips, n_dec, len(after), chunk),
         out_shape=[jax.ShapeDtypeStruct((n, width), jnp.bfloat16) for n in sizes],
-        in_specs=[SMEM_WHOLE] + [VMEM_WHOLE] * len(args) + [UNREAD] * len(after),
+        in_specs=[SMEM_WHOLE] + [VMEM_WHOLE] * n_whole + [IN_PLACE] * (3 + len(after)),
         out_specs=[VMEM_WHOLE] * len(sizes),
         scratch_shapes=[
             pltpu.VMEM((rows, width), jnp.bfloat16),
             pltpu.VMEM((rows, width), jnp.bfloat16),
             pltpu.VMEM((rows, units), jnp.bfloat16),
+            pltpu.VMEM((units // chunk, width, chunk), jnp.bfloat16),
+            pltpu.VMEM((units // chunk, width, chunk), jnp.bfloat16),
+            pltpu.VMEM((chunks, units, chunk), jnp.bfloat16),
+            pltpu.SemaphoreType.DMA((3, chunks)),
         ],
-        compiler_params=params(10),
+        compiler_params=params(40),
         cost_estimate=cost(6 * rows * width * units, 6 * width * units, rows * units),
         name="feed_forward",
     )(place, *args, *after)
@@ -422,7 +453,6 @@
     padded = -(-slots // 16) * 16
     heads = qkv_weight.shape[1]
     tokens = piece * tensor_count
-    half = width // 2
 
     def place_of(k):
         spots = [core, (chip + k) % chips, prefill_offset[0]]
@@ -430,7 +460,7 @@
 
     places = [place_of(k) for k in range(chips)]
     weight = in_vmem(qkv_weight.reshape(width, -1))
-    gate_weight, up_weight, down_weight = map(in_vmem, (gate_weight, up_weight, down_weight))
+    gate_weight, up_weight, down_weight = map(in_hbm, (gate_weight, up_weight, down_weight))
     prefill_cache, decode_cache = in_hbm(prefill_cache), in_hbm(decode_cache)
 
     mines = [prefill_rows] + [from_chip(prefill_rows, k) for k in range(1, chips)]
@@ -467,9 +497,9 @@
     for k in range(chips):
         last = k == chips - 1
         if last:
-            dealt = add(dealt, swap_cores(dealt))
-            dealt, queries[0] = lax.optimization_barrier((dealt, queries[0]))
-            dealt = add(dealt, *[from_chip(dealt, j) for j in range(1, chips)])
+            others = [from_chip(dealt, j) for j in range(1, chips)]
+            others += [from_other(dealt, j) for j in range(chips)]
+            dealt = add(dealt, *others)
         got = project(
             places[k],
             mines[k],
@@ -486,8 +516,7 @@
         if last:
             dec_query, dec_entries = got[2:]
 
-    col = pl.multiple_of((1 - core) * half, half)
-    sib_weight = in_vmem(swap_cores(lax.dynamic_slice_in_dim(out_weight, col, half, 1)))
+    sib_weight = in_vmem(swap_cores(out_weight))
     out_weight = in_vmem(out_weight)
 
     def finish(attended, place):

time: 141 us -> 128 us (0.908)
  local copies, waits for them, and re-layouts: 31.5 us -> 15.8 us
  Pallas kernels: 51.2 us -> 55.2 us
  waiting for transfers between devices: 26.5 us -> 24 us
    unnamed x59 -> x43, local copies, waits for them, and re-layouts: 28.1 us -> 13.5 us
    pallas_call x2, Pallas kernels: 21.4 us -> 24.9 us  [feed_forward(): pl.pallas_call(functools.partial(forward_kernel, chips, n_dec, len(after)...]
    ppermute x0 -> x2, waiting for transfers between devices: none -> 3.05 us  [from_other(): lax.ppermute(value, 'tensor', [(i, (i // 2 - step) % (count // 2) * 2 + 1...]
    pallas_call x3, Pallas kernels: 4.81 us -> 7.6 us  [out_project(): pl.pallas_call(out_kernel, out_shape=jax.ShapeDtypeStruct((rows, half), j...]
    ppermute x8, waiting for transfers between devices: 2.5 us -> 0.02 us  [swap_groups(): return lax.ppermute(value, 'dp', [(i, i ^ mask) for i in range(count)])]
    dynamic_slice x1 -> x0, local copies, waits for them, and re-layouts: 2.3 us -> none  [on_device(): lax.dynamic_slice_in_dim(out_weight, col, half, 1)]
    pallas_call x1, Pallas kernels: 9.82 us -> 7.71 us  [step_attend(): pl.pallas_call(functools.partial(step_kernel, heads, groups), out_shape=j...]
    ppermute x17 -> x16, waiting for transfers between devices: 8.24 us -> 6.62 us  [swap_cores(): return lax.ppermute(value, 'tensor', [(i, i ^ 1) for i in range(count)])]
  transfers between devices with their start and end apart: 32 -> 33, of which waited for: 13 -> 13; matrix products, arithmetic and copies ran while one was open for 11% -> 13% of each run, Pallas kernels for 35% -> 41%
where the time goes in v3:
time: 128 us
  Pallas kernels  55.2 us (43%)
  waiting for transfers between devices  24 us (19%)
  starting transfers between devices  21 us (16%)
  local copies, waits for them, and re-layouts  15.8 us (12%)
  other arithmetic  8.73 us (7%)
  between operations  1.77 us (1%)
    pallas_call x2, Pallas kernels, feed_forward(): pl.pallas_call(functools.partial(forward_kernel, chips, n_dec, len(after)...  24.9 us
    ppermute x7, waiting for transfers between devices, from_chip(): lax.ppermute(value, 'tensor', [(i, (i // 2 - step) % chips * 2 + i % 2) f...  14.3 us
    unnamed x43, local copies, waits for them, and re-layouts  13.5 us
    ppermute x8, starting transfers between devices, swap_groups(): return lax.ppermute(value, 'dp', [(i, i ^ mask) for i in range(count)])  11 us
    pallas_call x2, Pallas kernels, fill_attend(): pl.pallas_call(functools.partial(fill_kernel, groups, chips), out_shape=j...  9.94 us
    pallas_call x1, Pallas kernels, step_attend(): pl.pallas_call(functools.partial(step_kernel, heads, groups), out_shape=j...  7.71 us
    pallas_call x3, Pallas kernels, out_project(): pl.pallas_call(out_kernel, out_shape=jax.ShapeDtypeStruct((rows, half), j...  7.6 us
    ppermute x7, starting transfers between devices, from_chip(): lax.ppermute(value, 'tensor', [(i, (i // 2 - step) % chips * 2 + i % 2) f...  7 us
  transfers between devices with their start and end apart: 33, of which 13 were waited for; matrix products, arithmetic and copies ran while one was open for 13% of the time, Pallas kernels for 41%

profile of v3, /device:TPU:0, one launch (start us, length us, event | category | flops | bytes accessed | tf_op | source)
XLA Modules:
  0.0 127.6 jit_solution(283071817989520916)
XLA Ops:
  0.7 3.0 %collective-permute-start.5 = (bf16[128,2048]{1,0:T(8,128)(2,1)}, bf16[128,2048]{1,0:T(8,128)(2,1)S(1)}, u32[]{:S(2)}, u32[]{:S(2)}) collective-permute-start(bf16[128,2048]{1,0:T(8,128)(2,1)} %refs_0_.3), channel_id=1, source_target_pairs={{0,2},{1,3},{2,0},{3,1},{4,6},{5,7},{6,4},{7,5},{8,10},{9,11},{10,... | collective-permute-start | bytes 1572872 | tf_op jit(solution)/shard_map/ppermute | solution.py:26
  3.7 1.5 %collective-permute-start.1 = (bf16[2,2048]{1,0:T(2,128)(2,1)}, bf16[2,2048]{1,0:T(2,128)(2,1)S(1)}, u32[]{:S(2)}, u32[]{:S(2)}) collective-permute-start(bf16[2,2048]{1,0:T(2,128)(2,1)} %param.15), channel_id=1, source_target_pairs={{0,4},{4,0},{8,12},{12,8},{16,20},{20,16},{24,28},{28,24},{1,5},{5... | collective-permute-start | bytes 24584 | tf_op jit(solution)/shard_map/ppermute | solution.py:40
  5.9 1.0 fusion.2
  9.5 1.6 %collective-permute-start.2 = (bf16[4,2048]{1,0:T(4,128)(2,1)S(1)}, bf16[4,2048]{1,0:T(4,128)(2,1)S(1)}, u32[]{:S(2)}, u32[]{:S(2)}) collective-permute-start(bf16[4,2048]{1,0:T(4,128)(2,1)S(1)} %pad_maximum_fusion.2), channel_id=1, source_target_pairs={{0,8},{4,12},{8,0},{12,4},{16,24},{20,28},{24,16},{28,20},{1,9},{5... | collective-permute-start | bytes 49160 | tf_op jit(solution)/shard_map/ppermute | solution.py:40
  11.1 2.6 %collective-permute-start.3 = (bf16[4,2048]{1,0:T(4,128)(2,1)S(1)}, bf16[4,2048]{1,0:T(4,128)(2,1)S(1)}, u32[]{:S(2)}, u32[]{:S(2)}) collective-permute-start(bf16[4,2048]{1,0:T(4,128)(2,1)S(1)} %pad_maximum_fusion.2), channel_id=1, source_target_pairs={{0,16},{4,20},{8,24},{12,28},{16,0},{20,4},{24,8},{28,12},{1,17},{... | collective-permute-start | bytes 49160 | tf_op jit(solution)/shard_map/ppermute | solution.py:40
  14.2 5.4 %copy.25 = bf16[256,8,2,512]{3,1,2,0:T(8,128)(2,1)} copy(bf16[256,8,2,512]{3,2,1,0:T(2,128)(2,1)} %bitcast.29) | data formatting | bytes 8388608
  20.6 3.0 %collective-permute-done.9 = bf16[16,2048]{1,0:T(8,128)(2,1)S(1)} collective-permute-done((bf16[16,2048]{1,0:T(8,128)(2,1)S(1)}, bf16[16,2048]{1,0:T(8,128)(2,1)S(1)}, u32[]{:S(2)}, u32[]{:S(2)}) %collective-permute-start.9) | collective-permute-done | bytes 65568 | tf_op jit(solution)/shard_map/ppermute | solution.py:33
  24.4 3.7 %collective-permute-done.7 = bf16[16,2048]{1,0:T(8,128)(2,1)S(1)} collective-permute-done((bf16[16,2048]{1,0:T(8,128)(2,1)S(1)}, bf16[16,2048]{1,0:T(8,128)(2,1)S(1)}, u32[]{:S(2)}, u32[]{:S(2)}) %collective-permute-start.7) | collective-permute-done | bytes 65568 | tf_op jit(solution)/shard_map/ppermute | solution.py:26
  29.0 2.2 %copy-done = bf16[256,8,2,512]{3,1,2,0:T(8,128)(2,1)S(1)} copy-done((bf16[256,8,2,512]{3,1,2,0:T(8,128)(2,1)S(1)}, bf16[256,8,2,512]{3,1,2,0:T(8,128)(2,1)}, u32[]{:S(2)}) %copy-start) | copy-done | bytes 4194328
  31.1 1.0 copy-done.6
  32.2 1.0 copy-done.9
  33.2 2.4 %project.2 = (bf16[256,512]{1,0:T(8,128)(2,1)S(1)}, bf16[2,256,256]{2,1,0:T(8,128)(2,1)S(1)}) custom-call(s32[5]{0:T(128)S(1)} %stack.23.place, bf16[128,2048]{1,0:T(8,128)(2,1)S(1)} %copy-done.6, bf16[128,2048]{1,0:T(8,128)(2,1)S(1)} %copy-done.9, f32[1,2048]{1,0:T(1,128)S(1)} %bitcast.25, bf16[2048,1024]{1,0:T(8,128)(2,1)S(1)} %bitcast.23, ...), custom_call_target="tpu_custom_call" | custom-call | flops 1073741824 | bytes 6291456 | tf_op jit(solution)/shard_map/project/pallas_call | solution.py:138
  35.7 2.2 %copy-done.1 = bf16[256,8,2,512]{3,1,2,0:T(8,128)(2,1)S(1)} copy-done((bf16[256,8,2,512]{3,1,2,0:T(8,128)(2,1)S(1)}, bf16[256,8,2,512]{3,1,2,0:T(8,128)(2,1)}, u32[]{:S(2)}) %copy-start.1) | copy-done | bytes 4194328
  37.9 2.5 %project.3 = (bf16[256,512]{1,0:T(8,128)(2,1)S(1)}, bf16[2,256,256]{2,1,0:T(8,128)(2,1)S(1)}, bf16[16,512]{1,0:T(8,128)(2,1)S(1)}, bf16[2,16,256]{2,1,0:T(8,128)(2,1)S(1)}) custom-call(s32[5]{0:T(128)S(1)} %stack.24.place, bf16[128,2048]{1,0:T(8,128)(2,1)S(1)} %collective-permute-done.5.refs_0_, bf16[128,2048]{1,0:T(8,128)(2,1)S(1)} %collective-permute-done.6.refs_1_, ...), custom_call_target="tpu_custom_call" | custom-call | flops 1140850688 | bytes 6422528 | tf_op jit(solution)/shard_map/project/pallas_call | solution.py:138
  40.4 4.6 %fill_attend.2.mine = bf16[256,512]{1,0:T(8,128)(2,1)S(1)} custom-call(s32[5]{0:T(128)S(1)} %stack.23.place, bf16[256,512]{1,0:T(8,128)(2,1)S(1)} %get-tuple-element.19.query, bf16[2,1,1024,256]{3,2,1,0:T(8,128)(2,1)} %cache_value.3, bf16[2,1,1024,256]{3,2,1,0:T(8,128)(2,1)} %cache_value.3, bf16[2,256,256]{2,1,0:T(8,128)(2,1)S(1)} %get-tuple-element.20.refs_0_.refs_2_, ...), custom_call_target="tpu_custom_call" | custom-call | flops 1610612736 | bytes 1048576 | tf_op jit(solution)/shard_map/fill_attend/pallas_call | solution.py:191
  46.7 3.1 %out_project.3.refs_2_ = bf16[256,1024]{1,0:T(8,128)(2,1)} custom-call(s32[5]{0:T(128)S(1)} %stack.23.place, bf16[256,512]{1,0:T(8,128)(2,1)S(1)} %fill_attend.2.mine, bf16[256,512]{1,0:T(8,128)(2,1)S(1)} %collective-permute-done.10.sib, bf16[512,2048]{1,0:T(8,128)(2,1)S(1)} %copy-done.2, bf16[512,2048]{1,0:T(8,128)(2,1)} %collective-permute-done.11.sib_weight), custom_call_target="tpu_custom_call" | custom-call | flops 536870912 | bytes 3670016 | tf_op jit(solution)/shard_map/out_project/pallas_call | solution.py:292
  50.4 5.3 %fill_attend.3.mine = bf16[256,512]{1,0:T(8,128)(2,1)} custom-call(s32[5]{0:T(128)S(1)} %stack.24.place, bf16[256,512]{1,0:T(8,128)(2,1)S(1)} %get-tuple-element.22.query, bf16[2,1,1024,256]{3,2,1,0:T(8,128)(2,1)} %cache_value.3, bf16[2,1,1024,256]{3,2,1,0:T(8,128)(2,1)} %cache_value.3, bf16[2,256,256]{2,1,0:T(8,128)(2,1)S(1)} %get-tuple-element.20.refs_0_.refs_2_, ...), custom_call_target="tpu_custom_call" | custom-call | flops 1610612736 | bytes 1048576 | tf_op jit(solution)/shard_map/fill_attend/pallas_call | solution.py:191
  55.8 1.7 %collective-permute-done.13.sib = bf16[256,512]{1,0:T(8,128)(2,1)} collective-permute-done((bf16[256,512]{1,0:T(8,128)(2,1)}, bf16[256,512]{1,0:T(8,128)(2,1)}, u32[]{:S(2)}, u32[]{:S(2)}) %collective-permute-start.13) | collective-permute-done | bytes 262176 | tf_op jit(solution)/shard_map/ppermute | solution.py:20
  57.6 2.5 %out_project.4.refs_2_ = bf16[256,1024]{1,0:T(8,128)(2,1)S(1)} custom-call(s32[5]{0:T(128)S(1)} %stack.24.place, bf16[256,512]{1,0:T(8,128)(2,1)} %fill_attend.3.mine, bf16[256,512]{1,0:T(8,128)(2,1)} %collective-permute-done.13.sib, bf16[512,2048]{1,0:T(8,128)(2,1)S(1)} %copy-done.2, bf16[512,2048]{1,0:T(8,128)(2,1)} %collective-permute-done.11.sib_weight), custom_call_target="tpu_custom_call" | custom-call | flops 536870912 | bytes 3670016 | tf_op jit(solution)/shard_map/out_project/pallas_call | solution.py:292
  60.3 3.9 %collective-permute-done.15.refs_4_ = bf16[256,1024]{1,0:T(8,128)(2,1)} collective-permute-done((bf16[256,1024]{1,0:T(8,128)(2,1)}, bf16[256,1024]{1,0:T(8,128)(2,1)}, u32[]{:S(2)}, u32[]{:S(2)}) %collective-permute-start.15) | collective-permute-done | bytes 524320 | tf_op jit(solution)/shard_map/ppermute | solution.py:26
  64.9 7.7 %step_attend.1 = bf16[8,16,128]{2,1,0:T(8,128)(2,1)S(1)} custom-call(s32[8]{0:T(128)S(1)} %copy-done.15, bf16[8,16,256]{2,1,0:T(8,128)(2,1)S(1)} %pad.13.query, bf16[2,8,1024,256]{3,2,1,0:T(8,128)(2,1)} %cache.1, bf16[8,1,256]{2,1,0:T(2,128)(2,1)S(1)} %copy.23.new_key, bf16[8,1,256]{2,1,0:T(2,128)(2,1)S(1)} %copy.24.new_value), custom_call_target="tpu_custom_call" | custom-call | flops 268435456 | bytes 8388608 | tf_op jit(solution)/shard_map/step_attend/pallas_call | solution.py:265
  74.0 2.0 %out_project.5.refs_7_ = bf16[16,1024]{1,0:T(8,128)(2,1)S(1)} custom-call(s32[5]{0:T(128)S(1)} %stack.23.place, bf16[16,512]{1,0:T(8,128)(2,1)S(1)} %pad.14.mine, bf16[16,512]{1,0:T(8,128)(2,1)S(1)} %collective-permute-done.17.sib, bf16[512,2048]{1,0:T(8,128)(2,1)S(1)} %copy-done.2, bf16[512,2048]{1,0:T(8,128)(2,1)} %collective-permute-done.11.sib_weight), custom_call_target="tpu_custom_call" | custom-call | flops 33554432 | bytes 2195456 | tf_op jit(solution)/shard_map/out_project/pallas_call | solution.py:292
  76.6 3.3 %collective-permute-done.19.refs_9_ = bf16[16,1024]{1,0:T(8,128)(2,1)S(1)} collective-permute-done((bf16[16,1024]{1,0:T(8,128)(2,1)S(1)}, bf16[16,1024]{1,0:T(8,128)(2,1)S(1)}, u32[]{:S(2)}, u32[]{:S(2)}) %collective-permute-start.19) | collective-permute-done | bytes 32800 | tf_op jit(solution)/shard_map/ppermute | solution.py:26
  81.2 12.7 %feed_forward.2 = (bf16[128,2048]{1,0:T(8,128)(2,1)S(1)}, bf16[128,2048]{1,0:T(8,128)(2,1)S(1)}, bf16[128,2048]{1,0:T(8,128)(2,1)}, bf16[16,2048]{1,0:T(8,128)(2,1)S(1)}, bf16[16,2048]{1,0:T(8,128)(2,1)S(1)}) custom-call(s32[5]{0:T(128)S(1)} %stack.24.place, bf16[128,2048]{1,0:T(8,128)(2,1)S(1)} %collective-permute-done.5.refs_0_, ...), custom_call_target="tpu_custom_call" | custom-call | flops 6845104128 | bytes 25165824 | tf_op jit(solution)/shard_map/feed_forward/pallas_call | solution.py:391
  94.9 1.1 collective-permute-done.21
  96.9 3.4 %collective-permute-done.24 = bf16[16,2048]{1,0:T(8,128)(2,1)S(1)} collective-permute-done((bf16[16,2048]{1,0:T(8,128)(2,1)S(1)}, bf16[16,2048]{1,0:T(8,128)(2,1)S(1)}, u32[]{:S(2)}, u32[]{:S(2)}) %collective-permute-start.24) | collective-permute-done | bytes 65568 | tf_op jit(solution)/shard_map/ppermute | solution.py:26
  101.3 3.7 %collective-permute-start.31 = (bf16[4,2048]{1,0:T(4,128)(2,1)S(1)}, bf16[4,2048]{1,0:T(4,128)(2,1)S(1)}, u32[]{:S(2)}, u32[]{:S(2)}) collective-permute-start(bf16[4,2048]{1,0:T(4,128)(2,1)S(1)} %get-tuple-element.39), channel_id=1, source_target_pairs={{0,24},{4,28},{8,16},{12,20},{16,8},{20,12},{24,0},{28,4},{1,25},{... | collective-permute-start | bytes 49160 | tf_op jit(solution)/shard_map/ppermute | solution.py:40
  105.7 2.4 %fusion.1 = bf16[2,512,256]{2,1,0:T(8,128)(2,1)} fusion(s32[]{:T(128)S(6)} %select_n.82, bf16[2,256,256]{2,1,0:T(8,128)(2,1)S(1)} %get-tuple-element.20.refs_0_.refs_2_, bf16[2,256,256]{2,1,0:T(8,128)(2,1)} %copy-done.11), kind=kLoop, calls=%fused_computation.8 | loop fusion | flops 1572864 | bytes 1048580 | tf_op jit(solution)/shard_map/concatenate | solution.py:587
  108.1 1.3 %slice.49 = bf16[2,8,256]{2,1,0:T(8,128)(2,1)} slice(bf16[2,16,256]{2,1,0:T(8,128)(2,1)} %copy-done.14), slice={[0:2], [0:8], [0:256]} | slice | bytes 16384 | tf_op jit(solution)/shard_map/slice | solution.py:591
  110.7 0.9 collective-permute-start.28
  112.2 12.2 %feed_forward.3 = (bf16[128,2048]{1,0:T(8,128)(2,1)S(1)}, bf16[128,2048]{1,0:T(8,128)(2,1)S(1)}, bf16[128,2048]{1,0:T(8,128)(2,1)S(1)}) custom-call(s32[5]{0:T(128)S(1)} %stack.23.place, bf16[128,2048]{1,0:T(8,128)(2,1)S(1)} %copy-done.7, bf16[128,2048]{1,0:T(8,128)(2,1)S(1)} %copy-done.10, bf16[256,1024]{1,0:T(8,128)(2,1)} %out_project.3.refs_2_, ...), custom_call_target="tpu_custom_call" | custom-call | flops 6442450944 | bytes 25165824 | tf_op jit(solution)/shard_map/feed_forward/pallas_call | solution.py:391
  126.5 1.1 add_convert_fusion
  (127 shorter events, 19.5 us)
Async XLA Ops:
  0.7 23.5 %collective-permute-start.5 = (bf16[128,2048]{1,0:T(8,128)(2,1)}, bf16[128,2048]{1,0:T(8,128)(2,1)S(1)}, u32[]{:S(2)}, u32[]{:S(2)}) collective-permute-start(bf16[128,2048]{1,0:T(8,128)(2,1)} %refs_0_.3), channel_id=1, source_target_pairs={{0,2},{1,3},{2,0},{3,1},{4,6},{5,7},{6,4},{7,5},{8,10},{9,11},{10,... | collective-permute-start | bytes 1572872 | tf_op jit(solution)/shard_map/ppermute | solution.py:26
  3.7 5.1 %collective-permute-start.1 = (bf16[2,2048]{1,0:T(2,128)(2,1)}, bf16[2,2048]{1,0:T(2,128)(2,1)S(1)}, u32[]{:S(2)}, u32[]{:S(2)}) collective-permute-start(bf16[2,2048]{1,0:T(2,128)(2,1)} %param.15), channel_id=1, source_target_pairs={{0,4},{4,0},{8,12},{12,8},{16,20},{20,16},{24,28},{28,24},{1,5},{5... | collective-permute-start | bytes 24584 | tf_op jit(solution)/shard_map/ppermute | solution.py:40
  5.2 41.5 %collective-permute-start.11 = (bf16[512,2048]{1,0:T(8,128)(2,1)}, bf16[512,2048]{1,0:T(8,128)(2,1)}, u32[]{:S(2)}, u32[]{:S(2)}) collective-permute-start(bf16[512,2048]{1,0:T(8,128)(2,1)} %weight.5), channel_id=1, source_target_pairs={{0,1},{1,0},{2,3},{3,2},{4,5},{5,4},{6,7},{7,6},{8,9},{9,8},{10,11... | collective-permute-start | bytes 6291464 | tf_op jit(solution)/shard_map/ppermute | solution.py:20
  9.5 10.1 %collective-permute-start.2 = (bf16[4,2048]{1,0:T(4,128)(2,1)S(1)}, bf16[4,2048]{1,0:T(4,128)(2,1)S(1)}, u32[]{:S(2)}, u32[]{:S(2)}) collective-permute-start(bf16[4,2048]{1,0:T(4,128)(2,1)S(1)} %pad_maximum_fusion.2), channel_id=1, source_target_pairs={{0,8},{4,12},{8,0},{12,4},{16,24},{20,28},{24,16},{28,20},{1,9},{5... | collective-permute-start | bytes 49160 | tf_op jit(solution)/shard_map/ppermute | solution.py:40
  11.1 8.5 %collective-permute-start.3 = (bf16[4,2048]{1,0:T(4,128)(2,1)S(1)}, bf16[4,2048]{1,0:T(4,128)(2,1)S(1)}, u32[]{:S(2)}, u32[]{:S(2)}) collective-permute-start(bf16[4,2048]{1,0:T(4,128)(2,1)S(1)} %pad_maximum_fusion.2), channel_id=1, source_target_pairs={{0,16},{4,20},{8,24},{12,28},{16,0},{20,4},{24,8},{28,12},{1,17},{... | collective-permute-start | bytes 49160 | tf_op jit(solution)/shard_map/ppermute | solution.py:40
  13.7 5.9 %collective-permute-start.4 = (bf16[4,2048]{1,0:T(4,128)(2,1)S(1)}, bf16[4,2048]{1,0:T(4,128)(2,1)S(1)}, u32[]{:S(2)}, u32[]{:S(2)}) collective-permute-start(bf16[4,2048]{1,0:T(4,128)(2,1)S(1)} %pad_maximum_fusion.2), channel_id=1, source_target_pairs={{0,24},{4,28},{8,16},{12,20},{16,8},{20,12},{24,0},{28,4},{1,25},{... | collective-permute-start | bytes 49160 | tf_op jit(solution)/shard_map/ppermute | solution.py:40
  19.6 8.6 %collective-permute-start = (bf16[128,2048]{1,0:T(8,128)(2,1)S(1)}, bf16[128,2048]{1,0:T(8,128)(2,1)S(1)}, u32[]{:S(2)}, u32[]{:S(2)}) collective-permute-start(bf16[128,2048]{1,0:T(8,128)(2,1)S(1)} %copy-done.5), channel_id=1, source_target_pairs={{0,1},{1,0},{2,3},{3,2},{4,5},{5,4},{6,7},{7,6},{8,9},{9,8},{10,11... | collective-permute-start | bytes 1572872 | tf_op jit(solution)/shard_map/ppermute | solution.py:20
  19.8 3.8 %collective-permute-start.9 = (bf16[16,2048]{1,0:T(8,128)(2,1)S(1)}, bf16[16,2048]{1,0:T(8,128)(2,1)S(1)}, u32[]{:S(2)}, u32[]{:S(2)}) collective-permute-start(bf16[16,2048]{1,0:T(8,128)(2,1)S(1)} %convolution_convert_fusion.1.refs_6_), channel_id=1, source_target_pairs={{0,3},{1,2},{2,1},{3,0},{4,7},{5,6},{6,5},{7,4},{8,11},{9,10},{10,... | collective-permute-start | bytes 196616 | tf_op jit(solution)/shard_map/ppermute | solution.py:33
  20.6 3.8 %collective-permute-start.8 = (bf16[16,2048]{1,0:T(8,128)(2,1)S(1)}, bf16[16,2048]{1,0:T(8,128)(2,1)S(1)}, u32[]{:S(2)}, u32[]{:S(2)}) collective-permute-start(bf16[16,2048]{1,0:T(8,128)(2,1)S(1)} %convolution_convert_fusion.1.refs_6_), channel_id=1, source_target_pairs={{0,1},{1,0},{2,3},{3,2},{4,5},{5,4},{6,7},{7,6},{8,9},{9,8},{10,11... | collective-permute-start | bytes 196616 | tf_op jit(solution)/shard_map/ppermute | solution.py:33
  23.7 4.4 %collective-permute-start.7 = (bf16[16,2048]{1,0:T(8,128)(2,1)S(1)}, bf16[16,2048]{1,0:T(8,128)(2,1)S(1)}, u32[]{:S(2)}, u32[]{:S(2)}) collective-permute-start(bf16[16,2048]{1,0:T(8,128)(2,1)S(1)} %convolution_convert_fusion.1.refs_6_), channel_id=1, source_target_pairs={{0,2},{1,3},{2,0},{3,1},{4,6},{5,7},{6,4},{7,5},{8,10},{9,11},{10,... | collective-permute-start | bytes 196616 | tf_op jit(solution)/shard_map/ppermute | solution.py:26
  24.2 11.5 %collective-permute-start.6 = (bf16[128,2048]{1,0:T(8,128)(2,1)S(1)}, bf16[128,2048]{1,0:T(8,128)(2,1)S(1)}, u32[]{:S(2)}, u32[]{:S(2)}) collective-permute-start(bf16[128,2048]{1,0:T(8,128)(2,1)S(1)} %collective-permute-done.5.refs_0_), channel_id=1, source_target_pairs={{0,1},{1,0},{2,3},{3,2},{4,5},{5,4},{6,7},{7,6},{8,9},{9,8},{10,11... | collective-permute-start | bytes 1572872 | tf_op jit(solution)/shard_map/ppermute | solution.py:20
  45.1 1.6 %collective-permute-start.10 = (bf16[256,512]{1,0:T(8,128)(2,1)S(1)}, bf16[256,512]{1,0:T(8,128)(2,1)S(1)}, u32[]{:S(2)}, u32[]{:S(2)}) collective-permute-start(bf16[256,512]{1,0:T(8,128)(2,1)S(1)} %fill_attend.2.mine), channel_id=1, source_target_pairs={{0,1},{1,0},{2,3},{3,2},{4,5},{5,4},{6,7},{7,6},{8,9},{9,8},{10,11... | collective-permute-start | bytes 786440 | tf_op jit(solution)/shard_map/ppermute | solution.py:20
  49.9 14.3 %collective-permute-start.15 = (bf16[256,1024]{1,0:T(8,128)(2,1)}, bf16[256,1024]{1,0:T(8,128)(2,1)}, u32[]{:S(2)}, u32[]{:S(2)}) collective-permute-start(bf16[256,1024]{1,0:T(8,128)(2,1)} %out_project.3.refs_2_), channel_id=1, source_target_pairs={{0,2},{1,3},{2,0},{3,1},{4,6},{5,7},{6,4},{7,5},{8,10},{9,11},{10,... | collective-permute-start | bytes 1572872 | tf_op jit(solution)/shard_map/ppermute | solution.py:26
  55.7 1.9 %collective-permute-start.13 = (bf16[256,512]{1,0:T(8,128)(2,1)}, bf16[256,512]{1,0:T(8,128)(2,1)}, u32[]{:S(2)}, u32[]{:S(2)}) collective-permute-start(bf16[256,512]{1,0:T(8,128)(2,1)} %fill_attend.3.mine), channel_id=1, source_target_pairs={{0,1},{1,0},{2,3},{3,2},{4,5},{5,4},{6,7},{7,6},{8,9},{9,8},{10,11... | collective-permute-start | bytes 786440 | tf_op jit(solution)/shard_map/ppermute | solution.py:20
  60.1 21.1 %collective-permute-start.14 = (bf16[256,1024]{1,0:T(8,128)(2,1)S(1)}, bf16[256,1024]{1,0:T(8,128)(2,1)S(1)}, u32[]{:S(2)}, u32[]{:S(2)}) collective-permute-start(bf16[256,1024]{1,0:T(8,128)(2,1)S(1)} %out_project.4.refs_2_), channel_id=1, source_target_pairs={{0,1},{1,0},{2,3},{3,2},{4,5},{5,4},{6,7},{7,6},{8,9},{9,8},{10,11... | collective-permute-start | bytes 1572872 | tf_op jit(solution)/shard_map/ppermute | solution.py:20
  64.1 17.0 %collective-permute-start.16 = (bf16[256,1024]{1,0:T(8,128)(2,1)}, bf16[256,1024]{1,0:T(8,128)(2,1)S(1)}, u32[]{:S(2)}, u32[]{:S(2)}) collective-permute-start(bf16[256,1024]{1,0:T(8,128)(2,1)} %collective-permute-done.15.refs_4_), channel_id=1, source_target_pairs={{0,1},{1,0},{2,3},{3,2},{4,5},{5,4},{6,7},{7,6},{8,9},{9,8},{10,11... | collective-permute-start | bytes 1572872 | tf_op jit(solution)/shard_map/ppermute | solution.py:20
  72.6 1.4 %collective-permute-start.17 = (bf16[16,512]{1,0:T(8,128)(2,1)S(1)}, bf16[16,512]{1,0:T(8,128)(2,1)S(1)}, u32[]{:S(2)}, u32[]{:S(2)}) collective-permute-start(bf16[16,512]{1,0:T(8,128)(2,1)S(1)} %pad.14.mine), channel_id=1, source_target_pairs={{0,1},{1,0},{2,3},{3,2},{4,5},{5,4},{6,7},{7,6},{8,9},{9,8},{10,11... | collective-permute-start | bytes 49160 | tf_op jit(solution)/shard_map/ppermute | solution.py:20
  76.0 3.9 %collective-permute-start.19 = (bf16[16,1024]{1,0:T(8,128)(2,1)S(1)}, bf16[16,1024]{1,0:T(8,128)(2,1)S(1)}, u32[]{:S(2)}, u32[]{:S(2)}) collective-permute-start(bf16[16,1024]{1,0:T(8,128)(2,1)S(1)} %out_project.5.refs_7_), channel_id=1, source_target_pairs={{0,2},{1,3},{2,0},{3,1},{4,6},{5,7},{6,4},{7,5},{8,10},{9,11},{10,... | collective-permute-start | bytes 98312 | tf_op jit(solution)/shard_map/ppermute | solution.py:26
  76.6 3.9 %collective-permute-start.18 = (bf16[16,1024]{1,0:T(8,128)(2,1)S(1)}, bf16[16,1024]{1,0:T(8,128)(2,1)S(1)}, u32[]{:S(2)}, u32[]{:S(2)}) collective-permute-start(bf16[16,1024]{1,0:T(8,128)(2,1)S(1)} %out_project.5.refs_7_), channel_id=1, source_target_pairs={{0,1},{1,0},{2,3},{3,2},{4,5},{5,4},{6,7},{7,6},{8,9},{9,8},{10,11... | collective-permute-start | bytes 98312 | tf_op jit(solution)/shard_map/ppermute | solution.py:20
  79.9 16.1 %collective-permute-start.22 = (bf16[256,1024]{1,0:T(8,128)(2,1)S(1)}, bf16[256,1024]{1,0:T(8,128)(2,1)S(1)}, u32[]{:S(2)}, u32[]{:S(2)}) collective-permute-start(bf16[256,1024]{1,0:T(8,128)(2,1)S(1)} %out_project.4.refs_2_), channel_id=1, source_target_pairs={{0,2},{1,3},{2,0},{3,1},{4,6},{5,7},{6,4},{7,5},{8,10},{9,11},{10,... | collective-permute-start | bytes 1572872 | tf_op jit(solution)/shard_map/ppermute | solution.py:26
  94.7 1.3 collective-permute-start.21
  96.0 4.3 %collective-permute-start.24 = (bf16[16,2048]{1,0:T(8,128)(2,1)S(1)}, bf16[16,2048]{1,0:T(8,128)(2,1)S(1)}, u32[]{:S(2)}, u32[]{:S(2)}) collective-permute-start(bf16[16,2048]{1,0:T(8,128)(2,1)S(1)} %add_convert_fusion.3), channel_id=1, source_target_pairs={{0,2},{1,3},{2,0},{3,1},{4,6},{5,7},{6,4},{7,5},{8,10},{9,11},{10,... | collective-permute-start | bytes 196616 | tf_op jit(solution)/shard_map/ppermute | solution.py:26
  96.9 13.6 %collective-permute-start.27 = (bf16[128,2048]{1,0:T(8,128)(2,1)}, bf16[128,2048]{1,0:T(8,128)(2,1)S(1)}, u32[]{:S(2)}, u32[]{:S(2)}) collective-permute-start(bf16[128,2048]{1,0:T(8,128)(2,1)} %copy-done.16), channel_id=1, source_target_pairs={{0,1},{1,0},{2,3},{3,2},{4,5},{5,4},{6,7},{7,6},{8,9},{9,8},{10,11... | collective-permute-start | bytes 1572872 | tf_op jit(solution)/shard_map/ppermute | solution.py:20
  101.3 8.1 %collective-permute-start.31 = (bf16[4,2048]{1,0:T(4,128)(2,1)S(1)}, bf16[4,2048]{1,0:T(4,128)(2,1)S(1)}, u32[]{:S(2)}, u32[]{:S(2)}) collective-permute-start(bf16[4,2048]{1,0:T(4,128)(2,1)S(1)} %get-tuple-element.39), channel_id=1, source_target_pairs={{0,24},{4,28},{8,16},{12,20},{16,8},{20,12},{24,0},{28,4},{1,25},{... | collective-permute-start | bytes 49160 | tf_op jit(solution)/shard_map/ppermute | solution.py:40
  105.0 4.9 %collective-permute-start.30 = (bf16[4,2048]{1,0:T(4,128)(2,1)S(1)}, bf16[4,2048]{1,0:T(4,128)(2,1)S(1)}, u32[]{:S(2)}, u32[]{:S(2)}) collective-permute-start(bf16[4,2048]{1,0:T(4,128)(2,1)S(1)} %get-tuple-element.40), channel_id=1, source_target_pairs={{0,16},{4,20},{8,24},{12,28},{16,0},{20,4},{24,8},{28,12},{1,17},{... | collective-permute-start | bytes 49160 | tf_op jit(solution)/shard_map/ppermute | solution.py:40
  105.0 4.9 %collective-permute-start.29 = (bf16[4,2048]{1,0:T(4,128)(2,1)S(1)}, bf16[4,2048]{1,0:T(4,128)(2,1)S(1)}, u32[]{:S(2)}, u32[]{:S(2)}) collective-permute-start(bf16[4,2048]{1,0:T(4,128)(2,1)S(1)} %get-tuple-element.38), channel_id=1, source_target_pairs={{0,8},{4,12},{8,0},{12,4},{16,24},{20,28},{24,16},{28,20},{1,9},{5... | collective-permute-start | bytes 49160 | tf_op jit(solution)/shard_map/ppermute | solution.py:40
  109.4 2.8 %collective-permute-start.12 = (bf16[256,1024]{1,0:T(8,128)(2,1)}, bf16[256,1024]{1,0:T(8,128)(2,1)S(1)}, u32[]{:S(2)}, u32[]{:S(2)}) collective-permute-start(bf16[256,1024]{1,0:T(8,128)(2,1)} %out_project.3.refs_2_), channel_id=1, source_target_pairs={{0,1},{1,0},{2,3},{3,2},{4,5},{5,4},{6,7},{7,6},{8,9},{9,8},{10,11... | collective-permute-start | bytes 1572872 | tf_op jit(solution)/shard_map/ppermute | solution.py:20
  109.4 2.8 %collective-permute-start.23 = (bf16[256,1024]{1,0:T(8,128)(2,1)S(1)}, bf16[256,1024]{1,0:T(8,128)(2,1)S(1)}, u32[]{:S(2)}, u32[]{:S(2)}) collective-permute-start(bf16[256,1024]{1,0:T(8,128)(2,1)S(1)} %collective-permute-done.22.refs_4_), channel_id=1, source_target_pairs={{0,1},{1,0},{2,3},{3,2},{4,5},{5,4},{6,7},{7,6},{8,9},{9,8},{10,11... | collective-permute-start | bytes 1572872 | tf_op jit(solution)/shard_map/ppermute | solution.py:20
  110.0 15.1 %collective-permute-start.32 = (bf16[2,2048]{1,0:T(2,128)(2,1)S(1)}, bf16[2,2048]{1,0:T(2,128)(2,1)S(1)}, u32[]{:S(2)}, u32[]{:S(2)}) collective-permute-start(bf16[2,2048]{1,0:T(2,128)(2,1)S(1)} %slice.56), channel_id=1, source_target_pairs={{0,4},{4,0},{8,12},{12,8},{16,20},{20,16},{24,28},{28,24},{1,5},{5... | collective-permute-start | bytes 24584 | tf_op jit(solution)/shard_map/ppermute | solution.py:40
  110.7 15.8 %collective-permute-start.28 = (bf16[128,2048]{1,0:T(8,128)(2,1)S(1)}, bf16[128,2048]{1,0:T(8,128)(2,1)S(1)}, u32[]{:S(2)}, u32[]{:S(2)}) collective-permute-start(bf16[128,2048]{1,0:T(8,128)(2,1)S(1)} %add_convert_fusion.1), channel_id=1, source_target_pairs={{0,2},{1,3},{2,0},{3,1},{4,6},{5,7},{6,4},{7,5},{8,10},{9,11},{10,... | collective-permute-start | bytes 1572872 | tf_op jit(solution)/shard_map/ppermute | solution.py:26
  124.5 1.6 %collective-permute-start.26 = (bf16[128,1024]{1,0:T(8,128)(2,1)S(1)}, bf16[128,1024]{1,0:T(8,128)(2,1)S(1)}, u32[]{:S(2)}, u32[]{:S(2)}) collective-permute-start(bf16[128,1024]{1,0:T(8,128)(2,1)S(1)} %get-tuple-element.37), channel_id=1, source_target_pairs={{0,1},{1,0},{2,3},{3,2},{4,5},{5,4},{6,7},{7,6},{8,9},{9,8},{10,11... | collective-permute-start | bytes 786440 | tf_op jit(solution)/shard_map/ppermute | solution.py:20
  124.7 1.8 %collective-permute-start.25 = (bf16[128,1024]{1,0:T(8,128)(2,1)S(1)}, bf16[128,1024]{1,0:T(8,128)(2,1)S(1)}, u32[]{:S(2)}, u32[]{:S(2)}) collective-permute-start(bf16[128,1024]{1,0:T(8,128)(2,1)S(1)} %get-tuple-element.36), channel_id=1, source_target_pairs={{0,1},{1,0},{2,3},{3,2},{4,5},{5,4},{6,7},{7,6},{8,9},{9,8},{10,11... | collective-permute-start | bytes 786440 | tf_op jit(solution)/shard_map/ppermute | solution.py:20
  (21 other events, 325.0 us)

commit v4 on v3

--- a/solution.py
+++ b/solution.py
@@ -35,6 +35,11 @@
     )
 
 
+def from_rest(value):
+    chips = lax.axis_size("tensor") // 2
+    return [from_chip(value, k) for k in range(1, chips)] + [from_other(value, k) for k in range(chips)]
+
+
 def swap_groups(value, mask):
     count = lax.axis_size("dp")
     return lax.ppermute(value, "dp", [(i, i ^ mask) for i in range(count)])
@@ -76,79 +81,117 @@
 
 def project_kernel(n_dec, n_after, groups, heads, place, *refs):
     refs = list(refs)
-    mine, sib, gain, weight, cosine, sine = refs[:6]
+    mine, sib, weight, gain, cosine, sine = refs[:6]
     refs = refs[6:]
     if n_dec:
         dec, dec_cos, dec_sin = refs[:3]
         refs = refs[3:]
     refs = refs[n_after:]
-    query, entries = refs[:2]
-    if n_dec:
-        dec_query, dec_entries = refs[2:4]
-    inner = refs[-1]
+    query, entries, everything = refs[:3]
+    if n_dec:
+        dec_query, dec_entries = refs[3:5]
+    inner, rows_held, weight_held, row_sems, weight_sems, out_sem = refs[-6:]
     piece = mine.shape[0]
     core = place[0]
     scale = gain[...]
-    for ref, at in ((mine, core), (sib, 1 - core)):
+    depth = (groups + 2) * HD
+    row_copies = [
+        pltpu.make_async_copy(ref, rows_held.at[i], row_sems.at[i])
+        for i, ref in enumerate((mine, sib))
+    ]
+    weight_copies = [
+        pltpu.make_async_copy(
+            weight.at[:, pl.ds(j * depth, depth)], weight_held.at[j], weight_sems.at[j]
+        )
+        for j in range(heads)
+    ]
+    for copy in row_copies + weight_copies:
+        copy.start()
+    for i, at in enumerate((core, 1 - core)):
+        row_copies[i].wait()
         start = pl.multiple_of(at * piece, piece)
-        inner[pl.ds(start, piece), :] = normed(ref[...].astype(jnp.float32), scale)
+        inner[pl.ds(start, piece), :] = normed(rows_held[i].astype(jnp.float32), scale)
     if n_dec:
         inner[2 * piece :, :] = normed(dec[...].astype(jnp.float32), scale)
     here = pl.ds(pl.multiple_of(place[1] * 2 * piece, 2 * piece), 2 * piece)
-    depth = (groups + 2) * HD
     for j in range(heads):
-        mixed = jnp.dot(
-            inner[...],
-            weight[:, j * depth : (j + 1) * depth],
-            preferred_element_type=jnp.float32,
-        )
+        weight_copies[j].wait()
+        mixed = jnp.dot(inner[...], weight_held[j], preferred_element_type=jnp.float32)
 
         def put(rows, cos, sin, query_out, entry_out):
             for g in range(groups):
                 part = rows[:, g * HD : (g + 1) * HD]
                 at = (j * groups + g) * HD
-                query_out[:, at : at + HD] = turn(part, cos, sin).astype(jnp.bfloat16)
-            key = rows[:, groups * HD : (groups + 1) * HD]
-            entry_out[0, :, j * HD : (j + 1) * HD] = turn(key, cos, sin).astype(jnp.bfloat16)
-            entry_out[1, :, j * HD : (j + 1) * HD] = rows[:, (groups + 1) * HD :].astype(
-                jnp.bfloat16
-            )
+                turned = turn(part, cos, sin).astype(jnp.bfloat16)
+                query_out[:, at : at + HD] = turned.astype(query_out.dtype)
+            key = turn(rows[:, groups * HD : (groups + 1) * HD], cos, sin).astype(jnp.bfloat16)
+            value = rows[:, (groups + 1) * HD :].astype(jnp.bfloat16)
+            size = entry_out.shape[1]
+            entry_out[0, :, j * HD : (j + 1) * HD] = key[:size]
+            entry_out[1, :, j * HD : (j + 1) * HD] = value[:size]
 
         put(mixed[: 2 * piece], cosine[here, :], sine[here, :], query, entries)
         if n_dec:
             put(mixed[2 * piece :], dec_cos[...], dec_sin[...], dec_query, dec_entries)
-
-
-def project(place, mine, sib, gain, weight, tables, heads, dec=None, dec_tables=None, after=()):
+    keep = pltpu.make_async_copy(entries, everything.at[:, here, :], out_sem)
+    keep.start()
+    keep.wait()
+
+
+def project(
+    place, mine, sib, gain, weight, tables, heads, everything, dec=None, dec_tables=None, slots=0, after=()
+):
     piece, width = mine.shape
     depth = weight.shape[1] // heads
     groups = depth // HD - 2
     block = 2 * piece
     n_dec = 0 if dec is None else dec.shape[0]
-    args = [mine, sib, gain, weight, *tables]
+    args = [mine, sib, weight, gain, *tables]
     if n_dec:
         args += [dec, *dec_tables]
-    out_shape = []
-    for n in [block] + [n_dec] * bool(n_dec):
+    n_operands = len(args)
+    after = list(after)
+    aliases = {}
+    if everything is not None:
+        after.append(everything)
+        aliases = {n_operands + len(after): 2}
+    wide = heads * groups * HD
+    out_shape = [
+        jax.ShapeDtypeStruct((block, wide), jnp.bfloat16),
+        jax.ShapeDtypeStruct((2, block, heads * HD), jnp.bfloat16),
+        jax.ShapeDtypeStruct((2, tables[0].shape[0], heads * HD), jnp.bfloat16),
+    ]
+    if n_dec:
         out_shape += [
-            jax.ShapeDtypeStruct((n, heads * groups * HD), jnp.bfloat16),
-            jax.ShapeDtypeStruct((2, n, heads * HD), jnp.bfloat16),
+            jax.ShapeDtypeStruct((n_dec, wide), jnp.float32),
+            jax.ShapeDtypeStruct((2, slots, heads * HD), jnp.bfloat16),
         ]
     rows = block + n_dec
     return pl.pallas_call(
         functools.partial(project_kernel, n_dec, len(after), groups, heads),
         out_shape=out_shape,
-        in_specs=[SMEM_WHOLE] + [VMEM_WHOLE] * len(args) + [IN_PLACE] * len(after),
-        out_specs=[VMEM_WHOLE] * len(out_shape),
-        scratch_shapes=[pltpu.VMEM((rows, width), jnp.bfloat16)],
-        compiler_params=params(8),
+        in_specs=[SMEM_WHOLE]
+        + [IN_PLACE] * 3
+        + [VMEM_WHOLE] * (len(args) - 3)
+        + [IN_PLACE] * len(after),
+        out_specs=[VMEM_WHOLE] * 2 + [IN_PLACE] + [VMEM_WHOLE] * (len(out_shape) - 3),
+        scratch_shapes=[
+            pltpu.VMEM((rows, width), jnp.bfloat16),
+            pltpu.VMEM((2, piece, width), jnp.bfloat16),
+            pltpu.VMEM((heads, width, depth), jnp.bfloat16),
+            pltpu.SemaphoreType.DMA((2,)),
+            pltpu.SemaphoreType.DMA((heads,)),
+            pltpu.SemaphoreType.DMA(()),
+        ],
+        input_output_aliases=aliases,
+        compiler_params=params(20),
         cost_estimate=cost(2 * rows * weight.size, 2 * (weight.size + 2 * rows * width)),
         name="project",
     )(place, *args, *after)
 
 
 def fill_kernel(groups, chips, place, query, cache_key, cache_value, *refs):
-    new_keys, new_values, out = refs[:chips], refs[chips : 2 * chips], refs[2 * chips]
+    new_keys, new_values, out = refs[:chips], refs[chips : 2 * chips], refs[-1]
     scaling = 1.0 / math.sqrt(HD)
     count = query.shape[0]
     stored = cache_key.shape[2]
@@ -182,7 +225,7 @@
         out[:, g * HD : (g + 1) * HD] = (mix / total).astype(jnp.bfloat16)
 
 
-def fill_attend(place, query, cache, entries, heads):
+def fill_attend(place, query, cache, entries, heads, after=()):
     count = query.shape[0]
     groups = query.shape[1] // heads // HD
     stored = cache.shape[2]
@@ -200,85 +243,110 @@
                 pl.BlockSpec((1, 1, stored, HD), lambda j, s: (1, 0, 0, j)),
             ]
             + [pl.BlockSpec((1, count, HD), lambda j, s: (0, 0, j))] * chips
-            + [pl.BlockSpec((1, count, HD), lambda j, s: (1, 0, j))] * chips,
+            + [pl.BlockSpec((1, count, HD), lambda j, s: (1, 0, j))] * chips
+            + [IN_PLACE] * len(after),
             out_specs=pl.BlockSpec((count, groups * HD), lambda j, s: (0, j)),
         ),
         compiler_params=params(12),
         cost_estimate=cost(8 * pairs * HD, 2 * cache.size, pairs),
         name="fill_attend",
-    )(place, query, cache, cache, *entries, *entries)
-
-
-def step_kernel(heads, groups, lengths, query, cache, new_key, new_value, out, held, arrived):
+    )(place, query, cache, cache, *entries, *entries, *after)
+
+
+def step_kernel(
+    heads, lengths, query, entries, cache, weight, out, held, scores, shares, weight_held, arrived, weight_sem
+):
     scaling = 1.0 / math.sqrt(HD)
-    slots, stored = cache.shape[1], cache.shape[2]
+    slots, stored, width = cache.shape[1:]
+    groups = query.shape[1] // width
+    lanes = 8
     copies = [
-        [pltpu.make_async_copy(cache.at[w, s], held.at[w, s], arrived.at[w, s]) for w in range(2)]
-        for s in range(slots)
+        [pltpu.make_async_copy(cache.at[w, s], held.at[w, s], arrived.at[w, s]) for s in range(slots)]
+        for w in range(2)
     ]
-    for pair in copies:
-        for copy in pair:
-            copy.start()
+    weight_copy = pltpu.make_async_copy(weight, weight_held, weight_sem)
+    for copy in copies[0] + copies[1] + [weight_copy]:
+        copy.start()
     across = (((1,), (1,)), ((), ()))
     places = lax.broadcasted_iota(jnp.int32, (1, stored), 1)
+    blank = jnp.zeros((1, HD), jnp.float32)
+    new_keys = entries[0].astype(jnp.float32)
+    new_values = entries[1].astype(jnp.float32)
+    own_scores = []
     for s in range(slots):
-        rows = query[s]
-        copies[s][0].wait()
-        old = lax.dot_general(rows, held[0, s], across, preferred_element_type=jnp.float32)
-        old = jnp.where(places < lengths[s], old * scaling, NEGATIVE)
-        own = jnp.sum(
-            rows.astype(jnp.float32) * new_key[s].astype(jnp.float32), axis=-1, keepdims=True
-        )
-        own = own * scaling
-        top = jnp.maximum(jnp.max(old, axis=-1, keepdims=True), own)
-        old = jnp.exp(old - top)
-        own = jnp.exp(own - top)
-        total = jnp.sum(old, axis=-1, keepdims=True) + own
-        copies[s][1].wait()
+        rows = []
+        for j in range(heads):
+            for g in range(groups):
+                at = (j * groups + g) * HD
+                part = query[s : s + 1, at : at + HD]
+                rows.append(
+                    jnp.concatenate([part if i == j else blank for i in range(heads)], axis=1)
+                )
+        rows.append(jnp.zeros((lanes - heads * groups, width), jnp.float32))
+        rows = jnp.concatenate(rows, axis=0)
+        own_scores.append(jnp.sum(rows * new_keys[s : s + 1], axis=-1, keepdims=True))
+        copies[0][s].wait()
+        old = lax.dot_general(
+            rows.astype(jnp.bfloat16), held[0, s], across, preferred_element_type=jnp.float32
+        )
+        scores[s * lanes : (s + 1) * lanes, :] = jnp.where(
+            places < lengths[s], old * scaling, NEGATIVE
+        )
+    old = scores[...]
+    own = jnp.concatenate(own_scores, axis=0) * scaling
+    top = jnp.maximum(jnp.max(old, axis=-1, keepdims=True), own)
+    old = jnp.exp(old - top)
+    own = jnp.exp(own - top)
+    total = jnp.sum(old, axis=-1, keepdims=True) + own
+    shares[...] = old / total
+    own = (own / total).astype(jnp.bfloat16).astype(jnp.float32)
+    attended = []
+    for s in range(slots):
+        copies[1][s].wait()
+        here = slice(s * lanes, (s + 1) * lanes)
         mix = jnp.dot(
-            (old / total).astype(jnp.bfloat16), held[1, s], preferred_element_type=jnp.float32
-        )
-        own = (own / total).astype(jnp.bfloat16).astype(jnp.float32)
-        mix += own * new_value[s].astype(jnp.float32)
-        at = lax.broadcasted_iota(jnp.int32, (rows.shape[0], HD), 0) // groups
-        picked = mix[:, :HD]
-        for j in range(1, heads):
-            picked = jnp.where(at == j, mix[:, j * HD : (j + 1) * HD], picked)
-        out[s] = picked.astype(jnp.bfloat16)
-
-
-def step_attend(lengths, query, cache, entries, slots, heads):
-    groups = query.shape[1] // heads // HD
-    stored = cache.shape[2]
-    width = heads * HD
-    pad = 16
-    parts = query[:slots].reshape(slots, heads * groups, 1, HD)
-    own = (
-        jnp.arange(heads * groups, dtype=jnp.int32)[:, None] // groups
-        == jnp.arange(heads, dtype=jnp.int32)[None, :]
-    )
-    spread = jnp.where(own[None, :, :, None], parts, jnp.bfloat16(0.0))
-    spread = spread.reshape(slots, heads * groups, width)
-    spread = jnp.pad(spread, ((0, 0), (0, pad - heads * groups), (0, 0)))
-    new_key = entries[0, :slots].reshape(slots, 1, width)
-    new_value = entries[1, :slots].reshape(slots, 1, width)
-    out = pl.pallas_call(
-        functools.partial(step_kernel, heads, groups),
-        out_shape=jax.ShapeDtypeStruct((slots, pad, HD), jnp.bfloat16),
-        in_specs=[SMEM_WHOLE, VMEM_WHOLE, IN_PLACE, VMEM_WHOLE, VMEM_WHOLE],
+            shares[here, :].astype(jnp.bfloat16), held[1, s], preferred_element_type=jnp.float32
+        )
+        mix += own[here] * new_values[s : s + 1]
+        parts = []
+        for j in range(heads):
+            for g in range(groups):
+                row = j * groups + g
+                parts.append(mix[row : row + 1, j * HD : (j + 1) * HD])
+        attended.append(jnp.concatenate(parts, axis=1))
+    if out.shape[0] > slots:
+        attended.append(jnp.zeros((out.shape[0] - slots, query.shape[1]), jnp.float32))
+    attended = jnp.concatenate(attended, axis=0).astype(jnp.bfloat16)
+    weight_copy.wait()
+    part = jnp.dot(attended, weight_held[...], preferred_element_type=jnp.float32)
+    out[...] = part.astype(jnp.bfloat16)
+
+
+def step_attend(lengths, query, entries, cache, weight, heads):
+    slots, stored = cache.shape[1:3]
+    padded = query.shape[0]
+    rows = slots * 8
+    return pl.pallas_call(
+        functools.partial(step_kernel, heads),
+        out_shape=jax.ShapeDtypeStruct((padded, weight.shape[1]), jnp.bfloat16),
+        in_specs=[SMEM_WHOLE, VMEM_WHOLE, VMEM_WHOLE, IN_PLACE, IN_PLACE],
         out_specs=VMEM_WHOLE,
         scratch_shapes=[
             pltpu.VMEM(cache.shape, jnp.bfloat16),
+            pltpu.VMEM((rows, stored), jnp.float32),
+            pltpu.VMEM((rows, stored), jnp.float32),
+            pltpu.VMEM(weight.shape, jnp.bfloat16),
             pltpu.SemaphoreType.DMA((2, slots)),
+            pltpu.SemaphoreType.DMA(()),
         ],
-        compiler_params=params(16),
-        cost_estimate=cost(64 * cache.size, 2 * cache.size, slots * stored * pad),
+        compiler_params=params(20),
+        cost_estimate=cost(16 * cache.size, 2 * cache.size, rows * stored),
         name="step_attend",
-    )(lengths, spread, cache, new_key, new_value)
-    return out[:, : heads * groups].reshape(slots, heads * groups * HD)
-
-
-def out_kernel(place, mine, sib, weight, sib_weight, out):
+    )(lengths, query, entries, cache, weight)
+
+
+def out_kernel(place, mine, sib, weight, sib_weight, *refs):
+    out = refs[-1]
     half = out.shape[1]
     cols = pl.ds(pl.multiple_of(place[0] * half, half), half)
     part = jnp.dot(mine[...], weight[:, cols], preferred_element_type=jnp.float32)
@@ -286,18 +354,18 @@
     out[...] = part.astype(jnp.bfloat16)
 
 
-def out_project(place, mine, sib, weight, sib_weight):
+def out_project(place, mine, sib, weight, sib_weight, after=()):
     rows, depth = mine.shape
     half = weight.shape[1] // 2
     return pl.pallas_call(
         out_kernel,
         out_shape=jax.ShapeDtypeStruct((rows, half), jnp.bfloat16),
-        in_specs=[SMEM_WHOLE] + [VMEM_WHOLE] * 4,
+        in_specs=[SMEM_WHOLE] + [VMEM_WHOLE] * 4 + [IN_PLACE] * len(after),
         out_specs=VMEM_WHOLE,
         compiler_params=params(8),
         cost_estimate=cost(4 * rows * depth * half, 4 * depth * half + 6 * rows * half),
         name="out_project",
-    )(place, mine, sib, weight, sib_weight)
+    )(place, mine, sib, weight, sib_weight, *after)
 
 
 def forward_kernel(chips, n_dec, n_after, chunk, place, *refs):
@@ -334,22 +402,24 @@
     piece = mine.shape[0]
     half = shares[0].shape[1]
     core = place[0]
-    jobs = [(mine, shares, core * piece, 0), (sib, shares, (1 - core) * piece, piece)]
-    if n_dec:
-        jobs.append((dec, dec_shares, 0, 2 * piece))
-    for rows, parts, start, put in jobs:
-        size = rows.shape[0]
-        if not isinstance(start, int):
-            start = pl.multiple_of(start, piece)
+    for rows, at_rows, put in ((mine, core, 0), (sib, 1 - core, piece)):
+        here = pl.ds(pl.multiple_of(at_rows * piece, piece), piece)
         for side in range(2):
             at = core if side == 0 else 1 - core
             cols = pl.ds(pl.multiple_of(at * half, half), half)
-            added = parts[side][pl.ds(start, size), :].astype(jnp.float32)
+            added = shares[side][here, :].astype(jnp.float32)
             for k in range(1, chips):
-                added += parts[2 * k + side][pl.ds(start, size), :].astype(jnp.float32)
+                added += shares[2 * k + side][here, :].astype(jnp.float32)
             value = rows[:, cols].astype(jnp.float32) + added
-            held[put : put + size, cols] = value.astype(jnp.bfloat16)
-        inner[put : put + size, :] = normed(held[put : put + size, :].astype(jnp.float32), gain[...])
+            held[put : put + piece, cols] = value.astype(jnp.bfloat16)
+    if n_dec:
+        added = dec_shares[0][...].astype(jnp.float32)
+        for share in dec_shares[1:]:
+            added += share[...].astype(jnp.float32)
+        held[2 * piece :, :] = (dec[...].astype(jnp.float32) + added).astype(jnp.bfloat16)
+    for put in range(0, held.shape[0], piece):
+        here = slice(put, min(put + piece, held.shape[0]))
+        inner[here, :] = normed(held[here, :].astype(jnp.float32), gain[...])
     resid[...] = held[:piece, :]
     if n_dec:
         dec_resid[...] = held[2 * piece :, :]
@@ -459,7 +529,7 @@
         return jnp.stack(spots + [(chip + j) % chips for j in range(chips)]).astype(jnp.int32)
 
     places = [place_of(k) for k in range(chips)]
-    weight = in_vmem(qkv_weight.reshape(width, -1))
+    weight = in_hbm(qkv_weight.reshape(width, -1))
     gate_weight, up_weight, down_weight = map(in_hbm, (gate_weight, up_weight, down_weight))
     prefill_cache, decode_cache = in_hbm(prefill_cache), in_hbm(decode_cache)
 
@@ -493,42 +563,51 @@
     gain = attention_gain.reshape(1, width)
     tables = angle_tables(prefill_offset[0] + jnp.arange(tokens, dtype=jnp.int32))
     dec_tables = angle_tables(jnp.pad(cache_length, (0, padded - slots)))
-    queries, entries = [None] * chips, [None] * chips
+    queries, entries, everything = [None] * chips, [None] * chips, None
     for k in range(chips):
         last = k == chips - 1
         if last:
-            others = [from_chip(dealt, j) for j in range(1, chips)]
-            others += [from_other(dealt, j) for j in range(chips)]
-            dealt = add(dealt, *others)
+            dealt = add(dealt, *from_rest(dealt))
         got = project(
             places[k],
-            mines[k],
-            sibs[k],
+            in_hbm(mines[k]),
+            in_hbm(sibs[k]),
             gain,
             weight,
             tables,
             heads,
+            everything,
             dealt if last else None,
             dec_tables if last else None,
-            [dealt] if k == 0 else [],
-        )
-        queries[k], entries[k] = got[:2]
+            slots,
+            [queries[k - 1]] if k else [dealt],
+        )
+        queries[k], entries[k], everything = got[:3]
         if last:
-            dec_query, dec_entries = got[2:]
-
-    sib_weight = in_vmem(swap_cores(out_weight))
+            dec_query, dec_entries = got[3:]
+
+    out_share = out_weight
+    sib_weight, queries[-1] = lax.optimization_barrier((out_weight, queries[-1]))
+    sib_weight = in_vmem(swap_cores(sib_weight))
     out_weight = in_vmem(out_weight)
 
-    def finish(attended, place):
-        return out_project(place, attended, swap_cores(attended), out_weight, sib_weight)
+    def finish(attended, place, after):
+        sib = swap_cores(attended)
+        return out_project(place, attended, sib, out_weight, sib_weight, after)
 
     parts = []
+    dec_shares = []
     for k in range(chips):
-        attended = fill_attend(places[k], queries[k], prefill_cache, entries, heads)
-        parts.append(finish(attended, places[k]))
-    dec_att = step_attend(cache_length, dec_query, decode_cache, dec_entries, slots, heads)
-    dec_att = jnp.pad(dec_att, ((0, padded - slots), (0, 0)))
-    dec_part = finish(dec_att, places[0])
+        attended = fill_attend(
+            places[k], queries[k], prefill_cache, entries, heads, dec_shares[:1]
+        )
+        parts.append(finish(attended, places[k], dec_shares[1:]))
+        if k == 0:
+            lengths, parts[0] = lax.optimization_barrier((cache_length, parts[0]))
+            dec_part = step_attend(
+                lengths, dec_query, dec_entries, decode_cache, in_hbm(out_share), heads
+            )
+            dec_shares = [dec_part, *from_rest(dec_part)]
 
     def shares_of(own, others):
         pairs = []
@@ -536,7 +615,6 @@
             pairs += [value, swap_cores(value)]
         return pairs
 
-    dec_shares = shares_of(dec_part, [from_chip(dec_part, j) for j in range(1, chips)])
     gain = forward_gain.reshape(1, width)
     order = [*range(1, chips), 0]
 
@@ -557,7 +635,6 @@
             down_weight,
             dealt if n == 0 else None,
             dec_shares if n == 0 else None,
-            [routed] if n + 1 == chips else [],
         )
         keep, give, resid = got[:3]
         if n + 1 < chips:
@@ -565,14 +642,14 @@
             arrived.append(from_chip(add(keep, swap_cores(give)), chips - b))
         if n == 0:
             dec_sum, dec_resid = got[3:]
-            dec_sum = add(dec_sum, swap_cores(dec_sum))
-            dec_sum, theirs = lax.optimization_barrier((dec_sum, theirs))
-            final = add(dec_resid, dec_sum, *[from_chip(dec_sum, j) for j in range(1, chips)])
-            picker = in_group[:, None] == jnp.arange(padded, dtype=jnp.int32)[None, :]
-            picker = picker & (in_group[:, None] < slots)
-            routed = jnp.dot(
-                picker.astype(jnp.bfloat16), final, preferred_element_type=jnp.float32
-            ).astype(jnp.bfloat16)
+            dec_others = from_rest(dec_sum)
+    dec_sum, arrived[0] = lax.optimization_barrier((dec_sum, arrived[0]))
+    final = add(dec_resid, dec_sum, *dec_others)
+    picker = in_group[:, None] == jnp.arange(padded, dtype=jnp.int32)[None, :]
+    picker = picker & (in_group[:, None] < slots)
+    routed = jnp.dot(
+        picker.astype(jnp.bfloat16), final, preferred_element_type=jnp.float32
+    ).astype(jnp.bfloat16)
     give = jnp.concatenate([swap_cores(part) for part in jnp.split(give, 2, axis=1)], axis=1)
     prefill_out = add(resid, keep, give, *arrived)
 
@@ -584,11 +661,7 @@
     pairs = rows.reshape(low, per_device, width)
     routed = add(pairs[0], *[swap_groups(pairs[i], i) for i in range(1, low)])
 
-    around = jnp.concatenate(entries + entries[:-1], axis=1)
-    prefill_entries = lax.dynamic_slice_in_dim(
-        around, (chips - chip) % chips * 2 * piece, tokens, 1
-    )
-    return (prefill_out, routed, prefill_entries, dec_entries[:, :slots])
+    return (prefill_out, routed, everything, dec_entries)
 
 
 def solution(mesh):

time: 128 us -> 110 us (0.86)
  local copies, waits for them, and re-layouts: 15.8 us -> 6.53 us
  waiting for transfers between devices: 24 us -> 16.8 us
  starting transfers between devices: 21 us -> 26 us
  other arithmetic: 8.73 us -> 5.56 us
  Pallas kernels: 55.2 us -> 53.2 us
    ppermute x7, waiting for transfers between devices: 14.3 us -> 5.23 us  [from_chip(): lax.ppermute(value, 'tensor', [(i, (i // 2 - step) % chips * 2 + i % 2) f...]
    unnamed x43 -> x25, local copies, waits for them, and re-layouts: 13.5 us -> 6.2 us
    pallas_call x2, Pallas kernels: 4.98 us -> 10.6 us  [project(): pl.pallas_call(functools.partial(project_kernel, n_dec, len(after), group...]
    ppermute x8, waiting for transfers between devices: 0.02 us -> 5.53 us  [swap_groups(): return lax.ppermute(value, 'dp', [(i, i ^ mask) for i in range(count)])]
    pallas_call x3 -> x2, Pallas kernels: 7.6 us -> 2.5 us  [out_project(): pl.pallas_call(out_kernel, out_shape=jax.ShapeDtypeStruct((rows, half), j...]
    ppermute x16 -> x12, waiting for transfers between devices: 6.62 us -> 2.89 us  [swap_cores(): return lax.ppermute(value, 'tensor', [(i, i ^ 1) for i in range(count)])]
    ppermute x7, starting transfers between devices: 7 us -> 9.52 us  [from_chip(): lax.ppermute(value, 'tensor', [(i, (i // 2 - step) % chips * 2 + i % 2) f...]
    concatenate x2 -> x0, other arithmetic: 2.44 us -> none  [the longest x1 2.37 us: on_device(): around = jnp.concatenate(entries + entries[:-1], axis=1)]
  transfers between devices with their start and end apart: 33 -> 33, of which waited for: 13 -> 12; matrix products, arithmetic and copies ran while one was open for 13% -> 10% of each run, Pallas kernels for 41% -> 42%
where the time goes in v4:
time: 110 us
  Pallas kernels  53.2 us (48%)
  starting transfers between devices  26 us (24%)
  waiting for transfers between devices  16.8 us (15%)
  local copies, waits for them, and re-layouts  6.53 us (6%)
  other arithmetic  5.56 us (5%)
  between operations  1.69 us (2%)
    pallas_call x2, Pallas kernels, feed_forward(): pl.pallas_call(functools.partial(forward_kernel, chips, n_dec, len(after)...  23.8 us
    ppermute x8, starting transfers between devices, swap_groups(): return lax.ppermute(value, 'dp', [(i, i ^ mask) for i in range(count)])  10.8 us
    pallas_call x2, Pallas kernels, project(): pl.pallas_call(functools.partial(project_kernel, n_dec, len(after), group...  10.6 us
    pallas_call x2, Pallas kernels, fill_attend(): pl.pallas_call(functools.partial(fill_kernel, groups, chips), out_shape=j...  9.69 us
    ppermute x7, starting transfers between devices, from_chip(): lax.ppermute(value, 'tensor', [(i, (i // 2 - step) % chips * 2 + i % 2) f...  9.52 us
    pallas_call x1, Pallas kernels, step_attend(): pl.pallas_call(functools.partial(step_kernel, heads), out_shape=jax.Shape...  6.51 us
    unnamed x25, local copies, waits for them, and re-layouts  6.2 us
    ppermute x8, waiting for transfers between devices, swap_groups(): return lax.ppermute(value, 'dp', [(i, i ^ mask) for i in range(count)])  5.53 us
  transfers between devices with their start and end apart: 33, of which 12 were waited for; matrix products, arithmetic and copies ran while one was open for 10% of the time, Pallas kernels for 42%

profile of v4, /device:TPU:0, one launch (start us, length us, event | category | flops | bytes accessed | tf_op | source)
XLA Modules:
  0.0 110.1 jit_solution(15255841745569167609)
XLA Ops:
  1.2 2.6 %collective-permute-start.5 = (bf16[128,2048]{1,0:T(8,128)(2,1)}, bf16[128,2048]{1,0:T(8,128)(2,1)S(1)}, u32[]{:S(2)}, u32[]{:S(2)}) collective-permute-start(bf16[128,2048]{1,0:T(8,128)(2,1)} %refs_0_.3), channel_id=1, source_target_pairs={{0,2},{1,3},{2,0},{3,1},{4,6},{5,7},{6,4},{7,5},{8,10},{9,11},{10,... | collective-permute-start | bytes 1572872 | tf_op jit(solution)/shard_map/ppermute | solution.py:26
  3.7 1.5 %collective-permute-start.1 = (bf16[2,2048]{1,0:T(2,128)(2,1)}, bf16[2,2048]{1,0:T(2,128)(2,1)S(1)}, u32[]{:S(2)}, u32[]{:S(2)}) collective-permute-start(bf16[2,2048]{1,0:T(2,128)(2,1)} %param.15), channel_id=1, source_target_pairs={{0,4},{4,0},{8,12},{12,8},{16,20},{20,16},{24,28},{28,24},{1,5},{5... | collective-permute-start | bytes 24584 | tf_op jit(solution)/shard_map/ppermute | solution.py:45
  6.7 1.0 fusion
  7.7 0.8 select_reduce_fusion
  9.3 3.7 %collective-permute-start.4 = (bf16[4,2048]{1,0:T(4,128)(2,1)S(1)}, bf16[4,2048]{1,0:T(4,128)(2,1)S(1)}, u32[]{:S(2)}, u32[]{:S(2)}) collective-permute-start(bf16[4,2048]{1,0:T(4,128)(2,1)S(1)} %pad_maximum_fusion.2), channel_id=1, source_target_pairs={{0,24},{4,28},{8,16},{12,20},{16,8},{20,12},{24,0},{28,4},{1,25},{... | collective-permute-start | bytes 49160 | tf_op jit(solution)/shard_map/ppermute | solution.py:45
  14.2 5.4 %copy.19 = bf16[256,8,2,512]{3,1,2,0:T(8,128)(2,1)} copy(bf16[256,8,2,512]{3,2,1,0:T(2,128)(2,1)} %bitcast.16) | data formatting | bytes 8388608
  20.5 1.5 %collective-permute-start.7 = (bf16[16,2048]{1,0:T(8,128)(2,1)S(1)}, bf16[16,2048]{1,0:T(8,128)(2,1)S(1)}, u32[]{:S(2)}, u32[]{:S(2)}) collective-permute-start(bf16[16,2048]{1,0:T(8,128)(2,1)S(1)} %convolution_convert_fusion.1.refs_6_), channel_id=1, source_target_pairs={{0,2},{1,3},{2,0},{3,1},{4,6},{5,7},{6,4},{7,5},{8,10},{9,11},{10,... | collective-permute-start | bytes 196616 | tf_op jit(solution)/shard_map/ppermute | solution.py:26
  22.1 1.5 %collective-permute-done.9 = bf16[16,2048]{1,0:T(8,128)(2,1)S(1)} collective-permute-done((bf16[16,2048]{1,0:T(8,128)(2,1)S(1)}, bf16[16,2048]{1,0:T(8,128)(2,1)S(1)}, u32[]{:S(2)}, u32[]{:S(2)}) %collective-permute-start.9) | collective-permute-done | bytes 65568 | tf_op jit(solution)/shard_map/ppermute | solution.py:33
  23.6 1.4 %collective-permute-done.7 = bf16[16,2048]{1,0:T(8,128)(2,1)S(1)} collective-permute-done((bf16[16,2048]{1,0:T(8,128)(2,1)S(1)}, bf16[16,2048]{1,0:T(8,128)(2,1)S(1)}, u32[]{:S(2)}, u32[]{:S(2)}) %collective-permute-start.7) | collective-permute-done | bytes 65568 | tf_op jit(solution)/shard_map/ppermute | solution.py:26
  25.1 5.0 %project.2 = (bf16[256,512]{1,0:T(8,128)(2,1)S(1)}, bf16[2,256,256]{2,1,0:T(8,128)(2,1)S(1)}, bf16[2,512,256]{2,1,0:T(8,128)(2,1)}) custom-call(s32[5]{0:T(128)S(1)} %stack.23.place, bf16[128,2048]{1,0:T(8,128)(2,1)} %refs_0_.3, bf16[128,2048]{1,0:T(8,128)(2,1)} %collective-permute-done.refs_1_, bf16[2048,1024]{1,0:T(8,128)(2,1)} %bitcast.14, ...), custom_call_target="tpu_custom_call" | custom-call | flops 1073741824 | bytes 6291456 | tf_op jit(solution)/shard_map/project/pallas_call | solution.py:170
  30.9 5.6 %project.3 = (bf16[256,512]{1,0:T(8,128)(2,1)S(1)}, bf16[2,256,256]{2,1,0:T(8,128)(2,1)S(1)}, bf16[2,512,256]{2,1,0:T(8,128)(2,1)}, f32[16,512]{1,0:T(8,128)S(1)}, bf16[2,8,256]{2,1,0:T(8,128)(2,1)}) custom-call(s32[5]{0:T(128)S(1)} %stack.24.place, bf16[128,2048]{1,0:T(8,128)(2,1)} %copy-done.2, ...), custom_call_target="tpu_custom_call", output_to_operand_aliasing={{2}: (11, {})} | custom-call | flops 1140850688 | bytes 6422528 | tf_op jit(solution)/shard_map/project/pallas_call | solution.py:170
  36.6 4.8 %fill_attend.2.mine = bf16[256,512]{1,0:T(8,128)(2,1)S(1)} custom-call(s32[5]{0:T(128)S(1)} %stack.23.place, bf16[256,512]{1,0:T(8,128)(2,1)S(1)} %get-tuple-element.25.refs_9_.query, bf16[2,1,1024,256]{3,2,1,0:T(8,128)(2,1)} %cache_value.3, bf16[2,1,1024,256]{3,2,1,0:T(8,128)(2,1)} %cache_value.3, ...), custom_call_target="tpu_custom_call" | custom-call | flops 1610612736 | bytes 1048576 | tf_op jit(solution)/shard_map/fill_attend/pallas_call | solution.py:234
  42.0 1.2 %collective-permute-done.10.sib = bf16[256,512]{1,0:T(8,128)(2,1)S(1)} collective-permute-done((bf16[256,512]{1,0:T(8,128)(2,1)S(1)}, bf16[256,512]{1,0:T(8,128)(2,1)S(1)}, u32[]{:S(2)}, u32[]{:S(2)}) %collective-permute-start.10) | collective-permute-done | bytes 262176 | tf_op jit(solution)/shard_map/ppermute | solution.py:20
  43.2 1.3 %out_project.2.refs_2_ = bf16[256,1024]{1,0:T(8,128)(2,1)S(1)} custom-call(s32[5]{0:T(128)S(1)} %stack.23.place, bf16[256,512]{1,0:T(8,128)(2,1)S(1)} %fill_attend.2.mine, bf16[256,512]{1,0:T(8,128)(2,1)S(1)} %collective-permute-done.10.sib, bf16[512,2048]{1,0:T(8,128)(2,1)S(1)} %copy-done, bf16[512,2048]{1,0:T(8,128)(2,1)S(1)} %collective-permute-done.11.sib_weight), custom_call_target="tpu_custom_call" | custom-call | flops 536870912 | bytes 3670016 | tf_op jit(solution)/shard_map/out_project/pallas_call | solution.py:360
  44.5 1.3 %collective-permute-start.22 = (bf16[256,1024]{1,0:T(8,128)(2,1)S(1)}, bf16[256,1024]{1,0:T(8,128)(2,1)S(1)}, u32[]{:S(2)}, u32[]{:S(2)}) collective-permute-start(bf16[256,1024]{1,0:T(8,128)(2,1)S(1)} %out_project.2.refs_2_), channel_id=1, source_target_pairs={{0,2},{1,3},{2,0},{3,1},{4,6},{5,7},{6,4},{7,5},{8,10},{9,11},{10,... | collective-permute-start | bytes 1572872 | tf_op jit(solution)/shard_map/ppermute | solution.py:26
  45.8 6.5 %step_attend.1.refs_4_.refs_7_ = bf16[16,2048]{1,0:T(8,128)(2,1)S(1)} custom-call(s32[8]{0:T(128)S(1)} %copy-done.10, f32[16,512]{1,0:T(8,128)S(1)} %get-tuple-element.34.query, bf16[2,8,256]{2,1,0:T(8,128)(2,1)S(1)} %copy-done.9, bf16[2,8,1024,256]{3,2,1,0:T(8,128)(2,1)} %cache.1, bf16[512,2048]{1,0:T(8,128)(2,1)} %weight.5), custom_call_target="tpu_custom_call" | custom-call | flops 67108864 | bytes 8388608 | tf_op jit(solution)/shard_map/step_attend/pallas_call | solution.py:329
  52.3 4.9 %fill_attend.3.mine = bf16[256,512]{1,0:T(8,128)(2,1)S(1)} custom-call(s32[5]{0:T(128)S(1)} %stack.24.place, bf16[256,512]{1,0:T(8,128)(2,1)S(1)} %get-tuple-element.32.query, bf16[2,1,1024,256]{3,2,1,0:T(8,128)(2,1)} %cache_value.3, bf16[2,1,1024,256]{3,2,1,0:T(8,128)(2,1)} %cache_value.3, bf16[2,256,256]{2,1,0:T(8,128)(2,1)S(1)} %get-tuple-element.26.refs_0_.refs_2_, ...), custom_call_target="tpu_custom_call" | custom-call | flops 1610612736 | bytes 1048576 | tf_op jit(solution)/shard_map/fill_attend/pallas_call | solution.py:234
  58.2 1.3 %collective-permute-start.14 = (bf16[16,2048]{1,0:T(8,128)(2,1)S(1)}, bf16[16,2048]{1,0:T(8,128)(2,1)S(1)}, u32[]{:S(2)}, u32[]{:S(2)}) collective-permute-start(bf16[16,2048]{1,0:T(8,128)(2,1)S(1)} %step_attend.1.refs_4_.refs_7_), channel_id=1, source_target_pairs={{0,2},{1,3},{2,0},{3,1},{4,6},{5,7},{6,4},{7,5},{8,10},{9,11},{10,... | collective-permute-start | bytes 196616 | tf_op jit(solution)/shard_map/ppermute | solution.py:26
  59.5 1.7 %collective-permute-done.16.refs_2_.refs_10_ = bf16[16,2048]{1,0:T(8,128)(2,1)S(1)} collective-permute-done((bf16[16,2048]{1,0:T(8,128)(2,1)S(1)}, bf16[16,2048]{1,0:T(8,128)(2,1)S(1)}, u32[]{:S(2)}, u32[]{:S(2)}) %collective-permute-start.16) | collective-permute-done | bytes 65568 | tf_op jit(solution)/shard_map/ppermute | solution.py:33
  61.2 2.0 %collective-permute-done.14.refs_0_.refs_8_ = bf16[16,2048]{1,0:T(8,128)(2,1)S(1)} collective-permute-done((bf16[16,2048]{1,0:T(8,128)(2,1)S(1)}, bf16[16,2048]{1,0:T(8,128)(2,1)S(1)}, u32[]{:S(2)}, u32[]{:S(2)}) %collective-permute-start.14) | collective-permute-done | bytes 65568 | tf_op jit(solution)/shard_map/ppermute | solution.py:26
  63.1 1.2 %out_project.3.refs_2_ = bf16[256,1024]{1,0:T(8,128)(2,1)S(1)} custom-call(s32[5]{0:T(128)S(1)} %stack.24.place, bf16[256,512]{1,0:T(8,128)(2,1)S(1)} %fill_attend.3.mine, bf16[256,512]{1,0:T(8,128)(2,1)S(1)} %collective-permute-done.13.sib, bf16[512,2048]{1,0:T(8,128)(2,1)S(1)} %copy-done.1, bf16[512,2048]{1,0:T(8,128)(2,1)S(1)} %collective-permute-done.11.sib_weight, ...), custom_call_target="tpu_custom_call" | custom-call | flops 536870912 | bytes 3670016 | tf_op jit(solution)/shard_map/out_project/pallas_call | solution.py:360
  67.2 12.2 %feed_forward.3 = (bf16[128,2048]{1,0:T(8,128)(2,1)S(1)}, bf16[128,2048]{1,0:T(8,128)(2,1)S(1)}, bf16[128,2048]{1,0:T(8,128)(2,1)}, bf16[16,2048]{1,0:T(8,128)(2,1)S(1)}, bf16[16,2048]{1,0:T(8,128)(2,1)S(1)}) custom-call(s32[5]{0:T(128)S(1)} %stack.24.place, bf16[128,2048]{1,0:T(8,128)(2,1)S(1)} %copy-done.3, bf16[128,2048]{1,0:T(8,128)(2,1)S(1)} %copy-done.5, ...), custom_call_target="tpu_custom_call" | custom-call | flops 6845104128 | bytes 25165824 | tf_op jit(solution)/shard_map/feed_forward/pallas_call | solution.py:461
  81.3 0.9 collective-permute-start.26
  82.3 1.2 %collective-permute-start.25 = (bf16[128,2048]{1,0:T(8,128)(2,1)S(1)}, bf16[128,2048]{1,0:T(8,128)(2,1)S(1)}, u32[]{:S(2)}, u32[]{:S(2)}) collective-permute-start(bf16[128,2048]{1,0:T(8,128)(2,1)S(1)} %add_convert_fusion.1), channel_id=1, source_target_pairs={{0,2},{1,3},{2,0},{3,1},{4,6},{5,7},{6,4},{7,5},{8,10},{9,11},{10,... | collective-permute-start | bytes 1572872 | tf_op jit(solution)/shard_map/ppermute | solution.py:26
  83.5 11.7 %feed_forward.2 = (bf16[128,2048]{1,0:T(8,128)(2,1)S(1)}, bf16[128,2048]{1,0:T(8,128)(2,1)S(1)}, bf16[128,2048]{1,0:T(8,128)(2,1)S(1)}) custom-call(s32[5]{0:T(128)S(1)} %stack.23.place, bf16[128,2048]{1,0:T(8,128)(2,1)S(1)} %copy-done.6, bf16[128,2048]{1,0:T(8,128)(2,1)} %collective-permute-done.refs_1_, bf16[256,1024]{1,0:T(8,128)(2,1)S(1)} %out_project.2.refs_2_, ...), custom_call_target="tpu_custom_call" | custom-call | flops 6442450944 | bytes 25165824 | tf_op jit(solution)/shard_map/feed_forward/pallas_call | solution.py:461
  95.2 1.8 %collective-permute-done.25 = bf16[128,2048]{1,0:T(8,128)(2,1)S(1)} collective-permute-done((bf16[128,2048]{1,0:T(8,128)(2,1)S(1)}, bf16[128,2048]{1,0:T(8,128)(2,1)S(1)}, u32[]{:S(2)}, u32[]{:S(2)}) %collective-permute-start.25) | collective-permute-done | bytes 524320 | tf_op jit(solution)/shard_map/ppermute | solution.py:26
  97.3 1.3 %collective-permute-start.29 = (bf16[4,2048]{1,0:T(4,128)(2,1)S(1)}, bf16[4,2048]{1,0:T(4,128)(2,1)S(1)}, u32[]{:S(2)}, u32[]{:S(2)}) collective-permute-start(bf16[4,2048]{1,0:T(4,128)(2,1)S(1)} %get-tuple-element.50), channel_id=1, source_target_pairs={{0,8},{4,12},{8,0},{12,4},{16,24},{20,28},{24,16},{28,20},{1,9},{5... | collective-permute-start | bytes 49160 | tf_op jit(solution)/shard_map/ppermute | solution.py:45
  98.6 2.5 %collective-permute-start.31 = (bf16[4,2048]{1,0:T(4,128)(2,1)S(1)}, bf16[4,2048]{1,0:T(4,128)(2,1)S(1)}, u32[]{:S(2)}, u32[]{:S(2)}) collective-permute-start(bf16[4,2048]{1,0:T(4,128)(2,1)S(1)} %get-tuple-element.51), channel_id=1, source_target_pairs={{0,24},{4,28},{8,16},{12,20},{16,8},{20,12},{24,0},{28,4},{1,25},{... | collective-permute-start | bytes 49160 | tf_op jit(solution)/shard_map/ppermute | solution.py:45
  102.2 2.0 %collective-permute-done.31 = bf16[4,2048]{1,0:T(4,128)(2,1)S(1)} collective-permute-done((bf16[4,2048]{1,0:T(4,128)(2,1)S(1)}, bf16[4,2048]{1,0:T(4,128)(2,1)S(1)}, u32[]{:S(2)}, u32[]{:S(2)}) %collective-permute-start.31) | collective-permute-done | bytes 16416 | tf_op jit(solution)/shard_map/ppermute | solution.py:45
  104.2 1.5 %collective-permute-done.30 = bf16[4,2048]{1,0:T(4,128)(2,1)S(1)} collective-permute-done((bf16[4,2048]{1,0:T(4,128)(2,1)S(1)}, bf16[4,2048]{1,0:T(4,128)(2,1)S(1)}, u32[]{:S(2)}, u32[]{:S(2)}) %collective-permute-start.30) | collective-permute-done | bytes 16416 | tf_op jit(solution)/shard_map/ppermute | solution.py:45
  106.4 1.1 %add_convert_fusion = bf16[128,2048]{1,0:T(8,128)(2,1)} fusion(bf16[128,2048]{1,0:T(8,128)(2,1)S(1)} %collective-permute-done.25, bf16[128,2048]{1,0:T(8,128)(2,1)S(1)} %get-tuple-element.37, bf16[128,2048]{1,0:T(8,128)(2,1)S(1)} %get-tuple-element.36, bf16[128,1024]{1,0:T(8,128)(2,1)S(1)} %collective-permute-done.20, ...), kind=kLoop, calls=%fused_computation.2 | loop fusion | flops 2883584 | bytes 2621440 | tf_op jit(solution)/shard_map/convert_element_type | solution.py:494
  107.5 2.0 %collective-permute-done.32 = bf16[2,2048]{1,0:T(2,128)(2,1)S(1)} collective-permute-done((bf16[2,2048]{1,0:T(2,128)(2,1)S(1)}, bf16[2,2048]{1,0:T(2,128)(2,1)S(1)}, u32[]{:S(2)}, u32[]{:S(2)}) %collective-permute-start.32) | collective-permute-done | bytes 8224 | tf_op jit(solution)/shard_map/ppermute | solution.py:45
  (92 shorter events, 14.2 us)
Async XLA Ops:
  0.7 24.4 %collective-permute-start = (bf16[128,2048]{1,0:T(8,128)(2,1)}, bf16[128,2048]{1,0:T(8,128)(2,1)}, u32[]{:S(2)}, u32[]{:S(2)}) collective-permute-start(bf16[128,2048]{1,0:T(8,128)(2,1)} %refs_0_.3), channel_id=1, source_target_pairs={{0,1},{1,0},{2,3},{3,2},{4,5},{5,4},{6,7},{7,6},{8,9},{9,8},{10,11... | collective-permute-start | bytes 1572872 | tf_op jit(solution)/shard_map/ppermute | solution.py:20
  1.2 20.9 %collective-permute-start.5 = (bf16[128,2048]{1,0:T(8,128)(2,1)}, bf16[128,2048]{1,0:T(8,128)(2,1)S(1)}, u32[]{:S(2)}, u32[]{:S(2)}) collective-permute-start(bf16[128,2048]{1,0:T(8,128)(2,1)} %refs_0_.3), channel_id=1, source_target_pairs={{0,2},{1,3},{2,0},{3,1},{4,6},{5,7},{6,4},{7,5},{8,10},{9,11},{10,... | collective-permute-start | bytes 1572872 | tf_op jit(solution)/shard_map/ppermute | solution.py:26
  3.7 4.8 %collective-permute-start.1 = (bf16[2,2048]{1,0:T(2,128)(2,1)}, bf16[2,2048]{1,0:T(2,128)(2,1)S(1)}, u32[]{:S(2)}, u32[]{:S(2)}) collective-permute-start(bf16[2,2048]{1,0:T(2,128)(2,1)} %param.15), channel_id=1, source_target_pairs={{0,4},{4,0},{8,12},{12,8},{16,20},{20,16},{24,28},{28,24},{1,5},{5... | collective-permute-start | bytes 24584 | tf_op jit(solution)/shard_map/ppermute | solution.py:45
  9.3 10.2 %collective-permute-start.4 = (bf16[4,2048]{1,0:T(4,128)(2,1)S(1)}, bf16[4,2048]{1,0:T(4,128)(2,1)S(1)}, u32[]{:S(2)}, u32[]{:S(2)}) collective-permute-start(bf16[4,2048]{1,0:T(4,128)(2,1)S(1)} %pad_maximum_fusion.2), channel_id=1, source_target_pairs={{0,24},{4,28},{8,16},{12,20},{16,8},{20,12},{24,0},{28,4},{1,25},{... | collective-permute-start | bytes 49160 | tf_op jit(solution)/shard_map/ppermute | solution.py:45
  13.0 6.6 %collective-permute-start.3 = (bf16[4,2048]{1,0:T(4,128)(2,1)S(1)}, bf16[4,2048]{1,0:T(4,128)(2,1)S(1)}, u32[]{:S(2)}, u32[]{:S(2)}) collective-permute-start(bf16[4,2048]{1,0:T(4,128)(2,1)S(1)} %pad_maximum_fusion.2), channel_id=1, source_target_pairs={{0,16},{4,20},{8,24},{12,28},{16,0},{20,4},{24,8},{28,12},{1,17},{... | collective-permute-start | bytes 49160 | tf_op jit(solution)/shard_map/ppermute | solution.py:45
  13.0 6.6 %collective-permute-start.2 = (bf16[4,2048]{1,0:T(4,128)(2,1)S(1)}, bf16[4,2048]{1,0:T(4,128)(2,1)S(1)}, u32[]{:S(2)}, u32[]{:S(2)}) collective-permute-start(bf16[4,2048]{1,0:T(4,128)(2,1)S(1)} %pad_maximum_fusion.2), channel_id=1, source_target_pairs={{0,8},{4,12},{8,0},{12,4},{16,24},{20,28},{24,16},{28,20},{1,9},{5... | collective-permute-start | bytes 49160 | tf_op jit(solution)/shard_map/ppermute | solution.py:45
  19.8 3.8 %collective-permute-start.9 = (bf16[16,2048]{1,0:T(8,128)(2,1)S(1)}, bf16[16,2048]{1,0:T(8,128)(2,1)S(1)}, u32[]{:S(2)}, u32[]{:S(2)}) collective-permute-start(bf16[16,2048]{1,0:T(8,128)(2,1)S(1)} %convolution_convert_fusion.1.refs_6_), channel_id=1, source_target_pairs={{0,3},{1,2},{2,1},{3,0},{4,7},{5,6},{6,5},{7,4},{8,11},{9,10},{10,... | collective-permute-start | bytes 196616 | tf_op jit(solution)/shard_map/ppermute | solution.py:33
  19.9 3.7 %collective-permute-start.8 = (bf16[16,2048]{1,0:T(8,128)(2,1)S(1)}, bf16[16,2048]{1,0:T(8,128)(2,1)S(1)}, u32[]{:S(2)}, u32[]{:S(2)}) collective-permute-start(bf16[16,2048]{1,0:T(8,128)(2,1)S(1)} %convolution_convert_fusion.1.refs_6_), channel_id=1, source_target_pairs={{0,1},{1,0},{2,3},{3,2},{4,5},{5,4},{6,7},{7,6},{8,9},{9,8},{10,11... | collective-permute-start | bytes 196616 | tf_op jit(solution)/shard_map/ppermute | solution.py:33
  20.5 4.5 %collective-permute-start.7 = (bf16[16,2048]{1,0:T(8,128)(2,1)S(1)}, bf16[16,2048]{1,0:T(8,128)(2,1)S(1)}, u32[]{:S(2)}, u32[]{:S(2)}) collective-permute-start(bf16[16,2048]{1,0:T(8,128)(2,1)S(1)} %convolution_convert_fusion.1.refs_6_), channel_id=1, source_target_pairs={{0,2},{1,3},{2,0},{3,1},{4,6},{5,7},{6,4},{7,5},{8,10},{9,11},{10,... | collective-permute-start | bytes 196616 | tf_op jit(solution)/shard_map/ppermute | solution.py:26
  22.1 8.0 %collective-permute-start.6 = (bf16[128,2048]{1,0:T(8,128)(2,1)S(1)}, bf16[128,2048]{1,0:T(8,128)(2,1)S(1)}, u32[]{:S(2)}, u32[]{:S(2)}) collective-permute-start(bf16[128,2048]{1,0:T(8,128)(2,1)S(1)} %collective-permute-done.5.refs_0_), channel_id=1, source_target_pairs={{0,1},{1,0},{2,3},{3,2},{4,5},{5,4},{6,7},{7,6},{8,9},{9,8},{10,11... | collective-permute-start | bytes 1572872 | tf_op jit(solution)/shard_map/ppermute | solution.py:20
  36.6 6.6 %collective-permute-start.11 = (bf16[512,2048]{1,0:T(8,128)(2,1)S(1)}, bf16[512,2048]{1,0:T(8,128)(2,1)S(1)}, u32[]{:S(2)}, u32[]{:S(2)}) collective-permute-start(bf16[512,2048]{1,0:T(8,128)(2,1)S(1)} %copy-done), channel_id=1, source_target_pairs={{0,1},{1,0},{2,3},{3,2},{4,5},{5,4},{6,7},{7,6},{8,9},{9,8},{10,11... | collective-permute-start | bytes 6291464 | tf_op jit(solution)/shard_map/ppermute | solution.py:20
  44.5 20.0 %collective-permute-start.22 = (bf16[256,1024]{1,0:T(8,128)(2,1)S(1)}, bf16[256,1024]{1,0:T(8,128)(2,1)S(1)}, u32[]{:S(2)}, u32[]{:S(2)}) collective-permute-start(bf16[256,1024]{1,0:T(8,128)(2,1)S(1)} %out_project.2.refs_2_), channel_id=1, source_target_pairs={{0,2},{1,3},{2,0},{3,1},{4,6},{5,7},{6,4},{7,5},{8,10},{9,11},{10,... | collective-permute-start | bytes 1572872 | tf_op jit(solution)/shard_map/ppermute | solution.py:26
  57.2 5.9 %collective-permute-start.13 = (bf16[256,512]{1,0:T(8,128)(2,1)S(1)}, bf16[256,512]{1,0:T(8,128)(2,1)S(1)}, u32[]{:S(2)}, u32[]{:S(2)}) collective-permute-start(bf16[256,512]{1,0:T(8,128)(2,1)S(1)} %fill_attend.3.mine), channel_id=1, source_target_pairs={{0,1},{1,0},{2,3},{3,2},{4,5},{5,4},{6,7},{7,6},{8,9},{9,8},{10,11... | collective-permute-start | bytes 786440 | tf_op jit(solution)/shard_map/ppermute | solution.py:20
  57.3 3.8 %collective-permute-start.16 = (bf16[16,2048]{1,0:T(8,128)(2,1)S(1)}, bf16[16,2048]{1,0:T(8,128)(2,1)S(1)}, u32[]{:S(2)}, u32[]{:S(2)}) collective-permute-start(bf16[16,2048]{1,0:T(8,128)(2,1)S(1)} %step_attend.1.refs_4_.refs_7_), channel_id=1, source_target_pairs={{0,3},{1,2},{2,1},{3,0},{4,7},{5,6},{6,5},{7,4},{8,11},{9,10},{10,... | collective-permute-start | bytes 196616 | tf_op jit(solution)/shard_map/ppermute | solution.py:33
  58.2 3.0 %collective-permute-start.15 = (bf16[16,2048]{1,0:T(8,128)(2,1)S(1)}, bf16[16,2048]{1,0:T(8,128)(2,1)S(1)}, u32[]{:S(2)}, u32[]{:S(2)}) collective-permute-start(bf16[16,2048]{1,0:T(8,128)(2,1)S(1)} %step_attend.1.refs_4_.refs_7_), channel_id=1, source_target_pairs={{0,1},{1,0},{2,3},{3,2},{4,5},{5,4},{6,7},{7,6},{8,9},{9,8},{10,11... | collective-permute-start | bytes 196616 | tf_op jit(solution)/shard_map/ppermute | solution.py:33
  58.2 4.9 %collective-permute-start.14 = (bf16[16,2048]{1,0:T(8,128)(2,1)S(1)}, bf16[16,2048]{1,0:T(8,128)(2,1)S(1)}, u32[]{:S(2)}, u32[]{:S(2)}) collective-permute-start(bf16[16,2048]{1,0:T(8,128)(2,1)S(1)} %step_attend.1.refs_4_.refs_7_), channel_id=1, source_target_pairs={{0,2},{1,3},{2,0},{3,1},{4,6},{5,7},{6,4},{7,5},{8,10},{9,11},{10,... | collective-permute-start | bytes 196616 | tf_op jit(solution)/shard_map/ppermute | solution.py:26
  64.4 2.0 %collective-permute-start.21 = (bf16[256,1024]{1,0:T(8,128)(2,1)S(1)}, bf16[256,1024]{1,0:T(8,128)(2,1)S(1)}, u32[]{:S(2)}, u32[]{:S(2)}) collective-permute-start(bf16[256,1024]{1,0:T(8,128)(2,1)S(1)} %out_project.3.refs_2_), channel_id=1, source_target_pairs={{0,1},{1,0},{2,3},{3,2},{4,5},{5,4},{6,7},{7,6},{8,9},{9,8},{10,11... | collective-permute-start | bytes 1572872 | tf_op jit(solution)/shard_map/ppermute | solution.py:20
  64.5 2.6 %collective-permute-start.23 = (bf16[256,1024]{1,0:T(8,128)(2,1)S(1)}, bf16[256,1024]{1,0:T(8,128)(2,1)S(1)}, u32[]{:S(2)}, u32[]{:S(2)}) collective-permute-start(bf16[256,1024]{1,0:T(8,128)(2,1)S(1)} %collective-permute-done.22.refs_4_), channel_id=1, source_target_pairs={{0,1},{1,0},{2,3},{3,2},{4,5},{5,4},{6,7},{7,6},{8,9},{9,8},{10,11... | collective-permute-start | bytes 1572872 | tf_op jit(solution)/shard_map/ppermute | solution.py:20
  65.0 14.9 %collective-permute-start.17 = (bf16[256,1024]{1,0:T(8,128)(2,1)S(1)}, bf16[256,1024]{1,0:T(8,128)(2,1)S(1)}, u32[]{:S(2)}, u32[]{:S(2)}) collective-permute-start(bf16[256,1024]{1,0:T(8,128)(2,1)S(1)} %out_project.3.refs_2_), channel_id=1, source_target_pairs={{0,2},{1,3},{2,0},{3,1},{4,6},{5,7},{6,4},{7,5},{8,10},{9,11},{10,... | collective-permute-start | bytes 1572872 | tf_op jit(solution)/shard_map/ppermute | solution.py:26
  79.3 2.0 %collective-permute-start.24 = (bf16[128,2048]{1,0:T(8,128)(2,1)S(1)}, bf16[128,2048]{1,0:T(8,128)(2,1)S(1)}, u32[]{:S(2)}, u32[]{:S(2)}) collective-permute-start(bf16[128,2048]{1,0:T(8,128)(2,1)S(1)} %get-tuple-element.41), channel_id=1, source_target_pairs={{0,1},{1,0},{2,3},{3,2},{4,5},{5,4},{6,7},{7,6},{8,9},{9,8},{10,11... | collective-permute-start | bytes 1572872 | tf_op jit(solution)/shard_map/ppermute | solution.py:20
  79.5 2.8 %collective-permute-start.12 = (bf16[256,1024]{1,0:T(8,128)(2,1)S(1)}, bf16[256,1024]{1,0:T(8,128)(2,1)S(1)}, u32[]{:S(2)}, u32[]{:S(2)}) collective-permute-start(bf16[256,1024]{1,0:T(8,128)(2,1)S(1)} %out_project.2.refs_2_), channel_id=1, source_target_pairs={{0,1},{1,0},{2,3},{3,2},{4,5},{5,4},{6,7},{7,6},{8,9},{9,8},{10,11... | collective-permute-start | bytes 1572872 | tf_op jit(solution)/shard_map/ppermute | solution.py:20
  79.9 3.6 %collective-permute-start.18 = (bf16[256,1024]{1,0:T(8,128)(2,1)S(1)}, bf16[256,1024]{1,0:T(8,128)(2,1)S(1)}, u32[]{:S(2)}, u32[]{:S(2)}) collective-permute-start(bf16[256,1024]{1,0:T(8,128)(2,1)S(1)} %collective-permute-done.17.refs_4_), channel_id=1, source_target_pairs={{0,1},{1,0},{2,3},{3,2},{4,5},{5,4},{6,7},{7,6},{8,9},{9,8},{10,11... | collective-permute-start | bytes 1572872 | tf_op jit(solution)/shard_map/ppermute | solution.py:20
  80.0 17.1 %collective-permute-start.28 = (bf16[16,2048]{1,0:T(8,128)(2,1)S(1)}, bf16[16,2048]{1,0:T(8,128)(2,1)S(1)}, u32[]{:S(2)}, u32[]{:S(2)}) collective-permute-start(bf16[16,2048]{1,0:T(8,128)(2,1)S(1)} %get-tuple-element.44), channel_id=1, source_target_pairs={{0,3},{1,2},{2,1},{3,0},{4,7},{5,6},{6,5},{7,4},{8,11},{9,10},{10,... | collective-permute-start | bytes 196616 | tf_op jit(solution)/shard_map/ppermute | solution.py:33
  80.8 16.3 %collective-permute-start.27 = (bf16[16,2048]{1,0:T(8,128)(2,1)S(1)}, bf16[16,2048]{1,0:T(8,128)(2,1)S(1)}, u32[]{:S(2)}, u32[]{:S(2)}) collective-permute-start(bf16[16,2048]{1,0:T(8,128)(2,1)S(1)} %get-tuple-element.44), channel_id=1, source_target_pairs={{0,1},{1,0},{2,3},{3,2},{4,5},{5,4},{6,7},{7,6},{8,9},{9,8},{10,11... | collective-permute-start | bytes 196616 | tf_op jit(solution)/shard_map/ppermute | solution.py:33
  81.3 15.8 %collective-permute-start.26 = (bf16[16,2048]{1,0:T(8,128)(2,1)S(1)}, bf16[16,2048]{1,0:T(8,128)(2,1)S(1)}, u32[]{:S(2)}, u32[]{:S(2)}) collective-permute-start(bf16[16,2048]{1,0:T(8,128)(2,1)S(1)} %get-tuple-element.44), channel_id=1, source_target_pairs={{0,2},{1,3},{2,0},{3,1},{4,6},{5,7},{6,4},{7,5},{8,10},{9,11},{10,... | collective-permute-start | bytes 196616 | tf_op jit(solution)/shard_map/ppermute | solution.py:26
  82.3 14.7 %collective-permute-start.25 = (bf16[128,2048]{1,0:T(8,128)(2,1)S(1)}, bf16[128,2048]{1,0:T(8,128)(2,1)S(1)}, u32[]{:S(2)}, u32[]{:S(2)}) collective-permute-start(bf16[128,2048]{1,0:T(8,128)(2,1)S(1)} %add_convert_fusion.1), channel_id=1, source_target_pairs={{0,2},{1,3},{2,0},{3,1},{4,6},{5,7},{6,4},{7,5},{8,10},{9,11},{10,... | collective-permute-start | bytes 1572872 | tf_op jit(solution)/shard_map/ppermute | solution.py:26
  97.3 4.9 %collective-permute-start.29 = (bf16[4,2048]{1,0:T(4,128)(2,1)S(1)}, bf16[4,2048]{1,0:T(4,128)(2,1)S(1)}, u32[]{:S(2)}, u32[]{:S(2)}) collective-permute-start(bf16[4,2048]{1,0:T(4,128)(2,1)S(1)} %get-tuple-element.50), channel_id=1, source_target_pairs={{0,8},{4,12},{8,0},{12,4},{16,24},{20,28},{24,16},{28,20},{1,9},{5... | collective-permute-start | bytes 49160 | tf_op jit(solution)/shard_map/ppermute | solution.py:45
  98.6 5.5 %collective-permute-start.31 = (bf16[4,2048]{1,0:T(4,128)(2,1)S(1)}, bf16[4,2048]{1,0:T(4,128)(2,1)S(1)}, u32[]{:S(2)}, u32[]{:S(2)}) collective-permute-start(bf16[4,2048]{1,0:T(4,128)(2,1)S(1)} %get-tuple-element.51), channel_id=1, source_target_pairs={{0,24},{4,28},{8,16},{12,20},{16,8},{20,12},{24,0},{28,4},{1,25},{... | collective-permute-start | bytes 49160 | tf_op jit(solution)/shard_map/ppermute | solution.py:45
  101.1 4.6 %collective-permute-start.30 = (bf16[4,2048]{1,0:T(4,128)(2,1)S(1)}, bf16[4,2048]{1,0:T(4,128)(2,1)S(1)}, u32[]{:S(2)}, u32[]{:S(2)}) collective-permute-start(bf16[4,2048]{1,0:T(4,128)(2,1)S(1)} %get-tuple-element.52), channel_id=1, source_target_pairs={{0,16},{4,20},{8,24},{12,28},{16,0},{20,4},{24,8},{28,12},{1,17},{... | collective-permute-start | bytes 49160 | tf_op jit(solution)/shard_map/ppermute | solution.py:45
  101.6 4.8 %collective-permute-start.19 = (bf16[128,1024]{1,0:T(8,128)(2,1)S(1)}, bf16[128,1024]{1,0:T(8,128)(2,1)S(1)}, u32[]{:S(2)}, u32[]{:S(2)}) collective-permute-start(bf16[128,1024]{1,0:T(8,128)(2,1)S(1)} %get-tuple-element.48), channel_id=1, source_target_pairs={{0,1},{1,0},{2,3},{3,2},{4,5},{5,4},{6,7},{7,6},{8,9},{9,8},{10,11... | collective-permute-start | bytes 786440 | tf_op jit(solution)/shard_map/ppermute | solution.py:20
  101.7 4.7 %collective-permute-start.20 = (bf16[128,1024]{1,0:T(8,128)(2,1)S(1)}, bf16[128,1024]{1,0:T(8,128)(2,1)S(1)}, u32[]{:S(2)}, u32[]{:S(2)}) collective-permute-start(bf16[128,1024]{1,0:T(8,128)(2,1)S(1)} %get-tuple-element.49), channel_id=1, source_target_pairs={{0,1},{1,0},{2,3},{3,2},{4,5},{5,4},{6,7},{7,6},{8,9},{9,8},{10,11... | collective-permute-start | bytes 786440 | tf_op jit(solution)/shard_map/ppermute | solution.py:20
  105.8 3.7 %collective-permute-start.32 = (bf16[2,2048]{1,0:T(2,128)(2,1)S(1)}, bf16[2,2048]{1,0:T(2,128)(2,1)S(1)}, u32[]{:S(2)}, u32[]{:S(2)}) collective-permute-start(bf16[2,2048]{1,0:T(2,128)(2,1)S(1)} %slice.35), channel_id=1, source_target_pairs={{0,4},{4,0},{8,12},{12,8},{16,20},{20,16},{24,28},{28,24},{1,5},{5... | collective-permute-start | bytes 24584 | tf_op jit(solution)/shard_map/ppermute | solution.py:45
  (13 other events, 194.2 us)

commit v5 on v4

--- a/solution.py
+++ b/solution.py
@@ -200,29 +200,25 @@
         jnp.int32, (count, count), 0
     )
     across = (((1,), (1,)), ((), ()))
+    rows = jnp.concatenate([query[:, g * HD : (g + 1) * HD] for g in range(groups)], axis=0)
+    ahead = jnp.concatenate([ahead] * groups, axis=0)
+    scores = lax.dot_general(rows, cache_key[0, 0], across, preferred_element_type=jnp.float32)
+    scores = [jnp.where(old_seen, scores * scaling, NEGATIVE)]
+    for k in range(chips):
+        fresh = lax.dot_general(rows, new_keys[k][0], across, preferred_element_type=jnp.float32)
+        gap = (place[1] - place[3 + k]) * count
+        scores.append(jnp.where(ahead <= gap, fresh * scaling, NEGATIVE))
+    top = jnp.max(scores[0], axis=-1, keepdims=True)
+    for part in scores[1:]:
+        top = jnp.maximum(top, jnp.max(part, axis=-1, keepdims=True))
+    mix, total = 0.0, 0.0
+    for part, values in zip(scores, [cache_value[0, 0], *[v[0] for v in new_values]]):
+        weights = jnp.exp(part - top)
+        total += jnp.sum(weights, axis=-1, keepdims=True)
+        mix += jnp.dot(weights.astype(jnp.bfloat16), values, preferred_element_type=jnp.float32)
+    mix = (mix / total).astype(jnp.bfloat16)
     for g in range(groups):
-        rows = query[:, g * HD : (g + 1) * HD]
-        scores = lax.dot_general(
-            rows, cache_key[0, 0], across, preferred_element_type=jnp.float32
-        )
-        scores = [jnp.where(old_seen, scores * scaling, NEGATIVE)]
-        for k in range(chips):
-            fresh = lax.dot_general(
-                rows, new_keys[k][0], across, preferred_element_type=jnp.float32
-            )
-            gap = (place[1] - place[3 + k]) * count
-            scores.append(jnp.where(ahead <= gap, fresh * scaling, NEGATIVE))
-        top = jnp.max(scores[0], axis=-1, keepdims=True)
-        for part in scores[1:]:
-            top = jnp.maximum(top, jnp.max(part, axis=-1, keepdims=True))
-        mix, total = 0.0, 0.0
-        for part, values in zip(scores, [cache_value[0, 0], *[v[0] for v in new_values]]):
-            weights = jnp.exp(part - top)
-            total += jnp.sum(weights, axis=-1, keepdims=True)
-            mix += jnp.dot(
-                weights.astype(jnp.bfloat16), values, preferred_element_type=jnp.float32
-            )
-        out[:, g * HD : (g + 1) * HD] = (mix / total).astype(jnp.bfloat16)
+        out[:, g * HD : (g + 1) * HD] = mix[g * count : (g + 1) * count]
 
 
 def fill_attend(place, query, cache, entries, heads, after=()):
@@ -247,7 +243,7 @@
             + [IN_PLACE] * len(after),
             out_specs=pl.BlockSpec((count, groups * HD), lambda j, s: (0, j)),
         ),
-        compiler_params=params(12),
+        compiler_params=params(24),
         cost_estimate=cost(8 * pairs * HD, 2 * cache.size, pairs),
         name="fill_attend",
     )(place, query, cache, cache, *entries, *entries, *after)
@@ -368,7 +364,7 @@
     )(place, mine, sib, weight, sib_weight, *after)
 
 
-def forward_kernel(chips, n_dec, n_after, chunk, place, *refs):
+def forward_kernel(split, chips, n_dec, n_after, chunk, place, *refs):
     refs = list(refs)
     mine, sib = refs[:2]
     shares = refs[2 : 2 + 2 * chips]
@@ -376,29 +372,34 @@
     if n_dec:
         dec, dec_shares = refs[0], refs[1 : 1 + 2 * chips]
         refs = refs[1 + 2 * chips :]
-    gain, *weights = refs[:4]
-    refs = refs[4 + n_after :]
-    keep, give, resid = refs[:3]
-    refs = refs[3:]
-    if n_dec:
-        dec_out, dec_resid = refs[:2]
-        refs = refs[2:]
-    held, inner, hidden, gate, up, down, arrived = refs
-    chunks = gate.shape[0]
+    gain, *weights = refs[: 3 if split else 4]
+    refs = refs[(3 if split else 4) + n_after :]
+    if split:
+        resid, hidden = refs[:2]
+        held, inner, gate, up, arrived = refs[2:]
+        down = ()
+    else:
+        keep, give, resid = refs[:3]
+        refs = refs[3:]
+        if n_dec:
+            dec_out, dec_resid = refs[:2]
+            refs = refs[2:]
+        held, inner, hidden, gate, up, down, arrived = refs
     copies = [
         [
             pltpu.make_async_copy(
                 source.at[:, pl.ds(i * chunk, chunk)], target.at[i], arrived.at[w, i]
             )
-            for i in range(chunks)
+            for i in range(target.shape[0])
         ]
-        for w, (source, target) in enumerate(zip(weights, (gate, up, down)))
+        for w, (source, target) in enumerate(zip(weights, [gate, up, down]))
     ]
-    for i in range(chunks):
-        copies[0][i].start()
-        copies[1][i].start()
-    for i in range(chunks):
-        copies[2][i].start()
+    for pair in zip(copies[0], copies[1]):
+        for copy in pair:
+            copy.start()
+    for rest in copies[2:]:
+        for copy in rest:
+            copy.start()
     piece = mine.shape[0]
     half = shares[0].shape[1]
     core = place[0]
@@ -424,14 +425,14 @@
     if n_dec:
         dec_resid[...] = held[2 * piece :, :]
 
-    for i in range(chunks):
+    for i in range(gate.shape[0]):
         at = slice(i * chunk, (i + 1) * chunk)
         copies[0][i].wait()
         gated = jnp.dot(inner[...], gate[i], preferred_element_type=jnp.float32)
         copies[1][i].wait()
         raised = jnp.dot(inner[...], up[i], preferred_element_type=jnp.float32)
         hidden[:, at] = (gated / (1.0 + jnp.exp(-gated)) * raised).astype(jnp.bfloat16)
-    for i in range(chunks):
+    for i in range(0 if split else down.shape[0]):
         at = slice(i * chunk, (i + 1) * chunk)
         copies[2][i].wait()
         part = jnp.dot(hidden[...], down[i], preferred_element_type=jnp.float32)
@@ -442,8 +443,45 @@
             dec_out[:, at] = part[2 * piece :]
 
 
+def lower_kernel(chunk, hidden, weight, *refs):
+    keep, give, down, arrived = refs[-4:]
+    piece = keep.shape[0]
+    copies = [
+        pltpu.make_async_copy(weight.at[:, pl.ds(i * chunk, chunk)], down.at[i], arrived.at[i])
+        for i in range(down.shape[0])
+    ]
+    for copy in copies:
+        copy.start()
+    for i, copy in enumerate(copies):
+        at = slice(i * chunk, (i + 1) * chunk)
+        copy.wait()
+        part = jnp.dot(hidden[...], down[i], preferred_element_type=jnp.float32)
+        part = part.astype(jnp.bfloat16)
+        keep[:, at] = part[:piece]
+        give[:, at] = part[piece:]
+
+
+def lower(hidden, weight, after):
+    rows, units = hidden.shape
+    width = weight.shape[1]
+    chunk = width // 4
+    return pl.pallas_call(
+        functools.partial(lower_kernel, chunk),
+        out_shape=[jax.ShapeDtypeStruct((rows // 2, width), jnp.bfloat16)] * 2,
+        in_specs=[VMEM_WHOLE] + [IN_PLACE] * (1 + len(after)),
+        out_specs=[VMEM_WHOLE] * 2,
+        scratch_shapes=[
+            pltpu.VMEM((4, units, chunk), jnp.bfloat16),
+            pltpu.SemaphoreType.DMA((4,)),
+        ],
+        compiler_params=params(24),
+        cost_estimate=cost(2 * rows * width * units, 2 * width * units),
+        name="lower",
+    )(hidden, weight, *after)
+
+
 def feed_forward(
-    place, mine, sib, shares, gain, gate, up, down, dec=None, dec_shares=None, after=()
+    place, mine, sib, shares, gain, gate, up, down=None, dec=None, dec_shares=None, after=()
 ):
     piece, width = mine.shape
     chips = len(shares) // 2
@@ -456,22 +494,26 @@
     if n_dec:
         args += [dec, *dec_shares]
     n_whole = len(args) + 1
-    args += [gain, gate, up, down]
-    sizes = [piece] * 3 + [n_dec] * 2 * bool(n_dec)
+    split = down is None
+    args += [gain, gate, up] + [down] * (not split)
+    if split:
+        shapes = [(piece, width), (rows, units)]
+    else:
+        shapes = [(n, width) for n in [piece] * 3 + [n_dec] * 2 * bool(n_dec)]
+    n_weights = 2 if split else 3
     return pl.pallas_call(
-        functools.partial(forward_kernel, chips, n_dec, len(after), chunk),
-        out_shape=[jax.ShapeDtypeStruct((n, width), jnp.bfloat16) for n in sizes],
-        in_specs=[SMEM_WHOLE] + [VMEM_WHOLE] * n_whole + [IN_PLACE] * (3 + len(after)),
-        out_specs=[VMEM_WHOLE] * len(sizes),
+        functools.partial(forward_kernel, split, chips, n_dec, len(after), chunk),
+        out_shape=[jax.ShapeDtypeStruct(shape, jnp.bfloat16) for shape in shapes],
+        in_specs=[SMEM_WHOLE] + [VMEM_WHOLE] * n_whole + [IN_PLACE] * (n_weights + len(after)),
+        out_specs=[VMEM_WHOLE] * len(shapes),
         scratch_shapes=[
             pltpu.VMEM((rows, width), jnp.bfloat16),
             pltpu.VMEM((rows, width), jnp.bfloat16),
-            pltpu.VMEM((rows, units), jnp.bfloat16),
-            pltpu.VMEM((units // chunk, width, chunk), jnp.bfloat16),
-            pltpu.VMEM((units // chunk, width, chunk), jnp.bfloat16),
-            pltpu.VMEM((chunks, units, chunk), jnp.bfloat16),
-            pltpu.SemaphoreType.DMA((3, chunks)),
-        ],
+        ]
+        + [pltpu.VMEM((rows, units), jnp.bfloat16)] * (not split)
+        + [pltpu.VMEM((units // chunk, width, chunk), jnp.bfloat16)] * 2
+        + [pltpu.VMEM((chunks, units, chunk), jnp.bfloat16)] * (not split)
+        + [pltpu.SemaphoreType.DMA((n_weights, chunks))],
         compiler_params=params(40),
         cost_estimate=cost(6 * rows * width * units, 6 * width * units, rows * units),
         name="feed_forward",
@@ -567,7 +609,10 @@
     for k in range(chips):
         last = k == chips - 1
         if last:
-            dealt = add(dealt, *from_rest(dealt))
+            others = from_rest(dealt)
+            if k:
+                *others, queries[k - 1] = lax.optimization_barrier((*others, queries[k - 1]))
+            dealt = add(dealt, *others)
         got = project(
             places[k],
             in_hbm(mines[k]),
@@ -591,9 +636,10 @@
     sib_weight = in_vmem(swap_cores(sib_weight))
     out_weight = in_vmem(out_weight)
 
-    def finish(attended, place, after):
+    def finish(attended, place, before):
+        attended, *before = lax.optimization_barrier((attended, *before))
         sib = swap_cores(attended)
-        return out_project(place, attended, sib, out_weight, sib_weight, after)
+        return out_project(place, attended, sib, out_weight, sib_weight), before
 
     parts = []
     dec_shares = []
@@ -601,7 +647,8 @@
         attended = fill_attend(
             places[k], queries[k], prefill_cache, entries, heads, dec_shares[:1]
         )
-        parts.append(finish(attended, places[k], dec_shares[1:]))
+        part, dec_shares[1:] = finish(attended, places[k], dec_shares[1:])
+        parts.append(part)
         if k == 0:
             lengths, parts[0] = lax.optimization_barrier((cache_length, parts[0]))
             dec_part = step_attend(
@@ -632,35 +679,37 @@
             gain,
             gate_weight,
             up_weight,
-            down_weight,
+            down_weight if n + 1 < chips else None,
             dealt if n == 0 else None,
             dec_shares if n == 0 else None,
         )
-        keep, give, resid = got[:3]
         if n + 1 < chips:
-            theirs = fetch(order[n + 1])
-            arrived.append(from_chip(add(keep, swap_cores(give)), chips - b))
+            keep, give = got[:2]
+            *theirs, keep = lax.optimization_barrier((*fetch(order[n + 1]), keep))
+            both = add(keep, swap_cores(give))
+            arrived.append(from_chip(both, chips - b))
         if n == 0:
             dec_sum, dec_resid = got[3:]
             dec_others = from_rest(dec_sum)
-    dec_sum, arrived[0] = lax.optimization_barrier((dec_sum, arrived[0]))
+    resid, hidden = got
+    dec_sum, hidden = lax.optimization_barrier((dec_sum, hidden))
     final = add(dec_resid, dec_sum, *dec_others)
     picker = in_group[:, None] == jnp.arange(padded, dtype=jnp.int32)[None, :]
     picker = picker & (in_group[:, None] < slots)
     routed = jnp.dot(
         picker.astype(jnp.bfloat16), final, preferred_element_type=jnp.float32
     ).astype(jnp.bfloat16)
-    give = jnp.concatenate([swap_cores(part) for part in jnp.split(give, 2, axis=1)], axis=1)
-    prefill_out = add(resid, keep, give, *arrived)
-
+    keep, give = lower(hidden, down_weight, [routed])
     low = max(dp_count // 4, 1)
     pairs = routed.reshape(dp_count // low, low * per_device, width)
     rows = add(
         pairs[0], *[swap_groups(pairs[i], i * low) for i in range(1, dp_count // low)]
     )
+    *arrived, rows, give = lax.optimization_barrier((*arrived, rows, give))
     pairs = rows.reshape(low, per_device, width)
     routed = add(pairs[0], *[swap_groups(pairs[i], i) for i in range(1, low)])
 
+    prefill_out = add(resid, keep, swap_cores(give), *arrived)
     return (prefill_out, routed, everything, dec_entries)
 
 

time: 110 us -> 106 us (0.964)
  waiting for transfers between devices: 16.8 us -> 9.8 us
  Pallas kernels: 53.2 us -> 57.3 us
  starting transfers between devices: 26 us -> 24.2 us
    ppermute x7, waiting for transfers between devices: 5.23 us -> 1.35 us  [from_chip(): lax.ppermute(value, 'tensor', [(i, (i // 2 - step) % chips * 2 + i % 2) f...]
    ppermute x6, waiting for transfers between devices: 3.17 us -> 0.02 us  [from_other(): lax.ppermute(value, 'tensor', [(i, (i // 2 - step) % (count // 2) * 2 + 1...]
    pallas_call x2, Pallas kernels: 9.69 us -> 12.2 us  [fill_attend(): pl.pallas_call(functools.partial(fill_kernel, groups, chips), out_shape=j...]
    ppermute x12 -> x11, waiting for transfers between devices: 2.89 us -> 5.27 us  [swap_cores(): return lax.ppermute(value, 'tensor', [(i, i ^ 1) for i in range(count)])]
    ppermute x8, waiting for transfers between devices: 5.53 us -> 3.16 us  [swap_groups(): return lax.ppermute(value, 'dp', [(i, i ^ mask) for i in range(count)])]
    ppermute x7, starting transfers between devices: 9.52 us -> 7.81 us  [from_chip(): lax.ppermute(value, 'tensor', [(i, (i // 2 - step) % chips * 2 + i % 2) f...]
    pallas_call x2 -> x3, Pallas kernels: 23.8 us -> 25.5 us  [the longest x2 21 us: feed_forward(): pl.pallas_call(functools.partial(forward_kernel, split, chips, n_dec, len...]
    ppermute x12 -> x11, starting transfers between devices: 3.16 us -> 2.52 us  [swap_cores(): return lax.ppermute(value, 'tensor', [(i, i ^ 1) for i in range(count)])]
  transfers between devices with their start and end apart: 33 -> 32, of which waited for: 12 -> 7; matrix products, arithmetic and copies ran while one was open for 10% -> 10% of each run, Pallas kernels for 42% -> 48%
where the time goes in v5:
time: 106 us; the launch traced here: 105 us
  Pallas kernels  57.3 us (54%)
  starting transfers between devices  24.2 us (23%)
  waiting for transfers between devices  9.8 us (9%)
  local copies, waits for them, and re-layouts  6.48 us (6%)
  other arithmetic  5.57 us (5%)
  between operations  1.71 us (2%)
    pallas_call x2, Pallas kernels, feed_forward(): pl.pallas_call(functools.partial(forward_kernel, split, chips, n_dec, len...  21 us
    pallas_call x2, Pallas kernels, fill_attend(): pl.pallas_call(functools.partial(fill_kernel, groups, chips), out_shape=j...  12.2 us
    ppermute x8, starting transfers between devices, swap_groups(): return lax.ppermute(value, 'dp', [(i, i ^ mask) for i in range(count)])  10.8 us
    pallas_call x2, Pallas kernels, project(): pl.pallas_call(functools.partial(project_kernel, n_dec, len(after), group...  10.6 us
    ppermute x7, starting transfers between devices, from_chip(): lax.ppermute(value, 'tensor', [(i, (i // 2 - step) % chips * 2 + i % 2) f...  7.81 us
    pallas_call x1, Pallas kernels, step_attend(): pl.pallas_call(functools.partial(step_kernel, heads), out_shape=jax.Shape...  6.51 us
    unnamed x25, local copies, waits for them, and re-layouts  6.19 us
    ppermute x11, waiting for transfers between devices, swap_cores(): return lax.ppermute(value, 'tensor', [(i, i ^ 1) for i in range(count)])  5.27 us
  transfers between devices with their start and end apart: 32, of which 7 were waited for; matrix products, arithmetic and copies ran while one was open for 10% of the time, Pallas kernels for 48%

profile of v5, /device:TPU:0, one launch (start us, length us, event | category | flops | bytes accessed | tf_op | source)
XLA Modules:
  0.0 105.4 jit_solution(8520870801987330459)
XLA Ops:
  1.2 2.6 %collective-permute-start.8 = (bf16[128,2048]{1,0:T(8,128)(2,1)}, bf16[128,2048]{1,0:T(8,128)(2,1)S(1)}, u32[]{:S(2)}, u32[]{:S(2)}) collective-permute-start(bf16[128,2048]{1,0:T(8,128)(2,1)} %refs_0_.3), channel_id=1, source_target_pairs={{0,2},{1,3},{2,0},{3,1},{4,6},{5,7},{6,4},{7,5},{8,10},{9,11},{10,... | collective-permute-start | bytes 1572872 | tf_op jit(solution)/shard_map/ppermute | solution.py:26
  3.7 1.5 %collective-permute-start.1 = (bf16[2,2048]{1,0:T(2,128)(2,1)}, bf16[2,2048]{1,0:T(2,128)(2,1)S(1)}, u32[]{:S(2)}, u32[]{:S(2)}) collective-permute-start(bf16[2,2048]{1,0:T(2,128)(2,1)} %param.15), channel_id=1, source_target_pairs={{0,4},{4,0},{8,12},{12,8},{16,20},{20,16},{24,28},{28,24},{1,5},{5... | collective-permute-start | bytes 24584 | tf_op jit(solution)/shard_map/ppermute | solution.py:45
  6.7 1.0 fusion
  7.7 0.8 select_reduce_fusion
  8.8 0.7 pad_maximum_fusion.2
  9.5 3.7 %collective-permute-start.4 = (bf16[4,2048]{1,0:T(4,128)(2,1)S(1)}, bf16[4,2048]{1,0:T(4,128)(2,1)S(1)}, u32[]{:S(2)}, u32[]{:S(2)}) collective-permute-start(bf16[4,2048]{1,0:T(4,128)(2,1)S(1)} %pad_maximum_fusion.2), channel_id=1, source_target_pairs={{0,24},{4,28},{8,16},{12,20},{16,8},{20,12},{24,0},{28,4},{1,25},{... | collective-permute-start | bytes 49160 | tf_op jit(solution)/shard_map/ppermute | solution.py:45
  13.2 0.8 collective-permute-start.2
  14.2 5.3 %copy.19 = bf16[256,8,2,512]{3,1,2,0:T(8,128)(2,1)} copy(bf16[256,8,2,512]{3,2,1,0:T(2,128)(2,1)} %bitcast.16) | data formatting | bytes 8388608
  20.5 1.5 %collective-permute-start.5 = (bf16[16,2048]{1,0:T(8,128)(2,1)S(1)}, bf16[16,2048]{1,0:T(8,128)(2,1)S(1)}, u32[]{:S(2)}, u32[]{:S(2)}) collective-permute-start(bf16[16,2048]{1,0:T(8,128)(2,1)S(1)} %convolution_convert_fusion.1.refs_6_), channel_id=1, source_target_pairs={{0,2},{1,3},{2,0},{3,1},{4,6},{5,7},{6,4},{7,5},{8,10},{9,11},{10,... | collective-permute-start | bytes 196616 | tf_op jit(solution)/shard_map/ppermute | solution.py:26
  22.1 5.0 %project.2 = (bf16[256,512]{1,0:T(8,128)(2,1)S(1)}, bf16[2,256,256]{2,1,0:T(8,128)(2,1)S(1)}, bf16[2,512,256]{2,1,0:T(8,128)(2,1)}) custom-call(s32[5]{0:T(128)S(1)} %stack.23.place, bf16[128,2048]{1,0:T(8,128)(2,1)} %refs_0_.3, bf16[128,2048]{1,0:T(8,128)(2,1)} %collective-permute-done.refs_1_, bf16[2048,1024]{1,0:T(8,128)(2,1)} %bitcast.14, ...), custom_call_target="tpu_custom_call" | custom-call | flops 1073741824 | bytes 6291456 | tf_op jit(solution)/shard_map/project/pallas_call | solution.py:170
  27.1 0.8 copy-done.4
  27.9 5.6 %project.3 = (bf16[256,512]{1,0:T(8,128)(2,1)S(1)}, bf16[2,256,256]{2,1,0:T(8,128)(2,1)S(1)}, bf16[2,512,256]{2,1,0:T(8,128)(2,1)}, f32[16,512]{1,0:T(8,128)S(1)}, bf16[2,8,256]{2,1,0:T(8,128)(2,1)}) custom-call(s32[5]{0:T(128)S(1)} %stack.24.place, bf16[128,2048]{1,0:T(8,128)(2,1)} %copy-done.2, ...), custom_call_target="tpu_custom_call", output_to_operand_aliasing={{2}: (11, {})} | custom-call | flops 1140850688 | bytes 6422528 | tf_op jit(solution)/shard_map/project/pallas_call | solution.py:170
  34.2 6.1 %fill_attend.2.mine = bf16[256,512]{1,0:T(8,128)(2,1)S(1)} custom-call(s32[5]{0:T(128)S(1)} %stack.23.place, bf16[256,512]{1,0:T(8,128)(2,1)S(1)} %get-tuple-element.40.refs_9_.query, bf16[2,1,1024,256]{3,2,1,0:T(8,128)(2,1)} %cache_value.3, bf16[2,1,1024,256]{3,2,1,0:T(8,128)(2,1)} %cache_value.3, ...), custom_call_target="tpu_custom_call" | custom-call | flops 1610612736 | bytes 1048576 | tf_op jit(solution)/shard_map/fill_attend/pallas_call | solution.py:230
  40.4 1.5 %collective-permute-done.10.sib = bf16[256,512]{1,0:T(8,128)(2,1)S(1)} collective-permute-done((bf16[256,512]{1,0:T(8,128)(2,1)S(1)}, bf16[256,512]{1,0:T(8,128)(2,1)S(1)}, u32[]{:S(2)}, u32[]{:S(2)}) %collective-permute-start.10) | collective-permute-done | bytes 262176 | tf_op jit(solution)/shard_map/ppermute | solution.py:20
  41.9 1.3 %out_project.2.refs_2_ = bf16[256,1024]{1,0:T(8,128)(2,1)S(1)} custom-call(s32[5]{0:T(128)S(1)} %stack.23.place, bf16[256,512]{1,0:T(8,128)(2,1)S(1)} %fill_attend.2.mine, bf16[256,512]{1,0:T(8,128)(2,1)S(1)} %collective-permute-done.10.sib, bf16[512,2048]{1,0:T(8,128)(2,1)S(1)} %copy-done, bf16[512,2048]{1,0:T(8,128)(2,1)S(1)} %collective-permute-done.11.sib_weight), custom_call_target="tpu_custom_call" | custom-call | flops 536870912 | bytes 3670016 | tf_op jit(solution)/shard_map/out_project/pallas_call | solution.py:356
  43.8 6.5 %step_attend.1.refs_4_.refs_7_ = bf16[16,2048]{1,0:T(8,128)(2,1)S(1)} custom-call(s32[8]{0:T(128)S(1)} %copy-done.10, f32[16,512]{1,0:T(8,128)S(1)} %get-tuple-element.52.query, bf16[2,8,256]{2,1,0:T(8,128)(2,1)S(1)} %copy-done.9, bf16[2,8,1024,256]{3,2,1,0:T(8,128)(2,1)} %cache.1, bf16[512,2048]{1,0:T(8,128)(2,1)} %weight.6), custom_call_target="tpu_custom_call" | custom-call | flops 67108864 | bytes 8388608 | tf_op jit(solution)/shard_map/step_attend/pallas_call | solution.py:325
  50.3 1.0 collective-permute-start.15
  52.5 6.1 %fill_attend.3.mine = bf16[256,512]{1,0:T(8,128)(2,1)S(1)} custom-call(s32[5]{0:T(128)S(1)} %stack.24.place, bf16[256,512]{1,0:T(8,128)(2,1)S(1)} %get-tuple-element.50.query, bf16[2,1,1024,256]{3,2,1,0:T(8,128)(2,1)} %cache_value.3, bf16[2,1,1024,256]{3,2,1,0:T(8,128)(2,1)} %cache_value.3, bf16[2,256,256]{2,1,0:T(8,128)(2,1)S(1)} %get-tuple-element.41.refs_0_.refs_2_, ...), custom_call_target="tpu_custom_call" | custom-call | flops 1610612736 | bytes 1048576 | tf_op jit(solution)/shard_map/fill_attend/pallas_call | solution.py:230
  58.7 1.3 %collective-permute-done.13.refs_8_ = bf16[16,2048]{1,0:T(8,128)(2,1)S(1)} collective-permute-done((bf16[16,2048]{1,0:T(8,128)(2,1)S(1)}, bf16[16,2048]{1,0:T(8,128)(2,1)S(1)}, u32[]{:S(2)}, u32[]{:S(2)}) %collective-permute-start.13) | collective-permute-done | bytes 65568 | tf_op jit(solution)/shard_map/ppermute | solution.py:26
  60.0 1.5 %collective-permute-done.16.sib = bf16[256,512]{1,0:T(8,128)(2,1)S(1)} collective-permute-done((bf16[256,512]{1,0:T(8,128)(2,1)S(1)}, bf16[256,512]{1,0:T(8,128)(2,1)S(1)}, u32[]{:S(2)}, u32[]{:S(2)}) %collective-permute-start.16) | collective-permute-done | bytes 262176 | tf_op jit(solution)/shard_map/ppermute | solution.py:20
  61.5 1.2 %out_project.3.refs_2_ = bf16[256,1024]{1,0:T(8,128)(2,1)S(1)} custom-call(s32[5]{0:T(128)S(1)} %stack.24.place, bf16[256,512]{1,0:T(8,128)(2,1)S(1)} %fill_attend.3.mine, bf16[256,512]{1,0:T(8,128)(2,1)S(1)} %collective-permute-done.16.sib, bf16[512,2048]{1,0:T(8,128)(2,1)S(1)} %copy-done.1, bf16[512,2048]{1,0:T(8,128)(2,1)S(1)} %collective-permute-done.11.sib_weight), custom_call_target="tpu_custom_call" | custom-call | flops 536870912 | bytes 3670016 | tf_op jit(solution)/shard_map/out_project/pallas_call | solution.py:356
  63.9 0.9 collective-permute-done.18.refs_3_
  64.8 0.7 collective-permute-done.20.refs_5_
  65.5 12.1 %feed_forward.2 = (bf16[128,2048]{1,0:T(8,128)(2,1)S(1)}, bf16[128,2048]{1,0:T(8,128)(2,1)S(1)}, bf16[128,2048]{1,0:T(8,128)(2,1)}, bf16[16,2048]{1,0:T(8,128)(2,1)S(1)}, bf16[16,2048]{1,0:T(8,128)(2,1)S(1)}) custom-call(s32[5]{0:T(128)S(1)} %stack.24.place, bf16[128,2048]{1,0:T(8,128)(2,1)S(1)} %copy-done.3, bf16[128,2048]{1,0:T(8,128)(2,1)S(1)} %copy-done.5, ...), custom_call_target="tpu_custom_call" | custom-call | flops 6845104128 | bytes 25165824 | tf_op jit(solution)/shard_map/feed_forward/pallas_call | solution.py:504
  79.7 0.9 collective-permute-start.22
  80.7 1.2 %collective-permute-start.26 = (bf16[128,2048]{1,0:T(8,128)(2,1)S(1)}, bf16[128,2048]{1,0:T(8,128)(2,1)S(1)}, u32[]{:S(2)}, u32[]{:S(2)}) collective-permute-start(bf16[128,2048]{1,0:T(8,128)(2,1)S(1)} %add_convert_fusion.1), channel_id=1, source_target_pairs={{0,2},{1,3},{2,0},{3,1},{4,6},{5,7},{6,4},{7,5},{8,10},{9,11},{10,... | collective-permute-start | bytes 1572872 | tf_op jit(solution)/shard_map/ppermute | solution.py:26
  81.9 8.9 %feed_forward.3 = (bf16[128,2048]{1,0:T(8,128)(2,1)S(1)}, bf16[256,2048]{1,0:T(8,128)(2,1)S(1)}) custom-call(s32[5]{0:T(128)S(1)} %stack.23.place, bf16[128,2048]{1,0:T(8,128)(2,1)S(1)} %copy-done.6, bf16[128,2048]{1,0:T(8,128)(2,1)} %collective-permute-done.refs_1_, bf16[256,1024]{1,0:T(8,128)(2,1)S(1)} %out_project.2.refs_2_, ...), custom_call_target="tpu_custom_call" | custom-call | flops 6442450944 | bytes 25165824 | tf_op jit(solution)/shard_map/feed_forward/pallas_call | solution.py:504
  91.0 1.3 %collective-permute-start.27 = (bf16[4,2048]{1,0:T(4,128)(2,1)S(1)}, bf16[4,2048]{1,0:T(4,128)(2,1)S(1)}, u32[]{:S(2)}, u32[]{:S(2)}) collective-permute-start(bf16[4,2048]{1,0:T(4,128)(2,1)S(1)} %get-tuple-element.76), channel_id=1, source_target_pairs={{0,8},{4,12},{8,0},{12,4},{16,24},{20,28},{24,16},{28,20},{1,9},{5... | collective-permute-start | bytes 49160 | tf_op jit(solution)/shard_map/ppermute | solution.py:45
  92.4 2.4 %collective-permute-start.29 = (bf16[4,2048]{1,0:T(4,128)(2,1)S(1)}, bf16[4,2048]{1,0:T(4,128)(2,1)S(1)}, u32[]{:S(2)}, u32[]{:S(2)}) collective-permute-start(bf16[4,2048]{1,0:T(4,128)(2,1)S(1)} %get-tuple-element.77), channel_id=1, source_target_pairs={{0,24},{4,28},{8,16},{12,20},{16,8},{20,12},{24,0},{28,4},{1,25},{... | collective-permute-start | bytes 49160 | tf_op jit(solution)/shard_map/ppermute | solution.py:45
  95.3 4.5 %lower.1 = (bf16[128,2048]{1,0:T(8,128)(2,1)S(1)}, bf16[128,2048]{1,0:T(8,128)(2,1)S(1)}) custom-call(bf16[256,2048]{1,0:T(8,128)(2,1)S(1)} %get-tuple-element.63.hidden, bf16[2048,2048]{1,0:T(8,128)(2,1)} %weight.7, bf16[16,2048]{1,0:T(8,128)(2,1)S(1)} %convolution_convert_fusion.refs_0_), custom_call_target="tpu_custom_call" | custom-call | flops 2147483648 | bytes 8388608 | tf_op jit(solution)/shard_map/lower/pallas_call | solution.py:468
  100.5 3.1 %collective-permute-done.31 = bf16[2,2048]{1,0:T(2,128)(2,1)S(1)} collective-permute-done((bf16[2,2048]{1,0:T(2,128)(2,1)S(1)}, bf16[2,2048]{1,0:T(2,128)(2,1)S(1)}, u32[]{:S(2)}, u32[]{:S(2)}) %collective-permute-start.31) | collective-permute-done | bytes 8224 | tf_op jit(solution)/shard_map/ppermute | solution.py:45
  104.3 1.1 %add_convert_fusion = bf16[128,2048]{1,0:T(8,128)(2,1)} fusion(bf16[128,2048]{1,0:T(8,128)(2,1)S(1)} %collective-permute-done.26, bf16[128,2048]{1,0:T(8,128)(2,1)S(1)} %collective-permute-done.30, bf16[128,2048]{1,0:T(8,128)(2,1)S(1)} %get-tuple-element.66, bf16[128,2048]{1,0:T(8,128)(2,1)S(1)} %get-tuple-element.60), kind=kLoop, calls=%fused_computation.2 | loop fusion | flops 2097152 | bytes 2621440 | tf_op jit(solution)/shard_map/convert_element_type | solution.py:536
  (90 shorter events, 10.5 us)
Async XLA Ops:
  0.7 21.4 %collective-permute-start = (bf16[128,2048]{1,0:T(8,128)(2,1)}, bf16[128,2048]{1,0:T(8,128)(2,1)}, u32[]{:S(2)}, u32[]{:S(2)}) collective-permute-start(bf16[128,2048]{1,0:T(8,128)(2,1)} %refs_0_.3), channel_id=1, source_target_pairs={{0,1},{1,0},{2,3},{3,2},{4,5},{5,4},{6,7},{7,6},{8,9},{9,8},{10,11... | collective-permute-start | bytes 1572872 | tf_op jit(solution)/shard_map/ppermute | solution.py:20
  1.2 20.9 %collective-permute-start.8 = (bf16[128,2048]{1,0:T(8,128)(2,1)}, bf16[128,2048]{1,0:T(8,128)(2,1)S(1)}, u32[]{:S(2)}, u32[]{:S(2)}) collective-permute-start(bf16[128,2048]{1,0:T(8,128)(2,1)} %refs_0_.3), channel_id=1, source_target_pairs={{0,2},{1,3},{2,0},{3,1},{4,6},{5,7},{6,4},{7,5},{8,10},{9,11},{10,... | collective-permute-start | bytes 1572872 | tf_op jit(solution)/shard_map/ppermute | solution.py:26
  3.7 5.0 %collective-permute-start.1 = (bf16[2,2048]{1,0:T(2,128)(2,1)}, bf16[2,2048]{1,0:T(2,128)(2,1)S(1)}, u32[]{:S(2)}, u32[]{:S(2)}) collective-permute-start(bf16[2,2048]{1,0:T(2,128)(2,1)} %param.15), channel_id=1, source_target_pairs={{0,4},{4,0},{8,12},{12,8},{16,20},{20,16},{24,28},{28,24},{1,5},{5... | collective-permute-start | bytes 24584 | tf_op jit(solution)/shard_map/ppermute | solution.py:45
  9.5 10.0 %collective-permute-start.4 = (bf16[4,2048]{1,0:T(4,128)(2,1)S(1)}, bf16[4,2048]{1,0:T(4,128)(2,1)S(1)}, u32[]{:S(2)}, u32[]{:S(2)}) collective-permute-start(bf16[4,2048]{1,0:T(4,128)(2,1)S(1)} %pad_maximum_fusion.2), channel_id=1, source_target_pairs={{0,24},{4,28},{8,16},{12,20},{16,8},{20,12},{24,0},{28,4},{1,25},{... | collective-permute-start | bytes 49160 | tf_op jit(solution)/shard_map/ppermute | solution.py:45
  13.2 6.4 %collective-permute-start.3 = (bf16[4,2048]{1,0:T(4,128)(2,1)S(1)}, bf16[4,2048]{1,0:T(4,128)(2,1)S(1)}, u32[]{:S(2)}, u32[]{:S(2)}) collective-permute-start(bf16[4,2048]{1,0:T(4,128)(2,1)S(1)} %pad_maximum_fusion.2), channel_id=1, source_target_pairs={{0,16},{4,20},{8,24},{12,28},{16,0},{20,4},{24,8},{28,12},{1,17},{... | collective-permute-start | bytes 49160 | tf_op jit(solution)/shard_map/ppermute | solution.py:45
  13.2 6.4 %collective-permute-start.2 = (bf16[4,2048]{1,0:T(4,128)(2,1)S(1)}, bf16[4,2048]{1,0:T(4,128)(2,1)S(1)}, u32[]{:S(2)}, u32[]{:S(2)}) collective-permute-start(bf16[4,2048]{1,0:T(4,128)(2,1)S(1)} %pad_maximum_fusion.2), channel_id=1, source_target_pairs={{0,8},{4,12},{8,0},{12,4},{16,24},{20,28},{24,16},{28,20},{1,9},{5... | collective-permute-start | bytes 49160 | tf_op jit(solution)/shard_map/ppermute | solution.py:45
  19.8 7.2 %collective-permute-start.7 = (bf16[16,2048]{1,0:T(8,128)(2,1)S(1)}, bf16[16,2048]{1,0:T(8,128)(2,1)S(1)}, u32[]{:S(2)}, u32[]{:S(2)}) collective-permute-start(bf16[16,2048]{1,0:T(8,128)(2,1)S(1)} %convolution_convert_fusion.1.refs_6_), channel_id=1, source_target_pairs={{0,3},{1,2},{2,1},{3,0},{4,7},{5,6},{6,5},{7,4},{8,11},{9,10},{10,... | collective-permute-start | bytes 196616 | tf_op jit(solution)/shard_map/ppermute | solution.py:33
  19.9 7.2 %collective-permute-start.6 = (bf16[16,2048]{1,0:T(8,128)(2,1)S(1)}, bf16[16,2048]{1,0:T(8,128)(2,1)S(1)}, u32[]{:S(2)}, u32[]{:S(2)}) collective-permute-start(bf16[16,2048]{1,0:T(8,128)(2,1)S(1)} %convolution_convert_fusion.1.refs_6_), channel_id=1, source_target_pairs={{0,1},{1,0},{2,3},{3,2},{4,5},{5,4},{6,7},{7,6},{8,9},{9,8},{10,11... | collective-permute-start | bytes 196616 | tf_op jit(solution)/shard_map/ppermute | solution.py:33
  20.5 6.5 %collective-permute-start.5 = (bf16[16,2048]{1,0:T(8,128)(2,1)S(1)}, bf16[16,2048]{1,0:T(8,128)(2,1)S(1)}, u32[]{:S(2)}, u32[]{:S(2)}) collective-permute-start(bf16[16,2048]{1,0:T(8,128)(2,1)S(1)} %convolution_convert_fusion.1.refs_6_), channel_id=1, source_target_pairs={{0,2},{1,3},{2,0},{3,1},{4,6},{5,7},{6,4},{7,5},{8,10},{9,11},{10,... | collective-permute-start | bytes 196616 | tf_op jit(solution)/shard_map/ppermute | solution.py:26
  22.0 5.1 %collective-permute-start.9 = (bf16[128,2048]{1,0:T(8,128)(2,1)S(1)}, bf16[128,2048]{1,0:T(8,128)(2,1)S(1)}, u32[]{:S(2)}, u32[]{:S(2)}) collective-permute-start(bf16[128,2048]{1,0:T(8,128)(2,1)S(1)} %collective-permute-done.8.refs_0_), channel_id=1, source_target_pairs={{0,1},{1,0},{2,3},{3,2},{4,5},{5,4},{6,7},{7,6},{8,9},{9,8},{10,11... | collective-permute-start | bytes 1572872 | tf_op jit(solution)/shard_map/ppermute | solution.py:20
  33.6 8.3 %collective-permute-start.11 = (bf16[512,2048]{1,0:T(8,128)(2,1)S(1)}, bf16[512,2048]{1,0:T(8,128)(2,1)S(1)}, u32[]{:S(2)}, u32[]{:S(2)}) collective-permute-start(bf16[512,2048]{1,0:T(8,128)(2,1)S(1)} %copy-done), channel_id=1, source_target_pairs={{0,1},{1,0},{2,3},{3,2},{4,5},{5,4},{6,7},{7,6},{8,9},{9,8},{10,11... | collective-permute-start | bytes 6291464 | tf_op jit(solution)/shard_map/ppermute | solution.py:20
  40.3 1.6 %collective-permute-start.10 = (bf16[256,512]{1,0:T(8,128)(2,1)S(1)}, bf16[256,512]{1,0:T(8,128)(2,1)S(1)}, u32[]{:S(2)}, u32[]{:S(2)}) collective-permute-start(bf16[256,512]{1,0:T(8,128)(2,1)S(1)} %fill_attend.2.mine), channel_id=1, source_target_pairs={{0,1},{1,0},{2,3},{3,2},{4,5},{5,4},{6,7},{7,6},{8,9},{9,8},{10,11... | collective-permute-start | bytes 786440 | tf_op jit(solution)/shard_map/ppermute | solution.py:20
  43.1 19.8 %collective-permute-start.19 = (bf16[256,1024]{1,0:T(8,128)(2,1)S(1)}, bf16[256,1024]{1,0:T(8,128)(2,1)S(1)}, u32[]{:S(2)}, u32[]{:S(2)}) collective-permute-start(bf16[256,1024]{1,0:T(8,128)(2,1)S(1)} %out_project.2.refs_2_), channel_id=1, source_target_pairs={{0,2},{1,3},{2,0},{3,1},{4,6},{5,7},{6,4},{7,5},{8,10},{9,11},{10,... | collective-permute-start | bytes 1572872 | tf_op jit(solution)/shard_map/ppermute | solution.py:26
  50.3 8.4 %collective-permute-start.15 = (bf16[16,2048]{1,0:T(8,128)(2,1)S(1)}, bf16[16,2048]{1,0:T(8,128)(2,1)S(1)}, u32[]{:S(2)}, u32[]{:S(2)}) collective-permute-start(bf16[16,2048]{1,0:T(8,128)(2,1)S(1)} %step_attend.1.refs_4_.refs_7_), channel_id=1, source_target_pairs={{0,3},{1,2},{2,1},{3,0},{4,7},{5,6},{6,5},{7,4},{8,11},{9,10},{10,... | collective-permute-start | bytes 196616 | tf_op jit(solution)/shard_map/ppermute | solution.py:33
  51.3 7.3 %collective-permute-start.14 = (bf16[16,2048]{1,0:T(8,128)(2,1)S(1)}, bf16[16,2048]{1,0:T(8,128)(2,1)S(1)}, u32[]{:S(2)}, u32[]{:S(2)}) collective-permute-start(bf16[16,2048]{1,0:T(8,128)(2,1)S(1)} %step_attend.1.refs_4_.refs_7_), channel_id=1, source_target_pairs={{0,1},{1,0},{2,3},{3,2},{4,5},{5,4},{6,7},{7,6},{8,9},{9,8},{10,11... | collective-permute-start | bytes 196616 | tf_op jit(solution)/shard_map/ppermute | solution.py:33
  52.0 8.0 %collective-permute-start.13 = (bf16[16,2048]{1,0:T(8,128)(2,1)S(1)}, bf16[16,2048]{1,0:T(8,128)(2,1)S(1)}, u32[]{:S(2)}, u32[]{:S(2)}) collective-permute-start(bf16[16,2048]{1,0:T(8,128)(2,1)S(1)} %step_attend.1.refs_4_.refs_7_), channel_id=1, source_target_pairs={{0,2},{1,3},{2,0},{3,1},{4,6},{5,7},{6,4},{7,5},{8,10},{9,11},{10,... | collective-permute-start | bytes 196616 | tf_op jit(solution)/shard_map/ppermute | solution.py:26
  60.0 1.5 %collective-permute-start.16 = (bf16[256,512]{1,0:T(8,128)(2,1)S(1)}, bf16[256,512]{1,0:T(8,128)(2,1)S(1)}, u32[]{:S(2)}, u32[]{:S(2)}) collective-permute-start(bf16[256,512]{1,0:T(8,128)(2,1)S(1)} %fill_attend.3.mine), channel_id=1, source_target_pairs={{0,1},{1,0},{2,3},{3,2},{4,5},{5,4},{6,7},{7,6},{8,9},{9,8},{10,11... | collective-permute-start | bytes 786440 | tf_op jit(solution)/shard_map/ppermute | solution.py:20
  62.8 2.0 %collective-permute-start.18 = (bf16[256,1024]{1,0:T(8,128)(2,1)S(1)}, bf16[256,1024]{1,0:T(8,128)(2,1)S(1)}, u32[]{:S(2)}, u32[]{:S(2)}) collective-permute-start(bf16[256,1024]{1,0:T(8,128)(2,1)S(1)} %out_project.3.refs_2_), channel_id=1, source_target_pairs={{0,1},{1,0},{2,3},{3,2},{4,5},{5,4},{6,7},{7,6},{8,9},{9,8},{10,11... | collective-permute-start | bytes 1572872 | tf_op jit(solution)/shard_map/ppermute | solution.py:20
  63.0 2.5 %collective-permute-start.20 = (bf16[256,1024]{1,0:T(8,128)(2,1)S(1)}, bf16[256,1024]{1,0:T(8,128)(2,1)S(1)}, u32[]{:S(2)}, u32[]{:S(2)}) collective-permute-start(bf16[256,1024]{1,0:T(8,128)(2,1)S(1)} %collective-permute-done.19.refs_4_), channel_id=1, source_target_pairs={{0,1},{1,0},{2,3},{3,2},{4,5},{5,4},{6,7},{7,6},{8,9},{9,8},{10,11... | collective-permute-start | bytes 1572872 | tf_op jit(solution)/shard_map/ppermute | solution.py:20
  63.4 14.9 %collective-permute-start.17 = (bf16[256,1024]{1,0:T(8,128)(2,1)S(1)}, bf16[256,1024]{1,0:T(8,128)(2,1)S(1)}, u32[]{:S(2)}, u32[]{:S(2)}) collective-permute-start(bf16[256,1024]{1,0:T(8,128)(2,1)S(1)} %out_project.3.refs_2_), channel_id=1, source_target_pairs={{0,2},{1,3},{2,0},{3,1},{4,6},{5,7},{6,4},{7,5},{8,10},{9,11},{10,... | collective-permute-start | bytes 1572872 | tf_op jit(solution)/shard_map/ppermute | solution.py:26
  77.7 2.0 %collective-permute-start.25 = (bf16[128,2048]{1,0:T(8,128)(2,1)S(1)}, bf16[128,2048]{1,0:T(8,128)(2,1)S(1)}, u32[]{:S(2)}, u32[]{:S(2)}) collective-permute-start(bf16[128,2048]{1,0:T(8,128)(2,1)S(1)} %get-tuple-element.68), channel_id=1, source_target_pairs={{0,1},{1,0},{2,3},{3,2},{4,5},{5,4},{6,7},{7,6},{8,9},{9,8},{10,11... | collective-permute-start | bytes 1572872 | tf_op jit(solution)/shard_map/ppermute | solution.py:20
  77.9 2.8 %collective-permute-start.12 = (bf16[256,1024]{1,0:T(8,128)(2,1)S(1)}, bf16[256,1024]{1,0:T(8,128)(2,1)S(1)}, u32[]{:S(2)}, u32[]{:S(2)}) collective-permute-start(bf16[256,1024]{1,0:T(8,128)(2,1)S(1)} %out_project.2.refs_2_), channel_id=1, source_target_pairs={{0,1},{1,0},{2,3},{3,2},{4,5},{5,4},{6,7},{7,6},{8,9},{9,8},{10,11... | collective-permute-start | bytes 1572872 | tf_op jit(solution)/shard_map/ppermute | solution.py:20
  78.3 3.6 %collective-permute-start.21 = (bf16[256,1024]{1,0:T(8,128)(2,1)S(1)}, bf16[256,1024]{1,0:T(8,128)(2,1)S(1)}, u32[]{:S(2)}, u32[]{:S(2)}) collective-permute-start(bf16[256,1024]{1,0:T(8,128)(2,1)S(1)} %collective-permute-done.17.refs_4_), channel_id=1, source_target_pairs={{0,1},{1,0},{2,3},{3,2},{4,5},{5,4},{6,7},{7,6},{8,9},{9,8},{10,11... | collective-permute-start | bytes 1572872 | tf_op jit(solution)/shard_map/ppermute | solution.py:20
  78.4 12.4 %collective-permute-start.24 = (bf16[16,2048]{1,0:T(8,128)(2,1)S(1)}, bf16[16,2048]{1,0:T(8,128)(2,1)S(1)}, u32[]{:S(2)}, u32[]{:S(2)}) collective-permute-start(bf16[16,2048]{1,0:T(8,128)(2,1)S(1)} %get-tuple-element.65), channel_id=1, source_target_pairs={{0,3},{1,2},{2,1},{3,0},{4,7},{5,6},{6,5},{7,4},{8,11},{9,10},{10,... | collective-permute-start | bytes 196616 | tf_op jit(solution)/shard_map/ppermute | solution.py:33
  78.9 11.9 %collective-permute-start.23 = (bf16[16,2048]{1,0:T(8,128)(2,1)S(1)}, bf16[16,2048]{1,0:T(8,128)(2,1)S(1)}, u32[]{:S(2)}, u32[]{:S(2)}) collective-permute-start(bf16[16,2048]{1,0:T(8,128)(2,1)S(1)} %get-tuple-element.65), channel_id=1, source_target_pairs={{0,1},{1,0},{2,3},{3,2},{4,5},{5,4},{6,7},{7,6},{8,9},{9,8},{10,11... | collective-permute-start | bytes 196616 | tf_op jit(solution)/shard_map/ppermute | solution.py:33
  79.7 11.1 %collective-permute-start.22 = (bf16[16,2048]{1,0:T(8,128)(2,1)S(1)}, bf16[16,2048]{1,0:T(8,128)(2,1)S(1)}, u32[]{:S(2)}, u32[]{:S(2)}) collective-permute-start(bf16[16,2048]{1,0:T(8,128)(2,1)S(1)} %get-tuple-element.65), channel_id=1, source_target_pairs={{0,2},{1,3},{2,0},{3,1},{4,6},{5,7},{6,4},{7,5},{8,10},{9,11},{10,... | collective-permute-start | bytes 196616 | tf_op jit(solution)/shard_map/ppermute | solution.py:26
  80.7 19.1 %collective-permute-start.26 = (bf16[128,2048]{1,0:T(8,128)(2,1)S(1)}, bf16[128,2048]{1,0:T(8,128)(2,1)S(1)}, u32[]{:S(2)}, u32[]{:S(2)}) collective-permute-start(bf16[128,2048]{1,0:T(8,128)(2,1)S(1)} %add_convert_fusion.1), channel_id=1, source_target_pairs={{0,2},{1,3},{2,0},{3,1},{4,6},{5,7},{6,4},{7,5},{8,10},{9,11},{10,... | collective-permute-start | bytes 1572872 | tf_op jit(solution)/shard_map/ppermute | solution.py:26
  91.0 8.7 %collective-permute-start.27 = (bf16[4,2048]{1,0:T(4,128)(2,1)S(1)}, bf16[4,2048]{1,0:T(4,128)(2,1)S(1)}, u32[]{:S(2)}, u32[]{:S(2)}) collective-permute-start(bf16[4,2048]{1,0:T(4,128)(2,1)S(1)} %get-tuple-element.76), channel_id=1, source_target_pairs={{0,8},{4,12},{8,0},{12,4},{16,24},{20,28},{24,16},{28,20},{1,9},{5... | collective-permute-start | bytes 49160 | tf_op jit(solution)/shard_map/ppermute | solution.py:45
  92.4 7.4 %collective-permute-start.29 = (bf16[4,2048]{1,0:T(4,128)(2,1)S(1)}, bf16[4,2048]{1,0:T(4,128)(2,1)S(1)}, u32[]{:S(2)}, u32[]{:S(2)}) collective-permute-start(bf16[4,2048]{1,0:T(4,128)(2,1)S(1)} %get-tuple-element.77), channel_id=1, source_target_pairs={{0,24},{4,28},{8,16},{12,20},{16,8},{20,12},{24,0},{28,4},{1,25},{... | collective-permute-start | bytes 49160 | tf_op jit(solution)/shard_map/ppermute | solution.py:45
  94.8 5.0 %collective-permute-start.28 = (bf16[4,2048]{1,0:T(4,128)(2,1)S(1)}, bf16[4,2048]{1,0:T(4,128)(2,1)S(1)}, u32[]{:S(2)}, u32[]{:S(2)}) collective-permute-start(bf16[4,2048]{1,0:T(4,128)(2,1)S(1)} %get-tuple-element.78), channel_id=1, source_target_pairs={{0,16},{4,20},{8,24},{12,28},{16,0},{20,4},{24,8},{28,12},{1,17},{... | collective-permute-start | bytes 49160 | tf_op jit(solution)/shard_map/ppermute | solution.py:45
  99.8 4.4 %collective-permute-start.30 = (bf16[128,2048]{1,0:T(8,128)(2,1)S(1)}, bf16[128,2048]{1,0:T(8,128)(2,1)S(1)}, u32[]{:S(2)}, u32[]{:S(2)}) collective-permute-start(bf16[128,2048]{1,0:T(8,128)(2,1)S(1)} %get-tuple-element.70), channel_id=1, source_target_pairs={{0,1},{1,0},{2,3},{3,2},{4,5},{5,4},{6,7},{7,6},{8,9},{9,8},{10,11... | collective-permute-start | bytes 1572872 | tf_op jit(solution)/shard_map/ppermute | solution.py:20
  99.9 3.7 %collective-permute-start.31 = (bf16[2,2048]{1,0:T(2,128)(2,1)S(1)}, bf16[2,2048]{1,0:T(2,128)(2,1)S(1)}, u32[]{:S(2)}, u32[]{:S(2)}) collective-permute-start(bf16[2,2048]{1,0:T(2,128)(2,1)S(1)} %slice.29), channel_id=1, source_target_pairs={{0,4},{4,0},{8,12},{12,8},{16,20},{20,16},{24,28},{28,24},{1,5},{5... | collective-permute-start | bytes 24584 | tf_op jit(solution)/shard_map/ppermute | solution.py:45
  (12 other events, 186.3 us)

commit v6 on v5

--- a/solution.py
+++ b/solution.py
@@ -79,18 +79,8 @@
 IN_PLACE = pl.BlockSpec(memory_space=pl.ANY)
 
 
-def project_kernel(n_dec, n_after, groups, heads, place, *refs):
-    refs = list(refs)
-    mine, sib, weight, gain, cosine, sine = refs[:6]
-    refs = refs[6:]
-    if n_dec:
-        dec, dec_cos, dec_sin = refs[:3]
-        refs = refs[3:]
-    refs = refs[n_after:]
-    query, entries, everything = refs[:3]
-    if n_dec:
-        dec_query, dec_entries = refs[3:5]
-    inner, rows_held, weight_held, row_sems, weight_sems, out_sem = refs[-6:]
+def project_kernel(groups, heads, place, mine, sib, weight, gain, cosine, sine, *refs):
+    query, entries, everything, inner, rows_held, weight_held, row_sems, weight_sems, out_sem = refs[-9:]
     piece = mine.shape[0]
     core = place[0]
     scale = gain[...]
@@ -111,72 +101,46 @@
         row_copies[i].wait()
         start = pl.multiple_of(at * piece, piece)
         inner[pl.ds(start, piece), :] = normed(rows_held[i].astype(jnp.float32), scale)
-    if n_dec:
-        inner[2 * piece :, :] = normed(dec[...].astype(jnp.float32), scale)
     here = pl.ds(pl.multiple_of(place[1] * 2 * piece, 2 * piece), 2 * piece)
+    cos, sin = cosine[here, :], sine[here, :]
     for j in range(heads):
         weight_copies[j].wait()
         mixed = jnp.dot(inner[...], weight_held[j], preferred_element_type=jnp.float32)
-
-        def put(rows, cos, sin, query_out, entry_out):
-            for g in range(groups):
-                part = rows[:, g * HD : (g + 1) * HD]
-                at = (j * groups + g) * HD
-                turned = turn(part, cos, sin).astype(jnp.bfloat16)
-                query_out[:, at : at + HD] = turned.astype(query_out.dtype)
-            key = turn(rows[:, groups * HD : (groups + 1) * HD], cos, sin).astype(jnp.bfloat16)
-            value = rows[:, (groups + 1) * HD :].astype(jnp.bfloat16)
-            size = entry_out.shape[1]
-            entry_out[0, :, j * HD : (j + 1) * HD] = key[:size]
-            entry_out[1, :, j * HD : (j + 1) * HD] = value[:size]
-
-        put(mixed[: 2 * piece], cosine[here, :], sine[here, :], query, entries)
-        if n_dec:
-            put(mixed[2 * piece :], dec_cos[...], dec_sin[...], dec_query, dec_entries)
+        for g in range(groups):
+            at = (j * groups + g) * HD
+            part = mixed[:, g * HD : (g + 1) * HD]
+            query[:, at : at + HD] = turn(part, cos, sin).astype(jnp.bfloat16)
+        at = slice(j * HD, (j + 1) * HD)
+        key = mixed[:, groups * HD : (groups + 1) * HD]
+        entries[0, :, at] = turn(key, cos, sin).astype(jnp.bfloat16)
+        entries[1, :, at] = mixed[:, (groups + 1) * HD :].astype(jnp.bfloat16)
     keep = pltpu.make_async_copy(entries, everything.at[:, here, :], out_sem)
     keep.start()
     keep.wait()
 
 
-def project(
-    place, mine, sib, gain, weight, tables, heads, everything, dec=None, dec_tables=None, slots=0, after=()
-):
+def project(place, mine, sib, gain, weight, tables, heads, everything, after=()):
     piece, width = mine.shape
     depth = weight.shape[1] // heads
     groups = depth // HD - 2
     block = 2 * piece
-    n_dec = 0 if dec is None else dec.shape[0]
     args = [mine, sib, weight, gain, *tables]
-    if n_dec:
-        args += [dec, *dec_tables]
-    n_operands = len(args)
-    after = list(after)
+    extra = list(after)
     aliases = {}
     if everything is not None:
-        after.append(everything)
-        aliases = {n_operands + len(after): 2}
-    wide = heads * groups * HD
-    out_shape = [
-        jax.ShapeDtypeStruct((block, wide), jnp.bfloat16),
-        jax.ShapeDtypeStruct((2, block, heads * HD), jnp.bfloat16),
-        jax.ShapeDtypeStruct((2, tables[0].shape[0], heads * HD), jnp.bfloat16),
-    ]
-    if n_dec:
-        out_shape += [
-            jax.ShapeDtypeStruct((n_dec, wide), jnp.float32),
-            jax.ShapeDtypeStruct((2, slots, heads * HD), jnp.bfloat16),
-        ]
-    rows = block + n_dec
+        extra.append(everything)
+        aliases = {len(args) + len(extra): 2}
     return pl.pallas_call(
-        functools.partial(project_kernel, n_dec, len(after), groups, heads),
-        out_shape=out_shape,
-        in_specs=[SMEM_WHOLE]
-        + [IN_PLACE] * 3
-        + [VMEM_WHOLE] * (len(args) - 3)
-        + [IN_PLACE] * len(after),
-        out_specs=[VMEM_WHOLE] * 2 + [IN_PLACE] + [VMEM_WHOLE] * (len(out_shape) - 3),
+        functools.partial(project_kernel, groups, heads),
+        out_shape=[
+            jax.ShapeDtypeStruct((block, heads * groups * HD), jnp.bfloat16),
+            jax.ShapeDtypeStruct((2, block, heads * HD), jnp.bfloat16),
+            jax.ShapeDtypeStruct((2, tables[0].shape[0], heads * HD), jnp.bfloat16),
+        ],
+        in_specs=[SMEM_WHOLE] + [IN_PLACE] * 3 + [VMEM_WHOLE] * 3 + [IN_PLACE] * len(extra),
+        out_specs=[VMEM_WHOLE, VMEM_WHOLE, IN_PLACE],
         scratch_shapes=[
-            pltpu.VMEM((rows, width), jnp.bfloat16),
+            pltpu.VMEM((block, width), jnp.bfloat16),
             pltpu.VMEM((2, piece, width), jnp.bfloat16),
             pltpu.VMEM((heads, width, depth), jnp.bfloat16),
             pltpu.SemaphoreType.DMA((2,)),
@@ -185,14 +149,14 @@
         ],
         input_output_aliases=aliases,
         compiler_params=params(20),
-        cost_estimate=cost(2 * rows * weight.size, 2 * (weight.size + 2 * rows * width)),
+        cost_estimate=cost(2 * block * weight.size, 2 * (weight.size + 2 * block * width)),
         name="project",
-    )(place, *args, *after)
+    )(place, *args, *extra)
 
 
 def fill_kernel(groups, chips, place, query, cache_key, cache_value, *refs):
     new_keys, new_values, out = refs[:chips], refs[chips : 2 * chips], refs[-1]
-    scaling = 1.0 / math.sqrt(HD)
+    scaling = math.log2(math.e) / math.sqrt(HD)
     count = query.shape[0]
     stored = cache_key.shape[2]
     old_seen = lax.broadcasted_iota(jnp.int32, (1, stored), 1) < place[2]
@@ -200,25 +164,25 @@
         jnp.int32, (count, count), 0
     )
     across = (((1,), (1,)), ((), ()))
-    rows = jnp.concatenate([query[:, g * HD : (g + 1) * HD] for g in range(groups)], axis=0)
-    ahead = jnp.concatenate([ahead] * groups, axis=0)
-    scores = lax.dot_general(rows, cache_key[0, 0], across, preferred_element_type=jnp.float32)
-    scores = [jnp.where(old_seen, scores * scaling, NEGATIVE)]
-    for k in range(chips):
-        fresh = lax.dot_general(rows, new_keys[k][0], across, preferred_element_type=jnp.float32)
-        gap = (place[1] - place[3 + k]) * count
-        scores.append(jnp.where(ahead <= gap, fresh * scaling, NEGATIVE))
-    top = jnp.max(scores[0], axis=-1, keepdims=True)
-    for part in scores[1:]:
-        top = jnp.maximum(top, jnp.max(part, axis=-1, keepdims=True))
-    mix, total = 0.0, 0.0
-    for part, values in zip(scores, [cache_value[0, 0], *[v[0] for v in new_values]]):
-        weights = jnp.exp(part - top)
-        total += jnp.sum(weights, axis=-1, keepdims=True)
-        mix += jnp.dot(weights.astype(jnp.bfloat16), values, preferred_element_type=jnp.float32)
-    mix = (mix / total).astype(jnp.bfloat16)
     for g in range(groups):
-        out[:, g * HD : (g + 1) * HD] = mix[g * count : (g + 1) * count]
+        rows = query[:, g * HD : (g + 1) * HD]
+        scores = lax.dot_general(rows, cache_key[0, 0], across, preferred_element_type=jnp.float32)
+        scores = [jnp.where(old_seen, scores * scaling, NEGATIVE)]
+        for k in range(chips):
+            fresh = lax.dot_general(
+                rows, new_keys[k][0], across, preferred_element_type=jnp.float32
+            )
+            gap = (place[1] - place[3 + k]) * count
+            scores.append(jnp.where(ahead <= gap, fresh * scaling, NEGATIVE))
+        top = jnp.max(scores[0], axis=-1, keepdims=True)
+        for part in scores[1:]:
+            top = jnp.maximum(top, jnp.max(part, axis=-1, keepdims=True))
+        mix, total = 0.0, 0.0
+        for part, values in zip(scores, [cache_value[0, 0], *[v[0] for v in new_values]]):
+            weights = jnp.exp2(part - top)
+            total += jnp.sum(weights, axis=-1, keepdims=True)
+            mix += jnp.dot(weights.astype(jnp.bfloat16), values, preferred_element_type=jnp.float32)
+        out[:, g * HD : (g + 1) * HD] = (mix / total).astype(jnp.bfloat16)
 
 
 def fill_attend(place, query, cache, entries, heads, after=()):
@@ -243,38 +207,63 @@
             + [IN_PLACE] * len(after),
             out_specs=pl.BlockSpec((count, groups * HD), lambda j, s: (0, j)),
         ),
-        compiler_params=params(24),
+        compiler_params=params(16),
         cost_estimate=cost(8 * pairs * HD, 2 * cache.size, pairs),
         name="fill_attend",
     )(place, query, cache, cache, *entries, *entries, *after)
 
 
-def step_kernel(
-    heads, lengths, query, entries, cache, weight, out, held, scores, shares, weight_held, arrived, weight_sem
-):
+def step_kernel(heads, pieces, lengths, gain, cosine, sine, *refs):
+    dealt_parts, refs = refs[:pieces], refs[pieces:]
+    qkv, cache, weight, out, dealt, entries = refs[:6]
+    held, scores, shares, qkv_held, weight_held, arrived, qkv_sems, weight_sem = refs[6:]
     scaling = 1.0 / math.sqrt(HD)
     slots, stored, width = cache.shape[1:]
-    groups = query.shape[1] // width
+    depth = qkv.shape[1] // heads
+    groups = depth // HD - 2
     lanes = 8
+    qkv_copies = [
+        pltpu.make_async_copy(qkv.at[:, pl.ds(j * depth, depth)], qkv_held.at[j], qkv_sems.at[j])
+        for j in range(heads)
+    ]
     copies = [
         [pltpu.make_async_copy(cache.at[w, s], held.at[w, s], arrived.at[w, s]) for s in range(slots)]
         for w in range(2)
     ]
     weight_copy = pltpu.make_async_copy(weight, weight_held, weight_sem)
-    for copy in copies[0] + copies[1] + [weight_copy]:
+    for copy in qkv_copies + copies[0] + copies[1] + [weight_copy]:
         copy.start()
+    rows = dealt_parts[0][...].astype(jnp.float32)
+    for part in dealt_parts[1:]:
+        rows += part[...].astype(jnp.float32)
+    dealt[...] = rows.astype(jnp.bfloat16)
+    inner = normed(rows, gain[...])
+    cos, sin = cosine[...], sine[...]
+    queries, new_keys, new_values = [], [], []
+    for j in range(heads):
+        qkv_copies[j].wait()
+        mixed = jnp.dot(inner, qkv_held[j], preferred_element_type=jnp.float32)
+        for g in range(groups):
+            part = turn(mixed[:, g * HD : (g + 1) * HD], cos, sin)
+            queries.append(part.astype(jnp.bfloat16).astype(jnp.float32))
+        at = slice(j * HD, (j + 1) * HD)
+        key = turn(mixed[:, groups * HD : (groups + 1) * HD], cos, sin).astype(jnp.bfloat16)
+        value = mixed[:, (groups + 1) * HD :].astype(jnp.bfloat16)
+        entries[0, :, at] = key[:slots]
+        entries[1, :, at] = value[:slots]
+        new_keys.append(key.astype(jnp.float32))
+        new_values.append(value.astype(jnp.float32))
+    new_keys = jnp.concatenate(new_keys, axis=1)
+    new_values = jnp.concatenate(new_values, axis=1)
     across = (((1,), (1,)), ((), ()))
     places = lax.broadcasted_iota(jnp.int32, (1, stored), 1)
     blank = jnp.zeros((1, HD), jnp.float32)
-    new_keys = entries[0].astype(jnp.float32)
-    new_values = entries[1].astype(jnp.float32)
     own_scores = []
     for s in range(slots):
         rows = []
         for j in range(heads):
             for g in range(groups):
-                at = (j * groups + g) * HD
-                part = query[s : s + 1, at : at + HD]
+                part = queries[j * groups + g][s : s + 1]
                 rows.append(
                     jnp.concatenate([part if i == j else blank for i in range(heads)], axis=1)
                 )
@@ -311,34 +300,41 @@
                 parts.append(mix[row : row + 1, j * HD : (j + 1) * HD])
         attended.append(jnp.concatenate(parts, axis=1))
     if out.shape[0] > slots:
-        attended.append(jnp.zeros((out.shape[0] - slots, query.shape[1]), jnp.float32))
+        attended.append(jnp.zeros((out.shape[0] - slots, groups * width), jnp.float32))
     attended = jnp.concatenate(attended, axis=0).astype(jnp.bfloat16)
     weight_copy.wait()
     part = jnp.dot(attended, weight_held[...], preferred_element_type=jnp.float32)
     out[...] = part.astype(jnp.bfloat16)
 
 
-def step_attend(lengths, query, entries, cache, weight, heads):
-    slots, stored = cache.shape[1:3]
-    padded = query.shape[0]
+def step_attend(lengths, dealt_parts, gain, tables, qkv, cache, weight, heads):
+    slots, stored, width = cache.shape[1:]
+    padded, model = dealt_parts[0].shape
     rows = slots * 8
+    pieces = len(dealt_parts)
     return pl.pallas_call(
-        functools.partial(step_kernel, heads),
-        out_shape=jax.ShapeDtypeStruct((padded, weight.shape[1]), jnp.bfloat16),
-        in_specs=[SMEM_WHOLE, VMEM_WHOLE, VMEM_WHOLE, IN_PLACE, IN_PLACE],
-        out_specs=VMEM_WHOLE,
+        functools.partial(step_kernel, heads, pieces),
+        out_shape=[
+            jax.ShapeDtypeStruct((padded, model), jnp.bfloat16),
+            jax.ShapeDtypeStruct((padded, model), jnp.bfloat16),
+            jax.ShapeDtypeStruct((2, slots, width), jnp.bfloat16),
+        ],
+        in_specs=[SMEM_WHOLE] + [VMEM_WHOLE] * (3 + pieces) + [IN_PLACE] * 3,
+        out_specs=[VMEM_WHOLE] * 3,
         scratch_shapes=[
             pltpu.VMEM(cache.shape, jnp.bfloat16),
             pltpu.VMEM((rows, stored), jnp.float32),
             pltpu.VMEM((rows, stored), jnp.float32),
+            pltpu.VMEM((heads, model, qkv.shape[1] // heads), jnp.bfloat16),
             pltpu.VMEM(weight.shape, jnp.bfloat16),
             pltpu.SemaphoreType.DMA((2, slots)),
+            pltpu.SemaphoreType.DMA((heads,)),
             pltpu.SemaphoreType.DMA(()),
         ],
-        compiler_params=params(20),
-        cost_estimate=cost(16 * cache.size, 2 * cache.size, rows * stored),
+        compiler_params=params(24),
+        cost_estimate=cost(16 * cache.size, 3 * cache.size, rows * stored),
         name="step_attend",
-    )(lengths, query, entries, cache, weight)
+    )(lengths, gain, *tables, *dealt_parts, qkv, cache, weight)
 
 
 def out_kernel(place, mine, sib, weight, sib_weight, *refs):
@@ -464,15 +460,15 @@
 def lower(hidden, weight, after):
     rows, units = hidden.shape
     width = weight.shape[1]
-    chunk = width // 4
+    chunk = 256
     return pl.pallas_call(
         functools.partial(lower_kernel, chunk),
         out_shape=[jax.ShapeDtypeStruct((rows // 2, width), jnp.bfloat16)] * 2,
         in_specs=[VMEM_WHOLE] + [IN_PLACE] * (1 + len(after)),
         out_specs=[VMEM_WHOLE] * 2,
         scratch_shapes=[
-            pltpu.VMEM((4, units, chunk), jnp.bfloat16),
-            pltpu.SemaphoreType.DMA((4,)),
+            pltpu.VMEM((width // chunk, units, chunk), jnp.bfloat16),
+            pltpu.SemaphoreType.DMA((width // chunk,)),
         ],
         compiler_params=params(24),
         cost_estimate=cost(2 * rows * width * units, 2 * width * units),
@@ -486,8 +482,7 @@
     piece, width = mine.shape
     chips = len(shares) // 2
     units = gate.shape[1]
-    chunks = 4
-    chunk = width // chunks
+    chunk = 256
     n_dec = 0 if dec is None else dec.shape[0]
     rows = 2 * piece + n_dec
     args = [mine, sib, *shares]
@@ -512,8 +507,8 @@
         ]
         + [pltpu.VMEM((rows, units), jnp.bfloat16)] * (not split)
         + [pltpu.VMEM((units // chunk, width, chunk), jnp.bfloat16)] * 2
-        + [pltpu.VMEM((chunks, units, chunk), jnp.bfloat16)] * (not split)
-        + [pltpu.SemaphoreType.DMA((n_weights, chunks))],
+        + [pltpu.VMEM((width // chunk, units, chunk), jnp.bfloat16)] * (not split)
+        + [pltpu.SemaphoreType.DMA((n_weights, max(units, width) // chunk))],
         compiler_params=params(40),
         cost_estimate=cost(6 * rows * width * units, 6 * width * units, rows * units),
         name="feed_forward",
@@ -576,11 +571,11 @@
     prefill_cache, decode_cache = in_hbm(prefill_cache), in_hbm(decode_cache)
 
     mines = [prefill_rows] + [from_chip(prefill_rows, k) for k in range(1, chips)]
-    sibs = [swap_cores(rows) for rows in mines]
+    sibs = [swap_cores(prefill_rows)]
 
     low = max(dp_count // 4, 1)
     pool = [decode_rows] + [swap_groups(decode_rows, i) for i in range(1, low)]
-    pool = jnp.concatenate(pool, axis=0)
+    pool = near = jnp.concatenate(pool, axis=0)
     pool = [pool] + [swap_groups(pool, i * low) for i in range(1, dp_count // low)]
     pool = jnp.concatenate(pool, axis=0)
     index = jnp.arange(dp_count * per_device, dtype=jnp.int32)
@@ -605,15 +600,9 @@
     gain = attention_gain.reshape(1, width)
     tables = angle_tables(prefill_offset[0] + jnp.arange(tokens, dtype=jnp.int32))
     dec_tables = angle_tables(jnp.pad(cache_length, (0, padded - slots)))
-    queries, entries, everything = [None] * chips, [None] * chips, None
+    queries, entries, everything = [], [], None
     for k in range(chips):
-        last = k == chips - 1
-        if last:
-            others = from_rest(dealt)
-            if k:
-                *others, queries[k - 1] = lax.optimization_barrier((*others, queries[k - 1]))
-            dealt = add(dealt, *others)
-        got = project(
+        query, entry, everything = project(
             places[k],
             in_hbm(mines[k]),
             in_hbm(sibs[k]),
@@ -622,14 +611,14 @@
             tables,
             heads,
             everything,
-            dealt if last else None,
-            dec_tables if last else None,
-            slots,
-            [queries[k - 1]] if k else [dealt],
+            [query] if k else [near],
         )
-        queries[k], entries[k], everything = got[:3]
-        if last:
-            dec_query, dec_entries = got[3:]
+        if k == 0:
+            *mines[1:], query = lax.optimization_barrier((*mines[1:], query))
+            sibs += [swap_cores(rows) for rows in mines[1:]]
+        queries.append(query)
+        entries.append(entry)
+    dealt_parts = [dealt, *from_rest(dealt)]
 
     out_share = out_weight
     sib_weight, queries[-1] = lax.optimization_barrier((out_weight, queries[-1]))
@@ -644,15 +633,24 @@
     parts = []
     dec_shares = []
     for k in range(chips):
-        attended = fill_attend(
-            places[k], queries[k], prefill_cache, entries, heads, dec_shares[:1]
-        )
-        part, dec_shares[1:] = finish(attended, places[k], dec_shares[1:])
+        after = dec_shares[:1] if k else dealt_parts[:1]
+        attended = fill_attend(places[k], queries[k], prefill_cache, entries, heads, after)
+        if k == 0:
+            part, dealt_parts[1:] = finish(attended, places[k], dealt_parts[1:])
+        else:
+            part, dec_shares[1:] = finish(attended, places[k], dec_shares[1:])
         parts.append(part)
         if k == 0:
             lengths, parts[0] = lax.optimization_barrier((cache_length, parts[0]))
-            dec_part = step_attend(
-                lengths, dec_query, dec_entries, decode_cache, in_hbm(out_share), heads
+            dec_part, dealt, dec_entries = step_attend(
+                lengths,
+                dealt_parts,
+                gain,
+                dec_tables,
+                weight,
+                decode_cache,
+                in_hbm(out_share),
+                heads,
             )
             dec_shares = [dec_part, *from_rest(dec_part)]
 

time: 106 us -> 132 us (1.25)
  Pallas kernels: 57.3 us -> 75.8 us
  waiting for transfers between devices: 9.8 us -> 13.8 us
  local copies, waits for them, and re-layouts: 6.48 us -> 9.94 us
  other arithmetic: 5.57 us -> 3.51 us
  starting transfers between devices: 24.2 us -> 26.2 us
    pallas_call x2, Pallas kernels: 21 us -> 34 us  [feed_forward(): pl.pallas_call(functools.partial(forward_kernel, split, chips, n_dec, len...]
    ppermute x8, waiting for transfers between devices: 3.16 us -> 8.46 us  [swap_groups(): return lax.ppermute(value, 'dp', [(i, i ^ mask) for i in range(count)])]
    pallas_call x3, Pallas kernels: 17.1 us -> 20.8 us  [the longest x1 10.8 us: step_attend(): pl.pallas_call(functools.partial(step_kernel, heads, pieces), out_shape=[...]
    unnamed x25 -> x35, local copies, waits for them, and re-layouts: 6.19 us -> 9.66 us
    pallas_call x2, Pallas kernels: 12.2 us -> 9.46 us  [fill_attend(): pl.pallas_call(functools.partial(fill_kernel, groups, chips), out_shape=j...]
    pallas_call x1, Pallas kernels: 4.46 us -> 6.84 us  [lower(): pl.pallas_call(functools.partial(lower_kernel, chunk), out_shape=[jax.Sha...]
    pallas_call x2, Pallas kernels: 2.5 us -> 4.65 us  [out_project(): pl.pallas_call(out_kernel, out_shape=jax.ShapeDtypeStruct((rows, half), j...]
    ppermute x7, starting transfers between devices: 7.81 us -> 9.35 us  [from_chip(): lax.ppermute(value, 'tensor', [(i, (i // 2 - step) % chips * 2 + i % 2) f...]
  transfers between devices with their start and end apart: 32 -> 32, of which waited for: 7 -> 7; matrix products, arithmetic and copies ran while one was open for 10% -> 6% of each run, Pallas kernels for 48% -> 52%
where the time goes in v6:
time: 132 us; the launch traced here: 131 us
  Pallas kernels  75.8 us (57%)
  starting transfers between devices  26.2 us (20%)
  waiting for transfers between devices  13.8 us (10%)
  local copies, waits for them, and re-layouts  9.94 us (8%)
  other arithmetic  3.51 us (3%)
  between operations  1.77 us (1%)
    pallas_call x2, Pallas kernels, feed_forward(): pl.pallas_call(functools.partial(forward_kernel, split, chips, n_dec, len...  34 us
    ppermute x8, starting transfers between devices, swap_groups(): return lax.ppermute(value, 'dp', [(i, i ^ mask) for i in range(count)])  11 us
    pallas_call x1, Pallas kernels, step_attend(): pl.pallas_call(functools.partial(step_kernel, heads, pieces), out_shape=[...  10.8 us
    pallas_call x2, Pallas kernels, project(): pl.pallas_call(functools.partial(project_kernel, groups, heads), out_shap...  9.95 us
    unnamed x35, local copies, waits for them, and re-layouts  9.66 us
    pallas_call x2, Pallas kernels, fill_attend(): pl.pallas_call(functools.partial(fill_kernel, groups, chips), out_shape=j...  9.46 us
    ppermute x7, starting transfers between devices, from_chip(): lax.ppermute(value, 'tensor', [(i, (i // 2 - step) % chips * 2 + i % 2) f...  9.35 us
    ppermute x8, waiting for transfers between devices, swap_groups(): return lax.ppermute(value, 'dp', [(i, i ^ mask) for i in range(count)])  8.46 us
  transfers between devices with their start and end apart: 32, of which 7 were waited for; matrix products, arithmetic and copies ran while one was open for 6% of the time, Pallas kernels for 52%

profile of v6, /device:TPU:0, one launch (start us, length us, event | category | flops | bytes accessed | tf_op | source)
XLA Modules:
  0.0 131.3 jit_solution(18371205859677346053)
XLA Ops:
  0.7 3.0 %collective-permute-start.1 = (bf16[128,2048]{1,0:T(8,128)(2,1)}, bf16[128,2048]{1,0:T(8,128)(2,1)S(1)}, u32[]{:S(2)}, u32[]{:S(2)}) collective-permute-start(bf16[128,2048]{1,0:T(8,128)(2,1)} %refs_0_.1), channel_id=1, source_target_pairs={{0,2},{1,3},{2,0},{3,1},{4,6},{5,7},{6,4},{7,5},{8,10},{9,11},{10,... | collective-permute-start | bytes 1572872 | tf_op jit(solution)/shard_map/ppermute | solution.py:26
  3.7 1.5 %collective-permute-start.2 = (bf16[2,2048]{1,0:T(2,128)(2,1)}, bf16[2,2048]{1,0:T(2,128)(2,1)S(1)}, u32[]{:S(2)}, u32[]{:S(2)}) collective-permute-start(bf16[2,2048]{1,0:T(2,128)(2,1)} %param.15), channel_id=1, source_target_pairs={{0,4},{4,0},{8,12},{12,8},{16,20},{20,16},{24,28},{28,24},{1,5},{5... | collective-permute-start | bytes 24584 | tf_op jit(solution)/shard_map/ppermute | solution.py:45
  5.9 1.0 fusion
  7.1 5.5 %copy.19 = bf16[256,8,2,512]{3,1,2,0:T(8,128)(2,1)} copy(bf16[256,8,2,512]{3,2,1,0:T(2,128)(2,1)} %bitcast.18) | data formatting | bytes 8388608
  12.8 5.0 %project.2 = (bf16[256,512]{1,0:T(8,128)(2,1)S(1)}, bf16[2,256,256]{2,1,0:T(8,128)(2,1)S(1)}, bf16[2,512,256]{2,1,0:T(8,128)(2,1)}) custom-call(s32[5]{0:T(128)S(1)} %stack.23.place, bf16[128,2048]{1,0:T(8,128)(2,1)} %refs_0_.1, bf16[128,2048]{1,0:T(8,128)(2,1)} %collective-permute-done.sib.refs_1_, bf16[2048,1024]{1,0:T(8,128)(2,1)} %bitcast.15, ...), custom_call_target="tpu_custom_call" | custom-call | flops 1073741824 | bytes 6291456 | tf_op jit(solution)/shard_map/project/pallas_call | solution.py:133
  18.8 1.7 %collective-permute-done.3.sib.refs_1_ = bf16[128,2048]{1,0:T(8,128)(2,1)} collective-permute-done((bf16[128,2048]{1,0:T(8,128)(2,1)S(1)}, bf16[128,2048]{1,0:T(8,128)(2,1)}, u32[]{:S(2)}, u32[]{:S(2)}) %collective-permute-start.3) | collective-permute-done | bytes 524320 | tf_op jit(solution)/shard_map/ppermute | solution.py:20
  20.6 5.0 %project.3 = (bf16[256,512]{1,0:T(8,128)(2,1)S(1)}, bf16[2,256,256]{2,1,0:T(8,128)(2,1)S(1)}, bf16[2,512,256]{2,1,0:T(8,128)(2,1)}) custom-call(s32[5]{0:T(128)S(1)} %stack.24.place, bf16[128,2048]{1,0:T(8,128)(2,1)} %copy-done.2, bf16[128,2048]{1,0:T(8,128)(2,1)} %collective-permute-done.3.sib.refs_1_, ...), custom_call_target="tpu_custom_call", output_to_operand_aliasing={{2}: (8, {})} | custom-call | flops 1073741824 | bytes 6291456 | tf_op jit(solution)/shard_map/project/pallas_call | solution.py:133
  27.4 1.6 %collective-permute-start.4 = (bf16[4,2048]{1,0:T(4,128)(2,1)S(1)}, bf16[4,2048]{1,0:T(4,128)(2,1)S(1)}, u32[]{:S(2)}, u32[]{:S(2)}) collective-permute-start(bf16[4,2048]{1,0:T(4,128)(2,1)S(1)} %pad_maximum_fusion.2.refs_0_), channel_id=1, source_target_pairs={{0,8},{4,12},{8,0},{12,4},{16,24},{20,28},{24,16},{28,20},{1,9},{5... | collective-permute-start | bytes 49160 | tf_op jit(solution)/shard_map/ppermute | solution.py:45
  29.1 2.6 %collective-permute-start.5 = (bf16[4,2048]{1,0:T(4,128)(2,1)S(1)}, bf16[4,2048]{1,0:T(4,128)(2,1)S(1)}, u32[]{:S(2)}, u32[]{:S(2)}) collective-permute-start(bf16[4,2048]{1,0:T(4,128)(2,1)S(1)} %pad_maximum_fusion.2.refs_0_), channel_id=1, source_target_pairs={{0,16},{4,20},{8,24},{12,28},{16,0},{20,4},{24,8},{28,12},{1,17},{... | collective-permute-start | bytes 49160 | tf_op jit(solution)/shard_map/ppermute | solution.py:45
  31.9 1.9 %collective-permute-done.5 = bf16[4,2048]{1,0:T(4,128)(2,1)S(1)} collective-permute-done((bf16[4,2048]{1,0:T(4,128)(2,1)S(1)}, bf16[4,2048]{1,0:T(4,128)(2,1)S(1)}, u32[]{:S(2)}, u32[]{:S(2)}) %collective-permute-start.5) | collective-permute-done | bytes 16416 | tf_op jit(solution)/shard_map/ppermute | solution.py:45
  33.8 3.4 %collective-permute-done.6 = bf16[4,2048]{1,0:T(4,128)(2,1)S(1)} collective-permute-done((bf16[4,2048]{1,0:T(4,128)(2,1)S(1)}, bf16[4,2048]{1,0:T(4,128)(2,1)S(1)}, u32[]{:S(2)}, u32[]{:S(2)}) %collective-permute-start.6) | collective-permute-done | bytes 16416 | tf_op jit(solution)/shard_map/ppermute | solution.py:45
  38.0 1.6 %collective-permute-start.9 = (bf16[16,2048]{1,0:T(8,128)(2,1)S(1)}, bf16[16,2048]{1,0:T(8,128)(2,1)S(1)}, u32[]{:S(2)}, u32[]{:S(2)}) collective-permute-start(bf16[16,2048]{1,0:T(8,128)(2,1)S(1)} %convolution_convert_fusion.1.refs_4_.refs_0_), channel_id=1, source_target_pairs={{0,3},{1,2},{2,1},{3,0},{4,7},{5,6},{6,5},{7,4},{8,11},{9,10},{10,... | collective-permute-start | bytes 196616 | tf_op jit(solution)/shard_map/ppermute | solution.py:33
  39.6 0.9 copy-done.9
  40.6 0.9 copy-done.14
  41.5 4.7 %fill_attend.2.mine = bf16[256,512]{1,0:T(8,128)(2,1)S(1)} custom-call(s32[5]{0:T(128)S(1)} %stack.23.place, bf16[256,512]{1,0:T(8,128)(2,1)S(1)} %get-tuple-element.43.refs_0_.query, bf16[2,1,1024,256]{3,2,1,0:T(8,128)(2,1)} %cache_value.3, bf16[2,1,1024,256]{3,2,1,0:T(8,128)(2,1)} %cache_value.3, bf16[2,256,256]{2,1,0:T(8,128)(2,1)S(1)} %copy-done.9, ...), custom_call_target="tpu_custom_call" | custom-call | flops 1610612736 | bytes 1048576 | tf_op jit(solution)/shard_map/fill_attend/pallas_call | solution.py:194
  46.5 1.4 %collective-permute-done.10.sib = bf16[256,512]{1,0:T(8,128)(2,1)S(1)} collective-permute-done((bf16[256,512]{1,0:T(8,128)(2,1)S(1)}, bf16[256,512]{1,0:T(8,128)(2,1)S(1)}, u32[]{:S(2)}, u32[]{:S(2)}) %collective-permute-start.10) | collective-permute-done | bytes 262176 | tf_op jit(solution)/shard_map/ppermute | solution.py:20
  47.9 2.3 %out_project.2.refs_2_ = bf16[256,1024]{1,0:T(8,128)(2,1)S(1)} custom-call(s32[5]{0:T(128)S(1)} %stack.23.place, bf16[256,512]{1,0:T(8,128)(2,1)S(1)} %fill_attend.2.mine, bf16[256,512]{1,0:T(8,128)(2,1)S(1)} %collective-permute-done.10.sib, bf16[512,2048]{1,0:T(8,128)(2,1)S(1)} %copy-done, bf16[512,2048]{1,0:T(8,128)(2,1)} %collective-permute-done.11.sib_weight), custom_call_target="tpu_custom_call" | custom-call | flops 536870912 | bytes 3670016 | tf_op jit(solution)/shard_map/out_project/pallas_call | solution.py:352
  50.9 10.8 %step_attend.1 = (bf16[16,2048]{1,0:T(8,128)(2,1)S(1)}, bf16[16,2048]{1,0:T(8,128)(2,1)S(1)}, bf16[2,8,256]{2,1,0:T(8,128)(2,1)}) custom-call(s32[8]{0:T(128)S(1)} %copy-done.7, f32[1,2048]{1,0:T(1,128)S(1)} %bitcast.12, f32[16,128]{1,0:T(8,128)S(1)} %get-tuple-element.93.cosine, f32[16,128]{1,0:T(8,128)S(1)} %get-tuple-element.94.sine, ...), custom_call_target="tpu_custom_call" | custom-call | flops 67108864 | bytes 12582912 | tf_op jit(solution)/shard_map/step_attend/pallas_call | solution.py:315
  61.8 1.6 %collective-permute-start.13 = (bf16[16,2048]{1,0:T(8,128)(2,1)S(1)}, bf16[16,2048]{1,0:T(8,128)(2,1)S(1)}, u32[]{:S(2)}, u32[]{:S(2)}) collective-permute-start(bf16[16,2048]{1,0:T(8,128)(2,1)S(1)} %get-tuple-element.57.refs_4_.refs_7_), channel_id=1, source_target_pairs={{0,2},{1,3},{2,0},{3,1},{4,6},{5,7},{6,4},{7,5},{8,10},{9,11},{10,... | collective-permute-start | bytes 196616 | tf_op jit(solution)/shard_map/ppermute | solution.py:26
  64.0 4.8 %fill_attend.3.mine = bf16[256,512]{1,0:T(8,128)(2,1)S(1)} custom-call(s32[5]{0:T(128)S(1)} %stack.24.place, bf16[256,512]{1,0:T(8,128)(2,1)S(1)} %copy-done.12, bf16[2,1,1024,256]{3,2,1,0:T(8,128)(2,1)} %cache_value.3, bf16[2,1,1024,256]{3,2,1,0:T(8,128)(2,1)} %cache_value.3, bf16[2,256,256]{2,1,0:T(8,128)(2,1)S(1)} %copy-done.10, ...), custom_call_target="tpu_custom_call" | custom-call | flops 1610612736 | bytes 1048576 | tf_op jit(solution)/shard_map/fill_attend/pallas_call | solution.py:194
  68.9 1.5 %collective-permute-done.16.sib = bf16[256,512]{1,0:T(8,128)(2,1)S(1)} collective-permute-done((bf16[256,512]{1,0:T(8,128)(2,1)S(1)}, bf16[256,512]{1,0:T(8,128)(2,1)S(1)}, u32[]{:S(2)}, u32[]{:S(2)}) %collective-permute-start.16) | collective-permute-done | bytes 262176 | tf_op jit(solution)/shard_map/ppermute | solution.py:20
  70.4 2.3 %out_project.3.refs_2_ = bf16[256,1024]{1,0:T(8,128)(2,1)S(1)} custom-call(s32[5]{0:T(128)S(1)} %stack.24.place, bf16[256,512]{1,0:T(8,128)(2,1)S(1)} %fill_attend.3.mine, bf16[256,512]{1,0:T(8,128)(2,1)S(1)} %collective-permute-done.16.sib, bf16[512,2048]{1,0:T(8,128)(2,1)S(1)} %copy-done.1, bf16[512,2048]{1,0:T(8,128)(2,1)} %collective-permute-done.11.sib_weight), custom_call_target="tpu_custom_call" | custom-call | flops 536870912 | bytes 3670016 | tf_op jit(solution)/shard_map/out_project/pallas_call | solution.py:352
  73.3 1.5 %collective-permute-start.17 = (bf16[256,1024]{1,0:T(8,128)(2,1)S(1)}, bf16[256,1024]{1,0:T(8,128)(2,1)S(1)}, u32[]{:S(2)}, u32[]{:S(2)}) collective-permute-start(bf16[256,1024]{1,0:T(8,128)(2,1)S(1)} %out_project.3.refs_2_), channel_id=1, source_target_pairs={{0,2},{1,3},{2,0},{3,1},{4,6},{5,7},{6,4},{7,5},{8,10},{9,11},{10,... | collective-permute-start | bytes 1572872 | tf_op jit(solution)/shard_map/ppermute | solution.py:26
  75.5 20.3 %feed_forward.2 = (bf16[128,2048]{1,0:T(8,128)(2,1)S(1)}, bf16[128,2048]{1,0:T(8,128)(2,1)S(1)}, bf16[128,2048]{1,0:T(8,128)(2,1)}, bf16[16,2048]{1,0:T(8,128)(2,1)S(1)}, bf16[16,2048]{1,0:T(8,128)(2,1)S(1)}) custom-call(s32[5]{0:T(128)S(1)} %stack.24.place, bf16[128,2048]{1,0:T(8,128)(2,1)S(1)} %copy-done.3, ...), custom_call_target="tpu_custom_call" | custom-call | flops 6845104128 | bytes 25165824 | tf_op jit(solution)/shard_map/feed_forward/pallas_call | solution.py:499
  96.5 1.5 %collective-permute-start.24 = (bf16[16,2048]{1,0:T(8,128)(2,1)S(1)}, bf16[16,2048]{1,0:T(8,128)(2,1)S(1)}, u32[]{:S(2)}, u32[]{:S(2)}) collective-permute-start(bf16[16,2048]{1,0:T(8,128)(2,1)S(1)} %get-tuple-element.70), channel_id=1, source_target_pairs={{0,3},{1,2},{2,1},{3,0},{4,7},{5,6},{6,5},{7,4},{8,11},{9,10},{10,... | collective-permute-start | bytes 196616 | tf_op jit(solution)/shard_map/ppermute | solution.py:33
  98.2 1.1 collective-permute-start.22
  99.4 1.0 collective-permute-start.26
  100.4 13.7 %feed_forward.3 = (bf16[128,2048]{1,0:T(8,128)(2,1)S(1)}, bf16[256,2048]{1,0:T(8,128)(2,1)S(1)}) custom-call(s32[5]{0:T(128)S(1)} %stack.23.place, bf16[128,2048]{1,0:T(8,128)(2,1)S(1)} %copy-done.4, bf16[128,2048]{1,0:T(8,128)(2,1)} %collective-permute-done.sib.refs_1_, bf16[256,1024]{1,0:T(8,128)(2,1)S(1)} %out_project.2.refs_2_, ...), custom_call_target="tpu_custom_call" | custom-call | flops 6442450944 | bytes 25165824 | tf_op jit(solution)/shard_map/feed_forward/pallas_call | solution.py:499
  114.7 4.2 %collective-permute-start.27 = (bf16[4,2048]{1,0:T(4,128)(2,1)S(1)}, bf16[4,2048]{1,0:T(4,128)(2,1)S(1)}, u32[]{:S(2)}, u32[]{:S(2)}) collective-permute-start(bf16[4,2048]{1,0:T(4,128)(2,1)S(1)} %get-tuple-element.82), channel_id=1, source_target_pairs={{0,8},{4,12},{8,0},{12,4},{16,24},{20,28},{24,16},{28,20},{1,9},{5... | collective-permute-start | bytes 49160 | tf_op jit(solution)/shard_map/ppermute | solution.py:45
  118.8 6.8 %lower.1 = (bf16[128,2048]{1,0:T(8,128)(2,1)S(1)}, bf16[128,2048]{1,0:T(8,128)(2,1)S(1)}) custom-call(bf16[256,2048]{1,0:T(8,128)(2,1)S(1)} %get-tuple-element.68.hidden, bf16[2048,2048]{1,0:T(8,128)(2,1)} %weight.5, bf16[16,2048]{1,0:T(8,128)(2,1)S(1)} %convolution_convert_fusion.refs_0_), custom_call_target="tpu_custom_call" | custom-call | flops 2147483648 | bytes 8388608 | tf_op jit(solution)/shard_map/lower/pallas_call | solution.py:464
  126.4 3.1 %collective-permute-done.31 = bf16[2,2048]{1,0:T(2,128)(2,1)S(1)} collective-permute-done((bf16[2,2048]{1,0:T(2,128)(2,1)S(1)}, bf16[2,2048]{1,0:T(2,128)(2,1)S(1)}, u32[]{:S(2)}, u32[]{:S(2)}) %collective-permute-start.31) | collective-permute-done | bytes 8224 | tf_op jit(solution)/shard_map/ppermute | solution.py:45
  130.2 1.1 add_convert_fusion
  (99 shorter events, 10.1 us)
Async XLA Ops:
  0.7 17.9 %collective-permute-start.1 = (bf16[128,2048]{1,0:T(8,128)(2,1)}, bf16[128,2048]{1,0:T(8,128)(2,1)S(1)}, u32[]{:S(2)}, u32[]{:S(2)}) collective-permute-start(bf16[128,2048]{1,0:T(8,128)(2,1)} %refs_0_.1), channel_id=1, source_target_pairs={{0,2},{1,3},{2,0},{3,1},{4,6},{5,7},{6,4},{7,5},{8,10},{9,11},{10,... | collective-permute-start | bytes 1572872 | tf_op jit(solution)/shard_map/ppermute | solution.py:26
  3.7 9.1 %collective-permute-start = (bf16[128,2048]{1,0:T(8,128)(2,1)}, bf16[128,2048]{1,0:T(8,128)(2,1)}, u32[]{:S(2)}, u32[]{:S(2)}) collective-permute-start(bf16[128,2048]{1,0:T(8,128)(2,1)} %refs_0_.1), channel_id=1, source_target_pairs={{0,1},{1,0},{2,3},{3,2},{4,5},{5,4},{6,7},{7,6},{8,9},{9,8},{10,11... | collective-permute-start | bytes 1572872 | tf_op jit(solution)/shard_map/ppermute | solution.py:20
  3.7 9.1 %collective-permute-start.2 = (bf16[2,2048]{1,0:T(2,128)(2,1)}, bf16[2,2048]{1,0:T(2,128)(2,1)S(1)}, u32[]{:S(2)}, u32[]{:S(2)}) collective-permute-start(bf16[2,2048]{1,0:T(2,128)(2,1)} %param.15), channel_id=1, source_target_pairs={{0,4},{4,0},{8,12},{12,8},{16,20},{20,16},{24,28},{28,24},{1,5},{5... | collective-permute-start | bytes 24584 | tf_op jit(solution)/shard_map/ppermute | solution.py:45
  18.5 2.0 %collective-permute-start.3 = (bf16[128,2048]{1,0:T(8,128)(2,1)S(1)}, bf16[128,2048]{1,0:T(8,128)(2,1)}, u32[]{:S(2)}, u32[]{:S(2)}) collective-permute-start(bf16[128,2048]{1,0:T(8,128)(2,1)S(1)} %collective-permute-done.1.mine.refs_0_), channel_id=1, source_target_pairs={{0,1},{1,0},{2,3},{3,2},{4,5},{5,4},{6,7},{7,6},{8,9},{9,8},{10,11... | collective-permute-start | bytes 1572872 | tf_op jit(solution)/shard_map/ppermute | solution.py:20
  27.0 20.9 %collective-permute-start.11 = (bf16[512,2048]{1,0:T(8,128)(2,1)S(1)}, bf16[512,2048]{1,0:T(8,128)(2,1)}, u32[]{:S(2)}, u32[]{:S(2)}) collective-permute-start(bf16[512,2048]{1,0:T(8,128)(2,1)S(1)} %copy-done), channel_id=1, source_target_pairs={{0,1},{1,0},{2,3},{3,2},{4,5},{5,4},{6,7},{7,6},{8,9},{9,8},{10,11... | collective-permute-start | bytes 6291464 | tf_op jit(solution)/shard_map/ppermute | solution.py:20
  27.4 4.5 %collective-permute-start.4 = (bf16[4,2048]{1,0:T(4,128)(2,1)S(1)}, bf16[4,2048]{1,0:T(4,128)(2,1)S(1)}, u32[]{:S(2)}, u32[]{:S(2)}) collective-permute-start(bf16[4,2048]{1,0:T(4,128)(2,1)S(1)} %pad_maximum_fusion.2.refs_0_), channel_id=1, source_target_pairs={{0,8},{4,12},{8,0},{12,4},{16,24},{20,28},{24,16},{28,20},{1,9},{5... | collective-permute-start | bytes 49160 | tf_op jit(solution)/shard_map/ppermute | solution.py:45
  29.1 4.7 %collective-permute-start.5 = (bf16[4,2048]{1,0:T(4,128)(2,1)S(1)}, bf16[4,2048]{1,0:T(4,128)(2,1)S(1)}, u32[]{:S(2)}, u32[]{:S(2)}) collective-permute-start(bf16[4,2048]{1,0:T(4,128)(2,1)S(1)} %pad_maximum_fusion.2.refs_0_), channel_id=1, source_target_pairs={{0,16},{4,20},{8,24},{12,28},{16,0},{20,4},{24,8},{28,12},{1,17},{... | collective-permute-start | bytes 49160 | tf_op jit(solution)/shard_map/ppermute | solution.py:45
  31.7 5.5 %collective-permute-start.6 = (bf16[4,2048]{1,0:T(4,128)(2,1)S(1)}, bf16[4,2048]{1,0:T(4,128)(2,1)S(1)}, u32[]{:S(2)}, u32[]{:S(2)}) collective-permute-start(bf16[4,2048]{1,0:T(4,128)(2,1)S(1)} %pad_maximum_fusion.2.refs_0_), channel_id=1, source_target_pairs={{0,24},{4,28},{8,16},{12,20},{16,8},{20,12},{24,0},{28,4},{1,25},{... | collective-permute-start | bytes 49160 | tf_op jit(solution)/shard_map/ppermute | solution.py:45
  37.4 8.8 %collective-permute-start.7 = (bf16[16,2048]{1,0:T(8,128)(2,1)S(1)}, bf16[16,2048]{1,0:T(8,128)(2,1)S(1)}, u32[]{:S(2)}, u32[]{:S(2)}) collective-permute-start(bf16[16,2048]{1,0:T(8,128)(2,1)S(1)} %convolution_convert_fusion.1.refs_4_.refs_0_), channel_id=1, source_target_pairs={{0,2},{1,3},{2,0},{3,1},{4,6},{5,7},{6,4},{7,5},{8,10},{9,11},{10,... | collective-permute-start | bytes 196616 | tf_op jit(solution)/shard_map/ppermute | solution.py:26
  38.0 8.2 %collective-permute-start.8 = (bf16[16,2048]{1,0:T(8,128)(2,1)S(1)}, bf16[16,2048]{1,0:T(8,128)(2,1)S(1)}, u32[]{:S(2)}, u32[]{:S(2)}) collective-permute-start(bf16[16,2048]{1,0:T(8,128)(2,1)S(1)} %convolution_convert_fusion.1.refs_4_.refs_0_), channel_id=1, source_target_pairs={{0,1},{1,0},{2,3},{3,2},{4,5},{5,4},{6,7},{7,6},{8,9},{9,8},{10,11... | collective-permute-start | bytes 196616 | tf_op jit(solution)/shard_map/ppermute | solution.py:33
  38.0 8.2 %collective-permute-start.9 = (bf16[16,2048]{1,0:T(8,128)(2,1)S(1)}, bf16[16,2048]{1,0:T(8,128)(2,1)S(1)}, u32[]{:S(2)}, u32[]{:S(2)}) collective-permute-start(bf16[16,2048]{1,0:T(8,128)(2,1)S(1)} %convolution_convert_fusion.1.refs_4_.refs_0_), channel_id=1, source_target_pairs={{0,3},{1,2},{2,1},{3,0},{4,7},{5,6},{6,5},{7,4},{8,11},{9,10},{10,... | collective-permute-start | bytes 196616 | tf_op jit(solution)/shard_map/ppermute | solution.py:33
  46.3 1.6 %collective-permute-start.10 = (bf16[256,512]{1,0:T(8,128)(2,1)S(1)}, bf16[256,512]{1,0:T(8,128)(2,1)S(1)}, u32[]{:S(2)}, u32[]{:S(2)}) collective-permute-start(bf16[256,512]{1,0:T(8,128)(2,1)S(1)} %fill_attend.2.mine), channel_id=1, source_target_pairs={{0,1},{1,0},{2,3},{3,2},{4,5},{5,4},{6,7},{7,6},{8,9},{9,8},{10,11... | collective-permute-start | bytes 786440 | tf_op jit(solution)/shard_map/ppermute | solution.py:20
  50.3 22.7 %collective-permute-start.19 = (bf16[256,1024]{1,0:T(8,128)(2,1)S(1)}, bf16[256,1024]{1,0:T(8,128)(2,1)S(1)}, u32[]{:S(2)}, u32[]{:S(2)}) collective-permute-start(bf16[256,1024]{1,0:T(8,128)(2,1)S(1)} %out_project.2.refs_2_), channel_id=1, source_target_pairs={{0,2},{1,3},{2,0},{3,1},{4,6},{5,7},{6,4},{7,5},{8,10},{9,11},{10,... | collective-permute-start | bytes 1572872 | tf_op jit(solution)/shard_map/ppermute | solution.py:26
  61.8 7.0 %collective-permute-start.13 = (bf16[16,2048]{1,0:T(8,128)(2,1)S(1)}, bf16[16,2048]{1,0:T(8,128)(2,1)S(1)}, u32[]{:S(2)}, u32[]{:S(2)}) collective-permute-start(bf16[16,2048]{1,0:T(8,128)(2,1)S(1)} %get-tuple-element.57.refs_4_.refs_7_), channel_id=1, source_target_pairs={{0,2},{1,3},{2,0},{3,1},{4,6},{5,7},{6,4},{7,5},{8,10},{9,11},{10,... | collective-permute-start | bytes 196616 | tf_op jit(solution)/shard_map/ppermute | solution.py:26
  63.4 5.4 %collective-permute-start.14 = (bf16[16,2048]{1,0:T(8,128)(2,1)S(1)}, bf16[16,2048]{1,0:T(8,128)(2,1)S(1)}, u32[]{:S(2)}, u32[]{:S(2)}) collective-permute-start(bf16[16,2048]{1,0:T(8,128)(2,1)S(1)} %get-tuple-element.57.refs_4_.refs_7_), channel_id=1, source_target_pairs={{0,1},{1,0},{2,3},{3,2},{4,5},{5,4},{6,7},{7,6},{8,9},{9,8},{10,11... | collective-permute-start | bytes 196616 | tf_op jit(solution)/shard_map/ppermute | solution.py:33
  63.4 5.4 %collective-permute-start.15 = (bf16[16,2048]{1,0:T(8,128)(2,1)S(1)}, bf16[16,2048]{1,0:T(8,128)(2,1)S(1)}, u32[]{:S(2)}, u32[]{:S(2)}) collective-permute-start(bf16[16,2048]{1,0:T(8,128)(2,1)S(1)} %get-tuple-element.57.refs_4_.refs_7_), channel_id=1, source_target_pairs={{0,3},{1,2},{2,1},{3,0},{4,7},{5,6},{6,5},{7,4},{8,11},{9,10},{10,... | collective-permute-start | bytes 196616 | tf_op jit(solution)/shard_map/ppermute | solution.py:33
  68.8 1.6 %collective-permute-start.16 = (bf16[256,512]{1,0:T(8,128)(2,1)S(1)}, bf16[256,512]{1,0:T(8,128)(2,1)S(1)}, u32[]{:S(2)}, u32[]{:S(2)}) collective-permute-start(bf16[256,512]{1,0:T(8,128)(2,1)S(1)} %fill_attend.3.mine), channel_id=1, source_target_pairs={{0,1},{1,0},{2,3},{3,2},{4,5},{5,4},{6,7},{7,6},{8,9},{9,8},{10,11... | collective-permute-start | bytes 786440 | tf_op jit(solution)/shard_map/ppermute | solution.py:20
  72.7 2.1 %collective-permute-start.18 = (bf16[256,1024]{1,0:T(8,128)(2,1)S(1)}, bf16[256,1024]{1,0:T(8,128)(2,1)S(1)}, u32[]{:S(2)}, u32[]{:S(2)}) collective-permute-start(bf16[256,1024]{1,0:T(8,128)(2,1)S(1)} %out_project.3.refs_2_), channel_id=1, source_target_pairs={{0,1},{1,0},{2,3},{3,2},{4,5},{5,4},{6,7},{7,6},{8,9},{9,8},{10,11... | collective-permute-start | bytes 1572872 | tf_op jit(solution)/shard_map/ppermute | solution.py:20
  72.9 2.5 %collective-permute-start.20 = (bf16[256,1024]{1,0:T(8,128)(2,1)S(1)}, bf16[256,1024]{1,0:T(8,128)(2,1)S(1)}, u32[]{:S(2)}, u32[]{:S(2)}) collective-permute-start(bf16[256,1024]{1,0:T(8,128)(2,1)S(1)} %collective-permute-done.19.refs_4_), channel_id=1, source_target_pairs={{0,1},{1,0},{2,3},{3,2},{4,5},{5,4},{6,7},{7,6},{8,9},{9,8},{10,11... | collective-permute-start | bytes 1572872 | tf_op jit(solution)/shard_map/ppermute | solution.py:20
  73.3 23.1 %collective-permute-start.17 = (bf16[256,1024]{1,0:T(8,128)(2,1)S(1)}, bf16[256,1024]{1,0:T(8,128)(2,1)S(1)}, u32[]{:S(2)}, u32[]{:S(2)}) collective-permute-start(bf16[256,1024]{1,0:T(8,128)(2,1)S(1)} %out_project.3.refs_2_), channel_id=1, source_target_pairs={{0,2},{1,3},{2,0},{3,1},{4,6},{5,7},{6,4},{7,5},{8,10},{9,11},{10,... | collective-permute-start | bytes 1572872 | tf_op jit(solution)/shard_map/ppermute | solution.py:26
  95.8 2.3 %collective-permute-start.25 = (bf16[128,2048]{1,0:T(8,128)(2,1)S(1)}, bf16[128,2048]{1,0:T(8,128)(2,1)S(1)}, u32[]{:S(2)}, u32[]{:S(2)}) collective-permute-start(bf16[128,2048]{1,0:T(8,128)(2,1)S(1)} %get-tuple-element.73), channel_id=1, source_target_pairs={{0,1},{1,0},{2,3},{3,2},{4,5},{5,4},{6,7},{7,6},{8,9},{9,8},{10,11... | collective-permute-start | bytes 1572872 | tf_op jit(solution)/shard_map/ppermute | solution.py:20
  96.0 3.4 %collective-permute-start.12 = (bf16[256,1024]{1,0:T(8,128)(2,1)S(1)}, bf16[256,1024]{1,0:T(8,128)(2,1)S(1)}, u32[]{:S(2)}, u32[]{:S(2)}) collective-permute-start(bf16[256,1024]{1,0:T(8,128)(2,1)S(1)} %out_project.2.refs_2_), channel_id=1, source_target_pairs={{0,1},{1,0},{2,3},{3,2},{4,5},{5,4},{6,7},{7,6},{8,9},{9,8},{10,11... | collective-permute-start | bytes 1572872 | tf_op jit(solution)/shard_map/ppermute | solution.py:20
  96.4 4.0 %collective-permute-start.21 = (bf16[256,1024]{1,0:T(8,128)(2,1)S(1)}, bf16[256,1024]{1,0:T(8,128)(2,1)S(1)}, u32[]{:S(2)}, u32[]{:S(2)}) collective-permute-start(bf16[256,1024]{1,0:T(8,128)(2,1)S(1)} %collective-permute-done.17.refs_4_), channel_id=1, source_target_pairs={{0,1},{1,0},{2,3},{3,2},{4,5},{5,4},{6,7},{7,6},{8,9},{9,8},{10,11... | collective-permute-start | bytes 1572872 | tf_op jit(solution)/shard_map/ppermute | solution.py:20
  96.5 17.6 %collective-permute-start.24 = (bf16[16,2048]{1,0:T(8,128)(2,1)S(1)}, bf16[16,2048]{1,0:T(8,128)(2,1)S(1)}, u32[]{:S(2)}, u32[]{:S(2)}) collective-permute-start(bf16[16,2048]{1,0:T(8,128)(2,1)S(1)} %get-tuple-element.70), channel_id=1, source_target_pairs={{0,3},{1,2},{2,1},{3,0},{4,7},{5,6},{6,5},{7,4},{8,11},{9,10},{10,... | collective-permute-start | bytes 196616 | tf_op jit(solution)/shard_map/ppermute | solution.py:33
  98.0 16.1 %collective-permute-start.23 = (bf16[16,2048]{1,0:T(8,128)(2,1)S(1)}, bf16[16,2048]{1,0:T(8,128)(2,1)S(1)}, u32[]{:S(2)}, u32[]{:S(2)}) collective-permute-start(bf16[16,2048]{1,0:T(8,128)(2,1)S(1)} %get-tuple-element.70), channel_id=1, source_target_pairs={{0,1},{1,0},{2,3},{3,2},{4,5},{5,4},{6,7},{7,6},{8,9},{9,8},{10,11... | collective-permute-start | bytes 196616 | tf_op jit(solution)/shard_map/ppermute | solution.py:33
  98.2 16.0 %collective-permute-start.22 = (bf16[16,2048]{1,0:T(8,128)(2,1)S(1)}, bf16[16,2048]{1,0:T(8,128)(2,1)S(1)}, u32[]{:S(2)}, u32[]{:S(2)}) collective-permute-start(bf16[16,2048]{1,0:T(8,128)(2,1)S(1)} %get-tuple-element.70), channel_id=1, source_target_pairs={{0,2},{1,3},{2,0},{3,1},{4,6},{5,7},{6,4},{7,5},{8,10},{9,11},{10,... | collective-permute-start | bytes 196616 | tf_op jit(solution)/shard_map/ppermute | solution.py:26
  99.4 26.3 %collective-permute-start.26 = (bf16[128,2048]{1,0:T(8,128)(2,1)S(1)}, bf16[128,2048]{1,0:T(8,128)(2,1)S(1)}, u32[]{:S(2)}, u32[]{:S(2)}) collective-permute-start(bf16[128,2048]{1,0:T(8,128)(2,1)S(1)} %add_convert_fusion.1), channel_id=1, source_target_pairs={{0,2},{1,3},{2,0},{3,1},{4,6},{5,7},{6,4},{7,5},{8,10},{9,11},{10,... | collective-permute-start | bytes 1572872 | tf_op jit(solution)/shard_map/ppermute | solution.py:26
  114.4 11.3 %collective-permute-start.29 = (bf16[4,2048]{1,0:T(4,128)(2,1)S(1)}, bf16[4,2048]{1,0:T(4,128)(2,1)S(1)}, u32[]{:S(2)}, u32[]{:S(2)}) collective-permute-start(bf16[4,2048]{1,0:T(4,128)(2,1)S(1)} %get-tuple-element.83), channel_id=1, source_target_pairs={{0,24},{4,28},{8,16},{12,20},{16,8},{20,12},{24,0},{28,4},{1,25},{... | collective-permute-start | bytes 49160 | tf_op jit(solution)/shard_map/ppermute | solution.py:45
  114.7 11.0 %collective-permute-start.28 = (bf16[4,2048]{1,0:T(4,128)(2,1)S(1)}, bf16[4,2048]{1,0:T(4,128)(2,1)S(1)}, u32[]{:S(2)}, u32[]{:S(2)}) collective-permute-start(bf16[4,2048]{1,0:T(4,128)(2,1)S(1)} %get-tuple-element.84), channel_id=1, source_target_pairs={{0,16},{4,20},{8,24},{12,28},{16,0},{20,4},{24,8},{28,12},{1,17},{... | collective-permute-start | bytes 49160 | tf_op jit(solution)/shard_map/ppermute | solution.py:45
  114.7 11.0 %collective-permute-start.27 = (bf16[4,2048]{1,0:T(4,128)(2,1)S(1)}, bf16[4,2048]{1,0:T(4,128)(2,1)S(1)}, u32[]{:S(2)}, u32[]{:S(2)}) collective-permute-start(bf16[4,2048]{1,0:T(4,128)(2,1)S(1)} %get-tuple-element.82), channel_id=1, source_target_pairs={{0,8},{4,12},{8,0},{12,4},{16,24},{20,28},{24,16},{28,20},{1,9},{5... | collective-permute-start | bytes 49160 | tf_op jit(solution)/shard_map/ppermute | solution.py:45
  125.7 4.4 %collective-permute-start.30 = (bf16[128,2048]{1,0:T(8,128)(2,1)S(1)}, bf16[128,2048]{1,0:T(8,128)(2,1)S(1)}, u32[]{:S(2)}, u32[]{:S(2)}) collective-permute-start(bf16[128,2048]{1,0:T(8,128)(2,1)S(1)} %get-tuple-element.75), channel_id=1, source_target_pairs={{0,1},{1,0},{2,3},{3,2},{4,5},{5,4},{6,7},{7,6},{8,9},{9,8},{10,11... | collective-permute-start | bytes 1572872 | tf_op jit(solution)/shard_map/ppermute | solution.py:20
  125.8 3.7 %collective-permute-start.31 = (bf16[2,2048]{1,0:T(2,128)(2,1)S(1)}, bf16[2,2048]{1,0:T(2,128)(2,1)S(1)}, u32[]{:S(2)}, u32[]{:S(2)}) collective-permute-start(bf16[2,2048]{1,0:T(2,128)(2,1)S(1)} %slice.29), channel_id=1, source_target_pairs={{0,4},{4,0},{8,12},{12,8},{16,20},{20,16},{24,28},{28,24},{1,5},{5... | collective-permute-start | bytes 24584 | tf_op jit(solution)/shard_map/ppermute | solution.py:45
  (17 other events, 203.4 us)

commit v7 on v6

--- a/solution.py
+++ b/solution.py
@@ -80,7 +80,7 @@
 
 
 def project_kernel(groups, heads, place, mine, sib, weight, gain, cosine, sine, *refs):
-    query, entries, everything, inner, rows_held, weight_held, row_sems, weight_sems, out_sem = refs[-9:]
+    query, entries, everything, inner, rows_held, weight_held, row_sems, weight_sem, out_sem = refs[-9:]
     piece = mine.shape[0]
     core = place[0]
     scale = gain[...]
@@ -89,13 +89,8 @@
         pltpu.make_async_copy(ref, rows_held.at[i], row_sems.at[i])
         for i, ref in enumerate((mine, sib))
     ]
-    weight_copies = [
-        pltpu.make_async_copy(
-            weight.at[:, pl.ds(j * depth, depth)], weight_held.at[j], weight_sems.at[j]
-        )
-        for j in range(heads)
-    ]
-    for copy in row_copies + weight_copies:
+    weight_copy = pltpu.make_async_copy(weight, weight_held, weight_sem)
+    for copy in row_copies + [weight_copy]:
         copy.start()
     for i, at in enumerate((core, 1 - core)):
         row_copies[i].wait()
@@ -103,9 +98,10 @@
         inner[pl.ds(start, piece), :] = normed(rows_held[i].astype(jnp.float32), scale)
     here = pl.ds(pl.multiple_of(place[1] * 2 * piece, 2 * piece), 2 * piece)
     cos, sin = cosine[here, :], sine[here, :]
+    weight_copy.wait()
+    product = jnp.dot(inner[...], weight_held[...], preferred_element_type=jnp.float32)
     for j in range(heads):
-        weight_copies[j].wait()
-        mixed = jnp.dot(inner[...], weight_held[j], preferred_element_type=jnp.float32)
+        mixed = product[:, j * depth : (j + 1) * depth]
         for g in range(groups):
             at = (j * groups + g) * HD
             part = mixed[:, g * HD : (g + 1) * HD]
@@ -142,9 +138,9 @@
         scratch_shapes=[
             pltpu.VMEM((block, width), jnp.bfloat16),
             pltpu.VMEM((2, piece, width), jnp.bfloat16),
-            pltpu.VMEM((heads, width, depth), jnp.bfloat16),
+            pltpu.VMEM(weight.shape, jnp.bfloat16),
             pltpu.SemaphoreType.DMA((2,)),
-            pltpu.SemaphoreType.DMA((heads,)),
+            pltpu.SemaphoreType.DMA(()),
             pltpu.SemaphoreType.DMA(()),
         ],
         input_output_aliases=aliases,
@@ -207,7 +203,7 @@
             + [IN_PLACE] * len(after),
             out_specs=pl.BlockSpec((count, groups * HD), lambda j, s: (0, j)),
         ),
-        compiler_params=params(16),
+        compiler_params=params(12),
         cost_estimate=cost(8 * pairs * HD, 2 * cache.size, pairs),
         name="fill_attend",
     )(place, query, cache, cache, *entries, *entries, *after)
@@ -216,22 +212,19 @@
 def step_kernel(heads, pieces, lengths, gain, cosine, sine, *refs):
     dealt_parts, refs = refs[:pieces], refs[pieces:]
     qkv, cache, weight, out, dealt, entries = refs[:6]
-    held, scores, shares, qkv_held, weight_held, arrived, qkv_sems, weight_sem = refs[6:]
+    held, scores, shares, qkv_held, weight_held, arrived, qkv_sem, weight_sem = refs[6:]
     scaling = 1.0 / math.sqrt(HD)
     slots, stored, width = cache.shape[1:]
     depth = qkv.shape[1] // heads
     groups = depth // HD - 2
     lanes = 8
-    qkv_copies = [
-        pltpu.make_async_copy(qkv.at[:, pl.ds(j * depth, depth)], qkv_held.at[j], qkv_sems.at[j])
-        for j in range(heads)
-    ]
+    qkv_copy = pltpu.make_async_copy(qkv, qkv_held, qkv_sem)
     copies = [
         [pltpu.make_async_copy(cache.at[w, s], held.at[w, s], arrived.at[w, s]) for s in range(slots)]
         for w in range(2)
     ]
     weight_copy = pltpu.make_async_copy(weight, weight_held, weight_sem)
-    for copy in qkv_copies + copies[0] + copies[1] + [weight_copy]:
+    for copy in [qkv_copy] + copies[0] + copies[1] + [weight_copy]:
         copy.start()
     rows = dealt_parts[0][...].astype(jnp.float32)
     for part in dealt_parts[1:]:
@@ -240,9 +233,10 @@
     inner = normed(rows, gain[...])
     cos, sin = cosine[...], sine[...]
     queries, new_keys, new_values = [], [], []
+    qkv_copy.wait()
+    product = jnp.dot(inner, qkv_held[...], preferred_element_type=jnp.float32)
     for j in range(heads):
-        qkv_copies[j].wait()
-        mixed = jnp.dot(inner, qkv_held[j], preferred_element_type=jnp.float32)
+        mixed = product[:, j * depth : (j + 1) * depth]
         for g in range(groups):
             part = turn(mixed[:, g * HD : (g + 1) * HD], cos, sin)
             queries.append(part.astype(jnp.bfloat16).astype(jnp.float32))
@@ -325,13 +319,13 @@
             pltpu.VMEM(cache.shape, jnp.bfloat16),
             pltpu.VMEM((rows, stored), jnp.float32),
             pltpu.VMEM((rows, stored), jnp.float32),
-            pltpu.VMEM((heads, model, qkv.shape[1] // heads), jnp.bfloat16),
+            pltpu.VMEM(qkv.shape, jnp.bfloat16),
             pltpu.VMEM(weight.shape, jnp.bfloat16),
             pltpu.SemaphoreType.DMA((2, slots)),
-            pltpu.SemaphoreType.DMA((heads,)),
+            pltpu.SemaphoreType.DMA(()),
             pltpu.SemaphoreType.DMA(()),
         ],
-        compiler_params=params(24),
+        compiler_params=params(18),
         cost_estimate=cost(16 * cache.size, 3 * cache.size, rows * stored),
         name="step_attend",
     )(lengths, gain, *tables, *dealt_parts, qkv, cache, weight)
@@ -460,7 +454,7 @@
 def lower(hidden, weight, after):
     rows, units = hidden.shape
     width = weight.shape[1]
-    chunk = 256
+    chunk = 1024
     return pl.pallas_call(
         functools.partial(lower_kernel, chunk),
         out_shape=[jax.ShapeDtypeStruct((rows // 2, width), jnp.bfloat16)] * 2,
@@ -482,7 +476,7 @@
     piece, width = mine.shape
     chips = len(shares) // 2
     units = gate.shape[1]
-    chunk = 256
+    chunk = 1024
     n_dec = 0 if dec is None else dec.shape[0]
     rows = 2 * piece + n_dec
     args = [mine, sib, *shares]
@@ -577,7 +571,6 @@
     pool = [decode_rows] + [swap_groups(decode_rows, i) for i in range(1, low)]
     pool = near = jnp.concatenate(pool, axis=0)
     pool = [pool] + [swap_groups(pool, i * low) for i in range(1, dp_count // low)]
-    pool = jnp.concatenate(pool, axis=0)
     index = jnp.arange(dp_count * per_device, dtype=jnp.int32)
     origin = jnp.bitwise_xor(group_place, index // per_device)
     request = (origin * tensor_count + tensor_place) * per_device + index % per_device
@@ -593,10 +586,6 @@
     chooser = (jnp.arange(padded, dtype=jnp.int32)[:, None] == in_group[None, :]) & (
         in_group[None, :] < slots
     )
-    dealt = jnp.dot(
-        chooser.astype(jnp.bfloat16), pool, preferred_element_type=jnp.float32
-    ).astype(jnp.bfloat16)
-
     gain = attention_gain.reshape(1, width)
     tables = angle_tables(prefill_offset[0] + jnp.arange(tokens, dtype=jnp.int32))
     dec_tables = angle_tables(jnp.pad(cache_length, (0, padded - slots)))
@@ -614,10 +603,15 @@
             [query] if k else [near],
         )
         if k == 0:
-            *mines[1:], query = lax.optimization_barrier((*mines[1:], query))
+            first, *pool = pool
+            mines[1:], pool, query = lax.optimization_barrier((mines[1:], pool, query))
+            pool = jnp.concatenate([first, *pool], axis=0)
             sibs += [swap_cores(rows) for rows in mines[1:]]
         queries.append(query)
         entries.append(entry)
+    dealt = jnp.dot(
+        chooser.astype(jnp.bfloat16), pool, preferred_element_type=jnp.float32
+    ).astype(jnp.bfloat16)
     dealt_parts = [dealt, *from_rest(dealt)]
 
     out_share = out_weight

time: 132 us -> 112 us (0.85)
  Pallas kernels: 75.8 us -> 61.3 us
  waiting for transfers between devices: 13.8 us -> 8.66 us
    pallas_call x2, Pallas kernels: 34 us -> 21.1 us  [feed_forward(): pl.pallas_call(functools.partial(forward_kernel, split, chips, n_dec, len...]
    ppermute x8, waiting for transfers between devices: 8.46 us -> 3.16 us  [swap_groups(): return lax.ppermute(value, 'dp', [(i, i ^ mask) for i in range(count)])]
    pallas_call x1, Pallas kernels: 6.84 us -> 4.76 us  [lower(): pl.pallas_call(functools.partial(lower_kernel, chunk), out_shape=[jax.Sha...]
  transfers between devices with their start and end apart: 32 -> 32, of which waited for: 7 -> 5; matrix products, arithmetic and copies ran while one was open for 6% -> 8% of each run, Pallas kernels for 52% -> 48%
where the time goes in v7:
time: 112 us
  Pallas kernels  61.3 us (55%)
  starting transfers between devices  26 us (23%)
  local copies, waits for them, and re-layouts  9.95 us (9%)
  waiting for transfers between devices  8.66 us (8%)
  other arithmetic  3.52 us (3%)
  between operations  1.75 us (2%)
    pallas_call x2, Pallas kernels, feed_forward(): pl.pallas_call(functools.partial(forward_kernel, split, chips, n_dec, len...  21.1 us
    pallas_call x1, Pallas kernels, step_attend(): pl.pallas_call(functools.partial(step_kernel, heads, pieces), out_shape=[...  11.1 us
    ppermute x8, starting transfers between devices, swap_groups(): return lax.ppermute(value, 'dp', [(i, i ^ mask) for i in range(count)])  11 us
    pallas_call x2, Pallas kernels, project(): pl.pallas_call(functools.partial(project_kernel, groups, heads), out_shap...  10.3 us
    unnamed x35, local copies, waits for them, and re-layouts  9.66 us
    pallas_call x2, Pallas kernels, fill_attend(): pl.pallas_call(functools.partial(fill_kernel, groups, chips), out_shape=j...  9.47 us
    ppermute x7, starting transfers between devices, from_chip(): lax.ppermute(value, 'tensor', [(i, (i // 2 - step) % chips * 2 + i % 2) f...  9.37 us
    ppermute x11, waiting for transfers between devices, swap_cores(): return lax.ppermute(value, 'tensor', [(i, i ^ 1) for i in range(count)])  5.46 us
  transfers between devices with their start and end apart: 32, of which 5 were waited for; matrix products, arithmetic and copies ran while one was open for 8% of the time, Pallas kernels for 48%

profile of v7, /device:TPU:0, one launch (start us, length us, event | category | flops | bytes accessed | tf_op | source)
XLA Modules:
  0.0 111.6 jit_solution(2418375239213143969)
XLA Ops:
  0.7 3.0 %collective-permute-start.1 = (bf16[128,2048]{1,0:T(8,128)(2,1)}, bf16[128,2048]{1,0:T(8,128)(2,1)S(1)}, u32[]{:S(2)}, u32[]{:S(2)}) collective-permute-start(bf16[128,2048]{1,0:T(8,128)(2,1)} %refs_0_.1), channel_id=1, source_target_pairs={{0,2},{1,3},{2,0},{3,1},{4,6},{5,7},{6,4},{7,5},{8,10},{9,11},{10,... | collective-permute-start | bytes 1572872 | tf_op jit(solution)/shard_map/ppermute | solution.py:26
  3.7 1.5 %collective-permute-start.2 = (bf16[2,2048]{1,0:T(2,128)(2,1)}, bf16[2,2048]{1,0:T(2,128)(2,1)S(1)}, u32[]{:S(2)}, u32[]{:S(2)}) collective-permute-start(bf16[2,2048]{1,0:T(2,128)(2,1)} %param.15), channel_id=1, source_target_pairs={{0,4},{4,0},{8,12},{12,8},{16,20},{20,16},{24,28},{28,24},{1,5},{5... | collective-permute-start | bytes 24584 | tf_op jit(solution)/shard_map/ppermute | solution.py:45
  5.9 1.0 fusion
  7.1 5.5 %copy.19 = bf16[256,8,2,512]{3,1,2,0:T(8,128)(2,1)} copy(bf16[256,8,2,512]{3,2,1,0:T(2,128)(2,1)} %bitcast.18) | data formatting | bytes 8388608
  12.8 1.6 %collective-permute-start.3 = (bf16[4,2048]{1,0:T(4,128)(2,1)S(1)}, bf16[4,2048]{1,0:T(4,128)(2,1)S(1)}, u32[]{:S(2)}, u32[]{:S(2)}) collective-permute-start(bf16[4,2048]{1,0:T(4,128)(2,1)S(1)} %pad_maximum_fusion.2.refs_0_), channel_id=1, source_target_pairs={{0,8},{4,12},{8,0},{12,4},{16,24},{20,28},{24,16},{28,20},{1,9},{5... | collective-permute-start | bytes 49160 | tf_op jit(solution)/shard_map/ppermute | solution.py:45
  14.4 2.6 %collective-permute-start.4 = (bf16[4,2048]{1,0:T(4,128)(2,1)S(1)}, bf16[4,2048]{1,0:T(4,128)(2,1)S(1)}, u32[]{:S(2)}, u32[]{:S(2)}) collective-permute-start(bf16[4,2048]{1,0:T(4,128)(2,1)S(1)} %pad_maximum_fusion.2.refs_0_), channel_id=1, source_target_pairs={{0,16},{4,20},{8,24},{12,28},{16,0},{20,4},{24,8},{28,12},{1,17},{... | collective-permute-start | bytes 49160 | tf_op jit(solution)/shard_map/ppermute | solution.py:45
  17.2 5.1 %project.2 = (bf16[256,512]{1,0:T(8,128)(2,1)S(1)}, bf16[2,256,256]{2,1,0:T(8,128)(2,1)S(1)}, bf16[2,512,256]{2,1,0:T(8,128)(2,1)}) custom-call(s32[5]{0:T(128)S(1)} %stack.23.place, bf16[128,2048]{1,0:T(8,128)(2,1)} %refs_0_.1, bf16[128,2048]{1,0:T(8,128)(2,1)} %collective-permute-done.sib.refs_1_, bf16[2048,1024]{1,0:T(8,128)(2,1)} %bitcast.15, ...), custom_call_target="tpu_custom_call" | custom-call | flops 1073741824 | bytes 6291456 | tf_op jit(solution)/shard_map/project/pallas_call | solution.py:129
  23.3 1.9 %collective-permute-done.6.sib.refs_1_ = bf16[128,2048]{1,0:T(8,128)(2,1)} collective-permute-done((bf16[128,2048]{1,0:T(8,128)(2,1)S(1)}, bf16[128,2048]{1,0:T(8,128)(2,1)}, u32[]{:S(2)}, u32[]{:S(2)}) %collective-permute-start.6) | collective-permute-done | bytes 524320 | tf_op jit(solution)/shard_map/ppermute | solution.py:20
  25.3 5.1 %project.3 = (bf16[256,512]{1,0:T(8,128)(2,1)S(1)}, bf16[2,256,256]{2,1,0:T(8,128)(2,1)S(1)}, bf16[2,512,256]{2,1,0:T(8,128)(2,1)}) custom-call(s32[5]{0:T(128)S(1)} %stack.24.place, bf16[128,2048]{1,0:T(8,128)(2,1)} %copy-done.2, bf16[128,2048]{1,0:T(8,128)(2,1)} %collective-permute-done.6.sib.refs_1_, ...), custom_call_target="tpu_custom_call", output_to_operand_aliasing={{2}: (8, {})} | custom-call | flops 1073741824 | bytes 6291456 | tf_op jit(solution)/shard_map/project/pallas_call | solution.py:129
  30.4 0.7 copy-done.11
  33.1 1.5 %collective-permute-start.9 = (bf16[16,2048]{1,0:T(8,128)(2,1)S(1)}, bf16[16,2048]{1,0:T(8,128)(2,1)S(1)}, u32[]{:S(2)}, u32[]{:S(2)}) collective-permute-start(bf16[16,2048]{1,0:T(8,128)(2,1)S(1)} %convolution_convert_fusion.1.refs_4_.refs_0_), channel_id=1, source_target_pairs={{0,3},{1,2},{2,1},{3,0},{4,7},{5,6},{6,5},{7,4},{8,11},{9,10},{10,... | collective-permute-start | bytes 196616 | tf_op jit(solution)/shard_map/ppermute | solution.py:33
  34.7 0.9 copy-done.9
  35.6 0.9 copy-done.14
  36.6 4.7 %fill_attend.2.mine = bf16[256,512]{1,0:T(8,128)(2,1)S(1)} custom-call(s32[5]{0:T(128)S(1)} %stack.23.place, bf16[256,512]{1,0:T(8,128)(2,1)S(1)} %get-tuple-element.46.refs_0_.query, bf16[2,1,1024,256]{3,2,1,0:T(8,128)(2,1)} %cache_value.3, bf16[2,1,1024,256]{3,2,1,0:T(8,128)(2,1)} %cache_value.3, bf16[2,256,256]{2,1,0:T(8,128)(2,1)S(1)} %copy-done.9, ...), custom_call_target="tpu_custom_call" | custom-call | flops 1610612736 | bytes 1048576 | tf_op jit(solution)/shard_map/fill_attend/pallas_call | solution.py:190
  41.6 1.3 %collective-permute-done.10.sib = bf16[256,512]{1,0:T(8,128)(2,1)S(1)} collective-permute-done((bf16[256,512]{1,0:T(8,128)(2,1)S(1)}, bf16[256,512]{1,0:T(8,128)(2,1)S(1)}, u32[]{:S(2)}, u32[]{:S(2)}) %collective-permute-start.10) | collective-permute-done | bytes 262176 | tf_op jit(solution)/shard_map/ppermute | solution.py:20
  42.9 2.3 %out_project.2.refs_2_ = bf16[256,1024]{1,0:T(8,128)(2,1)S(1)} custom-call(s32[5]{0:T(128)S(1)} %stack.23.place, bf16[256,512]{1,0:T(8,128)(2,1)S(1)} %fill_attend.2.mine, bf16[256,512]{1,0:T(8,128)(2,1)S(1)} %collective-permute-done.10.sib, bf16[512,2048]{1,0:T(8,128)(2,1)S(1)} %copy-done, bf16[512,2048]{1,0:T(8,128)(2,1)} %collective-permute-done.11.sib_weight), custom_call_target="tpu_custom_call" | custom-call | flops 536870912 | bytes 3670016 | tf_op jit(solution)/shard_map/out_project/pallas_call | solution.py:346
  46.0 11.1 %step_attend.1 = (bf16[16,2048]{1,0:T(8,128)(2,1)S(1)}, bf16[16,2048]{1,0:T(8,128)(2,1)S(1)}, bf16[2,8,256]{2,1,0:T(8,128)(2,1)}) custom-call(s32[8]{0:T(128)S(1)} %copy-done.7, f32[1,2048]{1,0:T(1,128)S(1)} %bitcast.12, f32[16,128]{1,0:T(8,128)S(1)} %get-tuple-element.99.cosine, f32[16,128]{1,0:T(8,128)S(1)} %get-tuple-element.100.sine, ...), custom_call_target="tpu_custom_call" | custom-call | flops 67108864 | bytes 12582912 | tf_op jit(solution)/shard_map/step_attend/pallas_call | solution.py:309
  57.1 1.6 %collective-permute-start.13 = (bf16[16,2048]{1,0:T(8,128)(2,1)S(1)}, bf16[16,2048]{1,0:T(8,128)(2,1)S(1)}, u32[]{:S(2)}, u32[]{:S(2)}) collective-permute-start(bf16[16,2048]{1,0:T(8,128)(2,1)S(1)} %get-tuple-element.63.refs_4_.refs_7_), channel_id=1, source_target_pairs={{0,2},{1,3},{2,0},{3,1},{4,6},{5,7},{6,4},{7,5},{8,10},{9,11},{10,... | collective-permute-start | bytes 196616 | tf_op jit(solution)/shard_map/ppermute | solution.py:26
  59.3 4.8 %fill_attend.3.mine = bf16[256,512]{1,0:T(8,128)(2,1)S(1)} custom-call(s32[5]{0:T(128)S(1)} %stack.24.place, bf16[256,512]{1,0:T(8,128)(2,1)S(1)} %copy-done.12, bf16[2,1,1024,256]{3,2,1,0:T(8,128)(2,1)} %cache_value.3, bf16[2,1,1024,256]{3,2,1,0:T(8,128)(2,1)} %cache_value.3, bf16[2,256,256]{2,1,0:T(8,128)(2,1)S(1)} %copy-done.10, ...), custom_call_target="tpu_custom_call" | custom-call | flops 1610612736 | bytes 1048576 | tf_op jit(solution)/shard_map/fill_attend/pallas_call | solution.py:190
  64.2 1.5 %collective-permute-done.16.sib = bf16[256,512]{1,0:T(8,128)(2,1)S(1)} collective-permute-done((bf16[256,512]{1,0:T(8,128)(2,1)S(1)}, bf16[256,512]{1,0:T(8,128)(2,1)S(1)}, u32[]{:S(2)}, u32[]{:S(2)}) %collective-permute-start.16) | collective-permute-done | bytes 262176 | tf_op jit(solution)/shard_map/ppermute | solution.py:20
  65.7 2.3 %out_project.3.refs_2_ = bf16[256,1024]{1,0:T(8,128)(2,1)S(1)} custom-call(s32[5]{0:T(128)S(1)} %stack.24.place, bf16[256,512]{1,0:T(8,128)(2,1)S(1)} %fill_attend.3.mine, bf16[256,512]{1,0:T(8,128)(2,1)S(1)} %collective-permute-done.16.sib, bf16[512,2048]{1,0:T(8,128)(2,1)S(1)} %copy-done.1, bf16[512,2048]{1,0:T(8,128)(2,1)} %collective-permute-done.11.sib_weight), custom_call_target="tpu_custom_call" | custom-call | flops 536870912 | bytes 3670016 | tf_op jit(solution)/shard_map/out_project/pallas_call | solution.py:346
  68.6 1.5 %collective-permute-start.17 = (bf16[256,1024]{1,0:T(8,128)(2,1)S(1)}, bf16[256,1024]{1,0:T(8,128)(2,1)S(1)}, u32[]{:S(2)}, u32[]{:S(2)}) collective-permute-start(bf16[256,1024]{1,0:T(8,128)(2,1)S(1)} %out_project.3.refs_2_), channel_id=1, source_target_pairs={{0,2},{1,3},{2,0},{3,1},{4,6},{5,7},{6,4},{7,5},{8,10},{9,11},{10,... | collective-permute-start | bytes 1572872 | tf_op jit(solution)/shard_map/ppermute | solution.py:26
  70.8 12.2 %feed_forward.2 = (bf16[128,2048]{1,0:T(8,128)(2,1)S(1)}, bf16[128,2048]{1,0:T(8,128)(2,1)S(1)}, bf16[128,2048]{1,0:T(8,128)(2,1)}, bf16[16,2048]{1,0:T(8,128)(2,1)S(1)}, bf16[16,2048]{1,0:T(8,128)(2,1)S(1)}) custom-call(s32[5]{0:T(128)S(1)} %stack.24.place, bf16[128,2048]{1,0:T(8,128)(2,1)S(1)} %copy-done.3, ...), custom_call_target="tpu_custom_call" | custom-call | flops 6845104128 | bytes 25165824 | tf_op jit(solution)/shard_map/feed_forward/pallas_call | solution.py:493
  83.7 1.5 %collective-permute-start.24 = (bf16[16,2048]{1,0:T(8,128)(2,1)S(1)}, bf16[16,2048]{1,0:T(8,128)(2,1)S(1)}, u32[]{:S(2)}, u32[]{:S(2)}) collective-permute-start(bf16[16,2048]{1,0:T(8,128)(2,1)S(1)} %get-tuple-element.76), channel_id=1, source_target_pairs={{0,3},{1,2},{2,1},{3,0},{4,7},{5,6},{6,5},{7,4},{8,11},{9,10},{10,... | collective-permute-start | bytes 196616 | tf_op jit(solution)/shard_map/ppermute | solution.py:33
  85.4 1.1 %collective-permute-start.22 = (bf16[16,2048]{1,0:T(8,128)(2,1)S(1)}, bf16[16,2048]{1,0:T(8,128)(2,1)S(1)}, u32[]{:S(2)}, u32[]{:S(2)}) collective-permute-start(bf16[16,2048]{1,0:T(8,128)(2,1)S(1)} %get-tuple-element.76), channel_id=1, source_target_pairs={{0,2},{1,3},{2,0},{3,1},{4,6},{5,7},{6,4},{7,5},{8,10},{9,11},{10,... | collective-permute-start | bytes 196616 | tf_op jit(solution)/shard_map/ppermute | solution.py:26
  86.7 1.0 collective-permute-start.26
  87.6 8.8 %feed_forward.3 = (bf16[128,2048]{1,0:T(8,128)(2,1)S(1)}, bf16[256,2048]{1,0:T(8,128)(2,1)S(1)}) custom-call(s32[5]{0:T(128)S(1)} %stack.23.place, bf16[128,2048]{1,0:T(8,128)(2,1)S(1)} %copy-done.4, bf16[128,2048]{1,0:T(8,128)(2,1)} %collective-permute-done.sib.refs_1_, bf16[256,1024]{1,0:T(8,128)(2,1)S(1)} %out_project.2.refs_2_, ...), custom_call_target="tpu_custom_call" | custom-call | flops 6442450944 | bytes 25165824 | tf_op jit(solution)/shard_map/feed_forward/pallas_call | solution.py:493
  96.7 3.7 %collective-permute-start.29 = (bf16[4,2048]{1,0:T(4,128)(2,1)S(1)}, bf16[4,2048]{1,0:T(4,128)(2,1)S(1)}, u32[]{:S(2)}, u32[]{:S(2)}) collective-permute-start(bf16[4,2048]{1,0:T(4,128)(2,1)S(1)} %get-tuple-element.89), channel_id=1, source_target_pairs={{0,24},{4,28},{8,16},{12,20},{16,8},{20,12},{24,0},{28,4},{1,25},{... | collective-permute-start | bytes 49160 | tf_op jit(solution)/shard_map/ppermute | solution.py:45
  100.4 0.8 collective-permute-start.27
  101.2 4.8 %lower.1 = (bf16[128,2048]{1,0:T(8,128)(2,1)S(1)}, bf16[128,2048]{1,0:T(8,128)(2,1)S(1)}) custom-call(bf16[256,2048]{1,0:T(8,128)(2,1)S(1)} %get-tuple-element.74.hidden, bf16[2048,2048]{1,0:T(8,128)(2,1)} %weight.5, bf16[16,2048]{1,0:T(8,128)(2,1)S(1)} %convolution_convert_fusion.refs_0_), custom_call_target="tpu_custom_call" | custom-call | flops 2147483648 | bytes 8388608 | tf_op jit(solution)/shard_map/lower/pallas_call | solution.py:458
  106.7 3.1 %collective-permute-done.31 = bf16[2,2048]{1,0:T(2,128)(2,1)S(1)} collective-permute-done((bf16[2,2048]{1,0:T(2,128)(2,1)S(1)}, bf16[2,2048]{1,0:T(2,128)(2,1)S(1)}, u32[]{:S(2)}, u32[]{:S(2)}) %collective-permute-start.31) | collective-permute-done | bytes 8224 | tf_op jit(solution)/shard_map/ppermute | solution.py:45
  110.5 1.1 %add_convert_fusion = bf16[128,2048]{1,0:T(8,128)(2,1)} fusion(bf16[128,2048]{1,0:T(8,128)(2,1)S(1)} %collective-permute-done.26, bf16[128,2048]{1,0:T(8,128)(2,1)S(1)} %collective-permute-done.30, bf16[128,2048]{1,0:T(8,128)(2,1)S(1)} %get-tuple-element.77, bf16[128,2048]{1,0:T(8,128)(2,1)S(1)} %get-tuple-element.71), kind=kLoop, calls=%fused_computation.2 | loop fusion | flops 2097152 | bytes 2621440 | tf_op jit(solution)/shard_map/convert_element_type | solution.py:525
  (99 shorter events, 8.9 us)
Async XLA Ops:
  0.7 22.5 %collective-permute-start.1 = (bf16[128,2048]{1,0:T(8,128)(2,1)}, bf16[128,2048]{1,0:T(8,128)(2,1)S(1)}, u32[]{:S(2)}, u32[]{:S(2)}) collective-permute-start(bf16[128,2048]{1,0:T(8,128)(2,1)} %refs_0_.1), channel_id=1, source_target_pairs={{0,2},{1,3},{2,0},{3,1},{4,6},{5,7},{6,4},{7,5},{8,10},{9,11},{10,... | collective-permute-start | bytes 1572872 | tf_op jit(solution)/shard_map/ppermute | solution.py:26
  3.7 13.6 %collective-permute-start = (bf16[128,2048]{1,0:T(8,128)(2,1)}, bf16[128,2048]{1,0:T(8,128)(2,1)}, u32[]{:S(2)}, u32[]{:S(2)}) collective-permute-start(bf16[128,2048]{1,0:T(8,128)(2,1)} %refs_0_.1), channel_id=1, source_target_pairs={{0,1},{1,0},{2,3},{3,2},{4,5},{5,4},{6,7},{7,6},{8,9},{9,8},{10,11... | collective-permute-start | bytes 1572872 | tf_op jit(solution)/shard_map/ppermute | solution.py:20
  3.7 9.1 %collective-permute-start.2 = (bf16[2,2048]{1,0:T(2,128)(2,1)}, bf16[2,2048]{1,0:T(2,128)(2,1)S(1)}, u32[]{:S(2)}, u32[]{:S(2)}) collective-permute-start(bf16[2,2048]{1,0:T(2,128)(2,1)} %param.15), channel_id=1, source_target_pairs={{0,4},{4,0},{8,12},{12,8},{16,20},{20,16},{24,28},{28,24},{1,5},{5... | collective-permute-start | bytes 24584 | tf_op jit(solution)/shard_map/ppermute | solution.py:45
  12.8 10.4 %collective-permute-start.3 = (bf16[4,2048]{1,0:T(4,128)(2,1)S(1)}, bf16[4,2048]{1,0:T(4,128)(2,1)S(1)}, u32[]{:S(2)}, u32[]{:S(2)}) collective-permute-start(bf16[4,2048]{1,0:T(4,128)(2,1)S(1)} %pad_maximum_fusion.2.refs_0_), channel_id=1, source_target_pairs={{0,8},{4,12},{8,0},{12,4},{16,24},{20,28},{24,16},{28,20},{1,9},{5... | collective-permute-start | bytes 49160 | tf_op jit(solution)/shard_map/ppermute | solution.py:45
  14.4 8.7 %collective-permute-start.4 = (bf16[4,2048]{1,0:T(4,128)(2,1)S(1)}, bf16[4,2048]{1,0:T(4,128)(2,1)S(1)}, u32[]{:S(2)}, u32[]{:S(2)}) collective-permute-start(bf16[4,2048]{1,0:T(4,128)(2,1)S(1)} %pad_maximum_fusion.2.refs_0_), channel_id=1, source_target_pairs={{0,16},{4,20},{8,24},{12,28},{16,0},{20,4},{24,8},{28,12},{1,17},{... | collective-permute-start | bytes 49160 | tf_op jit(solution)/shard_map/ppermute | solution.py:45
  17.0 6.1 %collective-permute-start.5 = (bf16[4,2048]{1,0:T(4,128)(2,1)S(1)}, bf16[4,2048]{1,0:T(4,128)(2,1)S(1)}, u32[]{:S(2)}, u32[]{:S(2)}) collective-permute-start(bf16[4,2048]{1,0:T(4,128)(2,1)S(1)} %pad_maximum_fusion.2.refs_0_), channel_id=1, source_target_pairs={{0,24},{4,28},{8,16},{12,20},{16,8},{20,12},{24,0},{28,4},{1,25},{... | collective-permute-start | bytes 49160 | tf_op jit(solution)/shard_map/ppermute | solution.py:45
  23.2 2.1 %collective-permute-start.6 = (bf16[128,2048]{1,0:T(8,128)(2,1)S(1)}, bf16[128,2048]{1,0:T(8,128)(2,1)}, u32[]{:S(2)}, u32[]{:S(2)}) collective-permute-start(bf16[128,2048]{1,0:T(8,128)(2,1)S(1)} %collective-permute-done.1.mine.refs_0_), channel_id=1, source_target_pairs={{0,1},{1,0},{2,3},{3,2},{4,5},{5,4},{6,7},{7,6},{8,9},{9,8},{10,11... | collective-permute-start | bytes 1572872 | tf_op jit(solution)/shard_map/ppermute | solution.py:20
  31.9 11.1 %collective-permute-start.11 = (bf16[512,2048]{1,0:T(8,128)(2,1)S(1)}, bf16[512,2048]{1,0:T(8,128)(2,1)}, u32[]{:S(2)}, u32[]{:S(2)}) collective-permute-start(bf16[512,2048]{1,0:T(8,128)(2,1)S(1)} %copy-done), channel_id=1, source_target_pairs={{0,1},{1,0},{2,3},{3,2},{4,5},{5,4},{6,7},{7,6},{8,9},{9,8},{10,11... | collective-permute-start | bytes 6291464 | tf_op jit(solution)/shard_map/ppermute | solution.py:20
  32.5 8.9 %collective-permute-start.7 = (bf16[16,2048]{1,0:T(8,128)(2,1)S(1)}, bf16[16,2048]{1,0:T(8,128)(2,1)S(1)}, u32[]{:S(2)}, u32[]{:S(2)}) collective-permute-start(bf16[16,2048]{1,0:T(8,128)(2,1)S(1)} %convolution_convert_fusion.1.refs_4_.refs_0_), channel_id=1, source_target_pairs={{0,2},{1,3},{2,0},{3,1},{4,6},{5,7},{6,4},{7,5},{8,10},{9,11},{10,... | collective-permute-start | bytes 196616 | tf_op jit(solution)/shard_map/ppermute | solution.py:26
  33.1 8.3 %collective-permute-start.8 = (bf16[16,2048]{1,0:T(8,128)(2,1)S(1)}, bf16[16,2048]{1,0:T(8,128)(2,1)S(1)}, u32[]{:S(2)}, u32[]{:S(2)}) collective-permute-start(bf16[16,2048]{1,0:T(8,128)(2,1)S(1)} %convolution_convert_fusion.1.refs_4_.refs_0_), channel_id=1, source_target_pairs={{0,1},{1,0},{2,3},{3,2},{4,5},{5,4},{6,7},{7,6},{8,9},{9,8},{10,11... | collective-permute-start | bytes 196616 | tf_op jit(solution)/shard_map/ppermute | solution.py:33
  33.1 8.2 %collective-permute-start.9 = (bf16[16,2048]{1,0:T(8,128)(2,1)S(1)}, bf16[16,2048]{1,0:T(8,128)(2,1)S(1)}, u32[]{:S(2)}, u32[]{:S(2)}) collective-permute-start(bf16[16,2048]{1,0:T(8,128)(2,1)S(1)} %convolution_convert_fusion.1.refs_4_.refs_0_), channel_id=1, source_target_pairs={{0,3},{1,2},{2,1},{3,0},{4,7},{5,6},{6,5},{7,4},{8,11},{9,10},{10,... | collective-permute-start | bytes 196616 | tf_op jit(solution)/shard_map/ppermute | solution.py:33
  41.3 1.6 %collective-permute-start.10 = (bf16[256,512]{1,0:T(8,128)(2,1)S(1)}, bf16[256,512]{1,0:T(8,128)(2,1)S(1)}, u32[]{:S(2)}, u32[]{:S(2)}) collective-permute-start(bf16[256,512]{1,0:T(8,128)(2,1)S(1)} %fill_attend.2.mine), channel_id=1, source_target_pairs={{0,1},{1,0},{2,3},{3,2},{4,5},{5,4},{6,7},{7,6},{8,9},{9,8},{10,11... | collective-permute-start | bytes 786440 | tf_op jit(solution)/shard_map/ppermute | solution.py:20
  45.3 22.9 %collective-permute-start.19 = (bf16[256,1024]{1,0:T(8,128)(2,1)S(1)}, bf16[256,1024]{1,0:T(8,128)(2,1)S(1)}, u32[]{:S(2)}, u32[]{:S(2)}) collective-permute-start(bf16[256,1024]{1,0:T(8,128)(2,1)S(1)} %out_project.2.refs_2_), channel_id=1, source_target_pairs={{0,2},{1,3},{2,0},{3,1},{4,6},{5,7},{6,4},{7,5},{8,10},{9,11},{10,... | collective-permute-start | bytes 1572872 | tf_op jit(solution)/shard_map/ppermute | solution.py:26
  57.1 7.0 %collective-permute-start.13 = (bf16[16,2048]{1,0:T(8,128)(2,1)S(1)}, bf16[16,2048]{1,0:T(8,128)(2,1)S(1)}, u32[]{:S(2)}, u32[]{:S(2)}) collective-permute-start(bf16[16,2048]{1,0:T(8,128)(2,1)S(1)} %get-tuple-element.63.refs_4_.refs_7_), channel_id=1, source_target_pairs={{0,2},{1,3},{2,0},{3,1},{4,6},{5,7},{6,4},{7,5},{8,10},{9,11},{10,... | collective-permute-start | bytes 196616 | tf_op jit(solution)/shard_map/ppermute | solution.py:26
  58.7 5.4 %collective-permute-start.14 = (bf16[16,2048]{1,0:T(8,128)(2,1)S(1)}, bf16[16,2048]{1,0:T(8,128)(2,1)S(1)}, u32[]{:S(2)}, u32[]{:S(2)}) collective-permute-start(bf16[16,2048]{1,0:T(8,128)(2,1)S(1)} %get-tuple-element.63.refs_4_.refs_7_), channel_id=1, source_target_pairs={{0,1},{1,0},{2,3},{3,2},{4,5},{5,4},{6,7},{7,6},{8,9},{9,8},{10,11... | collective-permute-start | bytes 196616 | tf_op jit(solution)/shard_map/ppermute | solution.py:33
  58.7 5.4 %collective-permute-start.15 = (bf16[16,2048]{1,0:T(8,128)(2,1)S(1)}, bf16[16,2048]{1,0:T(8,128)(2,1)S(1)}, u32[]{:S(2)}, u32[]{:S(2)}) collective-permute-start(bf16[16,2048]{1,0:T(8,128)(2,1)S(1)} %get-tuple-element.63.refs_4_.refs_7_), channel_id=1, source_target_pairs={{0,3},{1,2},{2,1},{3,0},{4,7},{5,6},{6,5},{7,4},{8,11},{9,10},{10,... | collective-permute-start | bytes 196616 | tf_op jit(solution)/shard_map/ppermute | solution.py:33
  64.1 1.6 %collective-permute-start.16 = (bf16[256,512]{1,0:T(8,128)(2,1)S(1)}, bf16[256,512]{1,0:T(8,128)(2,1)S(1)}, u32[]{:S(2)}, u32[]{:S(2)}) collective-permute-start(bf16[256,512]{1,0:T(8,128)(2,1)S(1)} %fill_attend.3.mine), channel_id=1, source_target_pairs={{0,1},{1,0},{2,3},{3,2},{4,5},{5,4},{6,7},{7,6},{8,9},{9,8},{10,11... | collective-permute-start | bytes 786440 | tf_op jit(solution)/shard_map/ppermute | solution.py:20
  68.1 2.1 %collective-permute-start.18 = (bf16[256,1024]{1,0:T(8,128)(2,1)S(1)}, bf16[256,1024]{1,0:T(8,128)(2,1)S(1)}, u32[]{:S(2)}, u32[]{:S(2)}) collective-permute-start(bf16[256,1024]{1,0:T(8,128)(2,1)S(1)} %out_project.3.refs_2_), channel_id=1, source_target_pairs={{0,1},{1,0},{2,3},{3,2},{4,5},{5,4},{6,7},{7,6},{8,9},{9,8},{10,11... | collective-permute-start | bytes 1572872 | tf_op jit(solution)/shard_map/ppermute | solution.py:20
  68.3 2.5 %collective-permute-start.20 = (bf16[256,1024]{1,0:T(8,128)(2,1)S(1)}, bf16[256,1024]{1,0:T(8,128)(2,1)S(1)}, u32[]{:S(2)}, u32[]{:S(2)}) collective-permute-start(bf16[256,1024]{1,0:T(8,128)(2,1)S(1)} %collective-permute-done.19.refs_4_), channel_id=1, source_target_pairs={{0,1},{1,0},{2,3},{3,2},{4,5},{5,4},{6,7},{7,6},{8,9},{9,8},{10,11... | collective-permute-start | bytes 1572872 | tf_op jit(solution)/shard_map/ppermute | solution.py:20
  68.6 15.0 %collective-permute-start.17 = (bf16[256,1024]{1,0:T(8,128)(2,1)S(1)}, bf16[256,1024]{1,0:T(8,128)(2,1)S(1)}, u32[]{:S(2)}, u32[]{:S(2)}) collective-permute-start(bf16[256,1024]{1,0:T(8,128)(2,1)S(1)} %out_project.3.refs_2_), channel_id=1, source_target_pairs={{0,2},{1,3},{2,0},{3,1},{4,6},{5,7},{6,4},{7,5},{8,10},{9,11},{10,... | collective-permute-start | bytes 1572872 | tf_op jit(solution)/shard_map/ppermute | solution.py:26
  83.0 2.3 %collective-permute-start.25 = (bf16[128,2048]{1,0:T(8,128)(2,1)S(1)}, bf16[128,2048]{1,0:T(8,128)(2,1)S(1)}, u32[]{:S(2)}, u32[]{:S(2)}) collective-permute-start(bf16[128,2048]{1,0:T(8,128)(2,1)S(1)} %get-tuple-element.79), channel_id=1, source_target_pairs={{0,1},{1,0},{2,3},{3,2},{4,5},{5,4},{6,7},{7,6},{8,9},{9,8},{10,11... | collective-permute-start | bytes 1572872 | tf_op jit(solution)/shard_map/ppermute | solution.py:20
  83.2 3.4 %collective-permute-start.12 = (bf16[256,1024]{1,0:T(8,128)(2,1)S(1)}, bf16[256,1024]{1,0:T(8,128)(2,1)S(1)}, u32[]{:S(2)}, u32[]{:S(2)}) collective-permute-start(bf16[256,1024]{1,0:T(8,128)(2,1)S(1)} %out_project.2.refs_2_), channel_id=1, source_target_pairs={{0,1},{1,0},{2,3},{3,2},{4,5},{5,4},{6,7},{7,6},{8,9},{9,8},{10,11... | collective-permute-start | bytes 1572872 | tf_op jit(solution)/shard_map/ppermute | solution.py:20
  83.6 4.0 %collective-permute-start.21 = (bf16[256,1024]{1,0:T(8,128)(2,1)S(1)}, bf16[256,1024]{1,0:T(8,128)(2,1)S(1)}, u32[]{:S(2)}, u32[]{:S(2)}) collective-permute-start(bf16[256,1024]{1,0:T(8,128)(2,1)S(1)} %collective-permute-done.17.refs_4_), channel_id=1, source_target_pairs={{0,1},{1,0},{2,3},{3,2},{4,5},{5,4},{6,7},{7,6},{8,9},{9,8},{10,11... | collective-permute-start | bytes 1572872 | tf_op jit(solution)/shard_map/ppermute | solution.py:20
  83.7 12.7 %collective-permute-start.24 = (bf16[16,2048]{1,0:T(8,128)(2,1)S(1)}, bf16[16,2048]{1,0:T(8,128)(2,1)S(1)}, u32[]{:S(2)}, u32[]{:S(2)}) collective-permute-start(bf16[16,2048]{1,0:T(8,128)(2,1)S(1)} %get-tuple-element.76), channel_id=1, source_target_pairs={{0,3},{1,2},{2,1},{3,0},{4,7},{5,6},{6,5},{7,4},{8,11},{9,10},{10,... | collective-permute-start | bytes 196616 | tf_op jit(solution)/shard_map/ppermute | solution.py:33
  85.2 11.3 %collective-permute-start.23 = (bf16[16,2048]{1,0:T(8,128)(2,1)S(1)}, bf16[16,2048]{1,0:T(8,128)(2,1)S(1)}, u32[]{:S(2)}, u32[]{:S(2)}) collective-permute-start(bf16[16,2048]{1,0:T(8,128)(2,1)S(1)} %get-tuple-element.76), channel_id=1, source_target_pairs={{0,1},{1,0},{2,3},{3,2},{4,5},{5,4},{6,7},{7,6},{8,9},{9,8},{10,11... | collective-permute-start | bytes 196616 | tf_op jit(solution)/shard_map/ppermute | solution.py:33
  85.4 11.1 %collective-permute-start.22 = (bf16[16,2048]{1,0:T(8,128)(2,1)S(1)}, bf16[16,2048]{1,0:T(8,128)(2,1)S(1)}, u32[]{:S(2)}, u32[]{:S(2)}) collective-permute-start(bf16[16,2048]{1,0:T(8,128)(2,1)S(1)} %get-tuple-element.76), channel_id=1, source_target_pairs={{0,2},{1,3},{2,0},{3,1},{4,6},{5,7},{6,4},{7,5},{8,10},{9,11},{10,... | collective-permute-start | bytes 196616 | tf_op jit(solution)/shard_map/ppermute | solution.py:26
  86.7 19.4 %collective-permute-start.26 = (bf16[128,2048]{1,0:T(8,128)(2,1)S(1)}, bf16[128,2048]{1,0:T(8,128)(2,1)S(1)}, u32[]{:S(2)}, u32[]{:S(2)}) collective-permute-start(bf16[128,2048]{1,0:T(8,128)(2,1)S(1)} %add_convert_fusion.1), channel_id=1, source_target_pairs={{0,2},{1,3},{2,0},{3,1},{4,6},{5,7},{6,4},{7,5},{8,10},{9,11},{10,... | collective-permute-start | bytes 1572872 | tf_op jit(solution)/shard_map/ppermute | solution.py:26
  96.7 9.2 %collective-permute-start.29 = (bf16[4,2048]{1,0:T(4,128)(2,1)S(1)}, bf16[4,2048]{1,0:T(4,128)(2,1)S(1)}, u32[]{:S(2)}, u32[]{:S(2)}) collective-permute-start(bf16[4,2048]{1,0:T(4,128)(2,1)S(1)} %get-tuple-element.89), channel_id=1, source_target_pairs={{0,24},{4,28},{8,16},{12,20},{16,8},{20,12},{24,0},{28,4},{1,25},{... | collective-permute-start | bytes 49160 | tf_op jit(solution)/shard_map/ppermute | solution.py:45
  100.4 5.6 %collective-permute-start.28 = (bf16[4,2048]{1,0:T(4,128)(2,1)S(1)}, bf16[4,2048]{1,0:T(4,128)(2,1)S(1)}, u32[]{:S(2)}, u32[]{:S(2)}) collective-permute-start(bf16[4,2048]{1,0:T(4,128)(2,1)S(1)} %get-tuple-element.90), channel_id=1, source_target_pairs={{0,16},{4,20},{8,24},{12,28},{16,0},{20,4},{24,8},{28,12},{1,17},{... | collective-permute-start | bytes 49160 | tf_op jit(solution)/shard_map/ppermute | solution.py:45
  100.4 5.6 %collective-permute-start.27 = (bf16[4,2048]{1,0:T(4,128)(2,1)S(1)}, bf16[4,2048]{1,0:T(4,128)(2,1)S(1)}, u32[]{:S(2)}, u32[]{:S(2)}) collective-permute-start(bf16[4,2048]{1,0:T(4,128)(2,1)S(1)} %get-tuple-element.88), channel_id=1, source_target_pairs={{0,8},{4,12},{8,0},{12,4},{16,24},{20,28},{24,16},{28,20},{1,9},{5... | collective-permute-start | bytes 49160 | tf_op jit(solution)/shard_map/ppermute | solution.py:45
  106.0 4.4 %collective-permute-start.30 = (bf16[128,2048]{1,0:T(8,128)(2,1)S(1)}, bf16[128,2048]{1,0:T(8,128)(2,1)S(1)}, u32[]{:S(2)}, u32[]{:S(2)}) collective-permute-start(bf16[128,2048]{1,0:T(8,128)(2,1)S(1)} %get-tuple-element.81), channel_id=1, source_target_pairs={{0,1},{1,0},{2,3},{3,2},{4,5},{5,4},{6,7},{7,6},{8,9},{9,8},{10,11... | collective-permute-start | bytes 1572872 | tf_op jit(solution)/shard_map/ppermute | solution.py:20
  106.1 3.7 %collective-permute-start.31 = (bf16[2,2048]{1,0:T(2,128)(2,1)S(1)}, bf16[2,2048]{1,0:T(2,128)(2,1)S(1)}, u32[]{:S(2)}, u32[]{:S(2)}) collective-permute-start(bf16[2,2048]{1,0:T(2,128)(2,1)S(1)} %slice.29), channel_id=1, source_target_pairs={{0,4},{4,0},{8,12},{12,8},{16,20},{20,16},{24,28},{28,24},{1,5},{5... | collective-permute-start | bytes 24584 | tf_op jit(solution)/shard_map/ppermute | solution.py:45
  (17 other events, 200.9 us)

commit v8 on v5

--- a/solution.py
+++ b/solution.py
@@ -192,7 +192,7 @@
 
 def fill_kernel(groups, chips, place, query, cache_key, cache_value, *refs):
     new_keys, new_values, out = refs[:chips], refs[chips : 2 * chips], refs[-1]
-    scaling = 1.0 / math.sqrt(HD)
+    scaling = math.log2(math.e) / math.sqrt(HD)
     count = query.shape[0]
     stored = cache_key.shape[2]
     old_seen = lax.broadcasted_iota(jnp.int32, (1, stored), 1) < place[2]
@@ -200,25 +200,25 @@
         jnp.int32, (count, count), 0
     )
     across = (((1,), (1,)), ((), ()))
-    rows = jnp.concatenate([query[:, g * HD : (g + 1) * HD] for g in range(groups)], axis=0)
-    ahead = jnp.concatenate([ahead] * groups, axis=0)
-    scores = lax.dot_general(rows, cache_key[0, 0], across, preferred_element_type=jnp.float32)
-    scores = [jnp.where(old_seen, scores * scaling, NEGATIVE)]
-    for k in range(chips):
-        fresh = lax.dot_general(rows, new_keys[k][0], across, preferred_element_type=jnp.float32)
-        gap = (place[1] - place[3 + k]) * count
-        scores.append(jnp.where(ahead <= gap, fresh * scaling, NEGATIVE))
-    top = jnp.max(scores[0], axis=-1, keepdims=True)
-    for part in scores[1:]:
-        top = jnp.maximum(top, jnp.max(part, axis=-1, keepdims=True))
-    mix, total = 0.0, 0.0
-    for part, values in zip(scores, [cache_value[0, 0], *[v[0] for v in new_values]]):
-        weights = jnp.exp(part - top)
-        total += jnp.sum(weights, axis=-1, keepdims=True)
-        mix += jnp.dot(weights.astype(jnp.bfloat16), values, preferred_element_type=jnp.float32)
-    mix = (mix / total).astype(jnp.bfloat16)
     for g in range(groups):
-        out[:, g * HD : (g + 1) * HD] = mix[g * count : (g + 1) * count]
+        rows = query[:, g * HD : (g + 1) * HD]
+        scores = lax.dot_general(rows, cache_key[0, 0], across, preferred_element_type=jnp.float32)
+        scores = [jnp.where(old_seen, scores * scaling, NEGATIVE)]
+        for k in range(chips):
+            fresh = lax.dot_general(
+                rows, new_keys[k][0], across, preferred_element_type=jnp.float32
+            )
+            gap = (place[1] - place[3 + k]) * count
+            scores.append(jnp.where(ahead <= gap, fresh * scaling, NEGATIVE))
+        top = jnp.max(scores[0], axis=-1, keepdims=True)
+        for part in scores[1:]:
+            top = jnp.maximum(top, jnp.max(part, axis=-1, keepdims=True))
+        mix, total = 0.0, 0.0
+        for part, values in zip(scores, [cache_value[0, 0], *[v[0] for v in new_values]]):
+            weights = jnp.exp2(part - top)
+            total += jnp.sum(weights, axis=-1, keepdims=True)
+            mix += jnp.dot(weights.astype(jnp.bfloat16), values, preferred_element_type=jnp.float32)
+        out[:, g * HD : (g + 1) * HD] = (mix / total).astype(jnp.bfloat16)
 
 
 def fill_attend(place, query, cache, entries, heads, after=()):
@@ -243,7 +243,7 @@
             + [IN_PLACE] * len(after),
             out_specs=pl.BlockSpec((count, groups * HD), lambda j, s: (0, j)),
         ),
-        compiler_params=params(24),
+        compiler_params=params(12),
         cost_estimate=cost(8 * pairs * HD, 2 * cache.size, pairs),
         name="fill_attend",
     )(place, query, cache, cache, *entries, *entries, *after)
@@ -576,13 +576,12 @@
     prefill_cache, decode_cache = in_hbm(prefill_cache), in_hbm(decode_cache)
 
     mines = [prefill_rows] + [from_chip(prefill_rows, k) for k in range(1, chips)]
-    sibs = [swap_cores(rows) for rows in mines]
+    sibs = [swap_cores(prefill_rows)]
 
     low = max(dp_count // 4, 1)
     pool = [decode_rows] + [swap_groups(decode_rows, i) for i in range(1, low)]
-    pool = jnp.concatenate(pool, axis=0)
-    pool = [pool] + [swap_groups(pool, i * low) for i in range(1, dp_count // low)]
-    pool = jnp.concatenate(pool, axis=0)
+    near = jnp.concatenate(pool, axis=0)
+    pool = [near] + [swap_groups(near, i * low) for i in range(1, dp_count // low)]
     index = jnp.arange(dp_count * per_device, dtype=jnp.int32)
     origin = jnp.bitwise_xor(group_place, index // per_device)
     request = (origin * tensor_count + tensor_place) * per_device + index % per_device
@@ -598,21 +597,21 @@
     chooser = (jnp.arange(padded, dtype=jnp.int32)[:, None] == in_group[None, :]) & (
         in_group[None, :] < slots
     )
-    dealt = jnp.dot(
-        chooser.astype(jnp.bfloat16), pool, preferred_element_type=jnp.float32
-    ).astype(jnp.bfloat16)
-
     gain = attention_gain.reshape(1, width)
     tables = angle_tables(prefill_offset[0] + jnp.arange(tokens, dtype=jnp.int32))
     dec_tables = angle_tables(jnp.pad(cache_length, (0, padded - slots)))
     queries, entries, everything = [None] * chips, [None] * chips, None
     for k in range(chips):
         last = k == chips - 1
-        if last:
-            others = from_rest(dealt)
-            if k:
-                *others, queries[k - 1] = lax.optimization_barrier((*others, queries[k - 1]))
-            dealt = add(dealt, *others)
+        if k == 1:
+            far = pool[1:]
+            mines[1:], far, queries[0] = lax.optimization_barrier((mines[1:], far, queries[0]))
+            sibs += [swap_cores(rows) for rows in mines[1:]]
+            pool = jnp.concatenate([near, *far], axis=0)
+            dealt = jnp.dot(
+                chooser.astype(jnp.bfloat16), pool, preferred_element_type=jnp.float32
+            ).astype(jnp.bfloat16)
+            dealt = add(dealt, *from_rest(dealt))
         got = project(
             places[k],
             in_hbm(mines[k]),
@@ -625,7 +624,7 @@
             dealt if last else None,
             dec_tables if last else None,
             slots,
-            [queries[k - 1]] if k else [dealt],
+            [queries[k - 1]] if k else [near],
         )
         queries[k], entries[k], everything = got[:3]
         if last:

time: 106 us -> 110 us (1.038)
  local copies, waits for them, and re-layouts: 6.48 us -> 10.1 us
  waiting for transfers between devices: 9.8 us -> 13.2 us
  Pallas kernels: 57.3 us -> 54.6 us
    pallas_call x2, Pallas kernels: 12.2 us -> 9.46 us  [fill_attend(): pl.pallas_call(functools.partial(fill_kernel, groups, chips), out_shape=j...]
    ppermute x6, waiting for transfers between devices: 0.02 us -> 2.5 us  [from_other(): lax.ppermute(value, 'tensor', [(i, (i // 2 - step) % (count // 2) * 2 + 1...]
    unnamed x25 -> x35, local copies, waits for them, and re-layouts: 6.19 us -> 8.42 us
    ppermute x7, waiting for transfers between devices: 1.35 us -> 3.37 us  [from_chip(): lax.ppermute(value, 'tensor', [(i, (i // 2 - step) % chips * 2 + i % 2) f...]
    ppermute x7, starting transfers between devices: 7.81 us -> 9.39 us  [from_chip(): lax.ppermute(value, 'tensor', [(i, (i // 2 - step) % chips * 2 + i % 2) f...]
    concatenate x1, local copies, waits for them, and re-layouts: 0.08 us -> 1.5 us  [on_device(): pool = jnp.concatenate([near, *far], axis=0)]
    ppermute x11, waiting for transfers between devices: 5.27 us -> 4.16 us  [swap_cores(): return lax.ppermute(value, 'tensor', [(i, i ^ 1) for i in range(count)])]
  transfers between devices with their start and end apart: 32 -> 32, of which waited for: 7 -> 10; matrix products, arithmetic and copies ran while one was open for 10% -> 9% of each run, Pallas kernels for 48% -> 43%
where the time goes in v8:
time: 110 us
  Pallas kernels  54.6 us (50%)
  starting transfers between devices  25.1 us (23%)
  waiting for transfers between devices  13.2 us (12%)
  local copies, waits for them, and re-layouts  10.1 us (9%)
  other arithmetic  4.86 us (4%)
  between operations  1.74 us (2%)
    pallas_call x2, Pallas kernels, feed_forward(): pl.pallas_call(functools.partial(forward_kernel, split, chips, n_dec, len...  21 us
    ppermute x8, starting transfers between devices, swap_groups(): return lax.ppermute(value, 'dp', [(i, i ^ mask) for i in range(count)])  10.6 us
    pallas_call x2, Pallas kernels, project(): pl.pallas_call(functools.partial(project_kernel, n_dec, len(after), group...  10.6 us
    pallas_call x2, Pallas kernels, fill_attend(): pl.pallas_call(functools.partial(fill_kernel, groups, chips), out_shape=j...  9.46 us
    ppermute x7, starting transfers between devices, from_chip(): lax.ppermute(value, 'tensor', [(i, (i // 2 - step) % chips * 2 + i % 2) f...  9.39 us
    unnamed x35, local copies, waits for them, and re-layouts  8.42 us
    pallas_call x1, Pallas kernels, step_attend(): pl.pallas_call(functools.partial(step_kernel, heads), out_shape=jax.Shape...  6.51 us
    pallas_call x1, Pallas kernels, lower(): pl.pallas_call(functools.partial(lower_kernel, chunk), out_shape=[jax.Sha...  4.46 us
  transfers between devices with their start and end apart: 32, of which 10 were waited for; matrix products, arithmetic and copies ran while one was open for 9% of the time, Pallas kernels for 43%

profile of v8, /device:TPU:0, one launch (start us, length us, event | category | flops | bytes accessed | tf_op | source)
XLA Modules:
  0.0 109.9 jit_solution(17805637385645658049)
XLA Ops:
  0.7 3.0 %collective-permute-start.1 = (bf16[128,2048]{1,0:T(8,128)(2,1)}, bf16[128,2048]{1,0:T(8,128)(2,1)S(1)}, u32[]{:S(2)}, u32[]{:S(2)}) collective-permute-start(bf16[128,2048]{1,0:T(8,128)(2,1)} %refs_0_.3), channel_id=1, source_target_pairs={{0,2},{1,3},{2,0},{3,1},{4,6},{5,7},{6,4},{7,5},{8,10},{9,11},{10,... | collective-permute-start | bytes 1572872 | tf_op jit(solution)/shard_map/ppermute | solution.py:26
  3.7 1.5 %collective-permute-start.2 = (bf16[2,2048]{1,0:T(2,128)(2,1)}, bf16[2,2048]{1,0:T(2,128)(2,1)S(1)}, u32[]{:S(2)}, u32[]{:S(2)}) collective-permute-start(bf16[2,2048]{1,0:T(2,128)(2,1)} %param.15), channel_id=1, source_target_pairs={{0,4},{4,0},{8,12},{12,8},{16,20},{20,16},{24,28},{28,24},{1,5},{5... | collective-permute-start | bytes 24584 | tf_op jit(solution)/shard_map/ppermute | solution.py:45
  6.6 1.0 fusion
  8.9 5.4 %copy.19 = bf16[256,8,2,512]{3,1,2,0:T(8,128)(2,1)} copy(bf16[256,8,2,512]{3,2,1,0:T(2,128)(2,1)} %bitcast.16) | data formatting | bytes 8388608
  14.3 3.7 %collective-permute-start.5 = (bf16[4,2048]{1,0:T(4,128)(2,1)S(1)}, bf16[4,2048]{1,0:T(4,128)(2,1)S(1)}, u32[]{:S(2)}, u32[]{:S(2)}) collective-permute-start(bf16[4,2048]{1,0:T(4,128)(2,1)S(1)} %pad_maximum_fusion.2.refs_6_), channel_id=1, source_target_pairs={{0,24},{4,28},{8,16},{12,20},{16,8},{20,12},{24,0},{28,4},{1,25},{... | collective-permute-start | bytes 49160 | tf_op jit(solution)/shard_map/ppermute | solution.py:45
  18.8 5.0 %project.2 = (bf16[256,512]{1,0:T(8,128)(2,1)S(1)}, bf16[2,256,256]{2,1,0:T(8,128)(2,1)S(1)}, bf16[2,512,256]{2,1,0:T(8,128)(2,1)}) custom-call(s32[5]{0:T(128)S(1)} %stack.23.place, bf16[128,2048]{1,0:T(8,128)(2,1)} %refs_0_.3, bf16[128,2048]{1,0:T(8,128)(2,1)} %collective-permute-done.refs_1_, bf16[2048,1024]{1,0:T(8,128)(2,1)} %bitcast.14, ...), custom_call_target="tpu_custom_call" | custom-call | flops 1073741824 | bytes 6291456 | tf_op jit(solution)/shard_map/project/pallas_call | solution.py:170
  25.1 1.5 %concatenate.22 = bf16[16,2048]{1,0:T(8,128)(2,1)S(1)} concatenate(bf16[2,2048]{1,0:T(2,128)(2,1)S(1)} %copy-done.14, bf16[2,2048]{1,0:T(2,128)(2,1)S(1)} %collective-permute-done.2, bf16[4,2048]{1,0:T(4,128)(2,1)} %copy-done.16, bf16[4,2048]{1,0:T(4,128)(2,1)} %copy-done.15, bf16[4,2048]{1,0:T(4,128)(2,1)S(1)} %collective-permute-done.5), dimensions={0} | concatenate | bytes 131072 | tf_op jit(solution)/shard_map/concatenate | solution.py:610
  27.4 1.5 %collective-permute-start.7 = (bf16[16,2048]{1,0:T(8,128)(2,1)S(1)}, bf16[16,2048]{1,0:T(8,128)(2,1)S(1)}, u32[]{:S(2)}, u32[]{:S(2)}) collective-permute-start(bf16[16,2048]{1,0:T(8,128)(2,1)S(1)} %convolution_convert_fusion.1), channel_id=1, source_target_pairs={{0,2},{1,3},{2,0},{3,1},{4,6},{5,7},{6,4},{7,5},{8,10},{9,11},{10,... | collective-permute-start | bytes 196616 | tf_op jit(solution)/shard_map/ppermute | solution.py:26
  29.0 1.9 %collective-permute-done.9 = bf16[16,2048]{1,0:T(8,128)(2,1)S(1)} collective-permute-done((bf16[16,2048]{1,0:T(8,128)(2,1)S(1)}, bf16[16,2048]{1,0:T(8,128)(2,1)S(1)}, u32[]{:S(2)}, u32[]{:S(2)}) %collective-permute-start.9) | collective-permute-done | bytes 65568 | tf_op jit(solution)/shard_map/ppermute | solution.py:33
  30.9 1.4 %collective-permute-done.7 = bf16[16,2048]{1,0:T(8,128)(2,1)S(1)} collective-permute-done((bf16[16,2048]{1,0:T(8,128)(2,1)S(1)}, bf16[16,2048]{1,0:T(8,128)(2,1)S(1)}, u32[]{:S(2)}, u32[]{:S(2)}) %collective-permute-start.7) | collective-permute-done | bytes 65568 | tf_op jit(solution)/shard_map/ppermute | solution.py:26
  33.1 5.6 %project.3 = (bf16[256,512]{1,0:T(8,128)(2,1)S(1)}, bf16[2,256,256]{2,1,0:T(8,128)(2,1)S(1)}, bf16[2,512,256]{2,1,0:T(8,128)(2,1)}, f32[16,512]{1,0:T(8,128)S(1)}, bf16[2,8,256]{2,1,0:T(8,128)(2,1)}) custom-call(s32[5]{0:T(128)S(1)} %stack.24.place, bf16[128,2048]{1,0:T(8,128)(2,1)} %copy-done.2, ...), custom_call_target="tpu_custom_call", output_to_operand_aliasing={{2}: (11, {})} | custom-call | flops 1140850688 | bytes 6422528 | tf_op jit(solution)/shard_map/project/pallas_call | solution.py:170
  38.9 0.9 copy-done.12
  39.8 4.7 %fill_attend.2.mine = bf16[256,512]{1,0:T(8,128)(2,1)S(1)} custom-call(s32[5]{0:T(128)S(1)} %stack.23.place, bf16[256,512]{1,0:T(8,128)(2,1)S(1)} %get-tuple-element.41.refs_9_.query, bf16[2,1,1024,256]{3,2,1,0:T(8,128)(2,1)} %cache_value.3, bf16[2,1,1024,256]{3,2,1,0:T(8,128)(2,1)} %cache_value.3, bf16[2,256,256]{2,1,0:T(8,128)(2,1)S(1)} %copy-done.12, ...), custom_call_target="tpu_custom_call" | custom-call | flops 1610612736 | bytes 1048576 | tf_op jit(solution)/shard_map/fill_attend/pallas_call | solution.py:230
  45.1 1.2 %collective-permute-done.10.sib = bf16[256,512]{1,0:T(8,128)(2,1)S(1)} collective-permute-done((bf16[256,512]{1,0:T(8,128)(2,1)S(1)}, bf16[256,512]{1,0:T(8,128)(2,1)S(1)}, u32[]{:S(2)}, u32[]{:S(2)}) %collective-permute-start.10) | collective-permute-done | bytes 262176 | tf_op jit(solution)/shard_map/ppermute | solution.py:20
  46.3 1.3 %out_project.2.refs_2_ = bf16[256,1024]{1,0:T(8,128)(2,1)S(1)} custom-call(s32[5]{0:T(128)S(1)} %stack.23.place, bf16[256,512]{1,0:T(8,128)(2,1)S(1)} %fill_attend.2.mine, bf16[256,512]{1,0:T(8,128)(2,1)S(1)} %collective-permute-done.10.sib, bf16[512,2048]{1,0:T(8,128)(2,1)S(1)} %copy-done, bf16[512,2048]{1,0:T(8,128)(2,1)S(1)} %collective-permute-done.11.sib_weight), custom_call_target="tpu_custom_call" | custom-call | flops 536870912 | bytes 3670016 | tf_op jit(solution)/shard_map/out_project/pallas_call | solution.py:356
  47.6 1.0 collective-permute-start.19
  48.6 6.5 %step_attend.1.refs_4_.refs_7_ = bf16[16,2048]{1,0:T(8,128)(2,1)S(1)} custom-call(s32[8]{0:T(128)S(1)} %copy-done.10, f32[16,512]{1,0:T(8,128)S(1)} %get-tuple-element.54.query, bf16[2,8,256]{2,1,0:T(8,128)(2,1)S(1)} %copy-done.9, bf16[2,8,1024,256]{3,2,1,0:T(8,128)(2,1)} %cache.1, bf16[512,2048]{1,0:T(8,128)(2,1)} %weight.6), custom_call_target="tpu_custom_call" | custom-call | flops 67108864 | bytes 8388608 | tf_op jit(solution)/shard_map/step_attend/pallas_call | solution.py:325
  56.4 0.9 collective-permute-start.13
  57.3 4.8 %fill_attend.3.mine = bf16[256,512]{1,0:T(8,128)(2,1)S(1)} custom-call(s32[5]{0:T(128)S(1)} %stack.24.place, bf16[256,512]{1,0:T(8,128)(2,1)S(1)} %get-tuple-element.52.query, bf16[2,1,1024,256]{3,2,1,0:T(8,128)(2,1)} %cache_value.3, bf16[2,1,1024,256]{3,2,1,0:T(8,128)(2,1)} %cache_value.3, bf16[2,256,256]{2,1,0:T(8,128)(2,1)S(1)} %copy-done.13, ...), custom_call_target="tpu_custom_call" | custom-call | flops 1610612736 | bytes 1048576 | tf_op jit(solution)/shard_map/fill_attend/pallas_call | solution.py:230
  62.7 2.0 %collective-permute-done.13.refs_8_ = bf16[16,2048]{1,0:T(8,128)(2,1)S(1)} collective-permute-done((bf16[16,2048]{1,0:T(8,128)(2,1)S(1)}, bf16[16,2048]{1,0:T(8,128)(2,1)S(1)}, u32[]{:S(2)}, u32[]{:S(2)}) %collective-permute-start.13) | collective-permute-done | bytes 65568 | tf_op jit(solution)/shard_map/ppermute | solution.py:26
  64.7 1.5 %collective-permute-done.16.sib = bf16[256,512]{1,0:T(8,128)(2,1)S(1)} collective-permute-done((bf16[256,512]{1,0:T(8,128)(2,1)S(1)}, bf16[256,512]{1,0:T(8,128)(2,1)S(1)}, u32[]{:S(2)}, u32[]{:S(2)}) %collective-permute-start.16) | collective-permute-done | bytes 262176 | tf_op jit(solution)/shard_map/ppermute | solution.py:20
  66.2 1.2 %out_project.3.refs_2_ = bf16[256,1024]{1,0:T(8,128)(2,1)S(1)} custom-call(s32[5]{0:T(128)S(1)} %stack.24.place, bf16[256,512]{1,0:T(8,128)(2,1)S(1)} %fill_attend.3.mine, bf16[256,512]{1,0:T(8,128)(2,1)S(1)} %collective-permute-done.16.sib, bf16[512,2048]{1,0:T(8,128)(2,1)S(1)} %copy-done.1, bf16[512,2048]{1,0:T(8,128)(2,1)S(1)} %collective-permute-done.11.sib_weight), custom_call_target="tpu_custom_call" | custom-call | flops 536870912 | bytes 3670016 | tf_op jit(solution)/shard_map/out_project/pallas_call | solution.py:356
  68.1 0.9 collective-permute-start.17
  70.2 12.1 %feed_forward.2 = (bf16[128,2048]{1,0:T(8,128)(2,1)S(1)}, bf16[128,2048]{1,0:T(8,128)(2,1)S(1)}, bf16[128,2048]{1,0:T(8,128)(2,1)}, bf16[16,2048]{1,0:T(8,128)(2,1)S(1)}, bf16[16,2048]{1,0:T(8,128)(2,1)S(1)}) custom-call(s32[5]{0:T(128)S(1)} %stack.24.place, bf16[128,2048]{1,0:T(8,128)(2,1)S(1)} %copy-done.3, bf16[128,2048]{1,0:T(8,128)(2,1)S(1)} %copy-done.5, ...), custom_call_target="tpu_custom_call" | custom-call | flops 6845104128 | bytes 25165824 | tf_op jit(solution)/shard_map/feed_forward/pallas_call | solution.py:504
  84.3 0.9 collective-permute-start.22
  85.4 1.2 %collective-permute-start.26 = (bf16[128,2048]{1,0:T(8,128)(2,1)S(1)}, bf16[128,2048]{1,0:T(8,128)(2,1)S(1)}, u32[]{:S(2)}, u32[]{:S(2)}) collective-permute-start(bf16[128,2048]{1,0:T(8,128)(2,1)S(1)} %add_convert_fusion.1), channel_id=1, source_target_pairs={{0,2},{1,3},{2,0},{3,1},{4,6},{5,7},{6,4},{7,5},{8,10},{9,11},{10,... | collective-permute-start | bytes 1572872 | tf_op jit(solution)/shard_map/ppermute | solution.py:26
  86.6 8.9 %feed_forward.3 = (bf16[128,2048]{1,0:T(8,128)(2,1)S(1)}, bf16[256,2048]{1,0:T(8,128)(2,1)S(1)}) custom-call(s32[5]{0:T(128)S(1)} %stack.23.place, bf16[128,2048]{1,0:T(8,128)(2,1)S(1)} %copy-done.6, bf16[128,2048]{1,0:T(8,128)(2,1)} %collective-permute-done.refs_1_, bf16[256,1024]{1,0:T(8,128)(2,1)S(1)} %out_project.2.refs_2_, ...), custom_call_target="tpu_custom_call" | custom-call | flops 6442450944 | bytes 25165824 | tf_op jit(solution)/shard_map/feed_forward/pallas_call | solution.py:504
  95.7 1.4 %collective-permute-start.27 = (bf16[4,2048]{1,0:T(4,128)(2,1)S(1)}, bf16[4,2048]{1,0:T(4,128)(2,1)S(1)}, u32[]{:S(2)}, u32[]{:S(2)}) collective-permute-start(bf16[4,2048]{1,0:T(4,128)(2,1)S(1)} %get-tuple-element.78), channel_id=1, source_target_pairs={{0,8},{4,12},{8,0},{12,4},{16,24},{20,28},{24,16},{28,20},{1,9},{5... | collective-permute-start | bytes 49160 | tf_op jit(solution)/shard_map/ppermute | solution.py:45
  97.2 2.4 %collective-permute-start.29 = (bf16[4,2048]{1,0:T(4,128)(2,1)S(1)}, bf16[4,2048]{1,0:T(4,128)(2,1)S(1)}, u32[]{:S(2)}, u32[]{:S(2)}) collective-permute-start(bf16[4,2048]{1,0:T(4,128)(2,1)S(1)} %get-tuple-element.79), channel_id=1, source_target_pairs={{0,24},{4,28},{8,16},{12,20},{16,8},{20,12},{24,0},{28,4},{1,25},{... | collective-permute-start | bytes 49160 | tf_op jit(solution)/shard_map/ppermute | solution.py:45
  99.8 4.5 %lower.1 = (bf16[128,2048]{1,0:T(8,128)(2,1)S(1)}, bf16[128,2048]{1,0:T(8,128)(2,1)S(1)}) custom-call(bf16[256,2048]{1,0:T(8,128)(2,1)S(1)} %get-tuple-element.65.hidden, bf16[2048,2048]{1,0:T(8,128)(2,1)} %weight.7, bf16[16,2048]{1,0:T(8,128)(2,1)S(1)} %convolution_convert_fusion.refs_0_), custom_call_target="tpu_custom_call" | custom-call | flops 2147483648 | bytes 8388608 | tf_op jit(solution)/shard_map/lower/pallas_call | solution.py:468
  105.0 3.1 %collective-permute-done.31 = bf16[2,2048]{1,0:T(2,128)(2,1)S(1)} collective-permute-done((bf16[2,2048]{1,0:T(2,128)(2,1)S(1)}, bf16[2,2048]{1,0:T(2,128)(2,1)S(1)}, u32[]{:S(2)}, u32[]{:S(2)}) %collective-permute-start.31) | collective-permute-done | bytes 8224 | tf_op jit(solution)/shard_map/ppermute | solution.py:45
  108.8 1.1 %add_convert_fusion = bf16[128,2048]{1,0:T(8,128)(2,1)} fusion(bf16[128,2048]{1,0:T(8,128)(2,1)S(1)} %collective-permute-done.26, bf16[128,2048]{1,0:T(8,128)(2,1)S(1)} %collective-permute-done.30, bf16[128,2048]{1,0:T(8,128)(2,1)S(1)} %get-tuple-element.68, bf16[128,2048]{1,0:T(8,128)(2,1)S(1)} %get-tuple-element.62), kind=kLoop, calls=%fused_computation.2 | loop fusion | flops 2097152 | bytes 2621440 | tf_op jit(solution)/shard_map/convert_element_type | solution.py:536
  (100 shorter events, 14.2 us)
Async XLA Ops:
  0.7 23.9 %collective-permute-start.1 = (bf16[128,2048]{1,0:T(8,128)(2,1)}, bf16[128,2048]{1,0:T(8,128)(2,1)S(1)}, u32[]{:S(2)}, u32[]{:S(2)}) collective-permute-start(bf16[128,2048]{1,0:T(8,128)(2,1)} %refs_0_.3), channel_id=1, source_target_pairs={{0,2},{1,3},{2,0},{3,1},{4,6},{5,7},{6,4},{7,5},{8,10},{9,11},{10,... | collective-permute-start | bytes 1572872 | tf_op jit(solution)/shard_map/ppermute | solution.py:26
  3.7 15.1 %collective-permute-start = (bf16[128,2048]{1,0:T(8,128)(2,1)}, bf16[128,2048]{1,0:T(8,128)(2,1)}, u32[]{:S(2)}, u32[]{:S(2)}) collective-permute-start(bf16[128,2048]{1,0:T(8,128)(2,1)} %refs_0_.3), channel_id=1, source_target_pairs={{0,1},{1,0},{2,3},{3,2},{4,5},{5,4},{6,7},{7,6},{8,9},{9,8},{10,11... | collective-permute-start | bytes 1572872 | tf_op jit(solution)/shard_map/ppermute | solution.py:20
  3.7 10.6 %collective-permute-start.2 = (bf16[2,2048]{1,0:T(2,128)(2,1)}, bf16[2,2048]{1,0:T(2,128)(2,1)S(1)}, u32[]{:S(2)}, u32[]{:S(2)}) collective-permute-start(bf16[2,2048]{1,0:T(2,128)(2,1)} %param.15), channel_id=1, source_target_pairs={{0,4},{4,0},{8,12},{12,8},{16,20},{20,16},{24,28},{28,24},{1,5},{5... | collective-permute-start | bytes 24584 | tf_op jit(solution)/shard_map/ppermute | solution.py:45
  14.3 10.1 %collective-permute-start.5 = (bf16[4,2048]{1,0:T(4,128)(2,1)S(1)}, bf16[4,2048]{1,0:T(4,128)(2,1)S(1)}, u32[]{:S(2)}, u32[]{:S(2)}) collective-permute-start(bf16[4,2048]{1,0:T(4,128)(2,1)S(1)} %pad_maximum_fusion.2.refs_6_), channel_id=1, source_target_pairs={{0,24},{4,28},{8,16},{12,20},{16,8},{20,12},{24,0},{28,4},{1,25},{... | collective-permute-start | bytes 49160 | tf_op jit(solution)/shard_map/ppermute | solution.py:45
  18.0 6.5 %collective-permute-start.4 = (bf16[4,2048]{1,0:T(4,128)(2,1)S(1)}, bf16[4,2048]{1,0:T(4,128)(2,1)S(1)}, u32[]{:S(2)}, u32[]{:S(2)}) collective-permute-start(bf16[4,2048]{1,0:T(4,128)(2,1)S(1)} %pad_maximum_fusion.2.refs_6_), channel_id=1, source_target_pairs={{0,16},{4,20},{8,24},{12,28},{16,0},{20,4},{24,8},{28,12},{1,17},{... | collective-permute-start | bytes 49160 | tf_op jit(solution)/shard_map/ppermute | solution.py:45
  18.0 6.5 %collective-permute-start.3 = (bf16[4,2048]{1,0:T(4,128)(2,1)S(1)}, bf16[4,2048]{1,0:T(4,128)(2,1)S(1)}, u32[]{:S(2)}, u32[]{:S(2)}) collective-permute-start(bf16[4,2048]{1,0:T(4,128)(2,1)S(1)} %pad_maximum_fusion.2.refs_6_), channel_id=1, source_target_pairs={{0,8},{4,12},{8,0},{12,4},{16,24},{20,28},{24,16},{28,20},{1,9},{5... | collective-permute-start | bytes 49160 | tf_op jit(solution)/shard_map/ppermute | solution.py:45
  26.7 4.2 %collective-permute-start.9 = (bf16[16,2048]{1,0:T(8,128)(2,1)S(1)}, bf16[16,2048]{1,0:T(8,128)(2,1)S(1)}, u32[]{:S(2)}, u32[]{:S(2)}) collective-permute-start(bf16[16,2048]{1,0:T(8,128)(2,1)S(1)} %convolution_convert_fusion.1), channel_id=1, source_target_pairs={{0,3},{1,2},{2,1},{3,0},{4,7},{5,6},{6,5},{7,4},{8,11},{9,10},{10,... | collective-permute-start | bytes 196616 | tf_op jit(solution)/shard_map/ppermute | solution.py:33
  26.8 4.1 %collective-permute-start.8 = (bf16[16,2048]{1,0:T(8,128)(2,1)S(1)}, bf16[16,2048]{1,0:T(8,128)(2,1)S(1)}, u32[]{:S(2)}, u32[]{:S(2)}) collective-permute-start(bf16[16,2048]{1,0:T(8,128)(2,1)S(1)} %convolution_convert_fusion.1), channel_id=1, source_target_pairs={{0,1},{1,0},{2,3},{3,2},{4,5},{5,4},{6,7},{7,6},{8,9},{9,8},{10,11... | collective-permute-start | bytes 196616 | tf_op jit(solution)/shard_map/ppermute | solution.py:33
  27.4 4.8 %collective-permute-start.7 = (bf16[16,2048]{1,0:T(8,128)(2,1)S(1)}, bf16[16,2048]{1,0:T(8,128)(2,1)S(1)}, u32[]{:S(2)}, u32[]{:S(2)}) collective-permute-start(bf16[16,2048]{1,0:T(8,128)(2,1)S(1)} %convolution_convert_fusion.1), channel_id=1, source_target_pairs={{0,2},{1,3},{2,0},{3,1},{4,6},{5,7},{6,4},{7,5},{8,10},{9,11},{10,... | collective-permute-start | bytes 196616 | tf_op jit(solution)/shard_map/ppermute | solution.py:26
  28.9 3.4 %collective-permute-start.6 = (bf16[128,2048]{1,0:T(8,128)(2,1)S(1)}, bf16[128,2048]{1,0:T(8,128)(2,1)S(1)}, u32[]{:S(2)}, u32[]{:S(2)}) collective-permute-start(bf16[128,2048]{1,0:T(8,128)(2,1)S(1)} %collective-permute-done.1.refs_0_), channel_id=1, source_target_pairs={{0,1},{1,0},{2,3},{3,2},{4,5},{5,4},{6,7},{7,6},{8,9},{9,8},{10,11... | collective-permute-start | bytes 1572872 | tf_op jit(solution)/shard_map/ppermute | solution.py:20
  38.8 7.5 %collective-permute-start.11 = (bf16[512,2048]{1,0:T(8,128)(2,1)S(1)}, bf16[512,2048]{1,0:T(8,128)(2,1)S(1)}, u32[]{:S(2)}, u32[]{:S(2)}) collective-permute-start(bf16[512,2048]{1,0:T(8,128)(2,1)S(1)} %copy-done), channel_id=1, source_target_pairs={{0,1},{1,0},{2,3},{3,2},{4,5},{5,4},{6,7},{7,6},{8,9},{9,8},{10,11... | collective-permute-start | bytes 6291464 | tf_op jit(solution)/shard_map/ppermute | solution.py:20
  44.6 1.7 %collective-permute-start.10 = (bf16[256,512]{1,0:T(8,128)(2,1)S(1)}, bf16[256,512]{1,0:T(8,128)(2,1)S(1)}, u32[]{:S(2)}, u32[]{:S(2)}) collective-permute-start(bf16[256,512]{1,0:T(8,128)(2,1)S(1)} %fill_attend.2.mine), channel_id=1, source_target_pairs={{0,1},{1,0},{2,3},{3,2},{4,5},{5,4},{6,7},{7,6},{8,9},{9,8},{10,11... | collective-permute-start | bytes 786440 | tf_op jit(solution)/shard_map/ppermute | solution.py:20
  47.6 20.1 %collective-permute-start.19 = (bf16[256,1024]{1,0:T(8,128)(2,1)S(1)}, bf16[256,1024]{1,0:T(8,128)(2,1)S(1)}, u32[]{:S(2)}, u32[]{:S(2)}) collective-permute-start(bf16[256,1024]{1,0:T(8,128)(2,1)S(1)} %out_project.2.refs_2_), channel_id=1, source_target_pairs={{0,2},{1,3},{2,0},{3,1},{4,6},{5,7},{6,4},{7,5},{8,10},{9,11},{10,... | collective-permute-start | bytes 1572872 | tf_op jit(solution)/shard_map/ppermute | solution.py:26
  55.1 7.6 %collective-permute-start.15 = (bf16[16,2048]{1,0:T(8,128)(2,1)S(1)}, bf16[16,2048]{1,0:T(8,128)(2,1)S(1)}, u32[]{:S(2)}, u32[]{:S(2)}) collective-permute-start(bf16[16,2048]{1,0:T(8,128)(2,1)S(1)} %step_attend.1.refs_4_.refs_7_), channel_id=1, source_target_pairs={{0,3},{1,2},{2,1},{3,0},{4,7},{5,6},{6,5},{7,4},{8,11},{9,10},{10,... | collective-permute-start | bytes 196616 | tf_op jit(solution)/shard_map/ppermute | solution.py:33
  56.0 6.7 %collective-permute-start.14 = (bf16[16,2048]{1,0:T(8,128)(2,1)S(1)}, bf16[16,2048]{1,0:T(8,128)(2,1)S(1)}, u32[]{:S(2)}, u32[]{:S(2)}) collective-permute-start(bf16[16,2048]{1,0:T(8,128)(2,1)S(1)} %step_attend.1.refs_4_.refs_7_), channel_id=1, source_target_pairs={{0,1},{1,0},{2,3},{3,2},{4,5},{5,4},{6,7},{7,6},{8,9},{9,8},{10,11... | collective-permute-start | bytes 196616 | tf_op jit(solution)/shard_map/ppermute | solution.py:33
  56.4 8.2 %collective-permute-start.13 = (bf16[16,2048]{1,0:T(8,128)(2,1)S(1)}, bf16[16,2048]{1,0:T(8,128)(2,1)S(1)}, u32[]{:S(2)}, u32[]{:S(2)}) collective-permute-start(bf16[16,2048]{1,0:T(8,128)(2,1)S(1)} %step_attend.1.refs_4_.refs_7_), channel_id=1, source_target_pairs={{0,2},{1,3},{2,0},{3,1},{4,6},{5,7},{6,4},{7,5},{8,10},{9,11},{10,... | collective-permute-start | bytes 196616 | tf_op jit(solution)/shard_map/ppermute | solution.py:26
  64.7 1.5 %collective-permute-start.16 = (bf16[256,512]{1,0:T(8,128)(2,1)S(1)}, bf16[256,512]{1,0:T(8,128)(2,1)S(1)}, u32[]{:S(2)}, u32[]{:S(2)}) collective-permute-start(bf16[256,512]{1,0:T(8,128)(2,1)S(1)} %fill_attend.3.mine), channel_id=1, source_target_pairs={{0,1},{1,0},{2,3},{3,2},{4,5},{5,4},{6,7},{7,6},{8,9},{9,8},{10,11... | collective-permute-start | bytes 786440 | tf_op jit(solution)/shard_map/ppermute | solution.py:20
  67.5 2.0 %collective-permute-start.18 = (bf16[256,1024]{1,0:T(8,128)(2,1)S(1)}, bf16[256,1024]{1,0:T(8,128)(2,1)S(1)}, u32[]{:S(2)}, u32[]{:S(2)}) collective-permute-start(bf16[256,1024]{1,0:T(8,128)(2,1)S(1)} %out_project.3.refs_2_), channel_id=1, source_target_pairs={{0,1},{1,0},{2,3},{3,2},{4,5},{5,4},{6,7},{7,6},{8,9},{9,8},{10,11... | collective-permute-start | bytes 1572872 | tf_op jit(solution)/shard_map/ppermute | solution.py:20
  67.7 2.5 %collective-permute-start.20 = (bf16[256,1024]{1,0:T(8,128)(2,1)S(1)}, bf16[256,1024]{1,0:T(8,128)(2,1)S(1)}, u32[]{:S(2)}, u32[]{:S(2)}) collective-permute-start(bf16[256,1024]{1,0:T(8,128)(2,1)S(1)} %collective-permute-done.19.refs_4_), channel_id=1, source_target_pairs={{0,1},{1,0},{2,3},{3,2},{4,5},{5,4},{6,7},{7,6},{8,9},{9,8},{10,11... | collective-permute-start | bytes 1572872 | tf_op jit(solution)/shard_map/ppermute | solution.py:20
  68.1 14.9 %collective-permute-start.17 = (bf16[256,1024]{1,0:T(8,128)(2,1)S(1)}, bf16[256,1024]{1,0:T(8,128)(2,1)S(1)}, u32[]{:S(2)}, u32[]{:S(2)}) collective-permute-start(bf16[256,1024]{1,0:T(8,128)(2,1)S(1)} %out_project.3.refs_2_), channel_id=1, source_target_pairs={{0,2},{1,3},{2,0},{3,1},{4,6},{5,7},{6,4},{7,5},{8,10},{9,11},{10,... | collective-permute-start | bytes 1572872 | tf_op jit(solution)/shard_map/ppermute | solution.py:26
  82.4 2.0 %collective-permute-start.25 = (bf16[128,2048]{1,0:T(8,128)(2,1)S(1)}, bf16[128,2048]{1,0:T(8,128)(2,1)S(1)}, u32[]{:S(2)}, u32[]{:S(2)}) collective-permute-start(bf16[128,2048]{1,0:T(8,128)(2,1)S(1)} %get-tuple-element.70), channel_id=1, source_target_pairs={{0,1},{1,0},{2,3},{3,2},{4,5},{5,4},{6,7},{7,6},{8,9},{9,8},{10,11... | collective-permute-start | bytes 1572872 | tf_op jit(solution)/shard_map/ppermute | solution.py:20
  82.6 2.8 %collective-permute-start.12 = (bf16[256,1024]{1,0:T(8,128)(2,1)S(1)}, bf16[256,1024]{1,0:T(8,128)(2,1)S(1)}, u32[]{:S(2)}, u32[]{:S(2)}) collective-permute-start(bf16[256,1024]{1,0:T(8,128)(2,1)S(1)} %out_project.2.refs_2_), channel_id=1, source_target_pairs={{0,1},{1,0},{2,3},{3,2},{4,5},{5,4},{6,7},{7,6},{8,9},{9,8},{10,11... | collective-permute-start | bytes 1572872 | tf_op jit(solution)/shard_map/ppermute | solution.py:20
  82.9 3.6 %collective-permute-start.21 = (bf16[256,1024]{1,0:T(8,128)(2,1)S(1)}, bf16[256,1024]{1,0:T(8,128)(2,1)S(1)}, u32[]{:S(2)}, u32[]{:S(2)}) collective-permute-start(bf16[256,1024]{1,0:T(8,128)(2,1)S(1)} %collective-permute-done.17.refs_4_), channel_id=1, source_target_pairs={{0,1},{1,0},{2,3},{3,2},{4,5},{5,4},{6,7},{7,6},{8,9},{9,8},{10,11... | collective-permute-start | bytes 1572872 | tf_op jit(solution)/shard_map/ppermute | solution.py:20
  83.1 12.4 %collective-permute-start.24 = (bf16[16,2048]{1,0:T(8,128)(2,1)S(1)}, bf16[16,2048]{1,0:T(8,128)(2,1)S(1)}, u32[]{:S(2)}, u32[]{:S(2)}) collective-permute-start(bf16[16,2048]{1,0:T(8,128)(2,1)S(1)} %get-tuple-element.67), channel_id=1, source_target_pairs={{0,3},{1,2},{2,1},{3,0},{4,7},{5,6},{6,5},{7,4},{8,11},{9,10},{10,... | collective-permute-start | bytes 196616 | tf_op jit(solution)/shard_map/ppermute | solution.py:33
  84.0 11.5 %collective-permute-start.23 = (bf16[16,2048]{1,0:T(8,128)(2,1)S(1)}, bf16[16,2048]{1,0:T(8,128)(2,1)S(1)}, u32[]{:S(2)}, u32[]{:S(2)}) collective-permute-start(bf16[16,2048]{1,0:T(8,128)(2,1)S(1)} %get-tuple-element.67), channel_id=1, source_target_pairs={{0,1},{1,0},{2,3},{3,2},{4,5},{5,4},{6,7},{7,6},{8,9},{9,8},{10,11... | collective-permute-start | bytes 196616 | tf_op jit(solution)/shard_map/ppermute | solution.py:33
  84.3 11.1 %collective-permute-start.22 = (bf16[16,2048]{1,0:T(8,128)(2,1)S(1)}, bf16[16,2048]{1,0:T(8,128)(2,1)S(1)}, u32[]{:S(2)}, u32[]{:S(2)}) collective-permute-start(bf16[16,2048]{1,0:T(8,128)(2,1)S(1)} %get-tuple-element.67), channel_id=1, source_target_pairs={{0,2},{1,3},{2,0},{3,1},{4,6},{5,7},{6,4},{7,5},{8,10},{9,11},{10,... | collective-permute-start | bytes 196616 | tf_op jit(solution)/shard_map/ppermute | solution.py:26
  85.4 19.0 %collective-permute-start.26 = (bf16[128,2048]{1,0:T(8,128)(2,1)S(1)}, bf16[128,2048]{1,0:T(8,128)(2,1)S(1)}, u32[]{:S(2)}, u32[]{:S(2)}) collective-permute-start(bf16[128,2048]{1,0:T(8,128)(2,1)S(1)} %add_convert_fusion.1), channel_id=1, source_target_pairs={{0,2},{1,3},{2,0},{3,1},{4,6},{5,7},{6,4},{7,5},{8,10},{9,11},{10,... | collective-permute-start | bytes 1572872 | tf_op jit(solution)/shard_map/ppermute | solution.py:26
  95.7 8.6 %collective-permute-start.27 = (bf16[4,2048]{1,0:T(4,128)(2,1)S(1)}, bf16[4,2048]{1,0:T(4,128)(2,1)S(1)}, u32[]{:S(2)}, u32[]{:S(2)}) collective-permute-start(bf16[4,2048]{1,0:T(4,128)(2,1)S(1)} %get-tuple-element.78), channel_id=1, source_target_pairs={{0,8},{4,12},{8,0},{12,4},{16,24},{20,28},{24,16},{28,20},{1,9},{5... | collective-permute-start | bytes 49160 | tf_op jit(solution)/shard_map/ppermute | solution.py:45
  97.2 7.1 %collective-permute-start.29 = (bf16[4,2048]{1,0:T(4,128)(2,1)S(1)}, bf16[4,2048]{1,0:T(4,128)(2,1)S(1)}, u32[]{:S(2)}, u32[]{:S(2)}) collective-permute-start(bf16[4,2048]{1,0:T(4,128)(2,1)S(1)} %get-tuple-element.79), channel_id=1, source_target_pairs={{0,24},{4,28},{8,16},{12,20},{16,8},{20,12},{24,0},{28,4},{1,25},{... | collective-permute-start | bytes 49160 | tf_op jit(solution)/shard_map/ppermute | solution.py:45
  99.6 4.8 %collective-permute-start.28 = (bf16[4,2048]{1,0:T(4,128)(2,1)S(1)}, bf16[4,2048]{1,0:T(4,128)(2,1)S(1)}, u32[]{:S(2)}, u32[]{:S(2)}) collective-permute-start(bf16[4,2048]{1,0:T(4,128)(2,1)S(1)} %get-tuple-element.80), channel_id=1, source_target_pairs={{0,16},{4,20},{8,24},{12,28},{16,0},{20,4},{24,8},{28,12},{1,17},{... | collective-permute-start | bytes 49160 | tf_op jit(solution)/shard_map/ppermute | solution.py:45
  104.4 4.4 %collective-permute-start.30 = (bf16[128,2048]{1,0:T(8,128)(2,1)S(1)}, bf16[128,2048]{1,0:T(8,128)(2,1)S(1)}, u32[]{:S(2)}, u32[]{:S(2)}) collective-permute-start(bf16[128,2048]{1,0:T(8,128)(2,1)S(1)} %get-tuple-element.72), channel_id=1, source_target_pairs={{0,1},{1,0},{2,3},{3,2},{4,5},{5,4},{6,7},{7,6},{8,9},{9,8},{10,11... | collective-permute-start | bytes 1572872 | tf_op jit(solution)/shard_map/ppermute | solution.py:20
  104.5 3.7 %collective-permute-start.31 = (bf16[2,2048]{1,0:T(2,128)(2,1)S(1)}, bf16[2,2048]{1,0:T(2,128)(2,1)S(1)}, u32[]{:S(2)}, u32[]{:S(2)}) collective-permute-start(bf16[2,2048]{1,0:T(2,128)(2,1)S(1)} %slice.29), channel_id=1, source_target_pairs={{0,4},{4,0},{8,12},{12,8},{16,20},{20,16},{24,28},{28,24},{1,5},{5... | collective-permute-start | bytes 24584 | tf_op jit(solution)/shard_map/ppermute | solution.py:45
  (17 other events, 205.1 us)

commit v9 on v8

--- a/solution.py
+++ b/solution.py
@@ -72,6 +72,10 @@
 
 def in_hbm(value):
     return pltpu.with_memory_space_constraint(value, pltpu.HBM)
+
+
+def stays_in_vmem(shape):
+    return pltpu.VMEM(shape, jnp.bfloat16)
 
 
 VMEM_WHOLE = pl.BlockSpec(memory_space=pltpu.VMEM)
@@ -364,7 +368,7 @@
     )(place, mine, sib, weight, sib_weight, *after)
 
 
-def forward_kernel(split, chips, n_dec, n_after, chunk, place, *refs):
+def forward_kernel(loads, chips, n_dec, n_weights, n_after, chunk, place, *refs):
     refs = list(refs)
     mine, sib = refs[:2]
     shares = refs[2 : 2 + 2 * chips]
@@ -372,34 +376,45 @@
     if n_dec:
         dec, dec_shares = refs[0], refs[1 : 1 + 2 * chips]
         refs = refs[1 + 2 * chips :]
-    gain, *weights = refs[: 3 if split else 4]
-    refs = refs[(3 if split else 4) + n_after :]
+    split = n_weights == 2
+    gain, *weights = refs[: 1 + n_weights]
+    refs = refs[1 + n_weights + n_after :]
     if split:
         resid, hidden = refs[:2]
-        held, inner, gate, up, arrived = refs[2:]
-        down = ()
+        held, inner = refs[2:]
     else:
         keep, give, resid = refs[:3]
         refs = refs[3:]
         if n_dec:
             dec_out, dec_resid = refs[:2]
             refs = refs[2:]
-        held, inner, hidden, gate, up, down, arrived = refs
-    copies = [
-        [
-            pltpu.make_async_copy(
-                source.at[:, pl.ds(i * chunk, chunk)], target.at[i], arrived.at[w, i]
-            )
-            for i in range(target.shape[0])
+        if loads:
+            weights, refs = list(zip(weights, refs[:3])), refs[3:]
+        held, inner, hidden = refs[:3]
+    copies = []
+    if loads:
+        arrived = refs[3]
+        copies = [
+            [
+                pltpu.make_async_copy(
+                    source.at[:, pl.ds(i * chunk, chunk)], target.at[i], arrived.at[w, i]
+                )
+                for i in range(target.shape[0])
+            ]
+            for w, (source, target) in enumerate(weights)
         ]
-        for w, (source, target) in enumerate(zip(weights, [gate, up, down]))
-    ]
-    for pair in zip(copies[0], copies[1]):
-        for copy in pair:
+        weights = [target for _, target in weights]
+        for pair in zip(copies[0], copies[1]):
+            for copy in pair:
+                copy.start()
+        for copy in copies[2]:
             copy.start()
-    for rest in copies[2:]:
-        for copy in rest:
-            copy.start()
+
+    def ready(w, i):
+        if loads:
+            copies[w][i].wait()
+        return weights[w][i]
+
     piece = mine.shape[0]
     half = shares[0].shape[1]
     core = place[0]
@@ -425,17 +440,14 @@
     if n_dec:
         dec_resid[...] = held[2 * piece :, :]
 
-    for i in range(gate.shape[0]):
+    for i in range(weights[0].shape[0]):
         at = slice(i * chunk, (i + 1) * chunk)
-        copies[0][i].wait()
-        gated = jnp.dot(inner[...], gate[i], preferred_element_type=jnp.float32)
-        copies[1][i].wait()
-        raised = jnp.dot(inner[...], up[i], preferred_element_type=jnp.float32)
+        gated = jnp.dot(inner[...], ready(0, i), preferred_element_type=jnp.float32)
+        raised = jnp.dot(inner[...], ready(1, i), preferred_element_type=jnp.float32)
         hidden[:, at] = (gated / (1.0 + jnp.exp(-gated)) * raised).astype(jnp.bfloat16)
-    for i in range(0 if split else down.shape[0]):
+    for i in range(0 if split else weights[2].shape[0]):
         at = slice(i * chunk, (i + 1) * chunk)
-        copies[2][i].wait()
-        part = jnp.dot(hidden[...], down[i], preferred_element_type=jnp.float32)
+        part = jnp.dot(hidden[...], ready(2, i), preferred_element_type=jnp.float32)
         part = part.astype(jnp.bfloat16)
         keep[:, at] = part[:piece]
         give[:, at] = part[piece : 2 * piece]
@@ -443,81 +455,69 @@
             dec_out[:, at] = part[2 * piece :]
 
 
-def lower_kernel(chunk, hidden, weight, *refs):
-    keep, give, down, arrived = refs[-4:]
+def lower_kernel(hidden, down, *refs):
+    keep, give = refs[-2:]
     piece = keep.shape[0]
-    copies = [
-        pltpu.make_async_copy(weight.at[:, pl.ds(i * chunk, chunk)], down.at[i], arrived.at[i])
-        for i in range(down.shape[0])
-    ]
-    for copy in copies:
-        copy.start()
-    for i, copy in enumerate(copies):
+    chunk = down.shape[2]
+    for i in range(down.shape[0]):
         at = slice(i * chunk, (i + 1) * chunk)
-        copy.wait()
         part = jnp.dot(hidden[...], down[i], preferred_element_type=jnp.float32)
         part = part.astype(jnp.bfloat16)
         keep[:, at] = part[:piece]
         give[:, at] = part[piece:]
 
 
-def lower(hidden, weight, after):
+def lower(hidden, down, after):
     rows, units = hidden.shape
-    width = weight.shape[1]
-    chunk = width // 4
+    width = down.shape[0] * down.shape[2]
     return pl.pallas_call(
-        functools.partial(lower_kernel, chunk),
+        lower_kernel,
         out_shape=[jax.ShapeDtypeStruct((rows // 2, width), jnp.bfloat16)] * 2,
-        in_specs=[VMEM_WHOLE] + [IN_PLACE] * (1 + len(after)),
+        in_specs=[VMEM_WHOLE] * 2 + [IN_PLACE] * len(after),
         out_specs=[VMEM_WHOLE] * 2,
-        scratch_shapes=[
-            pltpu.VMEM((4, units, chunk), jnp.bfloat16),
-            pltpu.SemaphoreType.DMA((4,)),
-        ],
-        compiler_params=params(24),
+        compiler_params=params(8),
         cost_estimate=cost(2 * rows * width * units, 2 * width * units),
         name="lower",
-    )(hidden, weight, *after)
-
-
-def feed_forward(
-    place, mine, sib, shares, gain, gate, up, down=None, dec=None, dec_shares=None, after=()
-):
+    )(hidden, down, *after)
+
+
+def feed_forward(place, mine, sib, shares, gain, weights, loads, dec=None, dec_shares=None, after=()):
     piece, width = mine.shape
     chips = len(shares) // 2
-    units = gate.shape[1]
-    chunks = 4
-    chunk = width // chunks
     n_dec = 0 if dec is None else dec.shape[0]
     rows = 2 * piece + n_dec
     args = [mine, sib, *shares]
     if n_dec:
         args += [dec, *dec_shares]
-    n_whole = len(args) + 1
-    split = down is None
-    args += [gain, gate, up] + [down] * (not split)
+    args += [gain]
+    split = len(weights) == 2
+    chunk = width // 4 if loads else weights[0].shape[2]
+    units = weights[0].shape[1] if loads else weights[0].shape[0] * chunk
     if split:
         shapes = [(piece, width), (rows, units)]
     else:
         shapes = [(n, width) for n in [piece] * 3 + [n_dec] * 2 * bool(n_dec)]
-    n_weights = 2 if split else 3
+    out_shape = [jax.ShapeDtypeStruct(shape, jnp.bfloat16) for shape in shapes]
+    scratch = [pltpu.VMEM((rows, width), jnp.bfloat16)] * 2
+    if not split:
+        scratch.append(pltpu.VMEM((rows, units), jnp.bfloat16))
+    if loads:
+        out_shape += [stays_in_vmem((units // chunk, width, chunk))] * 2
+        out_shape += [stays_in_vmem((width // chunk, units, chunk))]
+        scratch.append(pltpu.SemaphoreType.DMA((3, max(units, width) // chunk)))
     return pl.pallas_call(
-        functools.partial(forward_kernel, split, chips, n_dec, len(after), chunk),
-        out_shape=[jax.ShapeDtypeStruct(shape, jnp.bfloat16) for shape in shapes],
-        in_specs=[SMEM_WHOLE] + [VMEM_WHOLE] * n_whole + [IN_PLACE] * (n_weights + len(after)),
-        out_specs=[VMEM_WHOLE] * len(shapes),
-        scratch_shapes=[
-            pltpu.VMEM((rows, width), jnp.bfloat16),
-            pltpu.VMEM((rows, width), jnp.bfloat16),
-        ]
-        + [pltpu.VMEM((rows, units), jnp.bfloat16)] * (not split)
-        + [pltpu.VMEM((units // chunk, width, chunk), jnp.bfloat16)] * 2
-        + [pltpu.VMEM((chunks, units, chunk), jnp.bfloat16)] * (not split)
-        + [pltpu.SemaphoreType.DMA((n_weights, chunks))],
-        compiler_params=params(40),
+        functools.partial(forward_kernel, loads, chips, n_dec, len(weights), len(after), chunk),
+        out_shape=out_shape,
+        in_specs=[SMEM_WHOLE]
+        + [VMEM_WHOLE] * len(args)
+        + [IN_PLACE if loads else VMEM_WHOLE] * len(weights)
+        + [IN_PLACE] * len(after),
+        out_specs=[VMEM_WHOLE] * len(out_shape),
+        scratch_shapes=scratch,
+        compiler_params=params(14),
         cost_estimate=cost(6 * rows * width * units, 6 * width * units, rows * units),
         name="feed_forward",
-    )(place, *args, *after)
+    )(place, *args, *weights, *after)
 
 
 def angle_tables(places):
@@ -576,12 +576,13 @@
     prefill_cache, decode_cache = in_hbm(prefill_cache), in_hbm(decode_cache)
 
     mines = [prefill_rows] + [from_chip(prefill_rows, k) for k in range(1, chips)]
-    sibs = [swap_cores(prefill_rows)]
+    sibs = [swap_cores(rows) for rows in mines]
 
     low = max(dp_count // 4, 1)
     pool = [decode_rows] + [swap_groups(decode_rows, i) for i in range(1, low)]
-    near = jnp.concatenate(pool, axis=0)
-    pool = [near] + [swap_groups(near, i * low) for i in range(1, dp_count // low)]
+    pool = jnp.concatenate(pool, axis=0)
+    pool = [pool] + [swap_groups(pool, i * low) for i in range(1, dp_count // low)]
+    pool = jnp.concatenate(pool, axis=0)
     index = jnp.arange(dp_count * per_device, dtype=jnp.int32)
     origin = jnp.bitwise_xor(group_place, index // per_device)
     request = (origin * tensor_count + tensor_place) * per_device + index % per_device
@@ -597,21 +598,21 @@
     chooser = (jnp.arange(padded, dtype=jnp.int32)[:, None] == in_group[None, :]) & (
         in_group[None, :] < slots
     )
+    dealt = jnp.dot(
+        chooser.astype(jnp.bfloat16), pool, preferred_element_type=jnp.float32
+    ).astype(jnp.bfloat16)
+
     gain = attention_gain.reshape(1, width)
     tables = angle_tables(prefill_offset[0] + jnp.arange(tokens, dtype=jnp.int32))
     dec_tables = angle_tables(jnp.pad(cache_length, (0, padded - slots)))
     queries, entries, everything = [None] * chips, [None] * chips, None
     for k in range(chips):
         last = k == chips - 1
-        if k == 1:
-            far = pool[1:]
-            mines[1:], far, queries[0] = lax.optimization_barrier((mines[1:], far, queries[0]))
-            sibs += [swap_cores(rows) for rows in mines[1:]]
-            pool = jnp.concatenate([near, *far], axis=0)
-            dealt = jnp.dot(
-                chooser.astype(jnp.bfloat16), pool, preferred_element_type=jnp.float32
-            ).astype(jnp.bfloat16)
-            dealt = add(dealt, *from_rest(dealt))
+        if last:
+            others = from_rest(dealt)
+            if k:
+                *others, queries[k - 1] = lax.optimization_barrier((*others, queries[k - 1]))
+            dealt = add(dealt, *others)
         got = project(
             places[k],
             in_hbm(mines[k]),
@@ -624,7 +625,7 @@
             dealt if last else None,
             dec_tables if last else None,
             slots,
-            [queries[k - 1]] if k else [near],
+            [queries[k - 1]] if k else [dealt],
         )
         queries[k], entries[k], everything = got[:3]
         if last:
@@ -668,7 +669,8 @@
         return [from_chip(parts[(b - j) % chips], j) for j in range(1, chips)]
 
     theirs = fetch(order[0])
-    arrived = []
+    weights = [gate_weight, up_weight, down_weight]
+    arrived, sent = [], []
     for n, b in enumerate(order):
         got = feed_forward(
             places[b],
@@ -676,19 +678,20 @@
             sibs[b],
             shares_of(parts[b], theirs),
             gain,
-            gate_weight,
-            up_weight,
-            down_weight if n + 1 < chips else None,
+            weights if n + 1 < chips else weights[:2],
+            n == 0,
             dealt if n == 0 else None,
             dec_shares if n == 0 else None,
+            sent,
         )
         if n + 1 < chips:
             keep, give = got[:2]
             *theirs, keep = lax.optimization_barrier((*fetch(order[n + 1]), keep))
             both = add(keep, swap_cores(give))
             arrived.append(from_chip(both, chips - b))
+            sent = [both]
         if n == 0:
-            dec_sum, dec_resid = got[3:]
+            dec_sum, dec_resid, *weights = got[3:]
             dec_others = from_rest(dec_sum)
     resid, hidden = got
     dec_sum, hidden = lax.optimization_barrier((dec_sum, hidden))
@@ -698,7 +701,7 @@
     routed = jnp.dot(
         picker.astype(jnp.bfloat16), final, preferred_element_type=jnp.float32
     ).astype(jnp.bfloat16)
-    keep, give = lower(hidden, down_weight, [routed])
+    keep, give = lower(hidden, weights[2], [routed])
     low = max(dp_count // 4, 1)
     pairs = routed.reshape(dp_count // low, low * per_device, width)
     rows = add(

time: 110 us -> 103 us (0.936)
  Pallas kernels: 54.6 us -> 50.3 us
  local copies, waits for them, and re-layouts: 10.1 us -> 6.48 us
    pallas_call x3, Pallas kernels: 25.5 us -> 21.2 us  [the longest x2 18.9 us: feed_forward(): pl.pallas_call(functools.partial(forward_kernel, loads, chips, n_dec, len...]
    ppermute x8, waiting for transfers between devices: 3.16 us -> 6.12 us  [swap_groups(): return lax.ppermute(value, 'dp', [(i, i ^ mask) for i in range(count)])]
    ppermute x6, waiting for transfers between devices: 2.5 us -> 0.02 us  [from_other(): lax.ppermute(value, 'tensor', [(i, (i // 2 - step) % (count // 2) * 2 + 1...]
    unnamed x35 -> x25, local copies, waits for them, and re-layouts: 8.42 us -> 6.19 us
    ppermute x7, starting transfers between devices: 9.39 us -> 7.34 us  [from_chip(): lax.ppermute(value, 'tensor', [(i, (i // 2 - step) % chips * 2 + i % 2) f...]
    concatenate x1, local copies, waits for them, and re-layouts: 1.5 us -> 0.08 us  [on_device(): pool = jnp.concatenate(pool, axis=0)]
    ppermute x7, waiting for transfers between devices: 3.37 us -> 2.05 us  [from_chip(): lax.ppermute(value, 'tensor', [(i, (i // 2 - step) % chips * 2 + i % 2) f...]
    ppermute x11, starting transfers between devices: 2 us -> 3.29 us  [swap_cores(): return lax.ppermute(value, 'tensor', [(i, i ^ 1) for i in range(count)])]
  transfers between devices with their start and end apart: 32 -> 32, of which waited for: 10 -> 8; matrix products, arithmetic and copies ran while one was open for 9% -> 10% of each run, Pallas kernels for 43% -> 42%
where the time goes in v9:
time: 103 us; the launch traced here: 102 us
  Pallas kernels  50.3 us (49%)
  starting transfers between devices  25 us (24%)
  waiting for transfers between devices  13 us (13%)
  local copies, waits for them, and re-layouts  6.48 us (6%)
  other arithmetic  5.57 us (5%)
  between operations  1.68 us (2%)
    pallas_call x2, Pallas kernels, feed_forward(): pl.pallas_call(functools.partial(forward_kernel, loads, chips, n_dec, len...  18.9 us
    ppermute x8, starting transfers between devices, swap_groups(): return lax.ppermute(value, 'dp', [(i, i ^ mask) for i in range(count)])  11 us
    pallas_call x2, Pallas kernels, project(): pl.pallas_call(functools.partial(project_kernel, n_dec, len(after), group...  10.6 us
    pallas_call x2, Pallas kernels, fill_attend(): pl.pallas_call(functools.partial(fill_kernel, groups, chips), out_shape=j...  9.47 us
    ppermute x7, starting transfers between devices, from_chip(): lax.ppermute(value, 'tensor', [(i, (i // 2 - step) % chips * 2 + i % 2) f...  7.34 us
    pallas_call x1, Pallas kernels, step_attend(): pl.pallas_call(functools.partial(step_kernel, heads), out_shape=jax.Shape...  6.51 us
    unnamed x25, local copies, waits for them, and re-layouts  6.19 us
    ppermute x8, waiting for transfers between devices, swap_groups(): return lax.ppermute(value, 'dp', [(i, i ^ mask) for i in range(count)])  6.12 us
  transfers between devices with their start and end apart: 32, of which 8 were waited for; matrix products, arithmetic and copies ran while one was open for 10% of the time, Pallas kernels for 42%

profile of v9, /device:TPU:0, one launch (start us, length us, event | category | flops | bytes accessed | tf_op | source)
XLA Modules:
  0.0 102.3 jit_solution(8969321225358563497)
XLA Ops:
  1.2 2.6 %collective-permute-start.8 = (bf16[128,2048]{1,0:T(8,128)(2,1)}, bf16[128,2048]{1,0:T(8,128)(2,1)S(1)}, u32[]{:S(2)}, u32[]{:S(2)}) collective-permute-start(bf16[128,2048]{1,0:T(8,128)(2,1)} %refs_0_.3), channel_id=1, source_target_pairs={{0,2},{1,3},{2,0},{3,1},{4,6},{5,7},{6,4},{7,5},{8,10},{9,11},{10,... | collective-permute-start | bytes 1572872 | tf_op jit(solution)/shard_map/ppermute | solution.py:26
  3.7 1.5 %collective-permute-start.1 = (bf16[2,2048]{1,0:T(2,128)(2,1)}, bf16[2,2048]{1,0:T(2,128)(2,1)S(1)}, u32[]{:S(2)}, u32[]{:S(2)}) collective-permute-start(bf16[2,2048]{1,0:T(2,128)(2,1)} %param.15), channel_id=1, source_target_pairs={{0,4},{4,0},{8,12},{12,8},{16,20},{20,16},{24,28},{28,24},{1,5},{5... | collective-permute-start | bytes 24584 | tf_op jit(solution)/shard_map/ppermute | solution.py:45
  6.6 1.0 fusion
  7.7 0.8 select_reduce_fusion
  9.5 1.6 %collective-permute-start.2 = (bf16[4,2048]{1,0:T(4,128)(2,1)S(1)}, bf16[4,2048]{1,0:T(4,128)(2,1)S(1)}, u32[]{:S(2)}, u32[]{:S(2)}) collective-permute-start(bf16[4,2048]{1,0:T(4,128)(2,1)S(1)} %pad_maximum_fusion.2), channel_id=1, source_target_pairs={{0,8},{4,12},{8,0},{12,4},{16,24},{20,28},{24,16},{28,20},{1,9},{5... | collective-permute-start | bytes 49160 | tf_op jit(solution)/shard_map/ppermute | solution.py:45
  11.2 2.6 %collective-permute-start.3 = (bf16[4,2048]{1,0:T(4,128)(2,1)S(1)}, bf16[4,2048]{1,0:T(4,128)(2,1)S(1)}, u32[]{:S(2)}, u32[]{:S(2)}) collective-permute-start(bf16[4,2048]{1,0:T(4,128)(2,1)S(1)} %pad_maximum_fusion.2), channel_id=1, source_target_pairs={{0,16},{4,20},{8,24},{12,28},{16,0},{20,4},{24,8},{28,12},{1,17},{... | collective-permute-start | bytes 49160 | tf_op jit(solution)/shard_map/ppermute | solution.py:45
  14.2 5.3 %copy.19 = bf16[256,8,2,512]{3,1,2,0:T(8,128)(2,1)} copy(bf16[256,8,2,512]{3,2,1,0:T(2,128)(2,1)} %bitcast.16) | data formatting | bytes 8388608
  20.4 1.6 %collective-permute-start.7 = (bf16[16,2048]{1,0:T(8,128)(2,1)S(1)}, bf16[16,2048]{1,0:T(8,128)(2,1)S(1)}, u32[]{:S(2)}, u32[]{:S(2)}) collective-permute-start(bf16[16,2048]{1,0:T(8,128)(2,1)S(1)} %convolution_convert_fusion.1.refs_6_), channel_id=1, source_target_pairs={{0,3},{1,2},{2,1},{3,0},{4,7},{5,6},{6,5},{7,4},{8,11},{9,10},{10,... | collective-permute-start | bytes 196616 | tf_op jit(solution)/shard_map/ppermute | solution.py:33
  22.1 5.0 %project.2 = (bf16[256,512]{1,0:T(8,128)(2,1)S(1)}, bf16[2,256,256]{2,1,0:T(8,128)(2,1)S(1)}, bf16[2,512,256]{2,1,0:T(8,128)(2,1)}) custom-call(s32[5]{0:T(128)S(1)} %stack.23.place, bf16[128,2048]{1,0:T(8,128)(2,1)} %refs_0_.3, bf16[128,2048]{1,0:T(8,128)(2,1)} %collective-permute-done.refs_1_, bf16[2048,1024]{1,0:T(8,128)(2,1)} %bitcast.14, ...), custom_call_target="tpu_custom_call" | custom-call | flops 1073741824 | bytes 6291456 | tf_op jit(solution)/shard_map/project/pallas_call | solution.py:174
  27.1 0.8 copy-done.4
  27.9 5.6 %project.3 = (bf16[256,512]{1,0:T(8,128)(2,1)S(1)}, bf16[2,256,256]{2,1,0:T(8,128)(2,1)S(1)}, bf16[2,512,256]{2,1,0:T(8,128)(2,1)}, f32[16,512]{1,0:T(8,128)S(1)}, bf16[2,8,256]{2,1,0:T(8,128)(2,1)}) custom-call(s32[5]{0:T(128)S(1)} %stack.24.place, bf16[128,2048]{1,0:T(8,128)(2,1)} %copy-done.2, ...), custom_call_target="tpu_custom_call", output_to_operand_aliasing={{2}: (11, {})} | custom-call | flops 1140850688 | bytes 6422528 | tf_op jit(solution)/shard_map/project/pallas_call | solution.py:174
  34.2 4.7 %fill_attend.2.mine = bf16[256,512]{1,0:T(8,128)(2,1)S(1)} custom-call(s32[5]{0:T(128)S(1)} %stack.23.place, bf16[256,512]{1,0:T(8,128)(2,1)S(1)} %get-tuple-element.43.refs_9_.query, bf16[2,1,1024,256]{3,2,1,0:T(8,128)(2,1)} %cache_value.3, bf16[2,1,1024,256]{3,2,1,0:T(8,128)(2,1)} %cache_value.3, ...), custom_call_target="tpu_custom_call" | custom-call | flops 1610612736 | bytes 1048576 | tf_op jit(solution)/shard_map/fill_attend/pallas_call | solution.py:234
  39.0 1.5 %collective-permute-done.10.sib = bf16[256,512]{1,0:T(8,128)(2,1)S(1)} collective-permute-done((bf16[256,512]{1,0:T(8,128)(2,1)S(1)}, bf16[256,512]{1,0:T(8,128)(2,1)S(1)}, u32[]{:S(2)}, u32[]{:S(2)}) %collective-permute-start.10) | collective-permute-done | bytes 262176 | tf_op jit(solution)/shard_map/ppermute | solution.py:20
  40.5 1.3 %out_project.2.refs_2_ = bf16[256,1024]{1,0:T(8,128)(2,1)S(1)} custom-call(s32[5]{0:T(128)S(1)} %stack.23.place, bf16[256,512]{1,0:T(8,128)(2,1)S(1)} %fill_attend.2.mine, bf16[256,512]{1,0:T(8,128)(2,1)S(1)} %collective-permute-done.10.sib, bf16[512,2048]{1,0:T(8,128)(2,1)S(1)} %copy-done, bf16[512,2048]{1,0:T(8,128)(2,1)S(1)} %collective-permute-done.11.sib_weight), custom_call_target="tpu_custom_call" | custom-call | flops 536870912 | bytes 3670016 | tf_op jit(solution)/shard_map/out_project/pallas_call | solution.py:360
  42.4 6.5 %step_attend.1.refs_4_.refs_7_ = bf16[16,2048]{1,0:T(8,128)(2,1)S(1)} custom-call(s32[8]{0:T(128)S(1)} %copy-done.10, f32[16,512]{1,0:T(8,128)S(1)} %get-tuple-element.55.query, bf16[2,8,256]{2,1,0:T(8,128)(2,1)S(1)} %copy-done.9, bf16[2,8,1024,256]{3,2,1,0:T(8,128)(2,1)} %cache.1, bf16[512,2048]{1,0:T(8,128)(2,1)} %weight.5), custom_call_target="tpu_custom_call" | custom-call | flops 67108864 | bytes 8388608 | tf_op jit(solution)/shard_map/step_attend/pallas_call | solution.py:329
  48.9 1.6 %collective-permute-start.13 = (bf16[16,2048]{1,0:T(8,128)(2,1)S(1)}, bf16[16,2048]{1,0:T(8,128)(2,1)S(1)}, u32[]{:S(2)}, u32[]{:S(2)}) collective-permute-start(bf16[16,2048]{1,0:T(8,128)(2,1)S(1)} %step_attend.1.refs_4_.refs_7_), channel_id=1, source_target_pairs={{0,2},{1,3},{2,0},{3,1},{4,6},{5,7},{6,4},{7,5},{8,10},{9,11},{10,... | collective-permute-start | bytes 196616 | tf_op jit(solution)/shard_map/ppermute | solution.py:26
  51.1 4.8 %fill_attend.3.mine = bf16[256,512]{1,0:T(8,128)(2,1)S(1)} custom-call(s32[5]{0:T(128)S(1)} %stack.24.place, bf16[256,512]{1,0:T(8,128)(2,1)S(1)} %get-tuple-element.53.query, bf16[2,1,1024,256]{3,2,1,0:T(8,128)(2,1)} %cache_value.3, bf16[2,1,1024,256]{3,2,1,0:T(8,128)(2,1)} %cache_value.3, bf16[2,256,256]{2,1,0:T(8,128)(2,1)S(1)} %get-tuple-element.44.refs_0_.refs_2_, ...), custom_call_target="tpu_custom_call" | custom-call | flops 1610612736 | bytes 1048576 | tf_op jit(solution)/shard_map/fill_attend/pallas_call | solution.py:234
  55.9 2.0 %collective-permute-done.13.refs_8_ = bf16[16,2048]{1,0:T(8,128)(2,1)S(1)} collective-permute-done((bf16[16,2048]{1,0:T(8,128)(2,1)S(1)}, bf16[16,2048]{1,0:T(8,128)(2,1)S(1)}, u32[]{:S(2)}, u32[]{:S(2)}) %collective-permute-start.13) | collective-permute-done | bytes 65568 | tf_op jit(solution)/shard_map/ppermute | solution.py:26
  58.4 1.2 %collective-permute-done.16.sib = bf16[256,512]{1,0:T(8,128)(2,1)S(1)} collective-permute-done((bf16[256,512]{1,0:T(8,128)(2,1)S(1)}, bf16[256,512]{1,0:T(8,128)(2,1)S(1)}, u32[]{:S(2)}, u32[]{:S(2)}) %collective-permute-start.16) | collective-permute-done | bytes 262176 | tf_op jit(solution)/shard_map/ppermute | solution.py:20
  59.6 1.2 %out_project.3.refs_2_ = bf16[256,1024]{1,0:T(8,128)(2,1)S(1)} custom-call(s32[5]{0:T(128)S(1)} %stack.24.place, bf16[256,512]{1,0:T(8,128)(2,1)S(1)} %fill_attend.3.mine, bf16[256,512]{1,0:T(8,128)(2,1)S(1)} %collective-permute-done.16.sib, bf16[512,2048]{1,0:T(8,128)(2,1)S(1)} %copy-done.1, bf16[512,2048]{1,0:T(8,128)(2,1)S(1)} %collective-permute-done.11.sib_weight), custom_call_target="tpu_custom_call" | custom-call | flops 536870912 | bytes 3670016 | tf_op jit(solution)/shard_map/out_project/pallas_call | solution.py:360
  62.0 0.9 collective-permute-done.18.refs_3_
  62.8 0.7 collective-permute-done.20.refs_5_
  63.6 12.1 %feed_forward.2 = (bf16[128,2048]{1,0:T(8,128)(2,1)S(1)}, bf16[128,2048]{1,0:T(8,128)(2,1)S(1)}, bf16[128,2048]{1,0:T(8,128)(2,1)}, bf16[16,2048]{1,0:T(8,128)(2...) custom-call(s32[5]{0:T(128)S(1)} %stack.24.place, ...), custom_call_target="tpu_custom_call" | custom-call | flops 6845104128 | bytes 25165824 | tf_op jit(solution)/shard_map/feed_forward/pallas_call | solution.py:508
  77.7 1.1 %collective-permute-start.25 = (bf16[16,2048]{1,0:T(8,128)(2,1)S(1)}, bf16[16,2048]{1,0:T(8,128)(2,1)S(1)}, u32[]{:S(2)}, u32[]{:S(2)}) collective-permute-start(bf16[16,2048]{1,0:T(8,128)(2,1)S(1)} %get-tuple-element.73), channel_id=1, source_target_pairs={{0,3},{1,2},{2,1},{3,0},{4,7},{5,6},{6,5},{7,4},{8,11},{9,10},{10,... | collective-permute-start | bytes 196616 | tf_op jit(solution)/shard_map/ppermute | solution.py:33
  79.0 0.9 collective-permute-start.26
  80.0 6.7 %feed_forward.3 = (bf16[128,2048]{1,0:T(8,128)(2,1)S(1)}, bf16[256,2048]{1,0:T(8,128)(2,1)S(1)}) custom-call(s32[5]{0:T(128)S(1)} %stack.23.place, bf16[128,2048]{1,0:T(8,128)(2,1)S(1)} %copy-done.6, bf16[128,2048]{1,0:T(8,128)(2,1)} %collective-permute-done.refs_1_, bf16[256,1024]{1,0:T(8,128)(2,1)S(1)} %out_project.2.refs_2_, ...), custom_call_target="tpu_custom_call" | custom-call | flops 6442450944 | bytes 25165824 | tf_op jit(solution)/shard_map/feed_forward/pallas_call | solution.py:508
  87.0 0.7 collective-permute-start.27
  87.7 3.5 %collective-permute-start.28 = (bf16[4,2048]{1,0:T(4,128)(2,1)S(1)}, bf16[4,2048]{1,0:T(4,128)(2,1)S(1)}, u32[]{:S(2)}, u32[]{:S(2)}) collective-permute-start(bf16[4,2048]{1,0:T(4,128)(2,1)S(1)} %get-tuple-element.84), channel_id=1, source_target_pairs={{0,16},{4,20},{8,24},{12,28},{16,0},{20,4},{24,8},{28,12},{1,17},{... | collective-permute-start | bytes 49160 | tf_op jit(solution)/shard_map/ppermute | solution.py:45
  91.4 2.3 %lower.1 = (bf16[128,2048]{1,0:T(8,128)(2,1)S(1)}, bf16[128,2048]{1,0:T(8,128)(2,1)S(1)}) custom-call(bf16[256,2048]{1,0:T(8,128)(2,1)S(1)} %get-tuple-element.70.hidden, bf16[4,2048,512]{2,1,0:T(8,128)(2,1)S(1)} %get-tuple-element.71.down, bf16[16,2048]{1,0:T(8,128)(2,1)S(1)} %convolution_convert_fusion.refs_0_), custom_call_target="tpu_custom_call" | custom-call | flops 2147483648 | bytes 8388608 | tf_op jit(solution)/shard_map/lower/pallas_call | solution.py:473
  93.8 3.0 %collective-permute-done.29 = bf16[4,2048]{1,0:T(4,128)(2,1)S(1)} collective-permute-done((bf16[4,2048]{1,0:T(4,128)(2,1)S(1)}, bf16[4,2048]{1,0:T(4,128)(2,1)S(1)}, u32[]{:S(2)}, u32[]{:S(2)}) %collective-permute-start.29) | collective-permute-done | bytes 16416 | tf_op jit(solution)/shard_map/ppermute | solution.py:45
  97.4 3.1 %collective-permute-done.31 = bf16[2,2048]{1,0:T(2,128)(2,1)S(1)} collective-permute-done((bf16[2,2048]{1,0:T(2,128)(2,1)S(1)}, bf16[2,2048]{1,0:T(2,128)(2,1)S(1)}, u32[]{:S(2)}, u32[]{:S(2)}) %collective-permute-start.31) | collective-permute-done | bytes 8224 | tf_op jit(solution)/shard_map/ppermute | solution.py:45
  101.2 1.1 %add_convert_fusion = bf16[128,2048]{1,0:T(8,128)(2,1)} fusion(bf16[128,2048]{1,0:T(8,128)(2,1)S(1)} %collective-permute-done.26, bf16[128,2048]{1,0:T(8,128)(2,1)S(1)} %collective-permute-done.30, bf16[128,2048]{1,0:T(8,128)(2,1)S(1)} %get-tuple-element.74, bf16[128,2048]{1,0:T(8,128)(2,1)S(1)} %get-tuple-element.67), kind=kLoop, calls=%fused_computation.2 | loop fusion | flops 2097152 | bytes 2621440 | tf_op jit(solution)/shard_map/convert_element_type | solution.py:536
  (90 shorter events, 11.1 us)
Async XLA Ops:
  0.7 21.4 %collective-permute-start = (bf16[128,2048]{1,0:T(8,128)(2,1)}, bf16[128,2048]{1,0:T(8,128)(2,1)}, u32[]{:S(2)}, u32[]{:S(2)}) collective-permute-start(bf16[128,2048]{1,0:T(8,128)(2,1)} %refs_0_.3), channel_id=1, source_target_pairs={{0,1},{1,0},{2,3},{3,2},{4,5},{5,4},{6,7},{7,6},{8,9},{9,8},{10,11... | collective-permute-start | bytes 1572872 | tf_op jit(solution)/shard_map/ppermute | solution.py:20
  1.2 20.9 %collective-permute-start.8 = (bf16[128,2048]{1,0:T(8,128)(2,1)}, bf16[128,2048]{1,0:T(8,128)(2,1)S(1)}, u32[]{:S(2)}, u32[]{:S(2)}) collective-permute-start(bf16[128,2048]{1,0:T(8,128)(2,1)} %refs_0_.3), channel_id=1, source_target_pairs={{0,2},{1,3},{2,0},{3,1},{4,6},{5,7},{6,4},{7,5},{8,10},{9,11},{10,... | collective-permute-start | bytes 1572872 | tf_op jit(solution)/shard_map/ppermute | solution.py:26
  3.7 5.1 %collective-permute-start.1 = (bf16[2,2048]{1,0:T(2,128)(2,1)}, bf16[2,2048]{1,0:T(2,128)(2,1)S(1)}, u32[]{:S(2)}, u32[]{:S(2)}) collective-permute-start(bf16[2,2048]{1,0:T(2,128)(2,1)} %param.15), channel_id=1, source_target_pairs={{0,4},{4,0},{8,12},{12,8},{16,20},{20,16},{24,28},{28,24},{1,5},{5... | collective-permute-start | bytes 24584 | tf_op jit(solution)/shard_map/ppermute | solution.py:45
  9.5 10.0 %collective-permute-start.2 = (bf16[4,2048]{1,0:T(4,128)(2,1)S(1)}, bf16[4,2048]{1,0:T(4,128)(2,1)S(1)}, u32[]{:S(2)}, u32[]{:S(2)}) collective-permute-start(bf16[4,2048]{1,0:T(4,128)(2,1)S(1)} %pad_maximum_fusion.2), channel_id=1, source_target_pairs={{0,8},{4,12},{8,0},{12,4},{16,24},{20,28},{24,16},{28,20},{1,9},{5... | collective-permute-start | bytes 49160 | tf_op jit(solution)/shard_map/ppermute | solution.py:45
  11.2 8.4 %collective-permute-start.3 = (bf16[4,2048]{1,0:T(4,128)(2,1)S(1)}, bf16[4,2048]{1,0:T(4,128)(2,1)S(1)}, u32[]{:S(2)}, u32[]{:S(2)}) collective-permute-start(bf16[4,2048]{1,0:T(4,128)(2,1)S(1)} %pad_maximum_fusion.2), channel_id=1, source_target_pairs={{0,16},{4,20},{8,24},{12,28},{16,0},{20,4},{24,8},{28,12},{1,17},{... | collective-permute-start | bytes 49160 | tf_op jit(solution)/shard_map/ppermute | solution.py:45
  13.8 5.8 %collective-permute-start.4 = (bf16[4,2048]{1,0:T(4,128)(2,1)S(1)}, bf16[4,2048]{1,0:T(4,128)(2,1)S(1)}, u32[]{:S(2)}, u32[]{:S(2)}) collective-permute-start(bf16[4,2048]{1,0:T(4,128)(2,1)S(1)} %pad_maximum_fusion.2), channel_id=1, source_target_pairs={{0,24},{4,28},{8,16},{12,20},{16,8},{20,12},{24,0},{28,4},{1,25},{... | collective-permute-start | bytes 49160 | tf_op jit(solution)/shard_map/ppermute | solution.py:45
  19.8 7.2 %collective-permute-start.5 = (bf16[16,2048]{1,0:T(8,128)(2,1)S(1)}, bf16[16,2048]{1,0:T(8,128)(2,1)S(1)}, u32[]{:S(2)}, u32[]{:S(2)}) collective-permute-start(bf16[16,2048]{1,0:T(8,128)(2,1)S(1)} %convolution_convert_fusion.1.refs_6_), channel_id=1, source_target_pairs={{0,2},{1,3},{2,0},{3,1},{4,6},{5,7},{6,4},{7,5},{8,10},{9,11},{10,... | collective-permute-start | bytes 196616 | tf_op jit(solution)/shard_map/ppermute | solution.py:26
  20.4 6.6 %collective-permute-start.6 = (bf16[16,2048]{1,0:T(8,128)(2,1)S(1)}, bf16[16,2048]{1,0:T(8,128)(2,1)S(1)}, u32[]{:S(2)}, u32[]{:S(2)}) collective-permute-start(bf16[16,2048]{1,0:T(8,128)(2,1)S(1)} %convolution_convert_fusion.1.refs_6_), channel_id=1, source_target_pairs={{0,1},{1,0},{2,3},{3,2},{4,5},{5,4},{6,7},{7,6},{8,9},{9,8},{10,11... | collective-permute-start | bytes 196616 | tf_op jit(solution)/shard_map/ppermute | solution.py:33
  20.4 6.6 %collective-permute-start.7 = (bf16[16,2048]{1,0:T(8,128)(2,1)S(1)}, bf16[16,2048]{1,0:T(8,128)(2,1)S(1)}, u32[]{:S(2)}, u32[]{:S(2)}) collective-permute-start(bf16[16,2048]{1,0:T(8,128)(2,1)S(1)} %convolution_convert_fusion.1.refs_6_), channel_id=1, source_target_pairs={{0,3},{1,2},{2,1},{3,0},{4,7},{5,6},{6,5},{7,4},{8,11},{9,10},{10,... | collective-permute-start | bytes 196616 | tf_op jit(solution)/shard_map/ppermute | solution.py:33
  22.0 5.1 %collective-permute-start.9 = (bf16[128,2048]{1,0:T(8,128)(2,1)S(1)}, bf16[128,2048]{1,0:T(8,128)(2,1)S(1)}, u32[]{:S(2)}, u32[]{:S(2)}) collective-permute-start(bf16[128,2048]{1,0:T(8,128)(2,1)S(1)} %collective-permute-done.8.refs_0_), channel_id=1, source_target_pairs={{0,1},{1,0},{2,3},{3,2},{4,5},{5,4},{6,7},{7,6},{8,9},{9,8},{10,11... | collective-permute-start | bytes 1572872 | tf_op jit(solution)/shard_map/ppermute | solution.py:20
  33.6 6.9 %collective-permute-start.11 = (bf16[512,2048]{1,0:T(8,128)(2,1)S(1)}, bf16[512,2048]{1,0:T(8,128)(2,1)S(1)}, u32[]{:S(2)}, u32[]{:S(2)}) collective-permute-start(bf16[512,2048]{1,0:T(8,128)(2,1)S(1)} %copy-done), channel_id=1, source_target_pairs={{0,1},{1,0},{2,3},{3,2},{4,5},{5,4},{6,7},{7,6},{8,9},{9,8},{10,11... | collective-permute-start | bytes 6291464 | tf_op jit(solution)/shard_map/ppermute | solution.py:20
  38.9 1.6 %collective-permute-start.10 = (bf16[256,512]{1,0:T(8,128)(2,1)S(1)}, bf16[256,512]{1,0:T(8,128)(2,1)S(1)}, u32[]{:S(2)}, u32[]{:S(2)}) collective-permute-start(bf16[256,512]{1,0:T(8,128)(2,1)S(1)} %fill_attend.2.mine), channel_id=1, source_target_pairs={{0,1},{1,0},{2,3},{3,2},{4,5},{5,4},{6,7},{7,6},{8,9},{9,8},{10,11... | collective-permute-start | bytes 786440 | tf_op jit(solution)/shard_map/ppermute | solution.py:20
  41.8 19.5 %collective-permute-start.19 = (bf16[256,1024]{1,0:T(8,128)(2,1)S(1)}, bf16[256,1024]{1,0:T(8,128)(2,1)S(1)}, u32[]{:S(2)}, u32[]{:S(2)}) collective-permute-start(bf16[256,1024]{1,0:T(8,128)(2,1)S(1)} %out_project.2.refs_2_), channel_id=1, source_target_pairs={{0,2},{1,3},{2,0},{3,1},{4,6},{5,7},{6,4},{7,5},{8,10},{9,11},{10,... | collective-permute-start | bytes 1572872 | tf_op jit(solution)/shard_map/ppermute | solution.py:26
  48.9 9.0 %collective-permute-start.13 = (bf16[16,2048]{1,0:T(8,128)(2,1)S(1)}, bf16[16,2048]{1,0:T(8,128)(2,1)S(1)}, u32[]{:S(2)}, u32[]{:S(2)}) collective-permute-start(bf16[16,2048]{1,0:T(8,128)(2,1)S(1)} %step_attend.1.refs_4_.refs_7_), channel_id=1, source_target_pairs={{0,2},{1,3},{2,0},{3,1},{4,6},{5,7},{6,4},{7,5},{8,10},{9,11},{10,... | collective-permute-start | bytes 196616 | tf_op jit(solution)/shard_map/ppermute | solution.py:26
  50.5 7.4 %collective-permute-start.14 = (bf16[16,2048]{1,0:T(8,128)(2,1)S(1)}, bf16[16,2048]{1,0:T(8,128)(2,1)S(1)}, u32[]{:S(2)}, u32[]{:S(2)}) collective-permute-start(bf16[16,2048]{1,0:T(8,128)(2,1)S(1)} %step_attend.1.refs_4_.refs_7_), channel_id=1, source_target_pairs={{0,1},{1,0},{2,3},{3,2},{4,5},{5,4},{6,7},{7,6},{8,9},{9,8},{10,11... | collective-permute-start | bytes 196616 | tf_op jit(solution)/shard_map/ppermute | solution.py:33
  50.5 7.4 %collective-permute-start.15 = (bf16[16,2048]{1,0:T(8,128)(2,1)S(1)}, bf16[16,2048]{1,0:T(8,128)(2,1)S(1)}, u32[]{:S(2)}, u32[]{:S(2)}) collective-permute-start(bf16[16,2048]{1,0:T(8,128)(2,1)S(1)} %step_attend.1.refs_4_.refs_7_), channel_id=1, source_target_pairs={{0,3},{1,2},{2,1},{3,0},{4,7},{5,6},{6,5},{7,4},{8,11},{9,10},{10,... | collective-permute-start | bytes 196616 | tf_op jit(solution)/shard_map/ppermute | solution.py:33
  57.9 1.7 %collective-permute-start.16 = (bf16[256,512]{1,0:T(8,128)(2,1)S(1)}, bf16[256,512]{1,0:T(8,128)(2,1)S(1)}, u32[]{:S(2)}, u32[]{:S(2)}) collective-permute-start(bf16[256,512]{1,0:T(8,128)(2,1)S(1)} %fill_attend.3.mine), channel_id=1, source_target_pairs={{0,1},{1,0},{2,3},{3,2},{4,5},{5,4},{6,7},{7,6},{8,9},{9,8},{10,11... | collective-permute-start | bytes 786440 | tf_op jit(solution)/shard_map/ppermute | solution.py:20
  60.9 2.0 %collective-permute-start.18 = (bf16[256,1024]{1,0:T(8,128)(2,1)S(1)}, bf16[256,1024]{1,0:T(8,128)(2,1)S(1)}, u32[]{:S(2)}, u32[]{:S(2)}) collective-permute-start(bf16[256,1024]{1,0:T(8,128)(2,1)S(1)} %out_project.3.refs_2_), channel_id=1, source_target_pairs={{0,1},{1,0},{2,3},{3,2},{4,5},{5,4},{6,7},{7,6},{8,9},{9,8},{10,11... | collective-permute-start | bytes 1572872 | tf_op jit(solution)/shard_map/ppermute | solution.py:20
  61.3 2.3 %collective-permute-start.20 = (bf16[256,1024]{1,0:T(8,128)(2,1)S(1)}, bf16[256,1024]{1,0:T(8,128)(2,1)S(1)}, u32[]{:S(2)}, u32[]{:S(2)}) collective-permute-start(bf16[256,1024]{1,0:T(8,128)(2,1)S(1)} %collective-permute-done.19.refs_4_), channel_id=1, source_target_pairs={{0,1},{1,0},{2,3},{3,2},{4,5},{5,4},{6,7},{7,6},{8,9},{9,8},{10,11... | collective-permute-start | bytes 1572872 | tf_op jit(solution)/shard_map/ppermute | solution.py:20
  61.4 14.9 %collective-permute-start.17 = (bf16[256,1024]{1,0:T(8,128)(2,1)S(1)}, bf16[256,1024]{1,0:T(8,128)(2,1)S(1)}, u32[]{:S(2)}, u32[]{:S(2)}) collective-permute-start(bf16[256,1024]{1,0:T(8,128)(2,1)S(1)} %out_project.3.refs_2_), channel_id=1, source_target_pairs={{0,2},{1,3},{2,0},{3,1},{4,6},{5,7},{6,4},{7,5},{8,10},{9,11},{10,... | collective-permute-start | bytes 1572872 | tf_op jit(solution)/shard_map/ppermute | solution.py:26
  75.8 2.0 %collective-permute-start.22 = (bf16[128,2048]{1,0:T(8,128)(2,1)S(1)}, bf16[128,2048]{1,0:T(8,128)(2,1)S(1)}, u32[]{:S(2)}, u32[]{:S(2)}) collective-permute-start(bf16[128,2048]{1,0:T(8,128)(2,1)S(1)} %get-tuple-element.66), channel_id=1, source_target_pairs={{0,1},{1,0},{2,3},{3,2},{4,5},{5,4},{6,7},{7,6},{8,9},{9,8},{10,11... | collective-permute-start | bytes 1572872 | tf_op jit(solution)/shard_map/ppermute | solution.py:20
  76.2 2.8 %collective-permute-start.12 = (bf16[256,1024]{1,0:T(8,128)(2,1)S(1)}, bf16[256,1024]{1,0:T(8,128)(2,1)S(1)}, u32[]{:S(2)}, u32[]{:S(2)}) collective-permute-start(bf16[256,1024]{1,0:T(8,128)(2,1)S(1)} %out_project.2.refs_2_), channel_id=1, source_target_pairs={{0,1},{1,0},{2,3},{3,2},{4,5},{5,4},{6,7},{7,6},{8,9},{9,8},{10,11... | collective-permute-start | bytes 1572872 | tf_op jit(solution)/shard_map/ppermute | solution.py:20
  76.3 3.6 %collective-permute-start.21 = (bf16[256,1024]{1,0:T(8,128)(2,1)S(1)}, bf16[256,1024]{1,0:T(8,128)(2,1)S(1)}, u32[]{:S(2)}, u32[]{:S(2)}) collective-permute-start(bf16[256,1024]{1,0:T(8,128)(2,1)S(1)} %collective-permute-done.17.refs_4_), channel_id=1, source_target_pairs={{0,1},{1,0},{2,3},{3,2},{4,5},{5,4},{6,7},{7,6},{8,9},{9,8},{10,11... | collective-permute-start | bytes 1572872 | tf_op jit(solution)/shard_map/ppermute | solution.py:20
  76.7 10.0 %collective-permute-start.23 = (bf16[16,2048]{1,0:T(8,128)(2,1)S(1)}, bf16[16,2048]{1,0:T(8,128)(2,1)S(1)}, u32[]{:S(2)}, u32[]{:S(2)}) collective-permute-start(bf16[16,2048]{1,0:T(8,128)(2,1)S(1)} %get-tuple-element.73), channel_id=1, source_target_pairs={{0,2},{1,3},{2,0},{3,1},{4,6},{5,7},{6,4},{7,5},{8,10},{9,11},{10,... | collective-permute-start | bytes 196616 | tf_op jit(solution)/shard_map/ppermute | solution.py:26
  77.3 9.5 %collective-permute-start.24 = (bf16[16,2048]{1,0:T(8,128)(2,1)S(1)}, bf16[16,2048]{1,0:T(8,128)(2,1)S(1)}, u32[]{:S(2)}, u32[]{:S(2)}) collective-permute-start(bf16[16,2048]{1,0:T(8,128)(2,1)S(1)} %get-tuple-element.73), channel_id=1, source_target_pairs={{0,1},{1,0},{2,3},{3,2},{4,5},{5,4},{6,7},{7,6},{8,9},{9,8},{10,11... | collective-permute-start | bytes 196616 | tf_op jit(solution)/shard_map/ppermute | solution.py:33
  77.7 9.0 %collective-permute-start.25 = (bf16[16,2048]{1,0:T(8,128)(2,1)S(1)}, bf16[16,2048]{1,0:T(8,128)(2,1)S(1)}, u32[]{:S(2)}, u32[]{:S(2)}) collective-permute-start(bf16[16,2048]{1,0:T(8,128)(2,1)S(1)} %get-tuple-element.73), channel_id=1, source_target_pairs={{0,3},{1,2},{2,1},{3,0},{4,7},{5,6},{6,5},{7,4},{8,11},{9,10},{10,... | collective-permute-start | bytes 196616 | tf_op jit(solution)/shard_map/ppermute | solution.py:33
  79.0 17.7 %collective-permute-start.26 = (bf16[128,2048]{1,0:T(8,128)(2,1)S(1)}, bf16[128,2048]{1,0:T(8,128)(2,1)S(1)}, u32[]{:S(2)}, u32[]{:S(2)}) collective-permute-start(bf16[128,2048]{1,0:T(8,128)(2,1)S(1)} %add_convert_fusion.1.refs_9_), channel_id=1, source_target_pairs={{0,2},{1,3},{2,0},{3,1},{4,6},{5,7},{6,4},{7,5},{8,10},{9,11},{10,... | collective-permute-start | bytes 1572872 | tf_op jit(solution)/shard_map/ppermute | solution.py:26
  87.0 6.8 %collective-permute-start.27 = (bf16[4,2048]{1,0:T(4,128)(2,1)S(1)}, bf16[4,2048]{1,0:T(4,128)(2,1)S(1)}, u32[]{:S(2)}, u32[]{:S(2)}) collective-permute-start(bf16[4,2048]{1,0:T(4,128)(2,1)S(1)} %get-tuple-element.82), channel_id=1, source_target_pairs={{0,8},{4,12},{8,0},{12,4},{16,24},{20,28},{24,16},{28,20},{1,9},{5... | collective-permute-start | bytes 49160 | tf_op jit(solution)/shard_map/ppermute | solution.py:45
  87.7 6.1 %collective-permute-start.28 = (bf16[4,2048]{1,0:T(4,128)(2,1)S(1)}, bf16[4,2048]{1,0:T(4,128)(2,1)S(1)}, u32[]{:S(2)}, u32[]{:S(2)}) collective-permute-start(bf16[4,2048]{1,0:T(4,128)(2,1)S(1)} %get-tuple-element.84), channel_id=1, source_target_pairs={{0,16},{4,20},{8,24},{12,28},{16,0},{20,4},{24,8},{28,12},{1,17},{... | collective-permute-start | bytes 49160 | tf_op jit(solution)/shard_map/ppermute | solution.py:45
  91.2 5.5 %collective-permute-start.29 = (bf16[4,2048]{1,0:T(4,128)(2,1)S(1)}, bf16[4,2048]{1,0:T(4,128)(2,1)S(1)}, u32[]{:S(2)}, u32[]{:S(2)}) collective-permute-start(bf16[4,2048]{1,0:T(4,128)(2,1)S(1)} %get-tuple-element.83), channel_id=1, source_target_pairs={{0,24},{4,28},{8,16},{12,20},{16,8},{20,12},{24,0},{28,4},{1,25},{... | collective-permute-start | bytes 49160 | tf_op jit(solution)/shard_map/ppermute | solution.py:45
  96.8 4.4 %collective-permute-start.30 = (bf16[128,2048]{1,0:T(8,128)(2,1)S(1)}, bf16[128,2048]{1,0:T(8,128)(2,1)S(1)}, u32[]{:S(2)}, u32[]{:S(2)}) collective-permute-start(bf16[128,2048]{1,0:T(8,128)(2,1)S(1)} %get-tuple-element.76), channel_id=1, source_target_pairs={{0,1},{1,0},{2,3},{3,2},{4,5},{5,4},{6,7},{7,6},{8,9},{9,8},{10,11... | collective-permute-start | bytes 1572872 | tf_op jit(solution)/shard_map/ppermute | solution.py:20
  96.9 3.7 %collective-permute-start.31 = (bf16[2,2048]{1,0:T(2,128)(2,1)S(1)}, bf16[2,2048]{1,0:T(2,128)(2,1)S(1)}, u32[]{:S(2)}, u32[]{:S(2)}) collective-permute-start(bf16[2,2048]{1,0:T(2,128)(2,1)S(1)} %slice.29), channel_id=1, source_target_pairs={{0,4},{4,0},{8,12},{12,8},{16,20},{20,16},{24,28},{28,24},{1,5},{5... | collective-permute-start | bytes 24584 | tf_op jit(solution)/shard_map/ppermute | solution.py:45
  (12 other events, 181.4 us)

commit v10 on v9

--- a/solution.py
+++ b/solution.py
@@ -194,8 +194,22 @@
     )(place, *args, *after)
 
 
-def fill_kernel(groups, chips, place, query, cache_key, cache_value, *refs):
-    new_keys, new_values, out = refs[:chips], refs[chips : 2 * chips], refs[-1]
+def fill_kernel(groups, chips, chunk, place, query, cache_key, cache_value, *refs):
+    new_keys, new_values = refs[:chips], refs[chips : 2 * chips]
+    source, (out, target, arrived) = refs[2 * chips], refs[-3:]
+    pieces = [
+        source.at[:, pl.ds(i * chunk, chunk)] if chunk else source.at[i]
+        for i in range(target.shape[0])
+    ]
+    copies = [
+        pltpu.make_async_copy(piece, target.at[i], arrived.at[i]) for i, piece in enumerate(pieces)
+    ]
+
+    @pl.when(pl.program_id(0) == 0)
+    def _():
+        for copy in copies:
+            copy.start()
+
     scaling = math.log2(math.e) / math.sqrt(HD)
     count = query.shape[0]
     stored = cache_key.shape[2]
@@ -224,16 +238,22 @@
             mix += jnp.dot(weights.astype(jnp.bfloat16), values, preferred_element_type=jnp.float32)
         out[:, g * HD : (g + 1) * HD] = (mix / total).astype(jnp.bfloat16)
 
-
-def fill_attend(place, query, cache, entries, heads, after=()):
+    @pl.when(pl.program_id(0) == pl.num_programs(0) - 1)
+    def _():
+        for copy in copies:
+            copy.wait()
+
+
+def fill_attend(place, query, cache, entries, heads, source, chunk, after=()):
     count = query.shape[0]
     groups = query.shape[1] // heads // HD
     stored = cache.shape[2]
     chips = len(entries)
     pairs = count * groups * heads * (stored + chips * count)
+    target = (source.shape[1] // chunk, source.shape[0], chunk) if chunk else source.shape
     return pl.pallas_call(
-        functools.partial(fill_kernel, groups, chips),
-        out_shape=jax.ShapeDtypeStruct(query.shape, jnp.bfloat16),
+        functools.partial(fill_kernel, groups, chips, chunk),
+        out_shape=[jax.ShapeDtypeStruct(query.shape, jnp.bfloat16), stays_in_vmem(target)],
         grid_spec=pltpu.PrefetchScalarGridSpec(
             num_scalar_prefetch=1,
             grid=(heads,),
@@ -244,29 +264,23 @@
             ]
             + [pl.BlockSpec((1, count, HD), lambda j, s: (0, 0, j))] * chips
             + [pl.BlockSpec((1, count, HD), lambda j, s: (1, 0, j))] * chips
-            + [IN_PLACE] * len(after),
-            out_specs=pl.BlockSpec((count, groups * HD), lambda j, s: (0, j)),
+            + [IN_PLACE] * (1 + len(after)),
+            out_specs=[pl.BlockSpec((count, groups * HD), lambda j, s: (0, j)), IN_PLACE],
+            scratch_shapes=[pltpu.SemaphoreType.DMA((target[0],))],
         ),
         compiler_params=params(12),
         cost_estimate=cost(8 * pairs * HD, 2 * cache.size, pairs),
         name="fill_attend",
-    )(place, query, cache, cache, *entries, *entries, *after)
-
-
-def step_kernel(
-    heads, lengths, query, entries, cache, weight, out, held, scores, shares, weight_held, arrived, weight_sem
-):
+    )(place, query, cache, cache, *entries, *entries, source, *after)
+
+
+def step_kernel(heads, lengths, query, entries, held, weight, out, scores, shares, weight_held, weight_sem):
     scaling = 1.0 / math.sqrt(HD)
-    slots, stored, width = cache.shape[1:]
+    slots, stored, width = held.shape[1:]
     groups = query.shape[1] // width
     lanes = 8
-    copies = [
-        [pltpu.make_async_copy(cache.at[w, s], held.at[w, s], arrived.at[w, s]) for s in range(slots)]
-        for w in range(2)
-    ]
     weight_copy = pltpu.make_async_copy(weight, weight_held, weight_sem)
-    for copy in copies[0] + copies[1] + [weight_copy]:
-        copy.start()
+    weight_copy.start()
     across = (((1,), (1,)), ((), ()))
     places = lax.broadcasted_iota(jnp.int32, (1, stored), 1)
     blank = jnp.zeros((1, HD), jnp.float32)
@@ -285,7 +299,6 @@
         rows.append(jnp.zeros((lanes - heads * groups, width), jnp.float32))
         rows = jnp.concatenate(rows, axis=0)
         own_scores.append(jnp.sum(rows * new_keys[s : s + 1], axis=-1, keepdims=True))
-        copies[0][s].wait()
         old = lax.dot_general(
             rows.astype(jnp.bfloat16), held[0, s], across, preferred_element_type=jnp.float32
         )
@@ -302,7 +315,6 @@
     own = (own / total).astype(jnp.bfloat16).astype(jnp.float32)
     attended = []
     for s in range(slots):
-        copies[1][s].wait()
         here = slice(s * lanes, (s + 1) * lanes)
         mix = jnp.dot(
             shares[here, :].astype(jnp.bfloat16), held[1, s], preferred_element_type=jnp.float32
@@ -329,17 +341,15 @@
     return pl.pallas_call(
         functools.partial(step_kernel, heads),
         out_shape=jax.ShapeDtypeStruct((padded, weight.shape[1]), jnp.bfloat16),
-        in_specs=[SMEM_WHOLE, VMEM_WHOLE, VMEM_WHOLE, IN_PLACE, IN_PLACE],
+        in_specs=[SMEM_WHOLE] + [VMEM_WHOLE] * 3 + [IN_PLACE],
         out_specs=VMEM_WHOLE,
         scratch_shapes=[
-            pltpu.VMEM(cache.shape, jnp.bfloat16),
             pltpu.VMEM((rows, stored), jnp.float32),
             pltpu.VMEM((rows, stored), jnp.float32),
             pltpu.VMEM(weight.shape, jnp.bfloat16),
-            pltpu.SemaphoreType.DMA((2, slots)),
             pltpu.SemaphoreType.DMA(()),
         ],
-        compiler_params=params(20),
+        compiler_params=params(12),
         cost_estimate=cost(16 * cache.size, 2 * cache.size, rows * stored),
         name="step_attend",
     )(lengths, query, entries, cache, weight)
@@ -389,30 +399,21 @@
             dec_out, dec_resid = refs[:2]
             refs = refs[2:]
         if loads:
-            weights, refs = list(zip(weights, refs[:3])), refs[3:]
+            sources, weights[1:], refs = weights[1:], refs[:2], refs[2:]
         held, inner, hidden = refs[:3]
-    copies = []
+    copies = {}
     if loads:
         arrived = refs[3]
-        copies = [
-            [
-                pltpu.make_async_copy(
-                    source.at[:, pl.ds(i * chunk, chunk)], target.at[i], arrived.at[w, i]
+        for w, source in enumerate(sources, 1):
+            for i in range(weights[w].shape[0]):
+                copies[w, i] = pltpu.make_async_copy(
+                    source.at[:, pl.ds(i * chunk, chunk)], weights[w].at[i], arrived.at[w - 1, i]
                 )
-                for i in range(target.shape[0])
-            ]
-            for w, (source, target) in enumerate(weights)
-        ]
-        weights = [target for _, target in weights]
-        for pair in zip(copies[0], copies[1]):
-            for copy in pair:
-                copy.start()
-        for copy in copies[2]:
-            copy.start()
+                copies[w, i].start()
 
     def ready(w, i):
-        if loads:
-            copies[w][i].wait()
+        if (w, i) in copies:
+            copies[w, i].wait()
         return weights[w][i]
 
     piece = mine.shape[0]
@@ -491,8 +492,8 @@
         args += [dec, *dec_shares]
     args += [gain]
     split = len(weights) == 2
-    chunk = width // 4 if loads else weights[0].shape[2]
-    units = weights[0].shape[1] if loads else weights[0].shape[0] * chunk
+    chunk = weights[0].shape[2]
+    units = weights[0].shape[0] * chunk
     if split:
         shapes = [(piece, width), (rows, units)]
     else:
@@ -502,19 +503,19 @@
     if not split:
         scratch.append(pltpu.VMEM((rows, units), jnp.bfloat16))
     if loads:
-        out_shape += [stays_in_vmem((units // chunk, width, chunk))] * 2
+        out_shape += [stays_in_vmem((units // chunk, width, chunk))]
         out_shape += [stays_in_vmem((width // chunk, units, chunk))]
-        scratch.append(pltpu.SemaphoreType.DMA((3, max(units, width) // chunk)))
+        scratch.append(pltpu.SemaphoreType.DMA((2, max(units, width) // chunk)))
     return pl.pallas_call(
         functools.partial(forward_kernel, loads, chips, n_dec, len(weights), len(after), chunk),
         out_shape=out_shape,
         in_specs=[SMEM_WHOLE]
-        + [VMEM_WHOLE] * len(args)
-        + [IN_PLACE if loads else VMEM_WHOLE] * len(weights)
+        + [VMEM_WHOLE] * (len(args) + 1)
+        + [IN_PLACE if loads else VMEM_WHOLE] * (len(weights) - 1)
         + [IN_PLACE] * len(after),
         out_specs=[VMEM_WHOLE] * len(out_shape),
         scratch_shapes=scratch,
-        compiler_params=params(14),
+        compiler_params=params(9),
         cost_estimate=cost(6 * rows * width * units, 6 * width * units, rows * units),
         name="feed_forward",
     )(place, *args, *weights, *after)
@@ -631,7 +632,7 @@
         if last:
             dec_query, dec_entries = got[3:]
 
-    out_share = out_weight
+    out_share = in_hbm(out_weight)
     sib_weight, queries[-1] = lax.optimization_barrier((out_weight, queries[-1]))
     sib_weight = in_vmem(swap_cores(sib_weight))
     out_weight = in_vmem(out_weight)
@@ -644,15 +645,25 @@
     parts = []
     dec_shares = []
     for k in range(chips):
-        attended = fill_attend(
-            places[k], queries[k], prefill_cache, entries, heads, dec_shares[:1]
+        wanted = decode_cache if k == 0 else gate_weight if k == 1 else out_share
+        attended, fetched = fill_attend(
+            places[k],
+            queries[k],
+            prefill_cache,
+            entries,
+            heads,
+            wanted,
+            width // 4 if k else 0,
+            dec_shares[:1],
         )
+        if k == 1:
+            held_gate = fetched
         part, dec_shares[1:] = finish(attended, places[k], dec_shares[1:])
         parts.append(part)
         if k == 0:
             lengths, parts[0] = lax.optimization_barrier((cache_length, parts[0]))
             dec_part = step_attend(
-                lengths, dec_query, dec_entries, decode_cache, in_hbm(out_share), heads
+                lengths, dec_query, dec_entries, fetched, out_share, heads
             )
             dec_shares = [dec_part, *from_rest(dec_part)]
 
@@ -669,7 +680,7 @@
         return [from_chip(parts[(b - j) % chips], j) for j in range(1, chips)]
 
     theirs = fetch(order[0])
-    weights = [gate_weight, up_weight, down_weight]
+    weights = [held_gate, up_weight, down_weight]
     arrived, sent = [], []
     for n, b in enumerate(order):
         got = feed_forward(
@@ -691,7 +702,7 @@
             arrived.append(from_chip(both, chips - b))
             sent = [both]
         if n == 0:
-            dec_sum, dec_resid, *weights = got[3:]
+            dec_sum, dec_resid, *weights[1:] = got[3:]
             dec_others = from_rest(dec_sum)
     resid, hidden = got
     dec_sum, hidden = lax.optimization_barrier((dec_sum, hidden))

time: 103 us -> 103 us (level)
  waiting for transfers between devices: 13 us -> 14.1 us
    pallas_call x2, Pallas kernels: 9.47 us -> 12.5 us  [fill_attend(): pl.pallas_call(functools.partial(fill_kernel, groups, chips, chunk), out_...]
    pallas_call x1, Pallas kernels: 6.51 us -> 3.71 us  [step_attend(): pl.pallas_call(functools.partial(step_kernel, heads), out_shape=jax.Shape...]
    ppermute x7, waiting for transfers between devices: 2.05 us -> 3.69 us  [from_chip(): lax.ppermute(value, 'tensor', [(i, (i // 2 - step) % chips * 2 + i % 2) f...]
    pallas_call x2, Pallas kernels: 18.9 us -> 17.6 us  [feed_forward(): pl.pallas_call(functools.partial(forward_kernel, loads, chips, n_dec, len...]
  transfers between devices with their start and end apart: 32 -> 32, of which waited for: 8 -> 9; matrix products, arithmetic and copies ran while one was open for 10% -> 10% of each run, Pallas kernels for 42% -> 41%
where the time goes in v10:
time: 103 us; the launch traced here: 102 us
  Pallas kernels  49.4 us (48%)
  starting transfers between devices  24.9 us (24%)
  waiting for transfers between devices  14.1 us (14%)
  local copies, waits for them, and re-layouts  6.49 us (6%)
  other arithmetic  5.56 us (5%)
  between operations  1.69 us (2%)
    pallas_call x2, Pallas kernels, feed_forward(): pl.pallas_call(functools.partial(forward_kernel, loads, chips, n_dec, len...  17.6 us
    pallas_call x2, Pallas kernels, fill_attend(): pl.pallas_call(functools.partial(fill_kernel, groups, chips, chunk), out_...  12.5 us
    ppermute x8, starting transfers between devices, swap_groups(): return lax.ppermute(value, 'dp', [(i, i ^ mask) for i in range(count)])  11 us
    pallas_call x2, Pallas kernels, project(): pl.pallas_call(functools.partial(project_kernel, n_dec, len(after), group...  10.6 us
    ppermute x7, starting transfers between devices, from_chip(): lax.ppermute(value, 'tensor', [(i, (i // 2 - step) % chips * 2 + i % 2) f...  7.17 us
    unnamed x25, local copies, waits for them, and re-layouts  6.2 us
    ppermute x8, waiting for transfers between devices, swap_groups(): return lax.ppermute(value, 'dp', [(i, i ^ mask) for i in range(count)])  5.99 us
    ppermute x11, waiting for transfers between devices, swap_cores(): return lax.ppermute(value, 'tensor', [(i, i ^ 1) for i in range(count)])  4.36 us
  transfers between devices with their start and end apart: 32, of which 9 were waited for; matrix products, arithmetic and copies ran while one was open for 10% of the time, Pallas kernels for 41%

profile of v10, /device:TPU:0, one launch (start us, length us, event | category | flops | bytes accessed | tf_op | source)
XLA Modules:
  0.0 102.5 jit_solution(11425664188203893199)
XLA Ops:
  1.2 2.6 %collective-permute-start.8 = (bf16[128,2048]{1,0:T(8,128)(2,1)}, bf16[128,2048]{1,0:T(8,128)(2,1)S(1)}, u32[]{:S(2)}, u32[]{:S(2)}) collective-permute-start(bf16[128,2048]{1,0:T(8,128)(2,1)} %refs_0_.3), channel_id=1, source_target_pairs={{0,2},{1,3},{2,0},{3,1},{4,6},{5,7},{6,4},{7,5},{8,10},{9,11},{10,... | collective-permute-start | bytes 1572872 | tf_op jit(solution)/shard_map/ppermute | solution.py:26
  3.7 1.5 %collective-permute-start.1 = (bf16[2,2048]{1,0:T(2,128)(2,1)}, bf16[2,2048]{1,0:T(2,128)(2,1)S(1)}, u32[]{:S(2)}, u32[]{:S(2)}) collective-permute-start(bf16[2,2048]{1,0:T(2,128)(2,1)} %param.15), channel_id=1, source_target_pairs={{0,4},{4,0},{8,12},{12,8},{16,20},{20,16},{24,28},{28,24},{1,5},{5... | collective-permute-start | bytes 24584 | tf_op jit(solution)/shard_map/ppermute | solution.py:45
  6.6 1.0 fusion
  7.7 0.8 select_reduce_fusion
  9.5 1.6 %collective-permute-start.2 = (bf16[4,2048]{1,0:T(4,128)(2,1)S(1)}, bf16[4,2048]{1,0:T(4,128)(2,1)S(1)}, u32[]{:S(2)}, u32[]{:S(2)}) collective-permute-start(bf16[4,2048]{1,0:T(4,128)(2,1)S(1)} %pad_maximum_fusion.2), channel_id=1, source_target_pairs={{0,8},{4,12},{8,0},{12,4},{16,24},{20,28},{24,16},{28,20},{1,9},{5... | collective-permute-start | bytes 49160 | tf_op jit(solution)/shard_map/ppermute | solution.py:45
  11.2 2.6 %collective-permute-start.3 = (bf16[4,2048]{1,0:T(4,128)(2,1)S(1)}, bf16[4,2048]{1,0:T(4,128)(2,1)S(1)}, u32[]{:S(2)}, u32[]{:S(2)}) collective-permute-start(bf16[4,2048]{1,0:T(4,128)(2,1)S(1)} %pad_maximum_fusion.2), channel_id=1, source_target_pairs={{0,16},{4,20},{8,24},{12,28},{16,0},{20,4},{24,8},{28,12},{1,17},{... | collective-permute-start | bytes 49160 | tf_op jit(solution)/shard_map/ppermute | solution.py:45
  14.2 5.4 %copy.19 = bf16[256,8,2,512]{3,1,2,0:T(8,128)(2,1)} copy(bf16[256,8,2,512]{3,2,1,0:T(2,128)(2,1)} %bitcast.16) | data formatting | bytes 8388608
  20.4 1.6 %collective-permute-start.7 = (bf16[16,2048]{1,0:T(8,128)(2,1)S(1)}, bf16[16,2048]{1,0:T(8,128)(2,1)S(1)}, u32[]{:S(2)}, u32[]{:S(2)}) collective-permute-start(bf16[16,2048]{1,0:T(8,128)(2,1)S(1)} %convolution_convert_fusion.1.refs_6_), channel_id=1, source_target_pairs={{0,3},{1,2},{2,1},{3,0},{4,7},{5,6},{6,5},{7,4},{8,11},{9,10},{10,... | collective-permute-start | bytes 196616 | tf_op jit(solution)/shard_map/ppermute | solution.py:33
  22.1 5.0 %project.2 = (bf16[256,512]{1,0:T(8,128)(2,1)S(1)}, bf16[2,256,256]{2,1,0:T(8,128)(2,1)S(1)}, bf16[2,512,256]{2,1,0:T(8,128)(2,1)}) custom-call(s32[5]{0:T(128)S(1)} %stack.23.place, bf16[128,2048]{1,0:T(8,128)(2,1)} %refs_0_.3, bf16[128,2048]{1,0:T(8,128)(2,1)} %collective-permute-done.refs_1_, bf16[2048,1024]{1,0:T(8,128)(2,1)} %bitcast.14, ...), custom_call_target="tpu_custom_call" | custom-call | flops 1073741824 | bytes 6291456 | tf_op jit(solution)/shard_map/project/pallas_call | solution.py:174
  27.2 0.8 copy-done.4
  27.9 5.6 %project.3 = (bf16[256,512]{1,0:T(8,128)(2,1)S(1)}, bf16[2,256,256]{2,1,0:T(8,128)(2,1)S(1)}, bf16[2,512,256]{2,1,0:T(8,128)(2,1)}, f32[16,512]{1,0:T(8,128)S(1)}, bf16[2,8,256]{2,1,0:T(8,128)(2,1)}) custom-call(s32[5]{0:T(128)S(1)} %stack.24.place, bf16[128,2048]{1,0:T(8,128)(2,1)} %copy-done.2, ...), custom_call_target="tpu_custom_call", output_to_operand_aliasing={{2}: (11, {})} | custom-call | flops 1140850688 | bytes 6422528 | tf_op jit(solution)/shard_map/project/pallas_call | solution.py:174
  34.2 6.1 %fill_attend.2 = (bf16[256,512]{1,0:T(8,128)(2,1)S(1)}, bf16[2,8,1024,256]{3,2,1,0:T(8,128)(2,1)S(1)}) custom-call(s32[5]{0:T(128)S(1)} %stack.23.place, bf16[256,512]{1,0:T(8,128)(2,1)S(1)} %get-tuple-element.46.refs_9_.query, bf16[2,1,1024,256]{3,2,1,0:T(8,128)(2,1)} %cache_value.3, bf16[2,1,1024,256]{3,2,1,0:T(8,128)(2,1)} %cache_value.3, ...), custom_call_target="tpu_custom_call" | custom-call | flops 1610612736 | bytes 1048576 | tf_op jit(solution)/shard_map/fill_attend/pallas_call | solution.py:254
  40.4 1.5 %collective-permute-done.10.sib = bf16[256,512]{1,0:T(8,128)(2,1)S(1)} collective-permute-done((bf16[256,512]{1,0:T(8,128)(2,1)S(1)}, bf16[256,512]{1,0:T(8,128)(2,1)S(1)}, u32[]{:S(2)}, u32[]{:S(2)}) %collective-permute-start.10) | collective-permute-done | bytes 262176 | tf_op jit(solution)/shard_map/ppermute | solution.py:20
  41.9 1.2 %out_project.2.refs_2_ = bf16[256,1024]{1,0:T(8,128)(2,1)S(1)} custom-call(s32[5]{0:T(128)S(1)} %stack.23.place, bf16[256,512]{1,0:T(8,128)(2,1)S(1)} %get-tuple-element.53.mine, bf16[256,512]{1,0:T(8,128)(2,1)S(1)} %collective-permute-done.10.sib, bf16[512,2048]{1,0:T(8,128)(2,1)S(1)} %copy-done, bf16[512,2048]{1,0:T(8,128)(2,1)S(1)} %collective-permute-done.11.sib_weight), custom_call_target="tpu_custom_call" | custom-call | flops 536870912 | bytes 3670016 | tf_op jit(solution)/shard_map/out_project/pallas_call | solution.py:370
  43.7 3.7 %step_attend.1.refs_5_.refs_7_ = bf16[16,2048]{1,0:T(8,128)(2,1)S(1)} custom-call(s32[8]{0:T(128)S(1)} %copy-done.10, f32[16,512]{1,0:T(8,128)S(1)} %get-tuple-element.59.query, bf16[2,8,256]{2,1,0:T(8,128)(2,1)S(1)} %copy-done.9, bf16[2,8,1024,256]{3,2,1,0:T(8,128)(2,1)S(1)} %get-tuple-element.61.held, bf16[512,2048]{1,0:T(8,128)(2,1)} %weight.5), custom_call_target="tpu_custom_call" | custom-call | flops 67108864 | bytes 8388608 | tf_op jit(solution)/shard_map/step_attend/pallas_call | solution.py:341
  47.5 1.6 %collective-permute-start.13 = (bf16[16,2048]{1,0:T(8,128)(2,1)S(1)}, bf16[16,2048]{1,0:T(8,128)(2,1)S(1)}, u32[]{:S(2)}, u32[]{:S(2)}) collective-permute-start(bf16[16,2048]{1,0:T(8,128)(2,1)S(1)} %step_attend.1.refs_5_.refs_7_), channel_id=1, source_target_pairs={{0,2},{1,3},{2,0},{3,1},{4,6},{5,7},{6,4},{7,5},{8,10},{9,11},{10,... | collective-permute-start | bytes 196616 | tf_op jit(solution)/shard_map/ppermute | solution.py:26
  49.7 6.4 %fill_attend.3 = (bf16[256,512]{1,0:T(8,128)(2,1)S(1)}, bf16[4,2048,512]{2,1,0:T(8,128)(2,1)S(1)}) custom-call(s32[5]{0:T(128)S(1)} %stack.24.place, bf16[256,512]{1,0:T(8,128)(2,1)S(1)} %get-tuple-element.57.query, bf16[2,1,1024,256]{3,2,1,0:T(8,128)(2,1)} %cache_value.3, bf16[2,1,1024,256]{3,2,1,0:T(8,128)(2,1)} %cache_value.3, ...), custom_call_target="tpu_custom_call" | custom-call | flops 1610612736 | bytes 1048576 | tf_op jit(solution)/shard_map/fill_attend/pallas_call | solution.py:254
  56.1 3.1 %collective-permute-done.13.refs_8_ = bf16[16,2048]{1,0:T(8,128)(2,1)S(1)} collective-permute-done((bf16[16,2048]{1,0:T(8,128)(2,1)S(1)}, bf16[16,2048]{1,0:T(8,128)(2,1)S(1)}, u32[]{:S(2)}, u32[]{:S(2)}) %collective-permute-start.13) | collective-permute-done | bytes 65568 | tf_op jit(solution)/shard_map/ppermute | solution.py:26
  59.8 1.2 %collective-permute-done.16.sib = bf16[256,512]{1,0:T(8,128)(2,1)S(1)} collective-permute-done((bf16[256,512]{1,0:T(8,128)(2,1)S(1)}, bf16[256,512]{1,0:T(8,128)(2,1)S(1)}, u32[]{:S(2)}, u32[]{:S(2)}) %collective-permute-start.16) | collective-permute-done | bytes 262176 | tf_op jit(solution)/shard_map/ppermute | solution.py:20
  61.0 1.2 %out_project.3.refs_2_ = bf16[256,1024]{1,0:T(8,128)(2,1)S(1)} custom-call(s32[5]{0:T(128)S(1)} %stack.24.place, bf16[256,512]{1,0:T(8,128)(2,1)S(1)} %get-tuple-element.63.mine, bf16[256,512]{1,0:T(8,128)(2,1)S(1)} %collective-permute-done.16.sib, bf16[512,2048]{1,0:T(8,128)(2,1)S(1)} %copy-done.1, bf16[512,2048]{1,0:T(8,128)(2,1)S(1)} %collective-permute-done.11.sib_weight), custom_call_target="tpu_custom_call" | custom-call | flops 536870912 | bytes 3670016 | tf_op jit(solution)/shard_map/out_project/pallas_call | solution.py:370
  63.4 0.8 collective-permute-done.18.refs_3_
  64.2 0.7 collective-permute-done.20.refs_5_
  65.0 10.9 %feed_forward.2 = (bf16[128,2048]{1,0:T(8,128)(2,1)S(1)}, bf16[128,2048]{1,0:T(8,128)(2,1)S(1)}, bf16[128,2048]{1,0:T(8,128)(2,1)}, bf16[16,2048]{1,0:T(8,128)(2...) custom-call(s32[5]{0:T(128)S(1)} %stack.24.place, ...), custom_call_target="tpu_custom_call" | custom-call | flops 6845104128 | bytes 25165824 | tf_op jit(solution)/shard_map/feed_forward/pallas_call | solution.py:509
  77.9 1.3 %collective-permute-start.25 = (bf16[16,2048]{1,0:T(8,128)(2,1)S(1)}, bf16[16,2048]{1,0:T(8,128)(2,1)S(1)}, u32[]{:S(2)}, u32[]{:S(2)}) collective-permute-start(bf16[16,2048]{1,0:T(8,128)(2,1)S(1)} %get-tuple-element.79), channel_id=1, source_target_pairs={{0,3},{1,2},{2,1},{3,0},{4,7},{5,6},{6,5},{7,4},{8,11},{9,10},{10,... | collective-permute-start | bytes 196616 | tf_op jit(solution)/shard_map/ppermute | solution.py:33
  79.3 0.8 collective-permute-start.26
  80.1 6.7 %feed_forward.3 = (bf16[128,2048]{1,0:T(8,128)(2,1)S(1)}, bf16[256,2048]{1,0:T(8,128)(2,1)S(1)}) custom-call(s32[5]{0:T(128)S(1)} %stack.23.place, bf16[128,2048]{1,0:T(8,128)(2,1)S(1)} %copy-done.6, bf16[128,2048]{1,0:T(8,128)(2,1)} %collective-permute-done.refs_1_, bf16[256,1024]{1,0:T(8,128)(2,1)S(1)} %out_project.2.refs_2_, ...), custom_call_target="tpu_custom_call" | custom-call | flops 6442450944 | bytes 25165824 | tf_op jit(solution)/shard_map/feed_forward/pallas_call | solution.py:509
  87.1 0.8 collective-permute-start.27
  87.9 3.4 %collective-permute-start.28 = (bf16[4,2048]{1,0:T(4,128)(2,1)S(1)}, bf16[4,2048]{1,0:T(4,128)(2,1)S(1)}, u32[]{:S(2)}, u32[]{:S(2)}) collective-permute-start(bf16[4,2048]{1,0:T(4,128)(2,1)S(1)} %get-tuple-element.90), channel_id=1, source_target_pairs={{0,16},{4,20},{8,24},{12,28},{16,0},{20,4},{24,8},{28,12},{1,17},{... | collective-permute-start | bytes 49160 | tf_op jit(solution)/shard_map/ppermute | solution.py:45
  91.5 2.4 %lower.1 = (bf16[128,2048]{1,0:T(8,128)(2,1)S(1)}, bf16[128,2048]{1,0:T(8,128)(2,1)S(1)}) custom-call(bf16[256,2048]{1,0:T(8,128)(2,1)S(1)} %get-tuple-element.76.hidden, bf16[4,2048,512]{2,1,0:T(8,128)(2,1)S(1)} %get-tuple-element.77.down, bf16[16,2048]{1,0:T(8,128)(2,1)S(1)} %convolution_convert_fusion.refs_0_), custom_call_target="tpu_custom_call" | custom-call | flops 2147483648 | bytes 8388608 | tf_op jit(solution)/shard_map/lower/pallas_call | solution.py:474
  94.0 2.9 %collective-permute-done.29 = bf16[4,2048]{1,0:T(4,128)(2,1)S(1)} collective-permute-done((bf16[4,2048]{1,0:T(4,128)(2,1)S(1)}, bf16[4,2048]{1,0:T(4,128)(2,1)S(1)}, u32[]{:S(2)}, u32[]{:S(2)}) %collective-permute-start.29) | collective-permute-done | bytes 16416 | tf_op jit(solution)/shard_map/ppermute | solution.py:45
  97.6 3.1 %collective-permute-done.31 = bf16[2,2048]{1,0:T(2,128)(2,1)S(1)} collective-permute-done((bf16[2,2048]{1,0:T(2,128)(2,1)S(1)}, bf16[2,2048]{1,0:T(2,128)(2,1)S(1)}, u32[]{:S(2)}, u32[]{:S(2)}) %collective-permute-start.31) | collective-permute-done | bytes 8224 | tf_op jit(solution)/shard_map/ppermute | solution.py:45
  101.3 1.1 %add_convert_fusion = bf16[128,2048]{1,0:T(8,128)(2,1)} fusion(bf16[128,2048]{1,0:T(8,128)(2,1)S(1)} %collective-permute-done.26, bf16[128,2048]{1,0:T(8,128)(2,1)S(1)} %collective-permute-done.30, bf16[128,2048]{1,0:T(8,128)(2,1)S(1)} %get-tuple-element.80, bf16[128,2048]{1,0:T(8,128)(2,1)S(1)} %get-tuple-element.73), kind=kLoop, calls=%fused_computation.2 | loop fusion | flops 2097152 | bytes 2621440 | tf_op jit(solution)/shard_map/convert_element_type | solution.py:537
  (90 shorter events, 11.1 us)
Async XLA Ops:
  0.7 21.4 %collective-permute-start = (bf16[128,2048]{1,0:T(8,128)(2,1)}, bf16[128,2048]{1,0:T(8,128)(2,1)}, u32[]{:S(2)}, u32[]{:S(2)}) collective-permute-start(bf16[128,2048]{1,0:T(8,128)(2,1)} %refs_0_.3), channel_id=1, source_target_pairs={{0,1},{1,0},{2,3},{3,2},{4,5},{5,4},{6,7},{7,6},{8,9},{9,8},{10,11... | collective-permute-start | bytes 1572872 | tf_op jit(solution)/shard_map/ppermute | solution.py:20
  1.2 20.9 %collective-permute-start.8 = (bf16[128,2048]{1,0:T(8,128)(2,1)}, bf16[128,2048]{1,0:T(8,128)(2,1)S(1)}, u32[]{:S(2)}, u32[]{:S(2)}) collective-permute-start(bf16[128,2048]{1,0:T(8,128)(2,1)} %refs_0_.3), channel_id=1, source_target_pairs={{0,2},{1,3},{2,0},{3,1},{4,6},{5,7},{6,4},{7,5},{8,10},{9,11},{10,... | collective-permute-start | bytes 1572872 | tf_op jit(solution)/shard_map/ppermute | solution.py:26
  3.7 5.1 %collective-permute-start.1 = (bf16[2,2048]{1,0:T(2,128)(2,1)}, bf16[2,2048]{1,0:T(2,128)(2,1)S(1)}, u32[]{:S(2)}, u32[]{:S(2)}) collective-permute-start(bf16[2,2048]{1,0:T(2,128)(2,1)} %param.15), channel_id=1, source_target_pairs={{0,4},{4,0},{8,12},{12,8},{16,20},{20,16},{24,28},{28,24},{1,5},{5... | collective-permute-start | bytes 24584 | tf_op jit(solution)/shard_map/ppermute | solution.py:45
  9.5 10.1 %collective-permute-start.2 = (bf16[4,2048]{1,0:T(4,128)(2,1)S(1)}, bf16[4,2048]{1,0:T(4,128)(2,1)S(1)}, u32[]{:S(2)}, u32[]{:S(2)}) collective-permute-start(bf16[4,2048]{1,0:T(4,128)(2,1)S(1)} %pad_maximum_fusion.2), channel_id=1, source_target_pairs={{0,8},{4,12},{8,0},{12,4},{16,24},{20,28},{24,16},{28,20},{1,9},{5... | collective-permute-start | bytes 49160 | tf_op jit(solution)/shard_map/ppermute | solution.py:45
  11.2 8.4 %collective-permute-start.3 = (bf16[4,2048]{1,0:T(4,128)(2,1)S(1)}, bf16[4,2048]{1,0:T(4,128)(2,1)S(1)}, u32[]{:S(2)}, u32[]{:S(2)}) collective-permute-start(bf16[4,2048]{1,0:T(4,128)(2,1)S(1)} %pad_maximum_fusion.2), channel_id=1, source_target_pairs={{0,16},{4,20},{8,24},{12,28},{16,0},{20,4},{24,8},{28,12},{1,17},{... | collective-permute-start | bytes 49160 | tf_op jit(solution)/shard_map/ppermute | solution.py:45
  13.8 5.8 %collective-permute-start.4 = (bf16[4,2048]{1,0:T(4,128)(2,1)S(1)}, bf16[4,2048]{1,0:T(4,128)(2,1)S(1)}, u32[]{:S(2)}, u32[]{:S(2)}) collective-permute-start(bf16[4,2048]{1,0:T(4,128)(2,1)S(1)} %pad_maximum_fusion.2), channel_id=1, source_target_pairs={{0,24},{4,28},{8,16},{12,20},{16,8},{20,12},{24,0},{28,4},{1,25},{... | collective-permute-start | bytes 49160 | tf_op jit(solution)/shard_map/ppermute | solution.py:45
  19.8 7.2 %collective-permute-start.5 = (bf16[16,2048]{1,0:T(8,128)(2,1)S(1)}, bf16[16,2048]{1,0:T(8,128)(2,1)S(1)}, u32[]{:S(2)}, u32[]{:S(2)}) collective-permute-start(bf16[16,2048]{1,0:T(8,128)(2,1)S(1)} %convolution_convert_fusion.1.refs_6_), channel_id=1, source_target_pairs={{0,2},{1,3},{2,0},{3,1},{4,6},{5,7},{6,4},{7,5},{8,10},{9,11},{10,... | collective-permute-start | bytes 196616 | tf_op jit(solution)/shard_map/ppermute | solution.py:26
  20.4 6.6 %collective-permute-start.6 = (bf16[16,2048]{1,0:T(8,128)(2,1)S(1)}, bf16[16,2048]{1,0:T(8,128)(2,1)S(1)}, u32[]{:S(2)}, u32[]{:S(2)}) collective-permute-start(bf16[16,2048]{1,0:T(8,128)(2,1)S(1)} %convolution_convert_fusion.1.refs_6_), channel_id=1, source_target_pairs={{0,1},{1,0},{2,3},{3,2},{4,5},{5,4},{6,7},{7,6},{8,9},{9,8},{10,11... | collective-permute-start | bytes 196616 | tf_op jit(solution)/shard_map/ppermute | solution.py:33
  20.4 6.6 %collective-permute-start.7 = (bf16[16,2048]{1,0:T(8,128)(2,1)S(1)}, bf16[16,2048]{1,0:T(8,128)(2,1)S(1)}, u32[]{:S(2)}, u32[]{:S(2)}) collective-permute-start(bf16[16,2048]{1,0:T(8,128)(2,1)S(1)} %convolution_convert_fusion.1.refs_6_), channel_id=1, source_target_pairs={{0,3},{1,2},{2,1},{3,0},{4,7},{5,6},{6,5},{7,4},{8,11},{9,10},{10,... | collective-permute-start | bytes 196616 | tf_op jit(solution)/shard_map/ppermute | solution.py:33
  22.1 5.1 %collective-permute-start.9 = (bf16[128,2048]{1,0:T(8,128)(2,1)S(1)}, bf16[128,2048]{1,0:T(8,128)(2,1)S(1)}, u32[]{:S(2)}, u32[]{:S(2)}) collective-permute-start(bf16[128,2048]{1,0:T(8,128)(2,1)S(1)} %collective-permute-done.8.refs_0_), channel_id=1, source_target_pairs={{0,1},{1,0},{2,3},{3,2},{4,5},{5,4},{6,7},{7,6},{8,9},{9,8},{10,11... | collective-permute-start | bytes 1572872 | tf_op jit(solution)/shard_map/ppermute | solution.py:20
  33.6 8.3 %collective-permute-start.11 = (bf16[512,2048]{1,0:T(8,128)(2,1)S(1)}, bf16[512,2048]{1,0:T(8,128)(2,1)S(1)}, u32[]{:S(2)}, u32[]{:S(2)}) collective-permute-start(bf16[512,2048]{1,0:T(8,128)(2,1)S(1)} %copy-done), channel_id=1, source_target_pairs={{0,1},{1,0},{2,3},{3,2},{4,5},{5,4},{6,7},{7,6},{8,9},{9,8},{10,11... | collective-permute-start | bytes 6291464 | tf_op jit(solution)/shard_map/ppermute | solution.py:20
  40.3 1.6 %collective-permute-start.10 = (bf16[256,512]{1,0:T(8,128)(2,1)S(1)}, bf16[256,512]{1,0:T(8,128)(2,1)S(1)}, u32[]{:S(2)}, u32[]{:S(2)}) collective-permute-start(bf16[256,512]{1,0:T(8,128)(2,1)S(1)} %get-tuple-element.53.mine), channel_id=1, source_target_pairs={{0,1},{1,0},{2,3},{3,2},{4,5},{5,4},{6,7},{7,6},{8,9},{9,8},{10,11... | collective-permute-start | bytes 786440 | tf_op jit(solution)/shard_map/ppermute | solution.py:20
  43.1 19.5 %collective-permute-start.19 = (bf16[256,1024]{1,0:T(8,128)(2,1)S(1)}, bf16[256,1024]{1,0:T(8,128)(2,1)S(1)}, u32[]{:S(2)}, u32[]{:S(2)}) collective-permute-start(bf16[256,1024]{1,0:T(8,128)(2,1)S(1)} %out_project.2.refs_2_), channel_id=1, source_target_pairs={{0,2},{1,3},{2,0},{3,1},{4,6},{5,7},{6,4},{7,5},{8,10},{9,11},{10,... | collective-permute-start | bytes 1572872 | tf_op jit(solution)/shard_map/ppermute | solution.py:26
  47.5 11.8 %collective-permute-start.13 = (bf16[16,2048]{1,0:T(8,128)(2,1)S(1)}, bf16[16,2048]{1,0:T(8,128)(2,1)S(1)}, u32[]{:S(2)}, u32[]{:S(2)}) collective-permute-start(bf16[16,2048]{1,0:T(8,128)(2,1)S(1)} %step_attend.1.refs_5_.refs_7_), channel_id=1, source_target_pairs={{0,2},{1,3},{2,0},{3,1},{4,6},{5,7},{6,4},{7,5},{8,10},{9,11},{10,... | collective-permute-start | bytes 196616 | tf_op jit(solution)/shard_map/ppermute | solution.py:26
  49.1 10.2 %collective-permute-start.14 = (bf16[16,2048]{1,0:T(8,128)(2,1)S(1)}, bf16[16,2048]{1,0:T(8,128)(2,1)S(1)}, u32[]{:S(2)}, u32[]{:S(2)}) collective-permute-start(bf16[16,2048]{1,0:T(8,128)(2,1)S(1)} %step_attend.1.refs_5_.refs_7_), channel_id=1, source_target_pairs={{0,1},{1,0},{2,3},{3,2},{4,5},{5,4},{6,7},{7,6},{8,9},{9,8},{10,11... | collective-permute-start | bytes 196616 | tf_op jit(solution)/shard_map/ppermute | solution.py:33
  49.1 10.2 %collective-permute-start.15 = (bf16[16,2048]{1,0:T(8,128)(2,1)S(1)}, bf16[16,2048]{1,0:T(8,128)(2,1)S(1)}, u32[]{:S(2)}, u32[]{:S(2)}) collective-permute-start(bf16[16,2048]{1,0:T(8,128)(2,1)S(1)} %step_attend.1.refs_5_.refs_7_), channel_id=1, source_target_pairs={{0,3},{1,2},{2,1},{3,0},{4,7},{5,6},{6,5},{7,4},{8,11},{9,10},{10,... | collective-permute-start | bytes 196616 | tf_op jit(solution)/shard_map/ppermute | solution.py:33
  59.3 1.7 %collective-permute-start.16 = (bf16[256,512]{1,0:T(8,128)(2,1)S(1)}, bf16[256,512]{1,0:T(8,128)(2,1)S(1)}, u32[]{:S(2)}, u32[]{:S(2)}) collective-permute-start(bf16[256,512]{1,0:T(8,128)(2,1)S(1)} %get-tuple-element.63.mine), channel_id=1, source_target_pairs={{0,1},{1,0},{2,3},{3,2},{4,5},{5,4},{6,7},{7,6},{8,9},{9,8},{10,11... | collective-permute-start | bytes 786440 | tf_op jit(solution)/shard_map/ppermute | solution.py:20
  62.2 2.0 %collective-permute-start.18 = (bf16[256,1024]{1,0:T(8,128)(2,1)S(1)}, bf16[256,1024]{1,0:T(8,128)(2,1)S(1)}, u32[]{:S(2)}, u32[]{:S(2)}) collective-permute-start(bf16[256,1024]{1,0:T(8,128)(2,1)S(1)} %out_project.3.refs_2_), channel_id=1, source_target_pairs={{0,1},{1,0},{2,3},{3,2},{4,5},{5,4},{6,7},{7,6},{8,9},{9,8},{10,11... | collective-permute-start | bytes 1572872 | tf_op jit(solution)/shard_map/ppermute | solution.py:20
  62.7 2.3 %collective-permute-start.20 = (bf16[256,1024]{1,0:T(8,128)(2,1)S(1)}, bf16[256,1024]{1,0:T(8,128)(2,1)S(1)}, u32[]{:S(2)}, u32[]{:S(2)}) collective-permute-start(bf16[256,1024]{1,0:T(8,128)(2,1)S(1)} %collective-permute-done.19.refs_4_), channel_id=1, source_target_pairs={{0,1},{1,0},{2,3},{3,2},{4,5},{5,4},{6,7},{7,6},{8,9},{9,8},{10,11... | collective-permute-start | bytes 1572872 | tf_op jit(solution)/shard_map/ppermute | solution.py:20
  62.8 14.2 %collective-permute-start.17 = (bf16[256,1024]{1,0:T(8,128)(2,1)S(1)}, bf16[256,1024]{1,0:T(8,128)(2,1)S(1)}, u32[]{:S(2)}, u32[]{:S(2)}) collective-permute-start(bf16[256,1024]{1,0:T(8,128)(2,1)S(1)} %out_project.3.refs_2_), channel_id=1, source_target_pairs={{0,2},{1,3},{2,0},{3,1},{4,6},{5,7},{6,4},{7,5},{8,10},{9,11},{10,... | collective-permute-start | bytes 1572872 | tf_op jit(solution)/shard_map/ppermute | solution.py:26
  75.9 2.0 %collective-permute-start.22 = (bf16[128,2048]{1,0:T(8,128)(2,1)S(1)}, bf16[128,2048]{1,0:T(8,128)(2,1)S(1)}, u32[]{:S(2)}, u32[]{:S(2)}) collective-permute-start(bf16[128,2048]{1,0:T(8,128)(2,1)S(1)} %get-tuple-element.72), channel_id=1, source_target_pairs={{0,1},{1,0},{2,3},{3,2},{4,5},{5,4},{6,7},{7,6},{8,9},{9,8},{10,11... | collective-permute-start | bytes 1572872 | tf_op jit(solution)/shard_map/ppermute | solution.py:20
  76.3 3.0 %collective-permute-start.12 = (bf16[256,1024]{1,0:T(8,128)(2,1)S(1)}, bf16[256,1024]{1,0:T(8,128)(2,1)S(1)}, u32[]{:S(2)}, u32[]{:S(2)}) collective-permute-start(bf16[256,1024]{1,0:T(8,128)(2,1)S(1)} %out_project.2.refs_2_), channel_id=1, source_target_pairs={{0,1},{1,0},{2,3},{3,2},{4,5},{5,4},{6,7},{7,6},{8,9},{9,8},{10,11... | collective-permute-start | bytes 1572872 | tf_op jit(solution)/shard_map/ppermute | solution.py:20
  77.0 3.1 %collective-permute-start.21 = (bf16[256,1024]{1,0:T(8,128)(2,1)S(1)}, bf16[256,1024]{1,0:T(8,128)(2,1)S(1)}, u32[]{:S(2)}, u32[]{:S(2)}) collective-permute-start(bf16[256,1024]{1,0:T(8,128)(2,1)S(1)} %collective-permute-done.17.refs_4_), channel_id=1, source_target_pairs={{0,1},{1,0},{2,3},{3,2},{4,5},{5,4},{6,7},{7,6},{8,9},{9,8},{10,11... | collective-permute-start | bytes 1572872 | tf_op jit(solution)/shard_map/ppermute | solution.py:20
  77.0 9.8 %collective-permute-start.23 = (bf16[16,2048]{1,0:T(8,128)(2,1)S(1)}, bf16[16,2048]{1,0:T(8,128)(2,1)S(1)}, u32[]{:S(2)}, u32[]{:S(2)}) collective-permute-start(bf16[16,2048]{1,0:T(8,128)(2,1)S(1)} %get-tuple-element.79), channel_id=1, source_target_pairs={{0,2},{1,3},{2,0},{3,1},{4,6},{5,7},{6,4},{7,5},{8,10},{9,11},{10,... | collective-permute-start | bytes 196616 | tf_op jit(solution)/shard_map/ppermute | solution.py:26
  77.5 9.3 %collective-permute-start.24 = (bf16[16,2048]{1,0:T(8,128)(2,1)S(1)}, bf16[16,2048]{1,0:T(8,128)(2,1)S(1)}, u32[]{:S(2)}, u32[]{:S(2)}) collective-permute-start(bf16[16,2048]{1,0:T(8,128)(2,1)S(1)} %get-tuple-element.79), channel_id=1, source_target_pairs={{0,1},{1,0},{2,3},{3,2},{4,5},{5,4},{6,7},{7,6},{8,9},{9,8},{10,11... | collective-permute-start | bytes 196616 | tf_op jit(solution)/shard_map/ppermute | solution.py:33
  77.9 9.0 %collective-permute-start.25 = (bf16[16,2048]{1,0:T(8,128)(2,1)S(1)}, bf16[16,2048]{1,0:T(8,128)(2,1)S(1)}, u32[]{:S(2)}, u32[]{:S(2)}) collective-permute-start(bf16[16,2048]{1,0:T(8,128)(2,1)S(1)} %get-tuple-element.79), channel_id=1, source_target_pairs={{0,3},{1,2},{2,1},{3,0},{4,7},{5,6},{6,5},{7,4},{8,11},{9,10},{10,... | collective-permute-start | bytes 196616 | tf_op jit(solution)/shard_map/ppermute | solution.py:33
  79.3 17.6 %collective-permute-start.26 = (bf16[128,2048]{1,0:T(8,128)(2,1)S(1)}, bf16[128,2048]{1,0:T(8,128)(2,1)S(1)}, u32[]{:S(2)}, u32[]{:S(2)}) collective-permute-start(bf16[128,2048]{1,0:T(8,128)(2,1)S(1)} %add_convert_fusion.1.refs_9_), channel_id=1, source_target_pairs={{0,2},{1,3},{2,0},{3,1},{4,6},{5,7},{6,4},{7,5},{8,10},{9,11},{10,... | collective-permute-start | bytes 1572872 | tf_op jit(solution)/shard_map/ppermute | solution.py:26
  87.1 6.9 %collective-permute-start.27 = (bf16[4,2048]{1,0:T(4,128)(2,1)S(1)}, bf16[4,2048]{1,0:T(4,128)(2,1)S(1)}, u32[]{:S(2)}, u32[]{:S(2)}) collective-permute-start(bf16[4,2048]{1,0:T(4,128)(2,1)S(1)} %get-tuple-element.88), channel_id=1, source_target_pairs={{0,8},{4,12},{8,0},{12,4},{16,24},{20,28},{24,16},{28,20},{1,9},{5... | collective-permute-start | bytes 49160 | tf_op jit(solution)/shard_map/ppermute | solution.py:45
  87.9 6.1 %collective-permute-start.28 = (bf16[4,2048]{1,0:T(4,128)(2,1)S(1)}, bf16[4,2048]{1,0:T(4,128)(2,1)S(1)}, u32[]{:S(2)}, u32[]{:S(2)}) collective-permute-start(bf16[4,2048]{1,0:T(4,128)(2,1)S(1)} %get-tuple-element.90), channel_id=1, source_target_pairs={{0,16},{4,20},{8,24},{12,28},{16,0},{20,4},{24,8},{28,12},{1,17},{... | collective-permute-start | bytes 49160 | tf_op jit(solution)/shard_map/ppermute | solution.py:45
  91.3 5.5 %collective-permute-start.29 = (bf16[4,2048]{1,0:T(4,128)(2,1)S(1)}, bf16[4,2048]{1,0:T(4,128)(2,1)S(1)}, u32[]{:S(2)}, u32[]{:S(2)}) collective-permute-start(bf16[4,2048]{1,0:T(4,128)(2,1)S(1)} %get-tuple-element.89), channel_id=1, source_target_pairs={{0,24},{4,28},{8,16},{12,20},{16,8},{20,12},{24,0},{28,4},{1,25},{... | collective-permute-start | bytes 49160 | tf_op jit(solution)/shard_map/ppermute | solution.py:45
  96.9 4.4 %collective-permute-start.30 = (bf16[128,2048]{1,0:T(8,128)(2,1)S(1)}, bf16[128,2048]{1,0:T(8,128)(2,1)S(1)}, u32[]{:S(2)}, u32[]{:S(2)}) collective-permute-start(bf16[128,2048]{1,0:T(8,128)(2,1)S(1)} %get-tuple-element.82), channel_id=1, source_target_pairs={{0,1},{1,0},{2,3},{3,2},{4,5},{5,4},{6,7},{7,6},{8,9},{9,8},{10,11... | collective-permute-start | bytes 1572872 | tf_op jit(solution)/shard_map/ppermute | solution.py:20
  97.0 3.7 %collective-permute-start.31 = (bf16[2,2048]{1,0:T(2,128)(2,1)S(1)}, bf16[2,2048]{1,0:T(2,128)(2,1)S(1)}, u32[]{:S(2)}, u32[]{:S(2)}) collective-permute-start(bf16[2,2048]{1,0:T(2,128)(2,1)S(1)} %slice.29), channel_id=1, source_target_pairs={{0,4},{4,0},{8,12},{12,8},{16,20},{20,16},{24,28},{28,24},{1,5},{5... | collective-permute-start | bytes 24584 | tf_op jit(solution)/shard_map/ppermute | solution.py:45
  (12 other events, 160.5 us)

commit v11 on v10

--- a/solution.py
+++ b/solution.py
@@ -637,10 +637,8 @@
     sib_weight = in_vmem(swap_cores(sib_weight))
     out_weight = in_vmem(out_weight)
 
-    def finish(attended, place, before):
-        attended, *before = lax.optimization_barrier((attended, *before))
-        sib = swap_cores(attended)
-        return out_project(place, attended, sib, out_weight, sib_weight), before
+    def finish(attended, place):
+        return out_project(place, attended, swap_cores(attended), out_weight, sib_weight)
 
     parts = []
     dec_shares = []
@@ -658,8 +656,7 @@
         )
         if k == 1:
             held_gate = fetched
-        part, dec_shares[1:] = finish(attended, places[k], dec_shares[1:])
-        parts.append(part)
+        parts.append(finish(attended, places[k]))
         if k == 0:
             lengths, parts[0] = lax.optimization_barrier((cache_length, parts[0]))
             dec_part = step_attend(
@@ -679,7 +676,7 @@
     def fetch(b):
         return [from_chip(parts[(b - j) % chips], j) for j in range(1, chips)]
 
-    theirs = fetch(order[0])
+    theirs, dec_shares[1:] = lax.optimization_barrier((fetch(order[0]), dec_shares[1:]))
     weights = [held_gate, up_weight, down_weight]
     arrived, sent = [], []
     for n, b in enumerate(order):
@@ -720,9 +717,10 @@
     )
     *arrived, rows, give = lax.optimization_barrier((*arrived, rows, give))
     pairs = rows.reshape(low, per_device, width)
-    routed = add(pairs[0], *[swap_groups(pairs[i], i) for i in range(1, low)])
-
+    others = [swap_groups(pairs[i], i) for i in range(1, low)]
     prefill_out = add(resid, keep, swap_cores(give), *arrived)
+    others, prefill_out = lax.optimization_barrier((others, prefill_out))
+    routed = add(pairs[0], *others)
     return (prefill_out, routed, everything, dec_entries)
 
 

time: 103 us -> 99.4 us (0.965)
  waiting for transfers between devices: 14.1 us -> 9.66 us
    ppermute x8, waiting for transfers between devices: 5.99 us -> 3.6 us  [swap_groups(): return lax.ppermute(value, 'dp', [(i, i ^ mask) for i in range(count)])]
    ppermute x7, starting transfers between devices: 7.17 us -> 9.25 us  [from_chip(): lax.ppermute(value, 'tensor', [(i, (i // 2 - step) % chips * 2 + i % 2) f...]
    ppermute x7, waiting for transfers between devices: 3.69 us -> 1.74 us  [from_chip(): lax.ppermute(value, 'tensor', [(i, (i // 2 - step) % chips * 2 + i % 2) f...]
    ppermute x11, waiting for transfers between devices: 4.36 us -> 3.16 us  [swap_cores(): return lax.ppermute(value, 'tensor', [(i, i ^ 1) for i in range(count)])]
    ppermute x6, waiting for transfers between devices: 0.02 us -> 1.16 us  [from_other(): lax.ppermute(value, 'tensor', [(i, (i // 2 - step) % (count // 2) * 2 + 1...]
  transfers between devices with their start and end apart: 32 -> 32, of which waited for: 9 -> 8; matrix products, arithmetic and copies ran while one was open for 10% -> 11% of each run, Pallas kernels for 41% -> 43%
where the time goes in v11:
time: 99.4 us; the launch traced here: 99 us
  Pallas kernels  49.5 us (50%)
  starting transfers between devices  25.8 us (26%)
  waiting for transfers between devices  9.66 us (10%)
  local copies, waits for them, and re-layouts  6.49 us (7%)
  other arithmetic  5.56 us (6%)
  between operations  1.7 us (2%)
    pallas_call x2, Pallas kernels, feed_forward(): pl.pallas_call(functools.partial(forward_kernel, loads, chips, n_dec, len...  17.6 us
    pallas_call x2, Pallas kernels, fill_attend(): pl.pallas_call(functools.partial(fill_kernel, groups, chips, chunk), out_...  12.6 us
    ppermute x8, starting transfers between devices, swap_groups(): return lax.ppermute(value, 'dp', [(i, i ^ mask) for i in range(count)])  11 us
    pallas_call x2, Pallas kernels, project(): pl.pallas_call(functools.partial(project_kernel, n_dec, len(after), group...  10.6 us
    ppermute x7, starting transfers between devices, from_chip(): lax.ppermute(value, 'tensor', [(i, (i // 2 - step) % chips * 2 + i % 2) f...  9.25 us
    unnamed x25, local copies, waits for them, and re-layouts  6.2 us
    pallas_call x1, Pallas kernels, step_attend(): pl.pallas_call(functools.partial(step_kernel, heads), out_shape=jax.Shape...  3.71 us
    ppermute x8, waiting for transfers between devices, swap_groups(): return lax.ppermute(value, 'dp', [(i, i ^ mask) for i in range(count)])  3.6 us
  transfers between devices with their start and end apart: 32, of which 8 were waited for; matrix products, arithmetic and copies ran while one was open for 11% of the time, Pallas kernels for 43%

profile of v11, /device:TPU:0, one launch (start us, length us, event | category | flops | bytes accessed | tf_op | source)
XLA Modules:
  0.0 99.0 jit_solution(1453522825404249552)
XLA Ops:
  1.2 2.6 %collective-permute-start = (bf16[128,2048]{1,0:T(8,128)(2,1)}, bf16[128,2048]{1,0:T(8,128)(2,1)S(1)}, u32[]{:S(2)}, u32[]{:S(2)}) collective-permute-start(bf16[128,2048]{1,0:T(8,128)(2,1)} %refs_0_.3), channel_id=1, source_target_pairs={{0,2},{1,3},{2,0},{3,1},{4,6},{5,7},{6,4},{7,5},{8,10},{9,11},{10,... | collective-permute-start | bytes 1572872 | tf_op jit(solution)/shard_map/ppermute | solution.py:26
  3.7 1.5 %collective-permute-start.2 = (bf16[2,2048]{1,0:T(2,128)(2,1)}, bf16[2,2048]{1,0:T(2,128)(2,1)S(1)}, u32[]{:S(2)}, u32[]{:S(2)}) collective-permute-start(bf16[2,2048]{1,0:T(2,128)(2,1)} %param.15), channel_id=1, source_target_pairs={{0,4},{4,0},{8,12},{12,8},{16,20},{20,16},{24,28},{28,24},{1,5},{5... | collective-permute-start | bytes 24584 | tf_op jit(solution)/shard_map/ppermute | solution.py:45
  6.6 1.0 fusion
  7.7 0.8 select_reduce_fusion
  9.5 1.6 %collective-permute-start.3 = (bf16[4,2048]{1,0:T(4,128)(2,1)S(1)}, bf16[4,2048]{1,0:T(4,128)(2,1)S(1)}, u32[]{:S(2)}, u32[]{:S(2)}) collective-permute-start(bf16[4,2048]{1,0:T(4,128)(2,1)S(1)} %pad_maximum_fusion.2), channel_id=1, source_target_pairs={{0,8},{4,12},{8,0},{12,4},{16,24},{20,28},{24,16},{28,20},{1,9},{5... | collective-permute-start | bytes 49160 | tf_op jit(solution)/shard_map/ppermute | solution.py:45
  11.2 2.6 %collective-permute-start.4 = (bf16[4,2048]{1,0:T(4,128)(2,1)S(1)}, bf16[4,2048]{1,0:T(4,128)(2,1)S(1)}, u32[]{:S(2)}, u32[]{:S(2)}) collective-permute-start(bf16[4,2048]{1,0:T(4,128)(2,1)S(1)} %pad_maximum_fusion.2), channel_id=1, source_target_pairs={{0,16},{4,20},{8,24},{12,28},{16,0},{20,4},{24,8},{28,12},{1,17},{... | collective-permute-start | bytes 49160 | tf_op jit(solution)/shard_map/ppermute | solution.py:45
  14.2 5.4 %copy.19 = bf16[256,8,2,512]{3,1,2,0:T(8,128)(2,1)} copy(bf16[256,8,2,512]{3,2,1,0:T(2,128)(2,1)} %bitcast.16) | data formatting | bytes 8388608
  20.4 1.6 %collective-permute-start.8 = (bf16[16,2048]{1,0:T(8,128)(2,1)S(1)}, bf16[16,2048]{1,0:T(8,128)(2,1)S(1)}, u32[]{:S(2)}, u32[]{:S(2)}) collective-permute-start(bf16[16,2048]{1,0:T(8,128)(2,1)S(1)} %convolution_convert_fusion.1.refs_6_), channel_id=1, source_target_pairs={{0,3},{1,2},{2,1},{3,0},{4,7},{5,6},{6,5},{7,4},{8,11},{9,10},{10,... | collective-permute-start | bytes 196616 | tf_op jit(solution)/shard_map/ppermute | solution.py:33
  22.1 5.0 %project.2 = (bf16[256,512]{1,0:T(8,128)(2,1)S(1)}, bf16[2,256,256]{2,1,0:T(8,128)(2,1)S(1)}, bf16[2,512,256]{2,1,0:T(8,128)(2,1)}) custom-call(s32[5]{0:T(128)S(1)} %stack.24.place, bf16[128,2048]{1,0:T(8,128)(2,1)} %refs_0_.3, bf16[128,2048]{1,0:T(8,128)(2,1)} %collective-permute-done.9.refs_1_, bf16[2048,1024]{1,0:T(8,128)(2,1)} %bitcast.14, ...), custom_call_target="tpu_custom_call" | custom-call | flops 1073741824 | bytes 6291456 | tf_op jit(solution)/shard_map/project/pallas_call | solution.py:174
  27.2 0.8 copy-done.4
  27.9 5.6 %project.3 = (bf16[256,512]{1,0:T(8,128)(2,1)S(1)}, bf16[2,256,256]{2,1,0:T(8,128)(2,1)S(1)}, bf16[2,512,256]{2,1,0:T(8,128)(2,1)}, f32[16,512]{1,0:T(8,128)S(1)}, bf16[2,8,256]{2,1,0:T(8,128)(2,1)}) custom-call(s32[5]{0:T(128)S(1)} %stack.23.place, bf16[128,2048]{1,0:T(8,128)(2,1)} %copy-done.2, ...), custom_call_target="tpu_custom_call", output_to_operand_aliasing={{2}: (11, {})} | custom-call | flops 1140850688 | bytes 6422528 | tf_op jit(solution)/shard_map/project/pallas_call | solution.py:174
  34.2 5.9 %fill_attend.2 = (bf16[256,512]{1,0:T(8,128)(2,1)S(1)}, bf16[2,8,1024,256]{3,2,1,0:T(8,128)(2,1)S(1)}) custom-call(s32[5]{0:T(128)S(1)} %stack.24.place, bf16[256,512]{1,0:T(8,128)(2,1)S(1)} %get-tuple-element.51.refs_9_.query, bf16[2,1,1024,256]{3,2,1,0:T(8,128)(2,1)} %cache_value.3, bf16[2,1,1024,256]{3,2,1,0:T(8,128)(2,1)} %cache_value.3, ...), custom_call_target="tpu_custom_call" | custom-call | flops 1610612736 | bytes 1048576 | tf_op jit(solution)/shard_map/fill_attend/pallas_call | solution.py:254
  40.2 1.5 %collective-permute-done.10.sib = bf16[256,512]{1,0:T(8,128)(2,1)S(1)} collective-permute-done((bf16[256,512]{1,0:T(8,128)(2,1)S(1)}, bf16[256,512]{1,0:T(8,128)(2,1)S(1)}, u32[]{:S(2)}, u32[]{:S(2)}) %collective-permute-start.10) | collective-permute-done | bytes 262176 | tf_op jit(solution)/shard_map/ppermute | solution.py:20
  41.7 1.2 %out_project.2.refs_2_ = bf16[256,1024]{1,0:T(8,128)(2,1)S(1)} custom-call(s32[5]{0:T(128)S(1)} %stack.24.place, bf16[256,512]{1,0:T(8,128)(2,1)S(1)} %get-tuple-element.57.mine, bf16[256,512]{1,0:T(8,128)(2,1)S(1)} %collective-permute-done.10.sib, bf16[512,2048]{1,0:T(8,128)(2,1)S(1)} %copy-done, bf16[512,2048]{1,0:T(8,128)(2,1)S(1)} %collective-permute-done.11.sib_weight), custom_call_target="tpu_custom_call" | custom-call | flops 536870912 | bytes 3670016 | tf_op jit(solution)/shard_map/out_project/pallas_call | solution.py:370
  43.6 3.7 %step_attend.1.refs_5_.refs_7_ = bf16[16,2048]{1,0:T(8,128)(2,1)S(1)} custom-call(s32[8]{0:T(128)S(1)} %copy-done.10, f32[16,512]{1,0:T(8,128)S(1)} %get-tuple-element.60.query, bf16[2,8,256]{2,1,0:T(8,128)(2,1)S(1)} %copy-done.9, bf16[2,8,1024,256]{3,2,1,0:T(8,128)(2,1)S(1)} %get-tuple-element.62.held, bf16[512,2048]{1,0:T(8,128)(2,1)} %weight.5), custom_call_target="tpu_custom_call" | custom-call | flops 67108864 | bytes 8388608 | tf_op jit(solution)/shard_map/step_attend/pallas_call | solution.py:341
  47.3 6.7 %fill_attend.3 = (bf16[256,512]{1,0:T(8,128)(2,1)S(1)}, bf16[4,2048,512]{2,1,0:T(8,128)(2,1)S(1)}) custom-call(s32[5]{0:T(128)S(1)} %stack.23.place, bf16[256,512]{1,0:T(8,128)(2,1)S(1)} %get-tuple-element.54.query, bf16[2,1,1024,256]{3,2,1,0:T(8,128)(2,1)} %cache_value.3, bf16[2,1,1024,256]{3,2,1,0:T(8,128)(2,1)} %cache_value.3, ...), custom_call_target="tpu_custom_call" | custom-call | flops 1610612736 | bytes 1048576 | tf_op jit(solution)/shard_map/fill_attend/pallas_call | solution.py:254
  54.1 1.6 %collective-permute-start.16 = (bf16[16,2048]{1,0:T(8,128)(2,1)S(1)}, bf16[16,2048]{1,0:T(8,128)(2,1)S(1)}, u32[]{:S(2)}, u32[]{:S(2)}) collective-permute-start(bf16[16,2048]{1,0:T(8,128)(2,1)S(1)} %step_attend.1.refs_5_.refs_7_), channel_id=1, source_target_pairs={{0,2},{1,3},{2,0},{3,1},{4,6},{5,7},{6,4},{7,5},{8,10},{9,11},{10,... | collective-permute-start | bytes 196616 | tf_op jit(solution)/shard_map/ppermute | solution.py:26
  56.3 1.2 %out_project.3.refs_2_ = bf16[256,1024]{1,0:T(8,128)(2,1)S(1)} custom-call(s32[5]{0:T(128)S(1)} %stack.23.place, bf16[256,512]{1,0:T(8,128)(2,1)S(1)} %get-tuple-element.63.mine, bf16[256,512]{1,0:T(8,128)(2,1)S(1)} %collective-permute-done.12.sib, bf16[512,2048]{1,0:T(8,128)(2,1)S(1)} %copy-done.1, bf16[512,2048]{1,0:T(8,128)(2,1)S(1)} %collective-permute-done.11.sib_weight), custom_call_target="tpu_custom_call" | custom-call | flops 536870912 | bytes 3670016 | tf_op jit(solution)/shard_map/out_project/pallas_call | solution.py:370
  57.8 0.8 collective-permute-done.16.refs_8_
  58.6 1.1 %collective-permute-done.18.refs_10_ = bf16[16,2048]{1,0:T(8,128)(2,1)S(1)} collective-permute-done((bf16[16,2048]{1,0:T(8,128)(2,1)S(1)}, bf16[16,2048]{1,0:T(8,128)(2,1)S(1)}, u32[]{:S(2)}, u32[]{:S(2)}) %collective-permute-start.18) | collective-permute-done | bytes 65568 | tf_op jit(solution)/shard_map/ppermute | solution.py:33
  60.0 1.3 %collective-permute-start.13 = (bf16[256,1024]{1,0:T(8,128)(2,1)S(1)}, bf16[256,1024]{1,0:T(8,128)(2,1)S(1)}, u32[]{:S(2)}, u32[]{:S(2)}) collective-permute-start(bf16[256,1024]{1,0:T(8,128)(2,1)S(1)} %out_project.3.refs_2_), channel_id=1, source_target_pairs={{0,2},{1,3},{2,0},{3,1},{4,6},{5,7},{6,4},{7,5},{8,10},{9,11},{10,... | collective-permute-start | bytes 1572872 | tf_op jit(solution)/shard_map/ppermute | solution.py:26
  61.7 10.9 %feed_forward.2 = (bf16[128,2048]{1,0:T(8,128)(2,1)S(1)}, bf16[128,2048]{1,0:T(8,128)(2,1)S(1)}, bf16[128,2048]{1,0:T(8,128)(2,1)}, bf16[16,2048]{1,0:T(8,128)(2...) custom-call(s32[5]{0:T(128)S(1)} %stack.23.place, ...), custom_call_target="tpu_custom_call" | custom-call | flops 6845104128 | bytes 25165824 | tf_op jit(solution)/shard_map/feed_forward/pallas_call | solution.py:509
  73.2 0.9 collective-permute-done.13.refs_4_
  74.1 1.3 %collective-permute-start.24 = (bf16[16,2048]{1,0:T(8,128)(2,1)S(1)}, bf16[16,2048]{1,0:T(8,128)(2,1)S(1)}, u32[]{:S(2)}, u32[]{:S(2)}) collective-permute-start(bf16[16,2048]{1,0:T(8,128)(2,1)S(1)} %get-tuple-element.78), channel_id=1, source_target_pairs={{0,2},{1,3},{2,0},{3,1},{4,6},{5,7},{6,4},{7,5},{8,10},{9,11},{10,... | collective-permute-start | bytes 196616 | tf_op jit(solution)/shard_map/ppermute | solution.py:26
  76.4 1.4 %collective-permute-start.21 = (bf16[128,2048]{1,0:T(8,128)(2,1)S(1)}, bf16[128,2048]{1,0:T(8,128)(2,1)S(1)}, u32[]{:S(2)}, u32[]{:S(2)}) collective-permute-start(bf16[128,2048]{1,0:T(8,128)(2,1)S(1)} %add_convert_fusion.1.refs_9_), channel_id=1, source_target_pairs={{0,2},{1,3},{2,0},{3,1},{4,6},{5,7},{6,4},{7,5},{8,10},{9,11},{10,... | collective-permute-start | bytes 1572872 | tf_op jit(solution)/shard_map/ppermute | solution.py:26
  77.8 6.7 %feed_forward.3 = (bf16[128,2048]{1,0:T(8,128)(2,1)S(1)}, bf16[256,2048]{1,0:T(8,128)(2,1)S(1)}) custom-call(s32[5]{0:T(128)S(1)} %stack.24.place, bf16[128,2048]{1,0:T(8,128)(2,1)S(1)} %copy-done.6, bf16[128,2048]{1,0:T(8,128)(2,1)} %collective-permute-done.9.refs_1_, bf16[256,1024]{1,0:T(8,128)(2,1)S(1)} %out_project.2.refs_2_, ...), custom_call_target="tpu_custom_call" | custom-call | flops 6442450944 | bytes 25165824 | tf_op jit(solution)/shard_map/feed_forward/pallas_call | solution.py:509
  84.8 0.7 collective-permute-start.27
  85.5 3.5 %collective-permute-start.28 = (bf16[4,2048]{1,0:T(4,128)(2,1)S(1)}, bf16[4,2048]{1,0:T(4,128)(2,1)S(1)}, u32[]{:S(2)}, u32[]{:S(2)}) collective-permute-start(bf16[4,2048]{1,0:T(4,128)(2,1)S(1)} %get-tuple-element.94), channel_id=1, source_target_pairs={{0,16},{4,20},{8,24},{12,28},{16,0},{20,4},{24,8},{28,12},{1,17},{... | collective-permute-start | bytes 49160 | tf_op jit(solution)/shard_map/ppermute | solution.py:45
  89.2 2.4 %lower.1 = (bf16[128,2048]{1,0:T(8,128)(2,1)S(1)}, bf16[128,2048]{1,0:T(8,128)(2,1)S(1)}) custom-call(bf16[256,2048]{1,0:T(8,128)(2,1)S(1)} %get-tuple-element.79.hidden, bf16[4,2048,512]{2,1,0:T(8,128)(2,1)S(1)} %get-tuple-element.80.down, bf16[16,2048]{1,0:T(8,128)(2,1)S(1)} %convolution_convert_fusion.refs_0_), custom_call_target="tpu_custom_call" | custom-call | flops 2147483648 | bytes 8388608 | tf_op jit(solution)/shard_map/lower/pallas_call | solution.py:474
  91.7 2.9 %collective-permute-done.29 = bf16[4,2048]{1,0:T(4,128)(2,1)S(1)} collective-permute-done((bf16[4,2048]{1,0:T(4,128)(2,1)S(1)}, bf16[4,2048]{1,0:T(4,128)(2,1)S(1)}, u32[]{:S(2)}, u32[]{:S(2)}) %collective-permute-start.29) | collective-permute-done | bytes 16416 | tf_op jit(solution)/shard_map/ppermute | solution.py:45
  95.3 1.3 %collective-permute-done.31 = bf16[128,2048]{1,0:T(8,128)(2,1)S(1)} collective-permute-done((bf16[128,2048]{1,0:T(8,128)(2,1)S(1)}, bf16[128,2048]{1,0:T(8,128)(2,1)S(1)}, u32[]{:S(2)}, u32[]{:S(2)}) %collective-permute-start.31) | collective-permute-done | bytes 524320 | tf_op jit(solution)/shard_map/ppermute | solution.py:20
  96.6 1.1 %add_convert_fusion = bf16[128,2048]{1,0:T(8,128)(2,1)} fusion(bf16[128,2048]{1,0:T(8,128)(2,1)S(1)} %collective-permute-done.21, bf16[128,2048]{1,0:T(8,128)(2,1)S(1)} %collective-permute-done.31, bf16[128,2048]{1,0:T(8,128)(2,1)S(1)} %get-tuple-element.84, bf16[128,2048]{1,0:T(8,128)(2,1)S(1)} %get-tuple-element.83), kind=kLoop, calls=%fused_computation.2 | loop fusion | flops 2097152 | bytes 2621440 | tf_op jit(solution)/shard_map/convert_element_type | solution.py:537
  (90 shorter events, 10.5 us)
Async XLA Ops:
  0.7 21.4 %collective-permute-start.9 = (bf16[128,2048]{1,0:T(8,128)(2,1)}, bf16[128,2048]{1,0:T(8,128)(2,1)}, u32[]{:S(2)}, u32[]{:S(2)}) collective-permute-start(bf16[128,2048]{1,0:T(8,128)(2,1)} %refs_0_.3), channel_id=1, source_target_pairs={{0,1},{1,0},{2,3},{3,2},{4,5},{5,4},{6,7},{7,6},{8,9},{9,8},{10,11... | collective-permute-start | bytes 1572872 | tf_op jit(solution)/shard_map/ppermute | solution.py:20
  1.2 20.9 %collective-permute-start = (bf16[128,2048]{1,0:T(8,128)(2,1)}, bf16[128,2048]{1,0:T(8,128)(2,1)S(1)}, u32[]{:S(2)}, u32[]{:S(2)}) collective-permute-start(bf16[128,2048]{1,0:T(8,128)(2,1)} %refs_0_.3), channel_id=1, source_target_pairs={{0,2},{1,3},{2,0},{3,1},{4,6},{5,7},{6,4},{7,5},{8,10},{9,11},{10,... | collective-permute-start | bytes 1572872 | tf_op jit(solution)/shard_map/ppermute | solution.py:26
  3.7 5.1 %collective-permute-start.2 = (bf16[2,2048]{1,0:T(2,128)(2,1)}, bf16[2,2048]{1,0:T(2,128)(2,1)S(1)}, u32[]{:S(2)}, u32[]{:S(2)}) collective-permute-start(bf16[2,2048]{1,0:T(2,128)(2,1)} %param.15), channel_id=1, source_target_pairs={{0,4},{4,0},{8,12},{12,8},{16,20},{20,16},{24,28},{28,24},{1,5},{5... | collective-permute-start | bytes 24584 | tf_op jit(solution)/shard_map/ppermute | solution.py:45
  9.5 10.1 %collective-permute-start.3 = (bf16[4,2048]{1,0:T(4,128)(2,1)S(1)}, bf16[4,2048]{1,0:T(4,128)(2,1)S(1)}, u32[]{:S(2)}, u32[]{:S(2)}) collective-permute-start(bf16[4,2048]{1,0:T(4,128)(2,1)S(1)} %pad_maximum_fusion.2), channel_id=1, source_target_pairs={{0,8},{4,12},{8,0},{12,4},{16,24},{20,28},{24,16},{28,20},{1,9},{5... | collective-permute-start | bytes 49160 | tf_op jit(solution)/shard_map/ppermute | solution.py:45
  11.2 8.4 %collective-permute-start.4 = (bf16[4,2048]{1,0:T(4,128)(2,1)S(1)}, bf16[4,2048]{1,0:T(4,128)(2,1)S(1)}, u32[]{:S(2)}, u32[]{:S(2)}) collective-permute-start(bf16[4,2048]{1,0:T(4,128)(2,1)S(1)} %pad_maximum_fusion.2), channel_id=1, source_target_pairs={{0,16},{4,20},{8,24},{12,28},{16,0},{20,4},{24,8},{28,12},{1,17},{... | collective-permute-start | bytes 49160 | tf_op jit(solution)/shard_map/ppermute | solution.py:45
  13.8 5.8 %collective-permute-start.5 = (bf16[4,2048]{1,0:T(4,128)(2,1)S(1)}, bf16[4,2048]{1,0:T(4,128)(2,1)S(1)}, u32[]{:S(2)}, u32[]{:S(2)}) collective-permute-start(bf16[4,2048]{1,0:T(4,128)(2,1)S(1)} %pad_maximum_fusion.2), channel_id=1, source_target_pairs={{0,24},{4,28},{8,16},{12,20},{16,8},{20,12},{24,0},{28,4},{1,25},{... | collective-permute-start | bytes 49160 | tf_op jit(solution)/shard_map/ppermute | solution.py:45
  19.8 7.2 %collective-permute-start.6 = (bf16[16,2048]{1,0:T(8,128)(2,1)S(1)}, bf16[16,2048]{1,0:T(8,128)(2,1)S(1)}, u32[]{:S(2)}, u32[]{:S(2)}) collective-permute-start(bf16[16,2048]{1,0:T(8,128)(2,1)S(1)} %convolution_convert_fusion.1.refs_6_), channel_id=1, source_target_pairs={{0,2},{1,3},{2,0},{3,1},{4,6},{5,7},{6,4},{7,5},{8,10},{9,11},{10,... | collective-permute-start | bytes 196616 | tf_op jit(solution)/shard_map/ppermute | solution.py:26
  20.4 6.6 %collective-permute-start.7 = (bf16[16,2048]{1,0:T(8,128)(2,1)S(1)}, bf16[16,2048]{1,0:T(8,128)(2,1)S(1)}, u32[]{:S(2)}, u32[]{:S(2)}) collective-permute-start(bf16[16,2048]{1,0:T(8,128)(2,1)S(1)} %convolution_convert_fusion.1.refs_6_), channel_id=1, source_target_pairs={{0,1},{1,0},{2,3},{3,2},{4,5},{5,4},{6,7},{7,6},{8,9},{9,8},{10,11... | collective-permute-start | bytes 196616 | tf_op jit(solution)/shard_map/ppermute | solution.py:33
  20.4 6.6 %collective-permute-start.8 = (bf16[16,2048]{1,0:T(8,128)(2,1)S(1)}, bf16[16,2048]{1,0:T(8,128)(2,1)S(1)}, u32[]{:S(2)}, u32[]{:S(2)}) collective-permute-start(bf16[16,2048]{1,0:T(8,128)(2,1)S(1)} %convolution_convert_fusion.1.refs_6_), channel_id=1, source_target_pairs={{0,3},{1,2},{2,1},{3,0},{4,7},{5,6},{6,5},{7,4},{8,11},{9,10},{10,... | collective-permute-start | bytes 196616 | tf_op jit(solution)/shard_map/ppermute | solution.py:33
  22.1 5.1 %collective-permute-start.1 = (bf16[128,2048]{1,0:T(8,128)(2,1)S(1)}, bf16[128,2048]{1,0:T(8,128)(2,1)S(1)}, u32[]{:S(2)}, u32[]{:S(2)}) collective-permute-start(bf16[128,2048]{1,0:T(8,128)(2,1)S(1)} %collective-permute-done.refs_0_), channel_id=1, source_target_pairs={{0,1},{1,0},{2,3},{3,2},{4,5},{5,4},{6,7},{7,6},{8,9},{9,8},{10,11... | collective-permute-start | bytes 1572872 | tf_op jit(solution)/shard_map/ppermute | solution.py:20
  33.6 8.1 %collective-permute-start.11 = (bf16[512,2048]{1,0:T(8,128)(2,1)S(1)}, bf16[512,2048]{1,0:T(8,128)(2,1)S(1)}, u32[]{:S(2)}, u32[]{:S(2)}) collective-permute-start(bf16[512,2048]{1,0:T(8,128)(2,1)S(1)} %copy-done), channel_id=1, source_target_pairs={{0,1},{1,0},{2,3},{3,2},{4,5},{5,4},{6,7},{7,6},{8,9},{9,8},{10,11... | collective-permute-start | bytes 6291464 | tf_op jit(solution)/shard_map/ppermute | solution.py:20
  40.1 1.6 %collective-permute-start.10 = (bf16[256,512]{1,0:T(8,128)(2,1)S(1)}, bf16[256,512]{1,0:T(8,128)(2,1)S(1)}, u32[]{:S(2)}, u32[]{:S(2)}) collective-permute-start(bf16[256,512]{1,0:T(8,128)(2,1)S(1)} %get-tuple-element.57.mine), channel_id=1, source_target_pairs={{0,1},{1,0},{2,3},{3,2},{4,5},{5,4},{6,7},{7,6},{8,9},{9,8},{10,11... | collective-permute-start | bytes 786440 | tf_op jit(solution)/shard_map/ppermute | solution.py:20
  43.0 16.8 %collective-permute-start.15 = (bf16[256,1024]{1,0:T(8,128)(2,1)S(1)}, bf16[256,1024]{1,0:T(8,128)(2,1)S(1)}, u32[]{:S(2)}, u32[]{:S(2)}) collective-permute-start(bf16[256,1024]{1,0:T(8,128)(2,1)S(1)} %out_project.2.refs_2_), channel_id=1, source_target_pairs={{0,2},{1,3},{2,0},{3,1},{4,6},{5,7},{6,4},{7,5},{8,10},{9,11},{10,... | collective-permute-start | bytes 1572872 | tf_op jit(solution)/shard_map/ppermute | solution.py:26
  54.0 2.3 %collective-permute-start.12 = (bf16[256,512]{1,0:T(8,128)(2,1)S(1)}, bf16[256,512]{1,0:T(8,128)(2,1)S(1)}, u32[]{:S(2)}, u32[]{:S(2)}) collective-permute-start(bf16[256,512]{1,0:T(8,128)(2,1)S(1)} %get-tuple-element.63.mine), channel_id=1, source_target_pairs={{0,1},{1,0},{2,3},{3,2},{4,5},{5,4},{6,7},{7,6},{8,9},{9,8},{10,11... | collective-permute-start | bytes 786440 | tf_op jit(solution)/shard_map/ppermute | solution.py:20
  54.1 4.5 %collective-permute-start.16 = (bf16[16,2048]{1,0:T(8,128)(2,1)S(1)}, bf16[16,2048]{1,0:T(8,128)(2,1)S(1)}, u32[]{:S(2)}, u32[]{:S(2)}) collective-permute-start(bf16[16,2048]{1,0:T(8,128)(2,1)S(1)} %step_attend.1.refs_5_.refs_7_), channel_id=1, source_target_pairs={{0,2},{1,3},{2,0},{3,1},{4,6},{5,7},{6,4},{7,5},{8,10},{9,11},{10,... | collective-permute-start | bytes 196616 | tf_op jit(solution)/shard_map/ppermute | solution.py:26
  55.7 3.0 %collective-permute-start.17 = (bf16[16,2048]{1,0:T(8,128)(2,1)S(1)}, bf16[16,2048]{1,0:T(8,128)(2,1)S(1)}, u32[]{:S(2)}, u32[]{:S(2)}) collective-permute-start(bf16[16,2048]{1,0:T(8,128)(2,1)S(1)} %step_attend.1.refs_5_.refs_7_), channel_id=1, source_target_pairs={{0,1},{1,0},{2,3},{3,2},{4,5},{5,4},{6,7},{7,6},{8,9},{9,8},{10,11... | collective-permute-start | bytes 196616 | tf_op jit(solution)/shard_map/ppermute | solution.py:33
  55.8 3.9 %collective-permute-start.18 = (bf16[16,2048]{1,0:T(8,128)(2,1)S(1)}, bf16[16,2048]{1,0:T(8,128)(2,1)S(1)}, u32[]{:S(2)}, u32[]{:S(2)}) collective-permute-start(bf16[16,2048]{1,0:T(8,128)(2,1)S(1)} %step_attend.1.refs_5_.refs_7_), channel_id=1, source_target_pairs={{0,3},{1,2},{2,1},{3,0},{4,7},{5,6},{6,5},{7,4},{8,11},{9,10},{10,... | collective-permute-start | bytes 196616 | tf_op jit(solution)/shard_map/ppermute | solution.py:33
  57.6 3.8 %collective-permute-start.14 = (bf16[256,1024]{1,0:T(8,128)(2,1)S(1)}, bf16[256,1024]{1,0:T(8,128)(2,1)S(1)}, u32[]{:S(2)}, u32[]{:S(2)}) collective-permute-start(bf16[256,1024]{1,0:T(8,128)(2,1)S(1)} %out_project.3.refs_2_), channel_id=1, source_target_pairs={{0,1},{1,0},{2,3},{3,2},{4,5},{5,4},{6,7},{7,6},{8,9},{9,8},{10,11... | collective-permute-start | bytes 1572872 | tf_op jit(solution)/shard_map/ppermute | solution.py:20
  59.8 1.9 %collective-permute-start.19 = (bf16[256,1024]{1,0:T(8,128)(2,1)S(1)}, bf16[256,1024]{1,0:T(8,128)(2,1)S(1)}, u32[]{:S(2)}, u32[]{:S(2)}) collective-permute-start(bf16[256,1024]{1,0:T(8,128)(2,1)S(1)} %collective-permute-done.15.refs_4_), channel_id=1, source_target_pairs={{0,1},{1,0},{2,3},{3,2},{4,5},{5,4},{6,7},{7,6},{8,9},{9,8},{10,11... | collective-permute-start | bytes 1572872 | tf_op jit(solution)/shard_map/ppermute | solution.py:20
  60.0 14.1 %collective-permute-start.13 = (bf16[256,1024]{1,0:T(8,128)(2,1)S(1)}, bf16[256,1024]{1,0:T(8,128)(2,1)S(1)}, u32[]{:S(2)}, u32[]{:S(2)}) collective-permute-start(bf16[256,1024]{1,0:T(8,128)(2,1)S(1)} %out_project.3.refs_2_), channel_id=1, source_target_pairs={{0,2},{1,3},{2,0},{3,1},{4,6},{5,7},{6,4},{7,5},{8,10},{9,11},{10,... | collective-permute-start | bytes 1572872 | tf_op jit(solution)/shard_map/ppermute | solution.py:26
  72.6 3.0 %collective-permute-start.20 = (bf16[128,2048]{1,0:T(8,128)(2,1)S(1)}, bf16[128,2048]{1,0:T(8,128)(2,1)S(1)}, u32[]{:S(2)}, u32[]{:S(2)}) collective-permute-start(bf16[128,2048]{1,0:T(8,128)(2,1)S(1)} %get-tuple-element.72), channel_id=1, source_target_pairs={{0,1},{1,0},{2,3},{3,2},{4,5},{5,4},{6,7},{7,6},{8,9},{9,8},{10,11... | collective-permute-start | bytes 1572872 | tf_op jit(solution)/shard_map/ppermute | solution.py:20
  73.0 3.4 %collective-permute-start.22 = (bf16[256,1024]{1,0:T(8,128)(2,1)S(1)}, bf16[256,1024]{1,0:T(8,128)(2,1)S(1)}, u32[]{:S(2)}, u32[]{:S(2)}) collective-permute-start(bf16[256,1024]{1,0:T(8,128)(2,1)S(1)} %out_project.2.refs_2_), channel_id=1, source_target_pairs={{0,1},{1,0},{2,3},{3,2},{4,5},{5,4},{6,7},{7,6},{8,9},{9,8},{10,11... | collective-permute-start | bytes 1572872 | tf_op jit(solution)/shard_map/ppermute | solution.py:20
  74.1 3.6 %collective-permute-start.23 = (bf16[256,1024]{1,0:T(8,128)(2,1)S(1)}, bf16[256,1024]{1,0:T(8,128)(2,1)S(1)}, u32[]{:S(2)}, u32[]{:S(2)}) collective-permute-start(bf16[256,1024]{1,0:T(8,128)(2,1)S(1)} %collective-permute-done.13.refs_4_), channel_id=1, source_target_pairs={{0,1},{1,0},{2,3},{3,2},{4,5},{5,4},{6,7},{7,6},{8,9},{9,8},{10,11... | collective-permute-start | bytes 1572872 | tf_op jit(solution)/shard_map/ppermute | solution.py:20
  74.1 10.4 %collective-permute-start.24 = (bf16[16,2048]{1,0:T(8,128)(2,1)S(1)}, bf16[16,2048]{1,0:T(8,128)(2,1)S(1)}, u32[]{:S(2)}, u32[]{:S(2)}) collective-permute-start(bf16[16,2048]{1,0:T(8,128)(2,1)S(1)} %get-tuple-element.78), channel_id=1, source_target_pairs={{0,2},{1,3},{2,0},{3,1},{4,6},{5,7},{6,4},{7,5},{8,10},{9,11},{10,... | collective-permute-start | bytes 196616 | tf_op jit(solution)/shard_map/ppermute | solution.py:26
  75.4 9.1 %collective-permute-start.25 = (bf16[16,2048]{1,0:T(8,128)(2,1)S(1)}, bf16[16,2048]{1,0:T(8,128)(2,1)S(1)}, u32[]{:S(2)}, u32[]{:S(2)}) collective-permute-start(bf16[16,2048]{1,0:T(8,128)(2,1)S(1)} %get-tuple-element.78), channel_id=1, source_target_pairs={{0,1},{1,0},{2,3},{3,2},{4,5},{5,4},{6,7},{7,6},{8,9},{9,8},{10,11... | collective-permute-start | bytes 196616 | tf_op jit(solution)/shard_map/ppermute | solution.py:33
  75.6 8.9 %collective-permute-start.26 = (bf16[16,2048]{1,0:T(8,128)(2,1)S(1)}, bf16[16,2048]{1,0:T(8,128)(2,1)S(1)}, u32[]{:S(2)}, u32[]{:S(2)}) collective-permute-start(bf16[16,2048]{1,0:T(8,128)(2,1)S(1)} %get-tuple-element.78), channel_id=1, source_target_pairs={{0,3},{1,2},{2,1},{3,0},{4,7},{5,6},{6,5},{7,4},{8,11},{9,10},{10,... | collective-permute-start | bytes 196616 | tf_op jit(solution)/shard_map/ppermute | solution.py:33
  76.4 18.2 %collective-permute-start.21 = (bf16[128,2048]{1,0:T(8,128)(2,1)S(1)}, bf16[128,2048]{1,0:T(8,128)(2,1)S(1)}, u32[]{:S(2)}, u32[]{:S(2)}) collective-permute-start(bf16[128,2048]{1,0:T(8,128)(2,1)S(1)} %add_convert_fusion.1.refs_9_), channel_id=1, source_target_pairs={{0,2},{1,3},{2,0},{3,1},{4,6},{5,7},{6,4},{7,5},{8,10},{9,11},{10,... | collective-permute-start | bytes 1572872 | tf_op jit(solution)/shard_map/ppermute | solution.py:26
  84.8 6.9 %collective-permute-start.27 = (bf16[4,2048]{1,0:T(4,128)(2,1)S(1)}, bf16[4,2048]{1,0:T(4,128)(2,1)S(1)}, u32[]{:S(2)}, u32[]{:S(2)}) collective-permute-start(bf16[4,2048]{1,0:T(4,128)(2,1)S(1)} %get-tuple-element.92), channel_id=1, source_target_pairs={{0,8},{4,12},{8,0},{12,4},{16,24},{20,28},{24,16},{28,20},{1,9},{5... | collective-permute-start | bytes 49160 | tf_op jit(solution)/shard_map/ppermute | solution.py:45
  85.5 6.1 %collective-permute-start.28 = (bf16[4,2048]{1,0:T(4,128)(2,1)S(1)}, bf16[4,2048]{1,0:T(4,128)(2,1)S(1)}, u32[]{:S(2)}, u32[]{:S(2)}) collective-permute-start(bf16[4,2048]{1,0:T(4,128)(2,1)S(1)} %get-tuple-element.94), channel_id=1, source_target_pairs={{0,16},{4,20},{8,24},{12,28},{16,0},{20,4},{24,8},{28,12},{1,17},{... | collective-permute-start | bytes 49160 | tf_op jit(solution)/shard_map/ppermute | solution.py:45
  89.0 5.5 %collective-permute-start.29 = (bf16[4,2048]{1,0:T(4,128)(2,1)S(1)}, bf16[4,2048]{1,0:T(4,128)(2,1)S(1)}, u32[]{:S(2)}, u32[]{:S(2)}) collective-permute-start(bf16[4,2048]{1,0:T(4,128)(2,1)S(1)} %get-tuple-element.93), channel_id=1, source_target_pairs={{0,24},{4,28},{8,16},{12,20},{16,8},{20,12},{24,0},{28,4},{1,25},{... | collective-permute-start | bytes 49160 | tf_op jit(solution)/shard_map/ppermute | solution.py:45
  94.6 2.0 %collective-permute-start.31 = (bf16[128,2048]{1,0:T(8,128)(2,1)S(1)}, bf16[128,2048]{1,0:T(8,128)(2,1)S(1)}, u32[]{:S(2)}, u32[]{:S(2)}) collective-permute-start(bf16[128,2048]{1,0:T(8,128)(2,1)S(1)} %get-tuple-element.85), channel_id=1, source_target_pairs={{0,1},{1,0},{2,3},{3,2},{4,5},{5,4},{6,7},{7,6},{8,9},{9,8},{10,11... | collective-permute-start | bytes 1572872 | tf_op jit(solution)/shard_map/ppermute | solution.py:20
  94.7 3.7 %collective-permute-start.30 = (bf16[2,2048]{1,0:T(2,128)(2,1)S(1)}, bf16[2,2048]{1,0:T(2,128)(2,1)S(1)}, u32[]{:S(2)}, u32[]{:S(2)}) collective-permute-start(bf16[2,2048]{1,0:T(2,128)(2,1)S(1)} %slice.28), channel_id=1, source_target_pairs={{0,4},{4,0},{8,12},{12,8},{16,20},{20,16},{24,28},{28,24},{1,5},{5... | collective-permute-start | bytes 24584 | tf_op jit(solution)/shard_map/ppermute | solution.py:45
  (12 other events, 147.4 us)

commit v12 on v11

--- a/solution.py
+++ b/solution.py
@@ -83,7 +83,7 @@
 IN_PLACE = pl.BlockSpec(memory_space=pl.ANY)
 
 
-def project_kernel(n_dec, n_after, groups, heads, place, *refs):
+def project_kernel(loads, n_dec, n_after, groups, heads, place, *refs):
     refs = list(refs)
     mine, sib, weight, gain, cosine, sine = refs[:6]
     refs = refs[6:]
@@ -94,7 +94,8 @@
     query, entries, everything = refs[:3]
     if n_dec:
         dec_query, dec_entries = refs[3:5]
-    inner, rows_held, weight_held, row_sems, weight_sems, out_sem = refs[-6:]
+    inner, rows_held, row_sems, weight_sems, out_sem = refs[-5:]
+    weight_held = refs[-6] if loads else weight
     piece = mine.shape[0]
     core = place[0]
     scale = gain[...]
@@ -107,7 +108,7 @@
         pltpu.make_async_copy(
             weight.at[:, pl.ds(j * depth, depth)], weight_held.at[j], weight_sems.at[j]
         )
-        for j in range(heads)
+        for j in range(heads if loads else 0)
     ]
     for copy in row_copies + weight_copies:
         copy.start()
@@ -119,7 +120,8 @@
         inner[2 * piece :, :] = normed(dec[...].astype(jnp.float32), scale)
     here = pl.ds(pl.multiple_of(place[1] * 2 * piece, 2 * piece), 2 * piece)
     for j in range(heads):
-        weight_copies[j].wait()
+        if loads:
+            weight_copies[j].wait()
         mixed = jnp.dot(inner[...], weight_held[j], preferred_element_type=jnp.float32)
 
         def put(rows, cos, sin, query_out, entry_out):
@@ -146,7 +148,8 @@
     place, mine, sib, gain, weight, tables, heads, everything, dec=None, dec_tables=None, slots=0, after=()
 ):
     piece, width = mine.shape
-    depth = weight.shape[1] // heads
+    loads = everything is None
+    depth = weight.shape[1] // heads if loads else weight.shape[2]
     groups = depth // HD - 2
     block = 2 * piece
     n_dec = 0 if dec is None else dec.shape[0]
@@ -170,25 +173,27 @@
             jax.ShapeDtypeStruct((n_dec, wide), jnp.float32),
             jax.ShapeDtypeStruct((2, slots, heads * HD), jnp.bfloat16),
         ]
+    if loads:
+        out_shape.append(stays_in_vmem((heads, width, depth)))
     rows = block + n_dec
     return pl.pallas_call(
-        functools.partial(project_kernel, n_dec, len(after), groups, heads),
+        functools.partial(project_kernel, loads, n_dec, len(after), groups, heads),
         out_shape=out_shape,
         in_specs=[SMEM_WHOLE]
-        + [IN_PLACE] * 3
+        + [IN_PLACE] * 2
+        + [IN_PLACE if loads else VMEM_WHOLE]
         + [VMEM_WHOLE] * (len(args) - 3)
         + [IN_PLACE] * len(after),
         out_specs=[VMEM_WHOLE] * 2 + [IN_PLACE] + [VMEM_WHOLE] * (len(out_shape) - 3),
         scratch_shapes=[
             pltpu.VMEM((rows, width), jnp.bfloat16),
             pltpu.VMEM((2, piece, width), jnp.bfloat16),
-            pltpu.VMEM((heads, width, depth), jnp.bfloat16),
             pltpu.SemaphoreType.DMA((2,)),
             pltpu.SemaphoreType.DMA((heads,)),
             pltpu.SemaphoreType.DMA(()),
         ],
         input_output_aliases=aliases,
-        compiler_params=params(20),
+        compiler_params=params(12),
         cost_estimate=cost(2 * rows * weight.size, 2 * (weight.size + 2 * rows * width)),
         name="project",
     )(place, *args, *after)
@@ -629,8 +634,10 @@
             [queries[k - 1]] if k else [dealt],
         )
         queries[k], entries[k], everything = got[:3]
+        if k == 0:
+            weight = got[-1]
         if last:
-            dec_query, dec_entries = got[3:]
+            dec_query, dec_entries = got[3:5]
 
     out_share = in_hbm(out_weight)
     sib_weight, queries[-1] = lax.optimization_barrier((out_weight, queries[-1]))

time: 99.4 us -> 98.5 us (level)
  no operation moved by 1% of the time
where the time goes in v12:
time: 98.5 us; the launch traced here: 98.2 us
  Pallas kernels  48.7 us (49%)
  starting transfers between devices  25.8 us (26%)
  waiting for transfers between devices  9.63 us (10%)
  local copies, waits for them, and re-layouts  6.49 us (7%)
  other arithmetic  5.56 us (6%)
  between operations  1.7 us (2%)
    pallas_call x2, Pallas kernels, feed_forward(): pl.pallas_call(functools.partial(forward_kernel, loads, chips, n_dec, len...  17.6 us
    pallas_call x2, Pallas kernels, fill_attend(): pl.pallas_call(functools.partial(fill_kernel, groups, chips, chunk), out_...  12.6 us
    ppermute x8, starting transfers between devices, swap_groups(): return lax.ppermute(value, 'dp', [(i, i ^ mask) for i in range(count)])  11 us
    pallas_call x2, Pallas kernels, project(): pl.pallas_call(functools.partial(project_kernel, loads, n_dec, len(after)...  9.81 us
    ppermute x7, starting transfers between devices, from_chip(): lax.ppermute(value, 'tensor', [(i, (i // 2 - step) % chips * 2 + i % 2) f...  9.26 us
    unnamed x25, local copies, waits for them, and re-layouts  6.2 us
    pallas_call x1, Pallas kernels, step_attend(): pl.pallas_call(functools.partial(step_kernel, heads), out_shape=jax.Shape...  3.71 us
    ppermute x8, waiting for transfers between devices, swap_groups(): return lax.ppermute(value, 'dp', [(i, i ^ mask) for i in range(count)])  3.56 us
  transfers between devices with their start and end apart: 32, of which 8 were waited for; matrix products, arithmetic and copies ran while one was open for 11% of the time, Pallas kernels for 43%

profile of v12, /device:TPU:0, one launch (start us, length us, event | category | flops | bytes accessed | tf_op | source)
XLA Modules:
  0.0 98.2 jit_solution(1637211072798341621)
XLA Ops:
  1.2 2.6 %collective-permute-start = (bf16[128,2048]{1,0:T(8,128)(2,1)}, bf16[128,2048]{1,0:T(8,128)(2,1)S(1)}, u32[]{:S(2)}, u32[]{:S(2)}) collective-permute-start(bf16[128,2048]{1,0:T(8,128)(2,1)} %refs_0_.3), channel_id=1, source_target_pairs={{0,2},{1,3},{2,0},{3,1},{4,6},{5,7},{6,4},{7,5},{8,10},{9,11},{10,... | collective-permute-start | bytes 1572872 | tf_op jit(solution)/shard_map/ppermute | solution.py:26
  3.7 1.5 %collective-permute-start.3 = (bf16[2,2048]{1,0:T(2,128)(2,1)}, bf16[2,2048]{1,0:T(2,128)(2,1)S(1)}, u32[]{:S(2)}, u32[]{:S(2)}) collective-permute-start(bf16[2,2048]{1,0:T(2,128)(2,1)} %param.15), channel_id=1, source_target_pairs={{0,4},{4,0},{8,12},{12,8},{16,20},{20,16},{24,28},{28,24},{1,5},{5... | collective-permute-start | bytes 24584 | tf_op jit(solution)/shard_map/ppermute | solution.py:45
  6.6 1.0 %fusion = (f32[512,64]{1,0:T(8,128)S(1)}, f32[512,64]{1,0:T(8,128)S(1)}, f32[512,64]{1,0:T(8,128)S(1)}) fusion(f32[64]{0:T(128)S(1)} %negate_power_fusion, f32[512]{0:T(512)S(1)} %add_convert_fusion.7), kind=kLoop, calls=%fused_computation.10 | loop fusion | flops 65536 | bytes 395520 | tf_op jit(solution)/shard_map/neg | solution.py:535
  7.7 0.8 select_reduce_fusion
  8.8 0.7 pad_maximum_fusion.2
  9.5 1.6 %collective-permute-start.4 = (bf16[4,2048]{1,0:T(4,128)(2,1)S(1)}, bf16[4,2048]{1,0:T(4,128)(2,1)S(1)}, u32[]{:S(2)}, u32[]{:S(2)}) collective-permute-start(bf16[4,2048]{1,0:T(4,128)(2,1)S(1)} %pad_maximum_fusion.2), channel_id=1, source_target_pairs={{0,8},{4,12},{8,0},{12,4},{16,24},{20,28},{24,16},{28,20},{1,9},{5... | collective-permute-start | bytes 49160 | tf_op jit(solution)/shard_map/ppermute | solution.py:45
  11.2 2.6 %collective-permute-start.5 = (bf16[4,2048]{1,0:T(4,128)(2,1)S(1)}, bf16[4,2048]{1,0:T(4,128)(2,1)S(1)}, u32[]{:S(2)}, u32[]{:S(2)}) collective-permute-start(bf16[4,2048]{1,0:T(4,128)(2,1)S(1)} %pad_maximum_fusion.2), channel_id=1, source_target_pairs={{0,16},{4,20},{8,24},{12,28},{16,0},{20,4},{24,8},{28,12},{1,17},{... | collective-permute-start | bytes 49160 | tf_op jit(solution)/shard_map/ppermute | solution.py:45
  14.2 5.4 %copy.19 = bf16[256,8,2,512]{3,1,2,0:T(8,128)(2,1)} copy(bf16[256,8,2,512]{3,2,1,0:T(2,128)(2,1)} %bitcast.15) | data formatting | bytes 8388608
  20.4 1.6 %collective-permute-start.9 = (bf16[16,2048]{1,0:T(8,128)(2,1)S(1)}, bf16[16,2048]{1,0:T(8,128)(2,1)S(1)}, u32[]{:S(2)}, u32[]{:S(2)}) collective-permute-start(bf16[16,2048]{1,0:T(8,128)(2,1)S(1)} %convolution_convert_fusion.1.refs_6_), channel_id=1, source_target_pairs={{0,3},{1,2},{2,1},{3,0},{4,7},{5,6},{6,5},{7,4},{8,11},{9,10},{10,... | collective-permute-start | bytes 196616 | tf_op jit(solution)/shard_map/ppermute | solution.py:33
  22.1 5.0 %project.2 = (bf16[256,512]{1,0:T(8,128)(2,1)S(1)}, bf16[2,256,256]{2,1,0:T(8,128)(2,1)S(1)}, bf16[2,512,256]{2,1,0:T(8,128)(2,1)}, bf16[2,2048,512]{2,1,0:T(8,128)(2,1)S(1)}) custom-call(s32[5]{0:T(128)S(1)} %stack.24.place, bf16[128,2048]{1,0:T(8,128)(2,1)} %refs_0_.3, bf16[128,2048]{1,0:T(8,128)(2,1)} %collective-permute-done.2.refs_1_, ...), custom_call_target="tpu_custom_call" | custom-call | flops 1073741824 | bytes 6291456 | tf_op jit(solution)/shard_map/project/pallas_call | solution.py:179
  27.2 0.8 copy-done.4
  27.9 4.8 %project.3 = (bf16[256,512]{1,0:T(8,128)(2,1)S(1)}, bf16[2,256,256]{2,1,0:T(8,128)(2,1)S(1)}, bf16[2,512,256]{2,1,0:T(8,128)(2,1)}, f32[16,512]{1,0:T(8,128)S(1)}, bf16[2,8,256]{2,1,0:T(8,128)(2,1)}) custom-call(s32[5]{0:T(128)S(1)} %stack.23.place, bf16[128,2048]{1,0:T(8,128)(2,1)} %copy-done.2, ...), custom_call_target="tpu_custom_call", output_to_operand_aliasing={{2}: (11, {})} | custom-call | flops 1140850688 | bytes 6422528 | tf_op jit(solution)/shard_map/project/pallas_call | solution.py:179
  33.4 5.9 %fill_attend.2 = (bf16[256,512]{1,0:T(8,128)(2,1)S(1)}, bf16[2,8,1024,256]{3,2,1,0:T(8,128)(2,1)S(1)}) custom-call(s32[5]{0:T(128)S(1)} %stack.24.place, bf16[256,512]{1,0:T(8,128)(2,1)S(1)} %get-tuple-element.53.refs_9_.query, bf16[2,1,1024,256]{3,2,1,0:T(8,128)(2,1)} %cache_value.3, bf16[2,1,1024,256]{3,2,1,0:T(8,128)(2,1)} %cache_value.3, ...), custom_call_target="tpu_custom_call" | custom-call | flops 1610612736 | bytes 1048576 | tf_op jit(solution)/shard_map/fill_attend/pallas_call | solution.py:259
  39.4 1.5 %collective-permute-done.10.sib = bf16[256,512]{1,0:T(8,128)(2,1)S(1)} collective-permute-done((bf16[256,512]{1,0:T(8,128)(2,1)S(1)}, bf16[256,512]{1,0:T(8,128)(2,1)S(1)}, u32[]{:S(2)}, u32[]{:S(2)}) %collective-permute-start.10) | collective-permute-done | bytes 262176 | tf_op jit(solution)/shard_map/ppermute | solution.py:20
  40.9 1.2 %out_project.2.refs_2_ = bf16[256,1024]{1,0:T(8,128)(2,1)S(1)} custom-call(s32[5]{0:T(128)S(1)} %stack.24.place, bf16[256,512]{1,0:T(8,128)(2,1)S(1)} %get-tuple-element.59.mine, bf16[256,512]{1,0:T(8,128)(2,1)S(1)} %collective-permute-done.10.sib, bf16[512,2048]{1,0:T(8,128)(2,1)S(1)} %copy-done, bf16[512,2048]{1,0:T(8,128)(2,1)S(1)} %collective-permute-done.11.sib_weight), custom_call_target="tpu_custom_call" | custom-call | flops 536870912 | bytes 3670016 | tf_op jit(solution)/shard_map/out_project/pallas_call | solution.py:375
  42.8 3.7 %step_attend.1.refs_5_.refs_7_ = bf16[16,2048]{1,0:T(8,128)(2,1)S(1)} custom-call(s32[8]{0:T(128)S(1)} %copy-done.10, f32[16,512]{1,0:T(8,128)S(1)} %get-tuple-element.62.query, bf16[2,8,256]{2,1,0:T(8,128)(2,1)S(1)} %copy-done.9, bf16[2,8,1024,256]{3,2,1,0:T(8,128)(2,1)S(1)} %get-tuple-element.64.held, bf16[512,2048]{1,0:T(8,128)(2,1)} %weight.5), custom_call_target="tpu_custom_call" | custom-call | flops 67108864 | bytes 8388608 | tf_op jit(solution)/shard_map/step_attend/pallas_call | solution.py:346
  46.5 6.7 %fill_attend.3 = (bf16[256,512]{1,0:T(8,128)(2,1)S(1)}, bf16[4,2048,512]{2,1,0:T(8,128)(2,1)S(1)}) custom-call(s32[5]{0:T(128)S(1)} %stack.23.place, bf16[256,512]{1,0:T(8,128)(2,1)S(1)} %get-tuple-element.56.query, bf16[2,1,1024,256]{3,2,1,0:T(8,128)(2,1)} %cache_value.3, bf16[2,1,1024,256]{3,2,1,0:T(8,128)(2,1)} %cache_value.3, ...), custom_call_target="tpu_custom_call" | custom-call | flops 1610612736 | bytes 1048576 | tf_op jit(solution)/shard_map/fill_attend/pallas_call | solution.py:259
  53.3 1.6 %collective-permute-start.16 = (bf16[16,2048]{1,0:T(8,128)(2,1)S(1)}, bf16[16,2048]{1,0:T(8,128)(2,1)S(1)}, u32[]{:S(2)}, u32[]{:S(2)}) collective-permute-start(bf16[16,2048]{1,0:T(8,128)(2,1)S(1)} %step_attend.1.refs_5_.refs_7_), channel_id=1, source_target_pairs={{0,2},{1,3},{2,0},{3,1},{4,6},{5,7},{6,4},{7,5},{8,10},{9,11},{10,... | collective-permute-start | bytes 196616 | tf_op jit(solution)/shard_map/ppermute | solution.py:26
  55.5 1.2 %out_project.3.refs_2_ = bf16[256,1024]{1,0:T(8,128)(2,1)S(1)} custom-call(s32[5]{0:T(128)S(1)} %stack.23.place, bf16[256,512]{1,0:T(8,128)(2,1)S(1)} %get-tuple-element.65.mine, bf16[256,512]{1,0:T(8,128)(2,1)S(1)} %collective-permute-done.12.sib, bf16[512,2048]{1,0:T(8,128)(2,1)S(1)} %copy-done.1, bf16[512,2048]{1,0:T(8,128)(2,1)S(1)} %collective-permute-done.11.sib_weight), custom_call_target="tpu_custom_call" | custom-call | flops 536870912 | bytes 3670016 | tf_op jit(solution)/shard_map/out_project/pallas_call | solution.py:375
  57.0 0.8 collective-permute-done.16.refs_8_
  57.8 1.2 %collective-permute-done.18.refs_10_ = bf16[16,2048]{1,0:T(8,128)(2,1)S(1)} collective-permute-done((bf16[16,2048]{1,0:T(8,128)(2,1)S(1)}, bf16[16,2048]{1,0:T(8,128)(2,1)S(1)}, u32[]{:S(2)}, u32[]{:S(2)}) %collective-permute-start.18) | collective-permute-done | bytes 65568 | tf_op jit(solution)/shard_map/ppermute | solution.py:33
  59.2 1.3 %collective-permute-start.13 = (bf16[256,1024]{1,0:T(8,128)(2,1)S(1)}, bf16[256,1024]{1,0:T(8,128)(2,1)S(1)}, u32[]{:S(2)}, u32[]{:S(2)}) collective-permute-start(bf16[256,1024]{1,0:T(8,128)(2,1)S(1)} %out_project.3.refs_2_), channel_id=1, source_target_pairs={{0,2},{1,3},{2,0},{3,1},{4,6},{5,7},{6,4},{7,5},{8,10},{9,11},{10,... | collective-permute-start | bytes 1572872 | tf_op jit(solution)/shard_map/ppermute | solution.py:26
  60.9 10.9 %feed_forward.2 = (bf16[128,2048]{1,0:T(8,128)(2,1)S(1)}, bf16[128,2048]{1,0:T(8,128)(2,1)S(1)}, bf16[128,2048]{1,0:T(8,128)(2,1)}, bf16[16,2048]{1,0:T(8,128)(2...) custom-call(s32[5]{0:T(128)S(1)} %stack.23.place, ...), custom_call_target="tpu_custom_call" | custom-call | flops 6845104128 | bytes 25165824 | tf_op jit(solution)/shard_map/feed_forward/pallas_call | solution.py:514
  72.4 0.9 collective-permute-done.13.refs_4_
  73.3 1.3 %collective-permute-start.24 = (bf16[16,2048]{1,0:T(8,128)(2,1)S(1)}, bf16[16,2048]{1,0:T(8,128)(2,1)S(1)}, u32[]{:S(2)}, u32[]{:S(2)}) collective-permute-start(bf16[16,2048]{1,0:T(8,128)(2,1)S(1)} %get-tuple-element.80), channel_id=1, source_target_pairs={{0,2},{1,3},{2,0},{3,1},{4,6},{5,7},{6,4},{7,5},{8,10},{9,11},{10,... | collective-permute-start | bytes 196616 | tf_op jit(solution)/shard_map/ppermute | solution.py:26
  75.6 1.4 %collective-permute-start.21 = (bf16[128,2048]{1,0:T(8,128)(2,1)S(1)}, bf16[128,2048]{1,0:T(8,128)(2,1)S(1)}, u32[]{:S(2)}, u32[]{:S(2)}) collective-permute-start(bf16[128,2048]{1,0:T(8,128)(2,1)S(1)} %add_convert_fusion.1.refs_9_), channel_id=1, source_target_pairs={{0,2},{1,3},{2,0},{3,1},{4,6},{5,7},{6,4},{7,5},{8,10},{9,11},{10,... | collective-permute-start | bytes 1572872 | tf_op jit(solution)/shard_map/ppermute | solution.py:26
  77.0 6.7 %feed_forward.3 = (bf16[128,2048]{1,0:T(8,128)(2,1)S(1)}, bf16[256,2048]{1,0:T(8,128)(2,1)S(1)}) custom-call(s32[5]{0:T(128)S(1)} %stack.24.place, bf16[128,2048]{1,0:T(8,128)(2,1)S(1)} %copy-done.6, bf16[128,2048]{1,0:T(8,128)(2,1)} %collective-permute-done.2.refs_1_, bf16[256,1024]{1,0:T(8,128)(2,1)S(1)} %out_project.2.refs_2_, ...), custom_call_target="tpu_custom_call" | custom-call | flops 6442450944 | bytes 25165824 | tf_op jit(solution)/shard_map/feed_forward/pallas_call | solution.py:514
  84.7 3.5 %collective-permute-start.28 = (bf16[4,2048]{1,0:T(4,128)(2,1)S(1)}, bf16[4,2048]{1,0:T(4,128)(2,1)S(1)}, u32[]{:S(2)}, u32[]{:S(2)}) collective-permute-start(bf16[4,2048]{1,0:T(4,128)(2,1)S(1)} %get-tuple-element.96), channel_id=1, source_target_pairs={{0,16},{4,20},{8,24},{12,28},{16,0},{20,4},{24,8},{28,12},{1,17},{... | collective-permute-start | bytes 49160 | tf_op jit(solution)/shard_map/ppermute | solution.py:45
  88.4 2.4 %lower.1 = (bf16[128,2048]{1,0:T(8,128)(2,1)S(1)}, bf16[128,2048]{1,0:T(8,128)(2,1)S(1)}) custom-call(bf16[256,2048]{1,0:T(8,128)(2,1)S(1)} %get-tuple-element.81.hidden, bf16[4,2048,512]{2,1,0:T(8,128)(2,1)S(1)} %get-tuple-element.82.down, bf16[16,2048]{1,0:T(8,128)(2,1)S(1)} %convolution_convert_fusion.refs_0_), custom_call_target="tpu_custom_call" | custom-call | flops 2147483648 | bytes 8388608 | tf_op jit(solution)/shard_map/lower/pallas_call | solution.py:479
  90.9 2.8 %collective-permute-done.29 = bf16[4,2048]{1,0:T(4,128)(2,1)S(1)} collective-permute-done((bf16[4,2048]{1,0:T(4,128)(2,1)S(1)}, bf16[4,2048]{1,0:T(4,128)(2,1)S(1)}, u32[]{:S(2)}, u32[]{:S(2)}) %collective-permute-start.29) | collective-permute-done | bytes 16416 | tf_op jit(solution)/shard_map/ppermute | solution.py:45
  94.4 1.3 %collective-permute-done.31 = bf16[128,2048]{1,0:T(8,128)(2,1)S(1)} collective-permute-done((bf16[128,2048]{1,0:T(8,128)(2,1)S(1)}, bf16[128,2048]{1,0:T(8,128)(2,1)S(1)}, u32[]{:S(2)}, u32[]{:S(2)}) %collective-permute-start.31) | collective-permute-done | bytes 524320 | tf_op jit(solution)/shard_map/ppermute | solution.py:20
  95.7 1.1 %add_convert_fusion = bf16[128,2048]{1,0:T(8,128)(2,1)} fusion(bf16[128,2048]{1,0:T(8,128)(2,1)S(1)} %collective-permute-done.21, bf16[128,2048]{1,0:T(8,128)(2,1)S(1)} %collective-permute-done.31, bf16[128,2048]{1,0:T(8,128)(2,1)S(1)} %get-tuple-element.86, bf16[128,2048]{1,0:T(8,128)(2,1)S(1)} %get-tuple-element.85), kind=kLoop, calls=%fused_computation.2 | loop fusion | flops 2097152 | bytes 2621440 | tf_op jit(solution)/shard_map/convert_element_type | solution.py:542
  (90 shorter events, 10.6 us)
Async XLA Ops:
  0.7 21.4 %collective-permute-start.2 = (bf16[128,2048]{1,0:T(8,128)(2,1)}, bf16[128,2048]{1,0:T(8,128)(2,1)}, u32[]{:S(2)}, u32[]{:S(2)}) collective-permute-start(bf16[128,2048]{1,0:T(8,128)(2,1)} %refs_0_.3), channel_id=1, source_target_pairs={{0,1},{1,0},{2,3},{3,2},{4,5},{5,4},{6,7},{7,6},{8,9},{9,8},{10,11... | collective-permute-start | bytes 1572872 | tf_op jit(solution)/shard_map/ppermute | solution.py:20
  1.2 20.9 %collective-permute-start = (bf16[128,2048]{1,0:T(8,128)(2,1)}, bf16[128,2048]{1,0:T(8,128)(2,1)S(1)}, u32[]{:S(2)}, u32[]{:S(2)}) collective-permute-start(bf16[128,2048]{1,0:T(8,128)(2,1)} %refs_0_.3), channel_id=1, source_target_pairs={{0,2},{1,3},{2,0},{3,1},{4,6},{5,7},{6,4},{7,5},{8,10},{9,11},{10,... | collective-permute-start | bytes 1572872 | tf_op jit(solution)/shard_map/ppermute | solution.py:26
  3.7 5.1 %collective-permute-start.3 = (bf16[2,2048]{1,0:T(2,128)(2,1)}, bf16[2,2048]{1,0:T(2,128)(2,1)S(1)}, u32[]{:S(2)}, u32[]{:S(2)}) collective-permute-start(bf16[2,2048]{1,0:T(2,128)(2,1)} %param.15), channel_id=1, source_target_pairs={{0,4},{4,0},{8,12},{12,8},{16,20},{20,16},{24,28},{28,24},{1,5},{5... | collective-permute-start | bytes 24584 | tf_op jit(solution)/shard_map/ppermute | solution.py:45
  9.5 10.1 %collective-permute-start.4 = (bf16[4,2048]{1,0:T(4,128)(2,1)S(1)}, bf16[4,2048]{1,0:T(4,128)(2,1)S(1)}, u32[]{:S(2)}, u32[]{:S(2)}) collective-permute-start(bf16[4,2048]{1,0:T(4,128)(2,1)S(1)} %pad_maximum_fusion.2), channel_id=1, source_target_pairs={{0,8},{4,12},{8,0},{12,4},{16,24},{20,28},{24,16},{28,20},{1,9},{5... | collective-permute-start | bytes 49160 | tf_op jit(solution)/shard_map/ppermute | solution.py:45
  11.2 8.4 %collective-permute-start.5 = (bf16[4,2048]{1,0:T(4,128)(2,1)S(1)}, bf16[4,2048]{1,0:T(4,128)(2,1)S(1)}, u32[]{:S(2)}, u32[]{:S(2)}) collective-permute-start(bf16[4,2048]{1,0:T(4,128)(2,1)S(1)} %pad_maximum_fusion.2), channel_id=1, source_target_pairs={{0,16},{4,20},{8,24},{12,28},{16,0},{20,4},{24,8},{28,12},{1,17},{... | collective-permute-start | bytes 49160 | tf_op jit(solution)/shard_map/ppermute | solution.py:45
  13.8 5.8 %collective-permute-start.6 = (bf16[4,2048]{1,0:T(4,128)(2,1)S(1)}, bf16[4,2048]{1,0:T(4,128)(2,1)S(1)}, u32[]{:S(2)}, u32[]{:S(2)}) collective-permute-start(bf16[4,2048]{1,0:T(4,128)(2,1)S(1)} %pad_maximum_fusion.2), channel_id=1, source_target_pairs={{0,24},{4,28},{8,16},{12,20},{16,8},{20,12},{24,0},{28,4},{1,25},{... | collective-permute-start | bytes 49160 | tf_op jit(solution)/shard_map/ppermute | solution.py:45
  19.8 7.2 %collective-permute-start.7 = (bf16[16,2048]{1,0:T(8,128)(2,1)S(1)}, bf16[16,2048]{1,0:T(8,128)(2,1)S(1)}, u32[]{:S(2)}, u32[]{:S(2)}) collective-permute-start(bf16[16,2048]{1,0:T(8,128)(2,1)S(1)} %convolution_convert_fusion.1.refs_6_), channel_id=1, source_target_pairs={{0,2},{1,3},{2,0},{3,1},{4,6},{5,7},{6,4},{7,5},{8,10},{9,11},{10,... | collective-permute-start | bytes 196616 | tf_op jit(solution)/shard_map/ppermute | solution.py:26
  20.4 6.6 %collective-permute-start.8 = (bf16[16,2048]{1,0:T(8,128)(2,1)S(1)}, bf16[16,2048]{1,0:T(8,128)(2,1)S(1)}, u32[]{:S(2)}, u32[]{:S(2)}) collective-permute-start(bf16[16,2048]{1,0:T(8,128)(2,1)S(1)} %convolution_convert_fusion.1.refs_6_), channel_id=1, source_target_pairs={{0,1},{1,0},{2,3},{3,2},{4,5},{5,4},{6,7},{7,6},{8,9},{9,8},{10,11... | collective-permute-start | bytes 196616 | tf_op jit(solution)/shard_map/ppermute | solution.py:33
  20.4 6.6 %collective-permute-start.9 = (bf16[16,2048]{1,0:T(8,128)(2,1)S(1)}, bf16[16,2048]{1,0:T(8,128)(2,1)S(1)}, u32[]{:S(2)}, u32[]{:S(2)}) collective-permute-start(bf16[16,2048]{1,0:T(8,128)(2,1)S(1)} %convolution_convert_fusion.1.refs_6_), channel_id=1, source_target_pairs={{0,3},{1,2},{2,1},{3,0},{4,7},{5,6},{6,5},{7,4},{8,11},{9,10},{10,... | collective-permute-start | bytes 196616 | tf_op jit(solution)/shard_map/ppermute | solution.py:33
  22.1 5.1 %collective-permute-start.1 = (bf16[128,2048]{1,0:T(8,128)(2,1)S(1)}, bf16[128,2048]{1,0:T(8,128)(2,1)S(1)}, u32[]{:S(2)}, u32[]{:S(2)}) collective-permute-start(bf16[128,2048]{1,0:T(8,128)(2,1)S(1)} %collective-permute-done.refs_0_), channel_id=1, source_target_pairs={{0,1},{1,0},{2,3},{3,2},{4,5},{5,4},{6,7},{7,6},{8,9},{9,8},{10,11... | collective-permute-start | bytes 1572872 | tf_op jit(solution)/shard_map/ppermute | solution.py:20
  32.8 8.1 %collective-permute-start.11 = (bf16[512,2048]{1,0:T(8,128)(2,1)S(1)}, bf16[512,2048]{1,0:T(8,128)(2,1)S(1)}, u32[]{:S(2)}, u32[]{:S(2)}) collective-permute-start(bf16[512,2048]{1,0:T(8,128)(2,1)S(1)} %copy-done), channel_id=1, source_target_pairs={{0,1},{1,0},{2,3},{3,2},{4,5},{5,4},{6,7},{7,6},{8,9},{9,8},{10,11... | collective-permute-start | bytes 6291464 | tf_op jit(solution)/shard_map/ppermute | solution.py:20
  39.3 1.6 %collective-permute-start.10 = (bf16[256,512]{1,0:T(8,128)(2,1)S(1)}, bf16[256,512]{1,0:T(8,128)(2,1)S(1)}, u32[]{:S(2)}, u32[]{:S(2)}) collective-permute-start(bf16[256,512]{1,0:T(8,128)(2,1)S(1)} %get-tuple-element.59.mine), channel_id=1, source_target_pairs={{0,1},{1,0},{2,3},{3,2},{4,5},{5,4},{6,7},{7,6},{8,9},{9,8},{10,11... | collective-permute-start | bytes 786440 | tf_op jit(solution)/shard_map/ppermute | solution.py:20
  42.2 16.8 %collective-permute-start.15 = (bf16[256,1024]{1,0:T(8,128)(2,1)S(1)}, bf16[256,1024]{1,0:T(8,128)(2,1)S(1)}, u32[]{:S(2)}, u32[]{:S(2)}) collective-permute-start(bf16[256,1024]{1,0:T(8,128)(2,1)S(1)} %out_project.2.refs_2_), channel_id=1, source_target_pairs={{0,2},{1,3},{2,0},{3,1},{4,6},{5,7},{6,4},{7,5},{8,10},{9,11},{10,... | collective-permute-start | bytes 1572872 | tf_op jit(solution)/shard_map/ppermute | solution.py:26
  53.2 2.3 %collective-permute-start.12 = (bf16[256,512]{1,0:T(8,128)(2,1)S(1)}, bf16[256,512]{1,0:T(8,128)(2,1)S(1)}, u32[]{:S(2)}, u32[]{:S(2)}) collective-permute-start(bf16[256,512]{1,0:T(8,128)(2,1)S(1)} %get-tuple-element.65.mine), channel_id=1, source_target_pairs={{0,1},{1,0},{2,3},{3,2},{4,5},{5,4},{6,7},{7,6},{8,9},{9,8},{10,11... | collective-permute-start | bytes 786440 | tf_op jit(solution)/shard_map/ppermute | solution.py:20
  53.3 4.5 %collective-permute-start.16 = (bf16[16,2048]{1,0:T(8,128)(2,1)S(1)}, bf16[16,2048]{1,0:T(8,128)(2,1)S(1)}, u32[]{:S(2)}, u32[]{:S(2)}) collective-permute-start(bf16[16,2048]{1,0:T(8,128)(2,1)S(1)} %step_attend.1.refs_5_.refs_7_), channel_id=1, source_target_pairs={{0,2},{1,3},{2,0},{3,1},{4,6},{5,7},{6,4},{7,5},{8,10},{9,11},{10,... | collective-permute-start | bytes 196616 | tf_op jit(solution)/shard_map/ppermute | solution.py:26
  54.9 3.0 %collective-permute-start.17 = (bf16[16,2048]{1,0:T(8,128)(2,1)S(1)}, bf16[16,2048]{1,0:T(8,128)(2,1)S(1)}, u32[]{:S(2)}, u32[]{:S(2)}) collective-permute-start(bf16[16,2048]{1,0:T(8,128)(2,1)S(1)} %step_attend.1.refs_5_.refs_7_), channel_id=1, source_target_pairs={{0,1},{1,0},{2,3},{3,2},{4,5},{5,4},{6,7},{7,6},{8,9},{9,8},{10,11... | collective-permute-start | bytes 196616 | tf_op jit(solution)/shard_map/ppermute | solution.py:33
  55.0 3.9 %collective-permute-start.18 = (bf16[16,2048]{1,0:T(8,128)(2,1)S(1)}, bf16[16,2048]{1,0:T(8,128)(2,1)S(1)}, u32[]{:S(2)}, u32[]{:S(2)}) collective-permute-start(bf16[16,2048]{1,0:T(8,128)(2,1)S(1)} %step_attend.1.refs_5_.refs_7_), channel_id=1, source_target_pairs={{0,3},{1,2},{2,1},{3,0},{4,7},{5,6},{6,5},{7,4},{8,11},{9,10},{10,... | collective-permute-start | bytes 196616 | tf_op jit(solution)/shard_map/ppermute | solution.py:33
  56.8 3.8 %collective-permute-start.14 = (bf16[256,1024]{1,0:T(8,128)(2,1)S(1)}, bf16[256,1024]{1,0:T(8,128)(2,1)S(1)}, u32[]{:S(2)}, u32[]{:S(2)}) collective-permute-start(bf16[256,1024]{1,0:T(8,128)(2,1)S(1)} %out_project.3.refs_2_), channel_id=1, source_target_pairs={{0,1},{1,0},{2,3},{3,2},{4,5},{5,4},{6,7},{7,6},{8,9},{9,8},{10,11... | collective-permute-start | bytes 1572872 | tf_op jit(solution)/shard_map/ppermute | solution.py:20
  59.0 1.9 %collective-permute-start.19 = (bf16[256,1024]{1,0:T(8,128)(2,1)S(1)}, bf16[256,1024]{1,0:T(8,128)(2,1)S(1)}, u32[]{:S(2)}, u32[]{:S(2)}) collective-permute-start(bf16[256,1024]{1,0:T(8,128)(2,1)S(1)} %collective-permute-done.15.refs_4_), channel_id=1, source_target_pairs={{0,1},{1,0},{2,3},{3,2},{4,5},{5,4},{6,7},{7,6},{8,9},{9,8},{10,11... | collective-permute-start | bytes 1572872 | tf_op jit(solution)/shard_map/ppermute | solution.py:20
  59.2 14.1 %collective-permute-start.13 = (bf16[256,1024]{1,0:T(8,128)(2,1)S(1)}, bf16[256,1024]{1,0:T(8,128)(2,1)S(1)}, u32[]{:S(2)}, u32[]{:S(2)}) collective-permute-start(bf16[256,1024]{1,0:T(8,128)(2,1)S(1)} %out_project.3.refs_2_), channel_id=1, source_target_pairs={{0,2},{1,3},{2,0},{3,1},{4,6},{5,7},{6,4},{7,5},{8,10},{9,11},{10,... | collective-permute-start | bytes 1572872 | tf_op jit(solution)/shard_map/ppermute | solution.py:26
  71.8 3.0 %collective-permute-start.20 = (bf16[128,2048]{1,0:T(8,128)(2,1)S(1)}, bf16[128,2048]{1,0:T(8,128)(2,1)S(1)}, u32[]{:S(2)}, u32[]{:S(2)}) collective-permute-start(bf16[128,2048]{1,0:T(8,128)(2,1)S(1)} %get-tuple-element.74), channel_id=1, source_target_pairs={{0,1},{1,0},{2,3},{3,2},{4,5},{5,4},{6,7},{7,6},{8,9},{9,8},{10,11... | collective-permute-start | bytes 1572872 | tf_op jit(solution)/shard_map/ppermute | solution.py:20
  72.1 3.4 %collective-permute-start.22 = (bf16[256,1024]{1,0:T(8,128)(2,1)S(1)}, bf16[256,1024]{1,0:T(8,128)(2,1)S(1)}, u32[]{:S(2)}, u32[]{:S(2)}) collective-permute-start(bf16[256,1024]{1,0:T(8,128)(2,1)S(1)} %out_project.2.refs_2_), channel_id=1, source_target_pairs={{0,1},{1,0},{2,3},{3,2},{4,5},{5,4},{6,7},{7,6},{8,9},{9,8},{10,11... | collective-permute-start | bytes 1572872 | tf_op jit(solution)/shard_map/ppermute | solution.py:20
  73.3 3.6 %collective-permute-start.23 = (bf16[256,1024]{1,0:T(8,128)(2,1)S(1)}, bf16[256,1024]{1,0:T(8,128)(2,1)S(1)}, u32[]{:S(2)}, u32[]{:S(2)}) collective-permute-start(bf16[256,1024]{1,0:T(8,128)(2,1)S(1)} %collective-permute-done.13.refs_4_), channel_id=1, source_target_pairs={{0,1},{1,0},{2,3},{3,2},{4,5},{5,4},{6,7},{7,6},{8,9},{9,8},{10,11... | collective-permute-start | bytes 1572872 | tf_op jit(solution)/shard_map/ppermute | solution.py:20
  73.3 10.4 %collective-permute-start.24 = (bf16[16,2048]{1,0:T(8,128)(2,1)S(1)}, bf16[16,2048]{1,0:T(8,128)(2,1)S(1)}, u32[]{:S(2)}, u32[]{:S(2)}) collective-permute-start(bf16[16,2048]{1,0:T(8,128)(2,1)S(1)} %get-tuple-element.80), channel_id=1, source_target_pairs={{0,2},{1,3},{2,0},{3,1},{4,6},{5,7},{6,4},{7,5},{8,10},{9,11},{10,... | collective-permute-start | bytes 196616 | tf_op jit(solution)/shard_map/ppermute | solution.py:26
  74.6 9.1 %collective-permute-start.25 = (bf16[16,2048]{1,0:T(8,128)(2,1)S(1)}, bf16[16,2048]{1,0:T(8,128)(2,1)S(1)}, u32[]{:S(2)}, u32[]{:S(2)}) collective-permute-start(bf16[16,2048]{1,0:T(8,128)(2,1)S(1)} %get-tuple-element.80), channel_id=1, source_target_pairs={{0,1},{1,0},{2,3},{3,2},{4,5},{5,4},{6,7},{7,6},{8,9},{9,8},{10,11... | collective-permute-start | bytes 196616 | tf_op jit(solution)/shard_map/ppermute | solution.py:33
  74.8 8.9 %collective-permute-start.26 = (bf16[16,2048]{1,0:T(8,128)(2,1)S(1)}, bf16[16,2048]{1,0:T(8,128)(2,1)S(1)}, u32[]{:S(2)}, u32[]{:S(2)}) collective-permute-start(bf16[16,2048]{1,0:T(8,128)(2,1)S(1)} %get-tuple-element.80), channel_id=1, source_target_pairs={{0,3},{1,2},{2,1},{3,0},{4,7},{5,6},{6,5},{7,4},{8,11},{9,10},{10,... | collective-permute-start | bytes 196616 | tf_op jit(solution)/shard_map/ppermute | solution.py:33
  75.6 18.1 %collective-permute-start.21 = (bf16[128,2048]{1,0:T(8,128)(2,1)S(1)}, bf16[128,2048]{1,0:T(8,128)(2,1)S(1)}, u32[]{:S(2)}, u32[]{:S(2)}) collective-permute-start(bf16[128,2048]{1,0:T(8,128)(2,1)S(1)} %add_convert_fusion.1.refs_9_), channel_id=1, source_target_pairs={{0,2},{1,3},{2,0},{3,1},{4,6},{5,7},{6,4},{7,5},{8,10},{9,11},{10,... | collective-permute-start | bytes 1572872 | tf_op jit(solution)/shard_map/ppermute | solution.py:26
  84.0 6.9 %collective-permute-start.27 = (bf16[4,2048]{1,0:T(4,128)(2,1)S(1)}, bf16[4,2048]{1,0:T(4,128)(2,1)S(1)}, u32[]{:S(2)}, u32[]{:S(2)}) collective-permute-start(bf16[4,2048]{1,0:T(4,128)(2,1)S(1)} %get-tuple-element.94), channel_id=1, source_target_pairs={{0,8},{4,12},{8,0},{12,4},{16,24},{20,28},{24,16},{28,20},{1,9},{5... | collective-permute-start | bytes 49160 | tf_op jit(solution)/shard_map/ppermute | solution.py:45
  84.7 6.2 %collective-permute-start.28 = (bf16[4,2048]{1,0:T(4,128)(2,1)S(1)}, bf16[4,2048]{1,0:T(4,128)(2,1)S(1)}, u32[]{:S(2)}, u32[]{:S(2)}) collective-permute-start(bf16[4,2048]{1,0:T(4,128)(2,1)S(1)} %get-tuple-element.96), channel_id=1, source_target_pairs={{0,16},{4,20},{8,24},{12,28},{16,0},{20,4},{24,8},{28,12},{1,17},{... | collective-permute-start | bytes 49160 | tf_op jit(solution)/shard_map/ppermute | solution.py:45
  88.2 5.5 %collective-permute-start.29 = (bf16[4,2048]{1,0:T(4,128)(2,1)S(1)}, bf16[4,2048]{1,0:T(4,128)(2,1)S(1)}, u32[]{:S(2)}, u32[]{:S(2)}) collective-permute-start(bf16[4,2048]{1,0:T(4,128)(2,1)S(1)} %get-tuple-element.95), channel_id=1, source_target_pairs={{0,24},{4,28},{8,16},{12,20},{16,8},{20,12},{24,0},{28,4},{1,25},{... | collective-permute-start | bytes 49160 | tf_op jit(solution)/shard_map/ppermute | solution.py:45
  93.7 2.0 %collective-permute-start.31 = (bf16[128,2048]{1,0:T(8,128)(2,1)S(1)}, bf16[128,2048]{1,0:T(8,128)(2,1)S(1)}, u32[]{:S(2)}, u32[]{:S(2)}) collective-permute-start(bf16[128,2048]{1,0:T(8,128)(2,1)S(1)} %get-tuple-element.87), channel_id=1, source_target_pairs={{0,1},{1,0},{2,3},{3,2},{4,5},{5,4},{6,7},{7,6},{8,9},{9,8},{10,11... | collective-permute-start | bytes 1572872 | tf_op jit(solution)/shard_map/ppermute | solution.py:20
  93.8 3.7 %collective-permute-start.30 = (bf16[2,2048]{1,0:T(2,128)(2,1)S(1)}, bf16[2,2048]{1,0:T(2,128)(2,1)S(1)}, u32[]{:S(2)}, u32[]{:S(2)}) collective-permute-start(bf16[2,2048]{1,0:T(2,128)(2,1)S(1)} %slice.28), channel_id=1, source_target_pairs={{0,4},{4,0},{8,12},{12,8},{16,20},{20,16},{24,28},{28,24},{1,5},{5... | collective-permute-start | bytes 24584 | tf_op jit(solution)/shard_map/ppermute | solution.py:45
  (12 other events, 146.6 us)

commit v13 on v12

--- a/solution.py
+++ b/solution.py
@@ -658,7 +658,7 @@
             entries,
             heads,
             wanted,
-            width // 4 if k else 0,
+            width // 2 if k else 0,
             dec_shares[:1],
         )
         if k == 1:

time: 98.5 us -> 98.5 us (level)
  no operation moved by 1% of the time
where the time goes in v13:
time: 98.5 us; the launch traced here: 98.1 us
  Pallas kernels  47.8 us (49%)
  starting transfers between devices  25.8 us (26%)
  waiting for transfers between devices  10.5 us (11%)
  local copies, waits for them, and re-layouts  6.49 us (7%)
  other arithmetic  5.56 us (6%)
  between operations  1.7 us (2%)
    pallas_call x2, Pallas kernels, feed_forward(): pl.pallas_call(functools.partial(forward_kernel, loads, chips, n_dec, len...  16.9 us
    pallas_call x2, Pallas kernels, fill_attend(): pl.pallas_call(functools.partial(fill_kernel, groups, chips, chunk), out_...  12.6 us
    ppermute x8, starting transfers between devices, swap_groups(): return lax.ppermute(value, 'dp', [(i, i ^ mask) for i in range(count)])  11 us
    pallas_call x2, Pallas kernels, project(): pl.pallas_call(functools.partial(project_kernel, loads, n_dec, len(after)...  9.81 us
    ppermute x7, starting transfers between devices, from_chip(): lax.ppermute(value, 'tensor', [(i, (i // 2 - step) % chips * 2 + i % 2) f...  9.26 us
    unnamed x25, local copies, waits for them, and re-layouts  6.2 us
    pallas_call x1, Pallas kernels, step_attend(): pl.pallas_call(functools.partial(step_kernel, heads), out_shape=jax.Shape...  3.71 us
    ppermute x8, waiting for transfers between devices, swap_groups(): return lax.ppermute(value, 'dp', [(i, i ^ mask) for i in range(count)])  3.68 us
  transfers between devices with their start and end apart: 32, of which 8 were waited for; matrix products, arithmetic and copies ran while one was open for 11% of the time, Pallas kernels for 43%

profile of v13, /device:TPU:0, one launch (start us, length us, event | category | flops | bytes accessed | tf_op | source)
XLA Modules:
  0.0 98.1 jit_solution(7867973625684115307)
XLA Ops:
  1.2 2.6 %collective-permute-start = (bf16[128,2048]{1,0:T(8,128)(2,1)}, bf16[128,2048]{1,0:T(8,128)(2,1)S(1)}, u32[]{:S(2)}, u32[]{:S(2)}) collective-permute-start(bf16[128,2048]{1,0:T(8,128)(2,1)} %refs_0_.3), channel_id=1, source_target_pairs={{0,2},{1,3},{2,0},{3,1},{4,6},{5,7},{6,4},{7,5},{8,10},{9,11},{10,... | collective-permute-start | bytes 1572872 | tf_op jit(solution)/shard_map/ppermute | solution.py:26
  3.7 1.5 %collective-permute-start.3 = (bf16[2,2048]{1,0:T(2,128)(2,1)}, bf16[2,2048]{1,0:T(2,128)(2,1)S(1)}, u32[]{:S(2)}, u32[]{:S(2)}) collective-permute-start(bf16[2,2048]{1,0:T(2,128)(2,1)} %param.15), channel_id=1, source_target_pairs={{0,4},{4,0},{8,12},{12,8},{16,20},{20,16},{24,28},{28,24},{1,5},{5... | collective-permute-start | bytes 24584 | tf_op jit(solution)/shard_map/ppermute | solution.py:45
  6.6 1.0 %fusion = (f32[512,64]{1,0:T(8,128)S(1)}, f32[512,64]{1,0:T(8,128)S(1)}, f32[512,64]{1,0:T(8,128)S(1)}) fusion(f32[64]{0:T(128)S(1)} %negate_power_fusion, f32[512]{0:T(512)S(1)} %add_convert_fusion.7), kind=kLoop, calls=%fused_computation.10 | loop fusion | flops 65536 | bytes 395520 | tf_op jit(solution)/shard_map/neg | solution.py:535
  7.7 0.8 select_reduce_fusion
  9.5 1.6 %collective-permute-start.4 = (bf16[4,2048]{1,0:T(4,128)(2,1)S(1)}, bf16[4,2048]{1,0:T(4,128)(2,1)S(1)}, u32[]{:S(2)}, u32[]{:S(2)}) collective-permute-start(bf16[4,2048]{1,0:T(4,128)(2,1)S(1)} %pad_maximum_fusion.2), channel_id=1, source_target_pairs={{0,8},{4,12},{8,0},{12,4},{16,24},{20,28},{24,16},{28,20},{1,9},{5... | collective-permute-start | bytes 49160 | tf_op jit(solution)/shard_map/ppermute | solution.py:45
  11.2 2.6 %collective-permute-start.5 = (bf16[4,2048]{1,0:T(4,128)(2,1)S(1)}, bf16[4,2048]{1,0:T(4,128)(2,1)S(1)}, u32[]{:S(2)}, u32[]{:S(2)}) collective-permute-start(bf16[4,2048]{1,0:T(4,128)(2,1)S(1)} %pad_maximum_fusion.2), channel_id=1, source_target_pairs={{0,16},{4,20},{8,24},{12,28},{16,0},{20,4},{24,8},{28,12},{1,17},{... | collective-permute-start | bytes 49160 | tf_op jit(solution)/shard_map/ppermute | solution.py:45
  14.2 5.4 %copy.19 = bf16[256,8,2,512]{3,1,2,0:T(8,128)(2,1)} copy(bf16[256,8,2,512]{3,2,1,0:T(2,128)(2,1)} %bitcast.15) | data formatting | bytes 8388608
  20.4 1.6 %collective-permute-start.9 = (bf16[16,2048]{1,0:T(8,128)(2,1)S(1)}, bf16[16,2048]{1,0:T(8,128)(2,1)S(1)}, u32[]{:S(2)}, u32[]{:S(2)}) collective-permute-start(bf16[16,2048]{1,0:T(8,128)(2,1)S(1)} %convolution_convert_fusion.1.refs_6_), channel_id=1, source_target_pairs={{0,3},{1,2},{2,1},{3,0},{4,7},{5,6},{6,5},{7,4},{8,11},{9,10},{10,... | collective-permute-start | bytes 196616 | tf_op jit(solution)/shard_map/ppermute | solution.py:33
  22.1 5.0 %project.2 = (bf16[256,512]{1,0:T(8,128)(2,1)S(1)}, bf16[2,256,256]{2,1,0:T(8,128)(2,1)S(1)}, bf16[2,512,256]{2,1,0:T(8,128)(2,1)}, bf16[2,2048,512]{2,1,0:T(8,128)(2,1)S(1)}) custom-call(s32[5]{0:T(128)S(1)} %stack.24.place, bf16[128,2048]{1,0:T(8,128)(2,1)} %refs_0_.3, bf16[128,2048]{1,0:T(8,128)(2,1)} %collective-permute-done.2.refs_1_, ...), custom_call_target="tpu_custom_call" | custom-call | flops 1073741824 | bytes 6291456 | tf_op jit(solution)/shard_map/project/pallas_call | solution.py:179
  27.2 0.8 copy-done.4
  27.9 4.8 %project.3 = (bf16[256,512]{1,0:T(8,128)(2,1)S(1)}, bf16[2,256,256]{2,1,0:T(8,128)(2,1)S(1)}, bf16[2,512,256]{2,1,0:T(8,128)(2,1)}, f32[16,512]{1,0:T(8,128)S(1)}, bf16[2,8,256]{2,1,0:T(8,128)(2,1)}) custom-call(s32[5]{0:T(128)S(1)} %stack.23.place, bf16[128,2048]{1,0:T(8,128)(2,1)} %copy-done.2, ...), custom_call_target="tpu_custom_call", output_to_operand_aliasing={{2}: (11, {})} | custom-call | flops 1140850688 | bytes 6422528 | tf_op jit(solution)/shard_map/project/pallas_call | solution.py:179
  33.4 5.9 %fill_attend.2 = (bf16[256,512]{1,0:T(8,128)(2,1)S(1)}, bf16[2,8,1024,256]{3,2,1,0:T(8,128)(2,1)S(1)}) custom-call(s32[5]{0:T(128)S(1)} %stack.24.place, bf16[256,512]{1,0:T(8,128)(2,1)S(1)} %get-tuple-element.53.refs_9_.query, bf16[2,1,1024,256]{3,2,1,0:T(8,128)(2,1)} %cache_value.3, bf16[2,1,1024,256]{3,2,1,0:T(8,128)(2,1)} %cache_value.3, ...), custom_call_target="tpu_custom_call" | custom-call | flops 1610612736 | bytes 1048576 | tf_op jit(solution)/shard_map/fill_attend/pallas_call | solution.py:259
  39.4 1.5 %collective-permute-done.10.sib = bf16[256,512]{1,0:T(8,128)(2,1)S(1)} collective-permute-done((bf16[256,512]{1,0:T(8,128)(2,1)S(1)}, bf16[256,512]{1,0:T(8,128)(2,1)S(1)}, u32[]{:S(2)}, u32[]{:S(2)}) %collective-permute-start.10) | collective-permute-done | bytes 262176 | tf_op jit(solution)/shard_map/ppermute | solution.py:20
  40.9 1.2 %out_project.2.refs_2_ = bf16[256,1024]{1,0:T(8,128)(2,1)S(1)} custom-call(s32[5]{0:T(128)S(1)} %stack.24.place, bf16[256,512]{1,0:T(8,128)(2,1)S(1)} %get-tuple-element.59.mine, bf16[256,512]{1,0:T(8,128)(2,1)S(1)} %collective-permute-done.10.sib, bf16[512,2048]{1,0:T(8,128)(2,1)S(1)} %copy-done, bf16[512,2048]{1,0:T(8,128)(2,1)S(1)} %collective-permute-done.11.sib_weight), custom_call_target="tpu_custom_call" | custom-call | flops 536870912 | bytes 3670016 | tf_op jit(solution)/shard_map/out_project/pallas_call | solution.py:375
  42.8 3.7 %step_attend.1.refs_5_.refs_7_ = bf16[16,2048]{1,0:T(8,128)(2,1)S(1)} custom-call(s32[8]{0:T(128)S(1)} %copy-done.10, f32[16,512]{1,0:T(8,128)S(1)} %get-tuple-element.62.query, bf16[2,8,256]{2,1,0:T(8,128)(2,1)S(1)} %copy-done.9, bf16[2,8,1024,256]{3,2,1,0:T(8,128)(2,1)S(1)} %get-tuple-element.64.held, bf16[512,2048]{1,0:T(8,128)(2,1)} %weight.5), custom_call_target="tpu_custom_call" | custom-call | flops 67108864 | bytes 8388608 | tf_op jit(solution)/shard_map/step_attend/pallas_call | solution.py:346
  46.5 6.6 %fill_attend.3 = (bf16[256,512]{1,0:T(8,128)(2,1)S(1)}, bf16[2,2048,1024]{2,1,0:T(8,128)(2,1)S(1)}) custom-call(s32[5]{0:T(128)S(1)} %stack.23.place, bf16[256,512]{1,0:T(8,128)(2,1)S(1)} %get-tuple-element.56.query, bf16[2,1,1024,256]{3,2,1,0:T(8,128)(2,1)} %cache_value.3, bf16[2,1,1024,256]{3,2,1,0:T(8,128)(2,1)} %cache_value.3, ...), custom_call_target="tpu_custom_call" | custom-call | flops 1610612736 | bytes 1048576 | tf_op jit(solution)/shard_map/fill_attend/pallas_call | solution.py:259
  53.2 1.6 %collective-permute-start.16 = (bf16[16,2048]{1,0:T(8,128)(2,1)S(1)}, bf16[16,2048]{1,0:T(8,128)(2,1)S(1)}, u32[]{:S(2)}, u32[]{:S(2)}) collective-permute-start(bf16[16,2048]{1,0:T(8,128)(2,1)S(1)} %step_attend.1.refs_5_.refs_7_), channel_id=1, source_target_pairs={{0,2},{1,3},{2,0},{3,1},{4,6},{5,7},{6,4},{7,5},{8,10},{9,11},{10,... | collective-permute-start | bytes 196616 | tf_op jit(solution)/shard_map/ppermute | solution.py:26
  55.4 1.2 %out_project.3.refs_2_ = bf16[256,1024]{1,0:T(8,128)(2,1)S(1)} custom-call(s32[5]{0:T(128)S(1)} %stack.23.place, bf16[256,512]{1,0:T(8,128)(2,1)S(1)} %get-tuple-element.65.mine, bf16[256,512]{1,0:T(8,128)(2,1)S(1)} %collective-permute-done.12.sib, bf16[512,2048]{1,0:T(8,128)(2,1)S(1)} %copy-done.1, bf16[512,2048]{1,0:T(8,128)(2,1)S(1)} %collective-permute-done.11.sib_weight), custom_call_target="tpu_custom_call" | custom-call | flops 536870912 | bytes 3670016 | tf_op jit(solution)/shard_map/out_project/pallas_call | solution.py:375
  56.9 0.8 collective-permute-done.16.refs_8_
  57.7 1.2 %collective-permute-done.18.refs_10_ = bf16[16,2048]{1,0:T(8,128)(2,1)S(1)} collective-permute-done((bf16[16,2048]{1,0:T(8,128)(2,1)S(1)}, bf16[16,2048]{1,0:T(8,128)(2,1)S(1)}, u32[]{:S(2)}, u32[]{:S(2)}) %collective-permute-start.18) | collective-permute-done | bytes 65568 | tf_op jit(solution)/shard_map/ppermute | solution.py:33
  59.2 1.3 %collective-permute-start.13 = (bf16[256,1024]{1,0:T(8,128)(2,1)S(1)}, bf16[256,1024]{1,0:T(8,128)(2,1)S(1)}, u32[]{:S(2)}, u32[]{:S(2)}) collective-permute-start(bf16[256,1024]{1,0:T(8,128)(2,1)S(1)} %out_project.3.refs_2_), channel_id=1, source_target_pairs={{0,2},{1,3},{2,0},{3,1},{4,6},{5,7},{6,4},{7,5},{8,10},{9,11},{10,... | collective-permute-start | bytes 1572872 | tf_op jit(solution)/shard_map/ppermute | solution.py:26
  60.8 10.2 %feed_forward.2 = (bf16[128,2048]{1,0:T(8,128)(2,1)S(1)}, bf16[128,2048]{1,0:T(8,128)(2,1)S(1)}, bf16[128,2048]{1,0:T(8,128)(2,1)}, bf16[16,2048]{1,0:T(8,128)(2...) custom-call(s32[5]{0:T(128)S(1)} %stack.23.place, ...), custom_call_target="tpu_custom_call" | custom-call | flops 6845104128 | bytes 25165824 | tf_op jit(solution)/shard_map/feed_forward/pallas_call | solution.py:514
  71.6 1.6 %collective-permute-done.13.refs_4_ = bf16[256,1024]{1,0:T(8,128)(2,1)S(1)} collective-permute-done((bf16[256,1024]{1,0:T(8,128)(2,1)S(1)}, bf16[256,1024]{1,0:T(8,128)(2,1)S(1)}, u32[]{:S(2)}, u32[]{:S(2)}) %collective-permute-start.13) | collective-permute-done | bytes 524320 | tf_op jit(solution)/shard_map/ppermute | solution.py:26
  73.2 1.3 %collective-permute-start.24 = (bf16[16,2048]{1,0:T(8,128)(2,1)S(1)}, bf16[16,2048]{1,0:T(8,128)(2,1)S(1)}, u32[]{:S(2)}, u32[]{:S(2)}) collective-permute-start(bf16[16,2048]{1,0:T(8,128)(2,1)S(1)} %get-tuple-element.80), channel_id=1, source_target_pairs={{0,2},{1,3},{2,0},{3,1},{4,6},{5,7},{6,4},{7,5},{8,10},{9,11},{10,... | collective-permute-start | bytes 196616 | tf_op jit(solution)/shard_map/ppermute | solution.py:26
  75.5 1.4 %collective-permute-start.21 = (bf16[128,2048]{1,0:T(8,128)(2,1)S(1)}, bf16[128,2048]{1,0:T(8,128)(2,1)S(1)}, u32[]{:S(2)}, u32[]{:S(2)}) collective-permute-start(bf16[128,2048]{1,0:T(8,128)(2,1)S(1)} %add_convert_fusion.1.refs_9_), channel_id=1, source_target_pairs={{0,2},{1,3},{2,0},{3,1},{4,6},{5,7},{6,4},{7,5},{8,10},{9,11},{10,... | collective-permute-start | bytes 1572872 | tf_op jit(solution)/shard_map/ppermute | solution.py:26
  76.9 6.7 %feed_forward.3 = (bf16[128,2048]{1,0:T(8,128)(2,1)S(1)}, bf16[256,2048]{1,0:T(8,128)(2,1)S(1)}) custom-call(s32[5]{0:T(128)S(1)} %stack.24.place, bf16[128,2048]{1,0:T(8,128)(2,1)S(1)} %copy-done.6, bf16[128,2048]{1,0:T(8,128)(2,1)} %collective-permute-done.2.refs_1_, bf16[256,1024]{1,0:T(8,128)(2,1)S(1)} %out_project.2.refs_2_, ...), custom_call_target="tpu_custom_call" | custom-call | flops 6442450944 | bytes 25165824 | tf_op jit(solution)/shard_map/feed_forward/pallas_call | solution.py:514
  83.9 0.7 collective-permute-start.27
  84.6 3.5 %collective-permute-start.28 = (bf16[4,2048]{1,0:T(4,128)(2,1)S(1)}, bf16[4,2048]{1,0:T(4,128)(2,1)S(1)}, u32[]{:S(2)}, u32[]{:S(2)}) collective-permute-start(bf16[4,2048]{1,0:T(4,128)(2,1)S(1)} %get-tuple-element.96), channel_id=1, source_target_pairs={{0,16},{4,20},{8,24},{12,28},{16,0},{20,4},{24,8},{28,12},{1,17},{... | collective-permute-start | bytes 49160 | tf_op jit(solution)/shard_map/ppermute | solution.py:45
  88.3 2.3 %lower.1 = (bf16[128,2048]{1,0:T(8,128)(2,1)S(1)}, bf16[128,2048]{1,0:T(8,128)(2,1)S(1)}) custom-call(bf16[256,2048]{1,0:T(8,128)(2,1)S(1)} %get-tuple-element.81.hidden, bf16[2,2048,1024]{2,1,0:T(8,128)(2,1)S(1)} %get-tuple-element.82.down, bf16[16,2048]{1,0:T(8,128)(2,1)S(1)} %convolution_convert_fusion.refs_0_), custom_call_target="tpu_custom_call" | custom-call | flops 2147483648 | bytes 8388608 | tf_op jit(solution)/shard_map/lower/pallas_call | solution.py:479
  90.7 2.9 %collective-permute-done.29 = bf16[4,2048]{1,0:T(4,128)(2,1)S(1)} collective-permute-done((bf16[4,2048]{1,0:T(4,128)(2,1)S(1)}, bf16[4,2048]{1,0:T(4,128)(2,1)S(1)}, u32[]{:S(2)}, u32[]{:S(2)}) %collective-permute-start.29) | collective-permute-done | bytes 16416 | tf_op jit(solution)/shard_map/ppermute | solution.py:45
  94.4 1.3 %collective-permute-done.31 = bf16[128,2048]{1,0:T(8,128)(2,1)S(1)} collective-permute-done((bf16[128,2048]{1,0:T(8,128)(2,1)S(1)}, bf16[128,2048]{1,0:T(8,128)(2,1)S(1)}, u32[]{:S(2)}, u32[]{:S(2)}) %collective-permute-start.31) | collective-permute-done | bytes 524320 | tf_op jit(solution)/shard_map/ppermute | solution.py:20
  95.7 1.1 %add_convert_fusion = bf16[128,2048]{1,0:T(8,128)(2,1)} fusion(bf16[128,2048]{1,0:T(8,128)(2,1)S(1)} %collective-permute-done.21, bf16[128,2048]{1,0:T(8,128)(2,1)S(1)} %collective-permute-done.31, bf16[128,2048]{1,0:T(8,128)(2,1)S(1)} %get-tuple-element.86, bf16[128,2048]{1,0:T(8,128)(2,1)S(1)} %get-tuple-element.85), kind=kLoop, calls=%fused_computation.2 | loop fusion | flops 2097152 | bytes 2621440 | tf_op jit(solution)/shard_map/convert_element_type | solution.py:542
  (90 shorter events, 10.6 us)
Async XLA Ops:
  0.7 21.4 %collective-permute-start.2 = (bf16[128,2048]{1,0:T(8,128)(2,1)}, bf16[128,2048]{1,0:T(8,128)(2,1)}, u32[]{:S(2)}, u32[]{:S(2)}) collective-permute-start(bf16[128,2048]{1,0:T(8,128)(2,1)} %refs_0_.3), channel_id=1, source_target_pairs={{0,1},{1,0},{2,3},{3,2},{4,5},{5,4},{6,7},{7,6},{8,9},{9,8},{10,11... | collective-permute-start | bytes 1572872 | tf_op jit(solution)/shard_map/ppermute | solution.py:20
  1.2 20.9 %collective-permute-start = (bf16[128,2048]{1,0:T(8,128)(2,1)}, bf16[128,2048]{1,0:T(8,128)(2,1)S(1)}, u32[]{:S(2)}, u32[]{:S(2)}) collective-permute-start(bf16[128,2048]{1,0:T(8,128)(2,1)} %refs_0_.3), channel_id=1, source_target_pairs={{0,2},{1,3},{2,0},{3,1},{4,6},{5,7},{6,4},{7,5},{8,10},{9,11},{10,... | collective-permute-start | bytes 1572872 | tf_op jit(solution)/shard_map/ppermute | solution.py:26
  3.7 5.1 %collective-permute-start.3 = (bf16[2,2048]{1,0:T(2,128)(2,1)}, bf16[2,2048]{1,0:T(2,128)(2,1)S(1)}, u32[]{:S(2)}, u32[]{:S(2)}) collective-permute-start(bf16[2,2048]{1,0:T(2,128)(2,1)} %param.15), channel_id=1, source_target_pairs={{0,4},{4,0},{8,12},{12,8},{16,20},{20,16},{24,28},{28,24},{1,5},{5... | collective-permute-start | bytes 24584 | tf_op jit(solution)/shard_map/ppermute | solution.py:45
  9.5 10.1 %collective-permute-start.4 = (bf16[4,2048]{1,0:T(4,128)(2,1)S(1)}, bf16[4,2048]{1,0:T(4,128)(2,1)S(1)}, u32[]{:S(2)}, u32[]{:S(2)}) collective-permute-start(bf16[4,2048]{1,0:T(4,128)(2,1)S(1)} %pad_maximum_fusion.2), channel_id=1, source_target_pairs={{0,8},{4,12},{8,0},{12,4},{16,24},{20,28},{24,16},{28,20},{1,9},{5... | collective-permute-start | bytes 49160 | tf_op jit(solution)/shard_map/ppermute | solution.py:45
  11.2 8.4 %collective-permute-start.5 = (bf16[4,2048]{1,0:T(4,128)(2,1)S(1)}, bf16[4,2048]{1,0:T(4,128)(2,1)S(1)}, u32[]{:S(2)}, u32[]{:S(2)}) collective-permute-start(bf16[4,2048]{1,0:T(4,128)(2,1)S(1)} %pad_maximum_fusion.2), channel_id=1, source_target_pairs={{0,16},{4,20},{8,24},{12,28},{16,0},{20,4},{24,8},{28,12},{1,17},{... | collective-permute-start | bytes 49160 | tf_op jit(solution)/shard_map/ppermute | solution.py:45
  13.8 5.8 %collective-permute-start.6 = (bf16[4,2048]{1,0:T(4,128)(2,1)S(1)}, bf16[4,2048]{1,0:T(4,128)(2,1)S(1)}, u32[]{:S(2)}, u32[]{:S(2)}) collective-permute-start(bf16[4,2048]{1,0:T(4,128)(2,1)S(1)} %pad_maximum_fusion.2), channel_id=1, source_target_pairs={{0,24},{4,28},{8,16},{12,20},{16,8},{20,12},{24,0},{28,4},{1,25},{... | collective-permute-start | bytes 49160 | tf_op jit(solution)/shard_map/ppermute | solution.py:45
  19.8 7.2 %collective-permute-start.7 = (bf16[16,2048]{1,0:T(8,128)(2,1)S(1)}, bf16[16,2048]{1,0:T(8,128)(2,1)S(1)}, u32[]{:S(2)}, u32[]{:S(2)}) collective-permute-start(bf16[16,2048]{1,0:T(8,128)(2,1)S(1)} %convolution_convert_fusion.1.refs_6_), channel_id=1, source_target_pairs={{0,2},{1,3},{2,0},{3,1},{4,6},{5,7},{6,4},{7,5},{8,10},{9,11},{10,... | collective-permute-start | bytes 196616 | tf_op jit(solution)/shard_map/ppermute | solution.py:26
  20.4 6.6 %collective-permute-start.8 = (bf16[16,2048]{1,0:T(8,128)(2,1)S(1)}, bf16[16,2048]{1,0:T(8,128)(2,1)S(1)}, u32[]{:S(2)}, u32[]{:S(2)}) collective-permute-start(bf16[16,2048]{1,0:T(8,128)(2,1)S(1)} %convolution_convert_fusion.1.refs_6_), channel_id=1, source_target_pairs={{0,1},{1,0},{2,3},{3,2},{4,5},{5,4},{6,7},{7,6},{8,9},{9,8},{10,11... | collective-permute-start | bytes 196616 | tf_op jit(solution)/shard_map/ppermute | solution.py:33
  20.4 6.6 %collective-permute-start.9 = (bf16[16,2048]{1,0:T(8,128)(2,1)S(1)}, bf16[16,2048]{1,0:T(8,128)(2,1)S(1)}, u32[]{:S(2)}, u32[]{:S(2)}) collective-permute-start(bf16[16,2048]{1,0:T(8,128)(2,1)S(1)} %convolution_convert_fusion.1.refs_6_), channel_id=1, source_target_pairs={{0,3},{1,2},{2,1},{3,0},{4,7},{5,6},{6,5},{7,4},{8,11},{9,10},{10,... | collective-permute-start | bytes 196616 | tf_op jit(solution)/shard_map/ppermute | solution.py:33
  22.1 5.1 %collective-permute-start.1 = (bf16[128,2048]{1,0:T(8,128)(2,1)S(1)}, bf16[128,2048]{1,0:T(8,128)(2,1)S(1)}, u32[]{:S(2)}, u32[]{:S(2)}) collective-permute-start(bf16[128,2048]{1,0:T(8,128)(2,1)S(1)} %collective-permute-done.refs_0_), channel_id=1, source_target_pairs={{0,1},{1,0},{2,3},{3,2},{4,5},{5,4},{6,7},{7,6},{8,9},{9,8},{10,11... | collective-permute-start | bytes 1572872 | tf_op jit(solution)/shard_map/ppermute | solution.py:20
  32.8 8.1 %collective-permute-start.11 = (bf16[512,2048]{1,0:T(8,128)(2,1)S(1)}, bf16[512,2048]{1,0:T(8,128)(2,1)S(1)}, u32[]{:S(2)}, u32[]{:S(2)}) collective-permute-start(bf16[512,2048]{1,0:T(8,128)(2,1)S(1)} %copy-done), channel_id=1, source_target_pairs={{0,1},{1,0},{2,3},{3,2},{4,5},{5,4},{6,7},{7,6},{8,9},{9,8},{10,11... | collective-permute-start | bytes 6291464 | tf_op jit(solution)/shard_map/ppermute | solution.py:20
  39.3 1.6 %collective-permute-start.10 = (bf16[256,512]{1,0:T(8,128)(2,1)S(1)}, bf16[256,512]{1,0:T(8,128)(2,1)S(1)}, u32[]{:S(2)}, u32[]{:S(2)}) collective-permute-start(bf16[256,512]{1,0:T(8,128)(2,1)S(1)} %get-tuple-element.59.mine), channel_id=1, source_target_pairs={{0,1},{1,0},{2,3},{3,2},{4,5},{5,4},{6,7},{7,6},{8,9},{9,8},{10,11... | collective-permute-start | bytes 786440 | tf_op jit(solution)/shard_map/ppermute | solution.py:20
  42.2 16.7 %collective-permute-start.15 = (bf16[256,1024]{1,0:T(8,128)(2,1)S(1)}, bf16[256,1024]{1,0:T(8,128)(2,1)S(1)}, u32[]{:S(2)}, u32[]{:S(2)}) collective-permute-start(bf16[256,1024]{1,0:T(8,128)(2,1)S(1)} %out_project.2.refs_2_), channel_id=1, source_target_pairs={{0,2},{1,3},{2,0},{3,1},{4,6},{5,7},{6,4},{7,5},{8,10},{9,11},{10,... | collective-permute-start | bytes 1572872 | tf_op jit(solution)/shard_map/ppermute | solution.py:26
  53.2 2.3 %collective-permute-start.12 = (bf16[256,512]{1,0:T(8,128)(2,1)S(1)}, bf16[256,512]{1,0:T(8,128)(2,1)S(1)}, u32[]{:S(2)}, u32[]{:S(2)}) collective-permute-start(bf16[256,512]{1,0:T(8,128)(2,1)S(1)} %get-tuple-element.65.mine), channel_id=1, source_target_pairs={{0,1},{1,0},{2,3},{3,2},{4,5},{5,4},{6,7},{7,6},{8,9},{9,8},{10,11... | collective-permute-start | bytes 786440 | tf_op jit(solution)/shard_map/ppermute | solution.py:20
  53.2 4.5 %collective-permute-start.16 = (bf16[16,2048]{1,0:T(8,128)(2,1)S(1)}, bf16[16,2048]{1,0:T(8,128)(2,1)S(1)}, u32[]{:S(2)}, u32[]{:S(2)}) collective-permute-start(bf16[16,2048]{1,0:T(8,128)(2,1)S(1)} %step_attend.1.refs_5_.refs_7_), channel_id=1, source_target_pairs={{0,2},{1,3},{2,0},{3,1},{4,6},{5,7},{6,4},{7,5},{8,10},{9,11},{10,... | collective-permute-start | bytes 196616 | tf_op jit(solution)/shard_map/ppermute | solution.py:26
  54.8 3.0 %collective-permute-start.17 = (bf16[16,2048]{1,0:T(8,128)(2,1)S(1)}, bf16[16,2048]{1,0:T(8,128)(2,1)S(1)}, u32[]{:S(2)}, u32[]{:S(2)}) collective-permute-start(bf16[16,2048]{1,0:T(8,128)(2,1)S(1)} %step_attend.1.refs_5_.refs_7_), channel_id=1, source_target_pairs={{0,1},{1,0},{2,3},{3,2},{4,5},{5,4},{6,7},{7,6},{8,9},{9,8},{10,11... | collective-permute-start | bytes 196616 | tf_op jit(solution)/shard_map/ppermute | solution.py:33
  55.0 3.9 %collective-permute-start.18 = (bf16[16,2048]{1,0:T(8,128)(2,1)S(1)}, bf16[16,2048]{1,0:T(8,128)(2,1)S(1)}, u32[]{:S(2)}, u32[]{:S(2)}) collective-permute-start(bf16[16,2048]{1,0:T(8,128)(2,1)S(1)} %step_attend.1.refs_5_.refs_7_), channel_id=1, source_target_pairs={{0,3},{1,2},{2,1},{3,0},{4,7},{5,6},{6,5},{7,4},{8,11},{9,10},{10,... | collective-permute-start | bytes 196616 | tf_op jit(solution)/shard_map/ppermute | solution.py:33
  56.7 3.8 %collective-permute-start.14 = (bf16[256,1024]{1,0:T(8,128)(2,1)S(1)}, bf16[256,1024]{1,0:T(8,128)(2,1)S(1)}, u32[]{:S(2)}, u32[]{:S(2)}) collective-permute-start(bf16[256,1024]{1,0:T(8,128)(2,1)S(1)} %out_project.3.refs_2_), channel_id=1, source_target_pairs={{0,1},{1,0},{2,3},{3,2},{4,5},{5,4},{6,7},{7,6},{8,9},{9,8},{10,11... | collective-permute-start | bytes 1572872 | tf_op jit(solution)/shard_map/ppermute | solution.py:20
  58.9 1.9 %collective-permute-start.19 = (bf16[256,1024]{1,0:T(8,128)(2,1)S(1)}, bf16[256,1024]{1,0:T(8,128)(2,1)S(1)}, u32[]{:S(2)}, u32[]{:S(2)}) collective-permute-start(bf16[256,1024]{1,0:T(8,128)(2,1)S(1)} %collective-permute-done.15.refs_4_), channel_id=1, source_target_pairs={{0,1},{1,0},{2,3},{3,2},{4,5},{5,4},{6,7},{7,6},{8,9},{9,8},{10,11... | collective-permute-start | bytes 1572872 | tf_op jit(solution)/shard_map/ppermute | solution.py:20
  59.2 14.1 %collective-permute-start.13 = (bf16[256,1024]{1,0:T(8,128)(2,1)S(1)}, bf16[256,1024]{1,0:T(8,128)(2,1)S(1)}, u32[]{:S(2)}, u32[]{:S(2)}) collective-permute-start(bf16[256,1024]{1,0:T(8,128)(2,1)S(1)} %out_project.3.refs_2_), channel_id=1, source_target_pairs={{0,2},{1,3},{2,0},{3,1},{4,6},{5,7},{6,4},{7,5},{8,10},{9,11},{10,... | collective-permute-start | bytes 1572872 | tf_op jit(solution)/shard_map/ppermute | solution.py:26
  71.0 3.7 %collective-permute-start.20 = (bf16[128,2048]{1,0:T(8,128)(2,1)S(1)}, bf16[128,2048]{1,0:T(8,128)(2,1)S(1)}, u32[]{:S(2)}, u32[]{:S(2)}) collective-permute-start(bf16[128,2048]{1,0:T(8,128)(2,1)S(1)} %get-tuple-element.74), channel_id=1, source_target_pairs={{0,1},{1,0},{2,3},{3,2},{4,5},{5,4},{6,7},{7,6},{8,9},{9,8},{10,11... | collective-permute-start | bytes 1572872 | tf_op jit(solution)/shard_map/ppermute | solution.py:20
  71.4 4.2 %collective-permute-start.22 = (bf16[256,1024]{1,0:T(8,128)(2,1)S(1)}, bf16[256,1024]{1,0:T(8,128)(2,1)S(1)}, u32[]{:S(2)}, u32[]{:S(2)}) collective-permute-start(bf16[256,1024]{1,0:T(8,128)(2,1)S(1)} %out_project.2.refs_2_), channel_id=1, source_target_pairs={{0,1},{1,0},{2,3},{3,2},{4,5},{5,4},{6,7},{7,6},{8,9},{9,8},{10,11... | collective-permute-start | bytes 1572872 | tf_op jit(solution)/shard_map/ppermute | solution.py:20
  73.2 3.6 %collective-permute-start.23 = (bf16[256,1024]{1,0:T(8,128)(2,1)S(1)}, bf16[256,1024]{1,0:T(8,128)(2,1)S(1)}, u32[]{:S(2)}, u32[]{:S(2)}) collective-permute-start(bf16[256,1024]{1,0:T(8,128)(2,1)S(1)} %collective-permute-done.13.refs_4_), channel_id=1, source_target_pairs={{0,1},{1,0},{2,3},{3,2},{4,5},{5,4},{6,7},{7,6},{8,9},{9,8},{10,11... | collective-permute-start | bytes 1572872 | tf_op jit(solution)/shard_map/ppermute | solution.py:20
  73.2 10.4 %collective-permute-start.24 = (bf16[16,2048]{1,0:T(8,128)(2,1)S(1)}, bf16[16,2048]{1,0:T(8,128)(2,1)S(1)}, u32[]{:S(2)}, u32[]{:S(2)}) collective-permute-start(bf16[16,2048]{1,0:T(8,128)(2,1)S(1)} %get-tuple-element.80), channel_id=1, source_target_pairs={{0,2},{1,3},{2,0},{3,1},{4,6},{5,7},{6,4},{7,5},{8,10},{9,11},{10,... | collective-permute-start | bytes 196616 | tf_op jit(solution)/shard_map/ppermute | solution.py:26
  74.5 9.1 %collective-permute-start.25 = (bf16[16,2048]{1,0:T(8,128)(2,1)S(1)}, bf16[16,2048]{1,0:T(8,128)(2,1)S(1)}, u32[]{:S(2)}, u32[]{:S(2)}) collective-permute-start(bf16[16,2048]{1,0:T(8,128)(2,1)S(1)} %get-tuple-element.80), channel_id=1, source_target_pairs={{0,1},{1,0},{2,3},{3,2},{4,5},{5,4},{6,7},{7,6},{8,9},{9,8},{10,11... | collective-permute-start | bytes 196616 | tf_op jit(solution)/shard_map/ppermute | solution.py:33
  74.8 8.9 %collective-permute-start.26 = (bf16[16,2048]{1,0:T(8,128)(2,1)S(1)}, bf16[16,2048]{1,0:T(8,128)(2,1)S(1)}, u32[]{:S(2)}, u32[]{:S(2)}) collective-permute-start(bf16[16,2048]{1,0:T(8,128)(2,1)S(1)} %get-tuple-element.80), channel_id=1, source_target_pairs={{0,3},{1,2},{2,1},{3,0},{4,7},{5,6},{6,5},{7,4},{8,11},{9,10},{10,... | collective-permute-start | bytes 196616 | tf_op jit(solution)/shard_map/ppermute | solution.py:33
  75.5 18.1 %collective-permute-start.21 = (bf16[128,2048]{1,0:T(8,128)(2,1)S(1)}, bf16[128,2048]{1,0:T(8,128)(2,1)S(1)}, u32[]{:S(2)}, u32[]{:S(2)}) collective-permute-start(bf16[128,2048]{1,0:T(8,128)(2,1)S(1)} %add_convert_fusion.1.refs_9_), channel_id=1, source_target_pairs={{0,2},{1,3},{2,0},{3,1},{4,6},{5,7},{6,4},{7,5},{8,10},{9,11},{10,... | collective-permute-start | bytes 1572872 | tf_op jit(solution)/shard_map/ppermute | solution.py:26
  83.9 6.8 %collective-permute-start.27 = (bf16[4,2048]{1,0:T(4,128)(2,1)S(1)}, bf16[4,2048]{1,0:T(4,128)(2,1)S(1)}, u32[]{:S(2)}, u32[]{:S(2)}) collective-permute-start(bf16[4,2048]{1,0:T(4,128)(2,1)S(1)} %get-tuple-element.94), channel_id=1, source_target_pairs={{0,8},{4,12},{8,0},{12,4},{16,24},{20,28},{24,16},{28,20},{1,9},{5... | collective-permute-start | bytes 49160 | tf_op jit(solution)/shard_map/ppermute | solution.py:45
  84.6 6.1 %collective-permute-start.28 = (bf16[4,2048]{1,0:T(4,128)(2,1)S(1)}, bf16[4,2048]{1,0:T(4,128)(2,1)S(1)}, u32[]{:S(2)}, u32[]{:S(2)}) collective-permute-start(bf16[4,2048]{1,0:T(4,128)(2,1)S(1)} %get-tuple-element.96), channel_id=1, source_target_pairs={{0,16},{4,20},{8,24},{12,28},{16,0},{20,4},{24,8},{28,12},{1,17},{... | collective-permute-start | bytes 49160 | tf_op jit(solution)/shard_map/ppermute | solution.py:45
  88.1 5.5 %collective-permute-start.29 = (bf16[4,2048]{1,0:T(4,128)(2,1)S(1)}, bf16[4,2048]{1,0:T(4,128)(2,1)S(1)}, u32[]{:S(2)}, u32[]{:S(2)}) collective-permute-start(bf16[4,2048]{1,0:T(4,128)(2,1)S(1)} %get-tuple-element.95), channel_id=1, source_target_pairs={{0,24},{4,28},{8,16},{12,20},{16,8},{20,12},{24,0},{28,4},{1,25},{... | collective-permute-start | bytes 49160 | tf_op jit(solution)/shard_map/ppermute | solution.py:45
  93.7 2.0 %collective-permute-start.31 = (bf16[128,2048]{1,0:T(8,128)(2,1)S(1)}, bf16[128,2048]{1,0:T(8,128)(2,1)S(1)}, u32[]{:S(2)}, u32[]{:S(2)}) collective-permute-start(bf16[128,2048]{1,0:T(8,128)(2,1)S(1)} %get-tuple-element.87), channel_id=1, source_target_pairs={{0,1},{1,0},{2,3},{3,2},{4,5},{5,4},{6,7},{7,6},{8,9},{9,8},{10,11... | collective-permute-start | bytes 1572872 | tf_op jit(solution)/shard_map/ppermute | solution.py:20
  93.8 3.7 %collective-permute-start.30 = (bf16[2,2048]{1,0:T(2,128)(2,1)S(1)}, bf16[2,2048]{1,0:T(2,128)(2,1)S(1)}, u32[]{:S(2)}, u32[]{:S(2)}) collective-permute-start(bf16[2,2048]{1,0:T(2,128)(2,1)S(1)} %slice.28), channel_id=1, source_target_pairs={{0,4},{4,0},{8,12},{12,8},{16,20},{20,16},{24,28},{28,24},{1,5},{5... | collective-permute-start | bytes 24584 | tf_op jit(solution)/shard_map/ppermute | solution.py:45
  (12 other events, 146.3 us)
